TPU v7x, 128 devices: a whole 4x4x4 slice. The times are simulated.
128 devices in a mesh: shard: 4 (over x), rep: 32 (over y, z, core).
Axes of the slice: x: 4, y: 4, z: 4, core: 2. Of those that a mesh axis runs over, the one named last changes fastest.
Arguments:
- tokens: bfloat16 [65536, 8192], P('rep', 'shard'), may hold values from -21 to 21
- key_cotangent: bfloat16 [65536, 1024], P('rep'), may hold values from -21 to 21
- value_cotangent: bfloat16 [65536, 1024], P('rep'), may hold values from -21 to 21
- key_weight: float32 [8192, 1024], P(('shard', 'rep')), may hold values from -0.75 to 0.75
- value_weight: float32 [8192, 1024], P(('shard', 'rep')), may hold values from -0.75 to 0.75
- key_moment: float32 [8192, 1024], P(('shard', 'rep')), may hold values from -6 to 6
- value_moment: float32 [8192, 1024], P(('shard', 'rep')), may hold values from -6 to 6
Outputs:
- new_key_weight: float32 [8192, 1024], P(('shard', 'rep'))
- new_value_weight: float32 [8192, 1024], P(('shard', 'rep'))
- new_key_moment: float32 [8192, 1024], P(('shard', 'rep'))
- new_value_moment: float32 [8192, 1024], P(('shard', 'rep'))
All inputs are finite; a program needn't handle non-finite values.
Results may differ from a plain program's by a relative error of at most 0.0003.
Values may be sent and summed in bfloat16 or wider, within the bound.
No kernel may reach another device: no remote copies, remote signals or barrier semaphores. Data moves between devices by JAX's collectives and lax.ppermute only.
A program may use at most 128 MiB of HBM per device.

v0:
```python
import math

import jax
import jax.numpy as jnp
from jax import lax
from jax.sharding import PartitionSpec as P

EPSILON = 1e-06
MOMENTUM_DECAY = 0.9
STEP_SIZE = 0.01


def from_partner(block, axis, apart):
    count = lax.axis_size(axis)
    route = []
    for low in range(count):
        high = low | 1 << apart
        if high != low and high < count:
            route += [(low, high), (high, low)]
    return lax.ppermute(block, axis, route)


def weight_grads(token_rows, cotangents):
    factor = 1.0 / math.sqrt(token_rows.shape[0])
    product = lax.dot_general(
        token_rows, cotangents, (((0,), (0,)), ((), ())), preferred_element_type=jnp.float32
    )
    return product * factor


def group_total(partials, level_index):
    summed = lax.psum(partials, "shard")
    for bit_index in range(level_index + 1):
        summed = summed + from_partner(summed, "rep", bit_index)
    return summed


def merge_pair(own_part, partner_part, own_bit, level_index):
    cross = jnp.sum(own_part * partner_part, axis=(0, 1, 3))
    own_square = jnp.sum(own_part * own_part, axis=(0, 1, 3))
    partner_square = jnp.sum(partner_part * partner_part, axis=(0, 1, 3))
    is_first = own_bit == 0
    first_square = jnp.where(is_first, own_square, partner_square)
    second_square = jnp.where(is_first, partner_square, own_square)
    partials = jnp.stack([cross, first_square, second_square])
    totals = group_total(partials, level_index)
    first_coef = 1.0 - totals[0] / (2.0 * (totals[1] + EPSILON))
    second_coef = 1.0 - totals[0] / (2.0 * (totals[2] + EPSILON))
    own_coef = jnp.where(is_first, first_coef, second_coef)[:, None]
    partner_coef = jnp.where(is_first, second_coef, first_coef)[:, None]
    return own_coef * own_part + partner_coef * partner_part


def halve_and_merge(region, level_index, device_index):
    own_bit = device_index >> level_index & 1
    paired = region.reshape((region.shape[0] // 2, 2) + region.shape[1:])
    kept = lax.dynamic_index_in_dim(paired, own_bit, 1, keepdims=False)
    outgoing = lax.dynamic_index_in_dim(paired, 1 - own_bit, 1, keepdims=False)
    arrived = from_partner(outgoing, "rep", level_index)
    return merge_pair(kept, arrived, own_bit, level_index)


def shards(
    tokens, key_cotangent, value_cotangent, key_weight, value_weight, key_moment, value_moment
):
    replicas = lax.axis_size("rep")
    device_index = lax.axis_index("rep")
    local_width = tokens.shape[1]
    features = key_cotangent.shape[1]
    block_rows = local_width // replicas
    levels = replicas.bit_length() - 1
    cotangents = jnp.concatenate([key_cotangent, value_cotangent], axis=1)
    region = weight_grads(tokens, cotangents).reshape(replicas, block_rows, 2, features)
    first_level = 0
    for level_index in range(first_level, levels):
        region = halve_and_merge(region, level_index, device_index)
    merged = region[0]
    new_key_moment = MOMENTUM_DECAY * key_moment + merged[:, 0, :]
    new_value_moment = MOMENTUM_DECAY * value_moment + merged[:, 1, :]
    new_key_weight = key_weight - STEP_SIZE * new_key_moment
    new_value_weight = value_weight - STEP_SIZE * new_value_moment
    return (new_key_weight, new_value_weight, new_key_moment, new_value_moment)


def solution(mesh):
    in_specs = (
        P("rep", "shard"),
        P("rep", None),
        P("rep", None),
        P(("shard", "rep"), None),
        P(("shard", "rep"), None),
        P(("shard", "rep"), None),
        P(("shard", "rep"), None),
    )
    out_specs = (
        P(("shard", "rep"), None),
        P(("shard", "rep"), None),
        P(("shard", "rep"), None),
        P(("shard", "rep"), None),
    )
    return jax.shard_map(shards, mesh=mesh, in_specs=in_specs, out_specs=out_specs, check_vma=False)
```

profile of v0, /device:TPU:1, one launch (start us, length us, event | category | flops | bytes accessed | tf_op | source)
XLA Modules:
  0.0 415.5 jit_solution(910739341039906963)
XLA Ops:
  0.6 24.6 %multiply_bitcast_fusion = f32[2048,2048]{0,1:T(8,128)} fusion(bf16[2048,2048]{1,0:T(8,128)(2,1)} %param.7, bf16[2048,1024]{1,0:T(8,128)(2,1)} %param.9, bf16[2048,1024]{1,0:T(8,128)(2,1)} %param.8), kind=kOutput, calls=%fused_computation | convolution fusion | flops 17200840704 | bytes 33554432 | tf_op jit(solution)/shard_map/dot_general | solution.py:25
  25.2 17.6 %copy.14 = f32[2048,2048]{1,0:T(8,128)} copy(f32[2048,2048]{0,1:T(8,128)} %multiply_bitcast_fusion) | data formatting | bytes 33554432 | tf_op jit(solution)/shard_map/mul | solution.py:28
  42.8 22.0 %reshape_reshape.3 = f32[16,2,64,2,1024]{4,3,2,1,0:T(2,128)} reshape(f32[2048,2048]{1,0:T(8,128)} %copy.14) | data formatting | bytes 33554432 | tf_op jit(solution)/shard_map/reshape;reshape | solution.py:56
  64.8 13.1 %constant_dynamic-slice_fusion.2 = (f32[16,1,64,2,1024]{4,3,2,1,0:T(2,128)}, f32[16,1,64,2,1024]{4,3,2,1,0:T(2,128)S(1)}) fusion(f32[16,2,64,2,1024]{4,3,2,1,0:T(2,128)} %reshape_reshape.3, s32[]{:T(128)S(6)} %select_n.272, s32[]{:T(128)S(6)} %select_n.273), kind=kLoop, calls=%fused_computation.48 | loop fusion | bytes 33554440 | tf_op jit(solution)/shard_map/jit(dynamic_index_in_dim)/dynamic_slice | solution.py:57
  77.9 5.8 %copy.21 = f32[16,1,64,2,1024]{4,2,3,1,0:T(8,128)} copy(f32[16,1,64,2,1024]{4,3,2,1,0:T(2,128)S(1)} %get-tuple-element.39) | data formatting | bytes 16777216 | tf_op jit(solution)/shard_map/jit(dynamic_index_in_dim)/dynamic_slice | solution.py:58
  85.1 13.1 %collective-permute-done = f32[16,64,2,1024]{3,1,2,0:T(8,128)} collective-permute-done((f32[16,64,2,1024]{3,1,2,0:T(8,128)}, f32[16,64,2,1024]{3,1,2,0:T(8,128)}, u32[]{:S(2)}, u32[]{:S(2)}) %collective-permute-start) | collective-permute-done | bytes 8388640 | tf_op jit(solution)/shard_map/ppermute | solution.py:20
  98.3 9.2 %fusion.3 = (f32[2]{0:T(128)S(1)}, f32[2]{0:T(128)S(1)}, f32[2]{0:T(128)S(1)}) fusion(f32[16,64,2,1024]{3,1,2,0:T(8,128)} %collective-permute-done, f32[16,1,64,2,1024]{4,3,2,1,0:T(2,128)} %get-tuple-element.38), kind=kLoop, calls=%fused_computation.7 | loop fusion | flops 12582906 | bytes 16777240 | tf_op jit(solution)/shard_map/reduce_sum | solution.py:39
  107.5 8.6 %psum.35 = f32[3,2]{1,0:T(4,128)S(1)} all-reduce(f32[3,2]{1,0:T(4,128)S(1)} %pad_maximum_fusion), channel_id=1, replica_groups=mesh['shard'=4,'rep'=32] {'shard'}, use_global_device_ids=true, to_apply=%region_3.4 | all-reduce | flops 6 | bytes 48 | tf_op jit(solution)/shard_map/psum | solution.py:32
  119.4 12.7 %fusion.5 = f32[16,64,2,1024]{3,1,2,0:T(8,128)} fusion(f32[16,64,2,1024]{3,1,2,0:T(8,128)} %collective-permute-done, f32[16,1,64,2,1024]{4,3,2,1,0:T(2,128)} %get-tuple-element.38, f32[2]{0:T(128)S(1)} %fusion.36, f32[2]{0:T(128)S(1)} %get-tuple-element.35), kind=kLoop, calls=%fused_computation.9 | loop fusion | flops 6291456 | bytes 25165840 | tf_op jit(solution)/shard_map/add | solution.py:51
  132.1 4.7 %dynamic-slice_bitcast_fusion = f32[8,64,2,1024]{3,1,2,0:T(8,128)} fusion(f32[8,2,64,2,1024]{4,2,3,1,0:T(8,128)} %bitcast.112, s32[]{:T(128)S(6)} %select_n.281), kind=kLoop, calls=%fused_computation.19 | loop fusion | bytes 8388612 | tf_op jit(solution)/shard_map/jit(dynamic_index_in_dim)/squeeze | solution.py:58
  138.5 90.9 %collective-permute-done.2 = f32[8,64,2,1024]{3,1,2,0:T(8,128)} collective-permute-done((f32[8,64,2,1024]{3,1,2,0:T(8,128)}, f32[8,64,2,1024]{3,1,2,0:T(8,128)}, u32[]{:S(2)}, u32[]{:S(2)}) %collective-permute-start.2) | collective-permute-done | bytes 4194336 | tf_op jit(solution)/shard_map/ppermute | solution.py:20
  229.4 4.8 %fusion.6 = (f32[2]{0:T(128)S(1)}, f32[2]{0:T(128)S(1)}, f32[2]{0:T(128)S(1)}) fusion(f32[8,64,2,1024]{3,1,2,0:T(8,128)} %collective-permute-done.2, f32[8,2,64,2,1024]{4,2,3,1,0:T(8,128)} %bitcast.113, s32[]{:T(128)S(6)} %select_n.280), kind=kLoop, calls=%fused_computation.15 | loop fusion | flops 6291450 | bytes 8388636 | tf_op jit(solution)/shard_map/reduce_sum | solution.py:39
  234.2 6.0 %psum.36 = f32[3,2]{1,0:T(4,128)S(1)} all-reduce(f32[3,2]{1,0:T(4,128)S(1)} %pad_maximum_fusion.1), channel_id=1, replica_groups=mesh['shard'=4,'rep'=32] {'shard'}, use_global_device_ids=true, to_apply=%region_7.8 | all-reduce | flops 6 | bytes 48 | tf_op jit(solution)/shard_map/psum | solution.py:32
  240.2 2.8 collective-permute-start.3
  246.3 4.5 %fusion.8 = f32[8,64,2,1024]{3,1,2,0:T(8,128)S(1)} fusion(f32[8,64,2,1024]{3,1,2,0:T(8,128)} %collective-permute-done.2, f32[8,2,64,2,1024]{4,2,3,1,0:T(8,128)} %bitcast.114, s32[]{:T(128)S(6)} %select_n.280, f32[2]{0:T(128)S(1)} %fusion.34, f32[2]{0:T(128)S(1)} %get-tuple-element.32), kind=kLoop, calls=%fused_computation.17 | loop fusion | flops 3145728 | bytes 12582932 | tf_op jit(solution)/shard_map/add | solution.py:51
  254.2 3.4 collective-permute-start.5
  257.6 44.7 %collective-permute-done.5 = f32[4,64,2,1024]{3,1,2,0:T(8,128)S(1)} collective-permute-done((f32[4,64,2,1024]{3,1,2,0:T(8,128)}, f32[4,64,2,1024]{3,1,2,0:T(8,128)S(1)}, u32[]{:S(2)}, u32[]{:S(2)}) %collective-permute-start.5) | collective-permute-done | bytes 2097184 | tf_op jit(solution)/shard_map/ppermute | solution.py:20
  302.3 3.0 fusion.9
  305.3 7.9 %psum.37 = f32[3,2]{1,0:T(4,128)S(1)} all-reduce(f32[3,2]{1,0:T(4,128)S(1)} %pad_maximum_fusion.2), channel_id=1, replica_groups=mesh['shard'=4,'rep'=32] {'shard'}, use_global_device_ids=true, to_apply=%region_11.12 | all-reduce | flops 6 | bytes 48 | tf_op jit(solution)/shard_map/psum | solution.py:32
  313.2 4.1 collective-permute-start.6
  320.5 3.0 collective-permute-start.8
  324.5 2.7 fusion.11
  329.6 20.9 %collective-permute-done.9 = f32[2,64,2,1024]{3,1,2,0:T(8,128)S(1)} collective-permute-done((f32[2,64,2,1024]{3,1,2,0:T(8,128)}, f32[2,64,2,1024]{3,1,2,0:T(8,128)S(1)}, u32[]{:S(2)}, u32[]{:S(2)}) %collective-permute-start.9) | collective-permute-done | bytes 1048608 | tf_op jit(solution)/shard_map/ppermute | solution.py:20
  351.0 6.0 %psum.38 = f32[3,2]{1,0:T(4,128)S(1)} all-reduce(f32[3,2]{1,0:T(4,128)S(1)} %pad_maximum_fusion.3), channel_id=1, replica_groups=mesh['shard'=4,'rep'=32] {'shard'}, use_global_device_ids=true, to_apply=%region_15.16 | all-reduce | flops 6 | bytes 48 | tf_op jit(solution)/shard_map/psum | solution.py:32
  357.0 5.4 %collective-permute-start.10 = (f32[3,2]{1,0:T(4,128)S(1)}, f32[3,2]{1,0:T(4,128)S(1)}, u32[]{:S(2)}, u32[]{:S(2)}) collective-permute-start(f32[3,2]{1,0:T(4,128)S(1)} %psum.38), channel_id=1, source_target_pairs={{0,1},{1,0},{2,3},{3,2},{4,5},{5,4},{6,7},{7,6},{8,9},{9,8},{10,11... | collective-permute-start | bytes 80 | tf_op jit(solution)/shard_map/ppermute | solution.py:20
  365.6 3.0 collective-permute-start.12
  373.6 3.0 collective-permute-start.14
  376.6 8.2 %collective-permute-done.14 = f32[1,64,2,1024]{3,1,2,0:T(8,128)S(1)} collective-permute-done((f32[1,64,2,1024]{3,1,2,0:T(8,128)S(1)}, f32[1,64,2,1024]{3,1,2,0:T(8,128)S(1)}, u32[]{:S(2)}, u32[]{:S(2)}) %collective-permute-start.14) | collective-permute-done | bytes 524320 | tf_op jit(solution)/shard_map/ppermute | solution.py:20
  385.0 7.7 %psum.39 = f32[3,2]{1,0:T(4,128)S(1)} all-reduce(f32[3,2]{1,0:T(4,128)S(1)} %pad_maximum_fusion.4), channel_id=1, replica_groups=mesh['shard'=4,'rep'=32] {'shard'}, use_global_device_ids=true, to_apply=%region_19.20 | all-reduce | flops 6 | bytes 48 | tf_op jit(solution)/shard_map/psum | solution.py:32
  392.8 6.8 %collective-permute-start.15 = (f32[3,2]{1,0:T(4,128)S(1)}, f32[3,2]{1,0:T(4,128)S(1)}, u32[]{:S(2)}, u32[]{:S(2)}) collective-permute-start(f32[3,2]{1,0:T(4,128)S(1)} %psum.39), channel_id=1, source_target_pairs={{0,1},{1,0},{2,3},{3,2},{4,5},{5,4},{6,7},{7,6},{8,9},{9,8},{10,11... | collective-permute-start | bytes 80 | tf_op jit(solution)/shard_map/ppermute | solution.py:20
  402.8 3.0 collective-permute-start.17
  409.2 2.9 collective-permute-start.19
  (76 shorter events, 38.6 us)
Async XLA Ops:
  83.7 14.6 %collective-permute-start = (f32[16,64,2,1024]{3,1,2,0:T(8,128)}, f32[16,64,2,1024]{3,1,2,0:T(8,128)}, u32[]{:S(2)}, u32[]{:S(2)}) collective-permute-start(f32[16,64,2,1024]{3,1,2,0:T(8,128)} %bitcast.111), channel_id=1, source_target_pairs={{0,1},{1,0},{2,3},{3,2},{4,5},{5,4},{6,7},{7,6},{8,9},{9,8},{10,11... | collective-permute-start | bytes 25165832 | tf_op jit(solution)/shard_map/ppermute | solution.py:20
  116.1 3.3 collective-permute-start.1
  136.9 92.5 %collective-permute-start.2 = (f32[8,64,2,1024]{3,1,2,0:T(8,128)}, f32[8,64,2,1024]{3,1,2,0:T(8,128)}, u32[]{:S(2)}, u32[]{:S(2)}) collective-permute-start(f32[8,64,2,1024]{3,1,2,0:T(8,128)} %dynamic-slice_bitcast_fusion), channel_id=1, source_target_pairs={{0,2},{2,0},{1,3},{3,1},{4,6},{6,4},{5,7},{7,5},{8,10},{10,8},{9,1... | collective-permute-start | bytes 12582920 | tf_op jit(solution)/shard_map/ppermute | solution.py:20
  240.2 3.6 collective-permute-start.3
  243.8 2.4 collective-permute-start.4
  250.8 1.9 copy-start
  254.2 48.1 %collective-permute-start.5 = (f32[4,64,2,1024]{3,1,2,0:T(8,128)}, f32[4,64,2,1024]{3,1,2,0:T(8,128)S(1)}, u32[]{:S(2)}, u32[]{:S(2)}) collective-permute-start(f32[4,64,2,1024]{3,1,2,0:T(8,128)} %dynamic-slice_bitcast_fusion.1), channel_id=1, source_target_pairs={{0,4},{4,0},{1,5},{5,1},{2,6},{6,2},{3,7},{7,3},{8,12},{12,8},{9,1... | collective-permute-start | bytes 6291464 | tf_op jit(solution)/shard_map/ppermute | solution.py:20
  302.3 22.2 %copy-start.1 = (f32[4,64,2,1024]{3,1,2,0:T(8,128)}, f32[4,64,2,1024]{3,1,2,0:T(8,128)S(1)}, u32[]{:S(2)}) copy-start(f32[4,64,2,1024]{3,1,2,0:T(8,128)S(1)} %collective-permute-done.5) | copy-start | bytes 6291460
  313.2 4.9 %collective-permute-start.6 = (f32[3,2]{1,0:T(4,128)S(1)}, f32[3,2]{1,0:T(4,128)S(1)}, u32[]{:S(2)}, u32[]{:S(2)}) collective-permute-start(f32[3,2]{1,0:T(4,128)S(1)} %psum.37), channel_id=1, source_target_pairs={{0,1},{1,0},{2,3},{3,2},{4,5},{5,4},{6,7},{7,6},{8,9},{9,8},{10,11... | collective-permute-start | bytes 80 | tf_op jit(solution)/shard_map/ppermute | solution.py:20
  318.1 2.4 collective-permute-start.7
  320.5 3.9 collective-permute-start.8
  328.3 22.2 %collective-permute-start.9 = (f32[2,64,2,1024]{3,1,2,0:T(8,128)}, f32[2,64,2,1024]{3,1,2,0:T(8,128)S(1)}, u32[]{:S(2)}, u32[]{:S(2)}) collective-permute-start(f32[2,64,2,1024]{3,1,2,0:T(8,128)} %dynamic-slice_bitcast_fusion.2), channel_id=1, source_target_pairs={{0,8},{8,0},{1,9},{9,1},{2,10},{10,2},{3,11},{11,3},{4,12},{12,4},... | collective-permute-start | bytes 3145736 | tf_op jit(solution)/shard_map/ppermute | solution.py:20
  329.6 83.7 %copy-start.3 = (f32[64,1024]{1,0:T(8,128)S(1)}, f32[64,1024]{1,0:T(8,128)}, u32[]{:S(2)}) copy-start(f32[64,1024]{1,0:T(8,128)} %param.11) | copy-start | bytes 786436
  350.6 21.5 %copy-start.2 = (f32[2,64,2,1024]{3,1,2,0:T(8,128)}, f32[2,64,2,1024]{3,1,2,0:T(8,128)S(1)}, u32[]{:S(2)}) copy-start(f32[2,64,2,1024]{3,1,2,0:T(8,128)S(1)} %collective-permute-done.9) | copy-start | bytes 3145732
  357.0 6.2 %collective-permute-start.10 = (f32[3,2]{1,0:T(4,128)S(1)}, f32[3,2]{1,0:T(4,128)S(1)}, u32[]{:S(2)}, u32[]{:S(2)}) collective-permute-start(f32[3,2]{1,0:T(4,128)S(1)} %psum.38), channel_id=1, source_target_pairs={{0,1},{1,0},{2,3},{3,2},{4,5},{5,4},{6,7},{7,6},{8,9},{9,8},{10,11... | collective-permute-start | bytes 80 | tf_op jit(solution)/shard_map/ppermute | solution.py:20
  363.2 2.4 collective-permute-start.11
  365.6 3.9 collective-permute-start.12
  369.5 2.4 collective-permute-start.13
  373.6 11.2 %collective-permute-start.14 = (f32[1,64,2,1024]{3,1,2,0:T(8,128)S(1)}, f32[1,64,2,1024]{3,1,2,0:T(8,128)S(1)}, u32[]{:S(2)}, u32[]{:S(2)}) collective-permute-start(f32[1,64,2,1024]{3,1,2,0:T(8,128)S(1)} %constant_dynamic-slice_fusion), channel_id=1, source_target_pairs={{0,16},{16,0},{1,17},{17,1},{2,18},{18,2},{3,19},{19,3},{4,20},{20... | collective-permute-start | bytes 1572872 | tf_op jit(solution)/shard_map/ppermute | solution.py:20
  392.8 7.6 %collective-permute-start.15 = (f32[3,2]{1,0:T(4,128)S(1)}, f32[3,2]{1,0:T(4,128)S(1)}, u32[]{:S(2)}, u32[]{:S(2)}) collective-permute-start(f32[3,2]{1,0:T(4,128)S(1)} %psum.39), channel_id=1, source_target_pairs={{0,1},{1,0},{2,3},{3,2},{4,5},{5,4},{6,7},{7,6},{8,9},{9,8},{10,11... | collective-permute-start | bytes 80 | tf_op jit(solution)/shard_map/ppermute | solution.py:20
  400.4 2.4 collective-permute-start.16
  402.8 3.9 collective-permute-start.17
  406.8 2.4 collective-permute-start.18
  409.2 3.9 collective-permute-start.19
where the time goes:
time: 420 us; the launch traced here: 415 us
  waiting for transfers between devices  193 us (46%)
  local copies, waits for them, and re-layouts  67.8 us (16%)
  starting transfers between devices  51 us (12%)
  other arithmetic  41.7 us (10%)
  blocking collectives  36.2 us (9%)
  matrix products  24.6 us (6%)
    ppermute x20, waiting for transfers between devices, from_partner(): return lax.ppermute(block, axis, route)  193 us
    ppermute x20, starting transfers between devices, from_partner(): return lax.ppermute(block, axis, route)  51 us
    psum x5, blocking collectives, group_total(): summed = lax.psum(partials, 'shard')  36.2 us
    dot_general x1, matrix products, weight_grads(): lax.dot_general(token_rows, cotangents, (((0,), (0,)), ((), ())), preferr...  24.6 us
    another operation x1, local copies, waits for them, and re-layouts, halve_and_merge(): paired = region.reshape((region.shape[0] // 2, 2) + region.shape[1:])  22 us
    add x4, other arithmetic, merge_pair(): return own_coef * own_part + partner_coef * partner_part  21.5 us
    reduce_sum x5, other arithmetic, merge_pair(): cross = jnp.sum(own_part * partner_part, axis=(0, 1, 3))  17.7 us
    mul x1, local copies, waits for them, and re-layouts, weight_grads(): return product * factor  17.6 us
  transfers between devices with their start and end apart: 20, of which 20 were waited for; matrix products, arithmetic and copies ran while one was open for 0% of the time, Pallas kernels for 0%

commit v1 on v0

v1 whole, which is shorter than its diff:
```python
import functools
import math

import jax
import jax.numpy as jnp
from jax import lax
from jax.experimental import pallas as pl
from jax.experimental.pallas import tpu as pltpu
from jax.sharding import PartitionSpec as P

EPSILON = 1e-06
MOMENTUM_DECAY = 0.9
STEP_SIZE = 0.01
CHIPS = 16
ROWS = 64
FEATURES = 1024
SENT_NORM = 16384.0
LIMIT = 60 << 20


def grad_kernel(core_ref, x_ref, y_ref, own_ref, other_ref, *, factor):
    product = lax.dot_general(
        x_ref[...], y_ref[...], (((0,), (0,)), ((), ())), preferred_element_type=jnp.float32
    )
    blocks = (product * factor).reshape(-1, 2, ROWS, FEATURES)
    first, second = blocks[:, 0], blocks[:, 1]
    is_first = core_ref[0] == 0
    own_ref[...] = jnp.where(is_first, first, second)
    other_ref[...] = jnp.where(is_first, second, first)


def half_grads(core, tokens, cotangent, start, count):
    depth = tokens.shape[0]
    width = 512
    steps = count // width
    first = start // width
    per = width // (2 * ROWS)
    out = jax.ShapeDtypeStruct((count // (2 * ROWS), ROWS, FEATURES), jnp.float32)
    spec = pl.BlockSpec((per, ROWS, FEATURES), lambda i, c: (i, 0, 0))
    return pl.pallas_call(
        functools.partial(grad_kernel, factor=1.0 / math.sqrt(depth)),
        out_shape=(out, out),
        grid_spec=pltpu.PrefetchScalarGridSpec(
            num_scalar_prefetch=1,
            grid=(steps,),
            in_specs=[
                pl.BlockSpec((depth, width), lambda i, c: (0, i + first)),
                pl.BlockSpec((depth, FEATURES), lambda i, c: (0, 0)),
            ],
            out_specs=[spec, spec],
        ),
        compiler_params=pltpu.CompilerParams(vmem_limit_bytes=LIMIT),
        cost_estimate=pl.CostEstimate(
            flops=2 * depth * count * FEATURES, bytes_accessed=16 << 20, transcendentals=0
        ),
    )(core, tokens, cotangent)


def pair_kernel(a_ref, b_ref, o_ref, acc_ref):
    step = pl.program_id(0)

    @pl.when(step == 0)
    def _():
        acc_ref[...] = jnp.zeros_like(acc_ref)

    a = a_ref[...].reshape(-1, 8, FEATURES)
    b = b_ref[...].reshape(-1, 8, FEATURES)
    acc_ref[0] += jnp.sum(a * b, axis=0)
    acc_ref[1] += jnp.sum(a * a, axis=0)
    acc_ref[2] += jnp.sum(b * b, axis=0)

    @pl.when(step == pl.num_programs(0) - 1)
    def _():
        for k in range(3):
            row = jnp.sum(acc_ref[k], axis=0, keepdims=True)
            total = jnp.sum(row.reshape(1, FEATURES), axis=1, keepdims=True)
            o_ref[pl.ds(k, 1), :] = jnp.broadcast_to(total, (1, 128))


def pair_sums(a, b):
    count = a.shape[0]
    spec = pl.BlockSpec((4, ROWS, FEATURES), lambda i: (i, 0, 0))
    return pl.pallas_call(
        pair_kernel,
        out_shape=jax.ShapeDtypeStruct((8, 128), jnp.float32),
        grid=(count // 4,),
        in_specs=[spec, spec],
        out_specs=pl.BlockSpec((8, 128), lambda i: (0, 0)),
        scratch_shapes=[pltpu.VMEM((3, 8, FEATURES), jnp.float32)],
        compiler_params=pltpu.CompilerParams(vmem_limit_bytes=LIMIT),
        cost_estimate=pl.CostEstimate(
            flops=6 * a.size, bytes_accessed=8 * a.size, transcendentals=0
        ),
    )(a, b)


def gram_kernel(v_ref, o_ref, t_ref):
    t_ref[...] = jnp.zeros_like(t_ref)
    for gi in range(4):
        for gj in range(gi, 4):
            pairs = [
                (i, j)
                for i in range(4 * gi, 4 * gi + 4)
                for j in range(4 * gj, 4 * gj + 4)
                if i <= j
            ]

            def body(r, sums, pairs=pairs):
                sums = list(sums)
                rows = pl.ds(pl.multiple_of(r * 8, 8), 8)
                for lane in range(FEATURES // 128):
                    held = {}
                    for i, j in pairs:
                        for k in (i, j):
                            if k not in held:
                                held[k] = v_ref[k, rows, pl.ds(lane * 128, 128)]
                    for n, (i, j) in enumerate(pairs):
                        sums[n] = sums[n] + held[i] * held[j]
                return tuple(sums)

            zero = jnp.zeros((8, 128), jnp.float32)
            sums = lax.fori_loop(0, ROWS // 8, body, (zero,) * len(pairs))
            for (i, j), total in zip(pairs, sums):
                t_ref[pl.ds(i * CHIPS + j, 1), :] = jnp.sum(total, axis=0, keepdims=True)
    for part in range(2):
        o_ref[:, pl.ds(part * 128, 128)] = jnp.sum(
            t_ref[pl.ds(part * 128, 128), :].T, axis=0, keepdims=True
        )


def gram(v):
    whole = pl.BlockSpec(memory_space=pltpu.VMEM)
    return pl.pallas_call(
        gram_kernel,
        out_shape=jax.ShapeDtypeStruct((1, CHIPS * CHIPS), jnp.float32),
        in_specs=[whole],
        out_specs=whole,
        scratch_shapes=[pltpu.VMEM((CHIPS * CHIPS, 128), jnp.float32)],
        compiler_params=pltpu.CompilerParams(vmem_limit_bytes=LIMIT),
        cost_estimate=pl.CostEstimate(
            flops=20 << 20, bytes_accessed=4 * v.size, transcendentals=0
        ),
    )(v)


def tree_coefs(read):
    count = CHIPS
    scales = [read(CHIPS * CHIPS + i) for i in range(count)]
    table = {
        (i, j): read(i * CHIPS + j) * (scales[i] * scales[j])
        for i in range(count)
        for j in range(i, count)
    }
    weights = list(scales)
    span = 1
    while count > 1:
        own = []
        for k in range(count // 2):
            cross = table[2 * k, 2 * k + 1]
            own.append(1.0 - cross / (2.0 * (table[2 * k, 2 * k] + EPSILON)))
            own.append(1.0 - cross / (2.0 * (table[2 * k + 1, 2 * k + 1] + EPSILON)))
        weights = [w * own[i // span] for i, w in enumerate(weights)]
        table = {key: value * (own[key[0]] * own[key[1]]) for key, value in table.items()}
        count //= 2
        merged = {}
        for k in range(count):
            merged[k, k] = (
                table[2 * k, 2 * k]
                + 2.0 * table[2 * k, 2 * k + 1]
                + table[2 * k + 1, 2 * k + 1]
            )
            for m in range(k + 1, count):
                merged[k, m] = (
                    table[2 * k, 2 * m]
                    + table[2 * k, 2 * m + 1]
                    + table[2 * k + 1, 2 * m]
                    + table[2 * k + 1, 2 * m + 1]
                )
        table = merged
        span *= 2
    return weights


def update_kernel(totals_ref, v_ref, weight_ref, moment_ref, new_weight_ref, new_moment_ref, coef_ref):
    @pl.when(pl.program_id(0) == 0)
    def _():
        for i, w in enumerate(tree_coefs(lambda n: totals_ref[n])):
            coef_ref[i] = w

    merged = coef_ref[0] * v_ref[0]
    for i in range(1, CHIPS):
        merged = merged + coef_ref[i] * v_ref[i]
    moment = MOMENTUM_DECAY * moment_ref[...] + merged
    new_moment_ref[...] = moment
    new_weight_ref[...] = weight_ref[...] - STEP_SIZE * moment


def update(totals, v, weight, moment):
    step = 16
    rows = pl.BlockSpec((step, FEATURES), lambda i: (i, 0))
    out = jax.ShapeDtypeStruct(weight.shape, jnp.float32)
    return pl.pallas_call(
        update_kernel,
        out_shape=(out, out),
        grid=(ROWS // step,),
        in_specs=[
            pl.BlockSpec(memory_space=pltpu.SMEM),
            pl.BlockSpec((CHIPS, step, FEATURES), lambda i: (0, i, 0)),
            rows,
            rows,
        ],
        out_specs=[rows, rows],
        scratch_shapes=[pltpu.SMEM((CHIPS,), jnp.float32)],
        compiler_params=pltpu.CompilerParams(vmem_limit_bytes=LIMIT),
        cost_estimate=pl.CostEstimate(
            flops=2 * v.size, bytes_accessed=4 * v.size, transcendentals=0
        ),
    )(totals, v, weight, moment)


def summed(vector, axes, groups, count):
    copies = jnp.broadcast_to(vector[None], (count,) + vector.shape)
    arrived = lax.all_to_all(copies, axes, 0, 0, axis_index_groups=groups)
    return jnp.sum(arrived, axis=0)


def shards(
    tokens, key_cotangent, value_cotangent, key_weight, value_weight, key_moment, value_moment
):
    shard_count, replicas = lax.axis_size("shard"), lax.axis_size("rep")
    index = lax.axis_index("rep")
    core = (index & 1).astype(jnp.int32)
    chip = index >> 1
    is_first = core == 0
    half = tokens.shape[1] // 2
    swap = [(i, i ^ 1) for i in range(replicas)]
    chip_groups = [
        [s * replicas + 2 * i + c for s in range(shard_count) for c in range(2)]
        for i in range(CHIPS)
    ]
    core_groups = [list(range(c, replicas, 2)) for c in range(2)]
    leader = (lax.axis_index("shard") == 0) & is_first
    place = jnp.where((jnp.arange(128) == chip) & leader, 1.0, 0.0)[None]

    def pair_merge(own, arrived):
        sums = pair_sums(own, arrived)[:3]
        ordered = jnp.stack(
            [
                sums[0],
                jnp.where(is_first, sums[1], sums[2]),
                jnp.where(is_first, sums[2], sums[1]),
            ]
        )
        cross, p, q = summed(ordered, ("shard", "rep"), chip_groups, 2 * shard_count)[:, 0]
        a = 1.0 - cross / (2.0 * (p + EPSILON))
        b = 1.0 - cross / (2.0 * (q + EPSILON))
        squares = a * a * p + b * b * q
        square = jnp.maximum(squares + 2.0 * a * b * cross, 1e-6 * squares)
        norm = jnp.sqrt(jnp.maximum(square, 1e-30))
        scale = SENT_NORM / norm
        own_coef = jnp.where(is_first, a, b) * scale
        other_coef = jnp.where(is_first, b, a) * scale
        merged = (own_coef * own + other_coef * arrived).astype(jnp.float16)
        return merged, norm * (1.0 / SENT_NORM)

    def gathered(merged):
        return lax.all_to_all(merged, "rep", 0, 0, axis_index_groups=core_groups)

    def finish(arrived, norm, weight, moment):
        v = arrived.astype(jnp.float32)
        vector = jnp.concatenate([gram(v), norm * place], axis=1)
        totals = summed(vector, ("shard", "rep"), None, shard_count * replicas)[0]
        return update(totals, v, weight, moment)

    cores = core[None]
    key_own, key_other = half_grads(cores, tokens, key_cotangent, 0, 2 * half)
    key_arrived = lax.ppermute(key_other, "rep", swap)
    value_own, value_other = half_grads(cores, tokens, value_cotangent, 0, 2 * half)
    value_arrived = lax.ppermute(value_other, "rep", swap)
    key_merged, key_norm = pair_merge(key_own, key_arrived)
    key_all = gathered(key_merged)
    value_merged, value_norm = pair_merge(value_own, value_arrived)
    value_all = gathered(value_merged)
    new_key_weight, new_key_moment = finish(key_all, key_norm, key_weight, key_moment)
    new_value_weight, new_value_moment = finish(value_all, value_norm, value_weight, value_moment)
    return (new_key_weight, new_value_weight, new_key_moment, new_value_moment)


def solution(mesh):
    in_specs = (
        P("rep", "shard"),
        P("rep", None),
        P("rep", None),
        P(("shard", "rep"), None),
        P(("shard", "rep"), None),
        P(("shard", "rep"), None),
        P(("shard", "rep"), None),
    )
    out_specs = (
        P(("shard", "rep"), None),
        P(("shard", "rep"), None),
        P(("shard", "rep"), None),
        P(("shard", "rep"), None),
    )
    return jax.shard_map(shards, mesh=mesh, in_specs=in_specs, out_specs=out_specs, check_vma=False)
```

time: 420 us -> 180 us (0.43)
  waiting for transfers between devices: 193 us -> 39.6 us
  local copies, waits for them, and re-layouts: 67.8 us -> 3.82 us
  Pallas kernels: 0 us -> 58.3 us
  blocking collectives: 36.2 us -> 0 us
  matrix products: 24.6 us -> 0 us
  other arithmetic: 41.7 us -> 23 us
  between operations: 0.78 us -> 10 us
  starting transfers between devices: 51 us -> 44.2 us
    ppermute x20 -> x2, waiting for transfers between devices: 193 us -> 0.01 us  [the longest x1 0.01 us: shards(): key_arrived = lax.ppermute(key_other, 'rep', swap)]
    pallas_call x0 -> x8, Pallas kernels: none -> 58.3 us  [the longest x2 27.3 us: half_grads(): pl.pallas_call(functools.partial(grad_kernel, factor=1.0 / math.sqrt(dept...]
    ppermute x20 -> x2, starting transfers between devices: 51 us -> 1.43 us  [the longest x1 1.42 us: shards(): key_arrived = lax.ppermute(key_other, 'rep', swap)]
    all_to_all x0 -> x6, starting transfers between devices: none -> 42.7 us  [the longest x4 29.2 us: summed(): arrived = lax.all_to_all(copies, axes, 0, 0, axis_index_groups=groups)]
    all_to_all x0 -> x6, waiting for transfers between devices: none -> 39.6 us  [the longest x2 34.6 us: gathered(): return lax.all_to_all(merged, 'rep', 0, 0, axis_index_groups=core_groups)]
    psum x5 -> x0, blocking collectives: 36.2 us -> none  [group_total(): summed = lax.psum(partials, 'shard')]
    dot_general x1 -> x0, matrix products: 24.6 us -> none  [weight_grads(): lax.dot_general(token_rows, cotangents, (((0,), (0,)), ((), ())), preferr...]
    add x19 -> x0, other arithmetic: 21.5 us -> none  [the longest x4 21.5 us: merge_pair(): return own_coef * own_part + partner_coef * partner_part]
  transfers between devices with their start and end apart: 20 -> 8, of which waited for: 20 -> 3; matrix products, arithmetic and copies ran while one was open for 0% -> 13% of each run, Pallas kernels for 0% -> 22%
where the time goes in v1:
time: 180 us; the launch traced here: 179 us
  Pallas kernels  58.3 us (32%)
  starting transfers between devices  44.2 us (25%)
  waiting for transfers between devices  39.6 us (22%)
  other arithmetic  23 us (13%)
  between operations  10 us (6%)
  local copies, waits for them, and re-layouts  3.82 us (2%)
    all_to_all x2, waiting for transfers between devices, gathered(): return lax.all_to_all(merged, 'rep', 0, 0, axis_index_groups=core_groups)  34.6 us
    all_to_all x4, starting transfers between devices, summed(): arrived = lax.all_to_all(copies, axes, 0, 0, axis_index_groups=groups)  29.2 us
    pallas_call x2, Pallas kernels, half_grads(): pl.pallas_call(functools.partial(grad_kernel, factor=1.0 / math.sqrt(dept...  27.3 us
    all_to_all x2, starting transfers between devices, gathered(): return lax.all_to_all(merged, 'rep', 0, 0, axis_index_groups=core_groups)  13.5 us
    convert_element_type x2, other arithmetic, pair_merge(): merged = (own_coef * own + other_coef * arrived).astype(jnp.float16)  11.9 us
    pallas_call x2, Pallas kernels, gram(): pl.pallas_call(gram_kernel, out_shape=jax.ShapeDtypeStruct((1, CHIPS * CH...  11.7 us
    pallas_call x2, Pallas kernels, pair_sums(): pl.pallas_call(pair_kernel, out_shape=jax.ShapeDtypeStruct((8, 128), jnp....  10.2 us
    pallas_call x2, Pallas kernels, update(): pl.pallas_call(update_kernel, out_shape=(out, out), grid=(ROWS // step,),...  9.1 us
  transfers between devices with their start and end apart: 8, of which 3 were waited for; matrix products, arithmetic and copies ran while one was open for 13% of the time, Pallas kernels for 22%

profile of v1, /device:TPU:1, one launch (start us, length us, event | category | flops | bytes accessed | tf_op | source)
XLA Modules:
  0.0 178.9 jit_solution(15514874750566830997)
XLA Ops:
  0.6 13.7 %shard_map.102 = (f32[16,64,1024]{2,1,0:T(8,128)}, f32[16,64,1024]{2,1,0:T(8,128)}) custom-call(s32[1]{0:T(128)} %bitcast.core_ref, bf16[2048,2048]{1,0:T(8,128)(2,1)} %x_ref.3, bf16[2048,1024]{1,0:T(8,128)(2,1)} %y_ref.2), custom_call_target="tpu_custom_call" | custom-call | flops 8589934592 | bytes 16777216 | tf_op jit(solution)/shard_map/pallas_call | solution.py:40
  14.3 1.4 collective-permute-start
  15.7 13.7 %shard_map.106 = (f32[16,64,1024]{2,1,0:T(8,128)}, f32[16,64,1024]{2,1,0:T(8,128)}) custom-call(s32[1]{0:T(128)} %bitcast.core_ref, bf16[2048,2048]{1,0:T(8,128)(2,1)} %x_ref.3, bf16[2048,1024]{1,0:T(8,128)(2,1)} %y_ref.3), custom_call_target="tpu_custom_call" | custom-call | flops 8589934592 | bytes 16777216 | tf_op jit(solution)/shard_map/pallas_call | solution.py:40
  29.4 5.1 %shard_map.103 = f32[8,128]{1,0:T(8,128)} custom-call(f32[16,64,1024]{2,1,0:T(8,128)} %get-tuple-element.12.a_ref, f32[16,64,1024]{2,1,0:T(8,128)} %collective-permute-done.b_ref), custom_call_target="tpu_custom_call" | custom-call | flops 6291456 | bytes 8388608 | tf_op jit(solution)/shard_map/pallas_call | solution.py:83
  34.5 0.8 fusion.1
  35.3 0.6 broadcast_in_dim.41
  36.0 4.9 %all-to-all-start = ((f32[8,3,128]{2,1,0:T(4,128)}), f32[8,3,128]{2,1,0:T(4,128)S(1)}, u32[]{:S(2)}, u32[]{:S(2)}) async-start(f32[8,3,128]{2,1,0:T(4,128)} %broadcast_in_dim.41), calls=%async_computation | async-start | bytes 32768 | tf_op jit(solution)/shard_map/all_to_all | solution.py:223
  40.8 5.1 %shard_map.107 = f32[8,128]{1,0:T(8,128)} custom-call(f32[16,64,1024]{2,1,0:T(8,128)} %get-tuple-element.15.a_ref, f32[16,64,1024]{2,1,0:T(8,128)} %collective-permute-done.1.b_ref), custom_call_target="tpu_custom_call" | custom-call | flops 6291456 | bytes 8388608 | tf_op jit(solution)/shard_map/pallas_call | solution.py:83
  45.9 0.8 fusion
  46.8 0.6 broadcast_in_dim.46
  47.4 4.8 %all-to-all-start.3 = ((f32[8,3,128]{2,1,0:T(4,128)}), f32[8,3,128]{2,1,0:T(4,128)S(1)}, u32[]{:S(2)}, u32[]{:S(2)}) async-start(f32[8,3,128]{2,1,0:T(4,128)} %broadcast_in_dim.46), calls=%async_computation.3 | async-start | bytes 32768 | tf_op jit(solution)/shard_map/all_to_all | solution.py:223
  57.4 5.9 %add_convert_fusion.1 = f16[16,64,1024]{2,1,0:T(8,128)(2,1)} fusion(f32[16,64,1024]{2,1,0:T(8,128)} %collective-permute-done.b_ref, f32[16,64,1024]{2,1,0:T(8,128)} %get-tuple-element.12.a_ref, f32[]{:T(128)S(6)} %mul.143, f32[]{:T(128)S(6)} %mul.140), kind=kLoop, calls=%fused_computation.1 | loop fusion | flops 4194304 | bytes 10485768 | tf_op jit(solution)/shard_map/convert_element_type | solution.py:263
  63.3 7.8 %all-to-all-start.1 = ((f16[16,64,1024]{2,1,0:T(8,128)(2,1)}), f16[16,64,1024]{2,1,0:T(8,128)(2,1)S(1)}, u32[]{:S(2)}, u32[]{:S(2)}) async-start(f16[16,64,1024]{2,1,0:T(8,128)(2,1)} %add_convert_fusion.1), calls=%async_computation.1 | async-start | bytes 4194304 | tf_op jit(solution)/shard_map/all_to_all | solution.py:267
  76.3 6.0 %add_convert_fusion = f16[16,64,1024]{2,1,0:T(8,128)(2,1)} fusion(f32[16,64,1024]{2,1,0:T(8,128)} %collective-permute-done.1.b_ref, f32[16,64,1024]{2,1,0:T(8,128)} %get-tuple-element.15.a_ref, f32[]{:T(128)S(6)} %mul.162, f32[]{:T(128)S(6)} %mul.159), kind=kLoop, calls=%fused_computation | loop fusion | flops 4194304 | bytes 10485768 | tf_op jit(solution)/shard_map/convert_element_type | solution.py:263
  82.2 18.0 %all-to-all-done.1 = f16[16,64,1024]{2,1,0:T(8,128)(2,1)S(1)} async-done(((f16[16,64,1024]{2,1,0:T(8,128)(2,1)}), f16[16,64,1024]{2,1,0:T(8,128)(2,1)S(1)}, u32[]{:S(2)}, u32[]{:S(2)}) %all-to-all-start.1) | async-done | bytes 2097184 | tf_op jit(solution)/shard_map/all_to_all | solution.py:267
  100.2 5.8 %all-to-all-start.4 = ((f16[16,64,1024]{2,1,0:T(8,128)(2,1)}), f16[16,64,1024]{2,1,0:T(8,128)(2,1)}, u32[]{:S(2)}, u32[]{:S(2)}) async-start(f16[16,64,1024]{2,1,0:T(8,128)(2,1)} %add_convert_fusion), calls=%async_computation.4 | async-start | bytes 4194304 | tf_op jit(solution)/shard_map/all_to_all | solution.py:267
  106.0 2.4 %convert_element_type.13.v_ref = f32[16,64,1024]{2,1,0:T(8,128)} convert(f16[16,64,1024]{2,1,0:T(8,128)(2,1)S(1)} %all-to-all-done.1) | non-fusion elementwise | flops 1048576 | bytes 6291456 | tf_op jit(solution)/shard_map/convert_element_type | solution.py:270
  108.4 5.8 %shard_map.104 = f32[1,256]{1,0:T(1,128)} custom-call(f32[16,64,1024]{2,1,0:T(8,128)} %convert_element_type.13.v_ref), custom_call_target="tpu_custom_call" | custom-call | flops 20971520 | bytes 4194304 | tf_op jit(solution)/shard_map/pallas_call | solution.py:133
  114.3 0.7 maximum_reduce_fusion
  115.0 16.6 %all-to-all-done.4 = f16[16,64,1024]{2,1,0:T(8,128)(2,1)} async-done(((f16[16,64,1024]{2,1,0:T(8,128)(2,1)}), f16[16,64,1024]{2,1,0:T(8,128)(2,1)}, u32[]{:S(2)}, u32[]{:S(2)}) %all-to-all-start.4) | async-done | bytes 2097184 | tf_op jit(solution)/shard_map/all_to_all | solution.py:267
  131.6 0.8 broadcast_in_dim.45
  132.4 9.8 %all-to-all-start.2 = ((f32[128,1,384]{2,1,0:T(1,128)}), f32[128,1,384]{2,1,0:T(1,128)S(1)}, u32[]{:S(2)}, u32[]{:S(2)}) async-start(f32[128,1,384]{2,1,0:T(1,128)} %broadcast_in_dim.45), calls=%async_computation.2 | async-start | bytes 393216 | tf_op jit(solution)/shard_map/all_to_all | solution.py:223
  142.1 4.1 %convert_element_type.15.v_ref = f32[16,64,1024]{2,1,0:T(8,128)} convert(f16[16,64,1024]{2,1,0:T(8,128)(2,1)} %all-to-all-done.4) | non-fusion elementwise | flops 1048576 | bytes 6291456 | tf_op jit(solution)/shard_map/convert_element_type | solution.py:270
  146.2 5.8 %shard_map.108 = f32[1,256]{1,0:T(1,128)} custom-call(f32[16,64,1024]{2,1,0:T(8,128)} %convert_element_type.15.v_ref), custom_call_target="tpu_custom_call" | custom-call | flops 20971520 | bytes 4194304 | tf_op jit(solution)/shard_map/pallas_call | solution.py:133
  152.0 0.7 maximum_reduce_fusion.1
  152.7 0.8 broadcast_in_dim.48
  153.5 9.8 %all-to-all-start.5 = ((f32[128,1,384]{2,1,0:T(1,128)}), f32[128,1,384]{2,1,0:T(1,128)S(1)}, u32[]{:S(2)}, u32[]{:S(2)}) async-start(f32[128,1,384]{2,1,0:T(1,128)} %broadcast_in_dim.48), calls=%async_computation.5 | async-start | bytes 393216 | tf_op jit(solution)/shard_map/all_to_all | solution.py:223
  163.3 0.8 reduce_sum.37.totals_ref
  164.0 4.5 %shard_map.105 = (f32[64,1024]{1,0:T(8,128)}, f32[64,1024]{1,0:T(8,128)}) custom-call(f32[384]{0:T(512)} %reduce_sum.37.totals_ref, f32[16,64,1024]{2,1,0:T(8,128)} %convert_element_type.13.v_ref, f32[64,1024]{1,0:T(8,128)} %weight_ref.2, f32[64,1024]{1,0:T(8,128)} %moment_ref.2), custom_call_target="tpu_custom_call" | custom-call | flops 2097152 | bytes 4194304 | tf_op jit(solution)/shard_map/pallas_call | solution.py:202
  168.6 5.0 %all-to-all-done.5 = f32[128,1,384]{2,1,0:T(1,128)S(1)} async-done(((f32[128,1,384]{2,1,0:T(1,128)}), f32[128,1,384]{2,1,0:T(1,128)S(1)}, u32[]{:S(2)}, u32[]{:S(2)}) %all-to-all-start.5) | async-done | bytes 196640 | tf_op jit(solution)/shard_map/all_to_all | solution.py:223
  173.6 0.8 reduce_sum.39.totals_ref
  174.3 4.5 %shard_map.109 = (f32[64,1024]{1,0:T(8,128)}, f32[64,1024]{1,0:T(8,128)}) custom-call(f32[384]{0:T(512)} %reduce_sum.39.totals_ref, f32[16,64,1024]{2,1,0:T(8,128)} %convert_element_type.15.v_ref, f32[64,1024]{1,0:T(8,128)} %weight_ref.3, f32[64,1024]{1,0:T(8,128)} %moment_ref.3), custom_call_target="tpu_custom_call" | custom-call | flops 2097152 | bytes 4194304 | tf_op jit(solution)/shard_map/pallas_call | solution.py:202
  (13 shorter events, 1.1 us)
Async XLA Ops:
  14.3 15.1 %collective-permute-start = (f32[16,64,1024]{2,1,0:T(8,128)}, f32[16,64,1024]{2,1,0:T(8,128)}, u32[]{:S(2)}, u32[]{:S(2)}) collective-permute-start(f32[16,64,1024]{2,1,0:T(8,128)} %get-tuple-element.13), channel_id=1, source_target_pairs={{0,1},{1,0},{2,3},{3,2},{4,5},{5,4},{6,7},{7,6},{8,9},{9,8},{10,11... | collective-permute-start | bytes 12582920 | tf_op jit(solution)/shard_map/ppermute | solution.py:277
  29.4 11.4 %collective-permute-start.1 = (f32[16,64,1024]{2,1,0:T(8,128)}, f32[16,64,1024]{2,1,0:T(8,128)}, u32[]{:S(2)}, u32[]{:S(2)}) collective-permute-start(f32[16,64,1024]{2,1,0:T(8,128)} %get-tuple-element.16), channel_id=1, source_target_pairs={{0,1},{1,0},{2,3},{3,2},{4,5},{5,4},{6,7},{7,6},{8,9},{9,8},{10,11... | collective-permute-start | bytes 12582920 | tf_op jit(solution)/shard_map/ppermute | solution.py:279
  36.0 10.8 %all-to-all-start = ((f32[8,3,128]{2,1,0:T(4,128)}), f32[8,3,128]{2,1,0:T(4,128)S(1)}, u32[]{:S(2)}, u32[]{:S(2)}) async-start(f32[8,3,128]{2,1,0:T(4,128)} %broadcast_in_dim.41), calls=%async_computation | async-start | bytes 32768 | tf_op jit(solution)/shard_map/all_to_all | solution.py:223
  47.4 15.9 %all-to-all-start.3 = ((f32[8,3,128]{2,1,0:T(4,128)}), f32[8,3,128]{2,1,0:T(4,128)S(1)}, u32[]{:S(2)}, u32[]{:S(2)}) async-start(f32[8,3,128]{2,1,0:T(4,128)} %broadcast_in_dim.46), calls=%async_computation.3 | async-start | bytes 32768 | tf_op jit(solution)/shard_map/all_to_all | solution.py:223
  63.3 36.9 %all-to-all-start.1 = ((f16[16,64,1024]{2,1,0:T(8,128)(2,1)}), f16[16,64,1024]{2,1,0:T(8,128)(2,1)S(1)}, u32[]{:S(2)}, u32[]{:S(2)}) async-start(f16[16,64,1024]{2,1,0:T(8,128)(2,1)} %add_convert_fusion.1), calls=%async_computation.1 | async-start | bytes 4194304 | tf_op jit(solution)/shard_map/all_to_all | solution.py:267
  100.2 31.4 %all-to-all-start.4 = ((f16[16,64,1024]{2,1,0:T(8,128)(2,1)}), f16[16,64,1024]{2,1,0:T(8,128)(2,1)}, u32[]{:S(2)}, u32[]{:S(2)}) async-start(f16[16,64,1024]{2,1,0:T(8,128)(2,1)} %add_convert_fusion), calls=%async_computation.4 | async-start | bytes 4194304 | tf_op jit(solution)/shard_map/all_to_all | solution.py:267
  132.4 20.4 %all-to-all-start.2 = ((f32[128,1,384]{2,1,0:T(1,128)}), f32[128,1,384]{2,1,0:T(1,128)S(1)}, u32[]{:S(2)}, u32[]{:S(2)}) async-start(f32[128,1,384]{2,1,0:T(1,128)} %broadcast_in_dim.45), calls=%async_computation.2 | async-start | bytes 393216 | tf_op jit(solution)/shard_map/all_to_all | solution.py:223
  153.5 20.0 %all-to-all-start.5 = ((f32[128,1,384]{2,1,0:T(1,128)}), f32[128,1,384]{2,1,0:T(1,128)S(1)}, u32[]{:S(2)}, u32[]{:S(2)}) async-start(f32[128,1,384]{2,1,0:T(1,128)} %broadcast_in_dim.48), calls=%async_computation.5 | async-start | bytes 393216 | tf_op jit(solution)/shard_map/all_to_all | solution.py:223

commit v2 on v1

v2 whole, which is shorter than its diff:
```python
import functools
import math

import jax
import jax.numpy as jnp
from jax import lax
from jax.experimental import pallas as pl
from jax.experimental.pallas import tpu as pltpu
from jax.sharding import PartitionSpec as P

EPSILON = 1e-06
MOMENTUM_DECAY = 0.9
STEP_SIZE = 0.01
CHIPS = 16
ROWS = 64
FEATURES = 1024
SENT_NORM = 16384.0
MIB = 1 << 20
PAIRS = {pair: n for n, pair in enumerate((i, j) for i in range(CHIPS) for j in range(i, CHIPS))}


def params(mib):
    return pltpu.CompilerParams(vmem_limit_bytes=mib * MIB)


def cost(flops, moved):
    return pl.CostEstimate(flops=flops, bytes_accessed=moved, transcendentals=0)


VMEM = pl.BlockSpec(memory_space=pltpu.VMEM)
SMEM = pl.BlockSpec(memory_space=pltpu.SMEM)


def scaled_dot(rows, cotangent):
    product = jnp.dot(rows, cotangent, preferred_element_type=jnp.float32)
    return (product * (1.0 / math.sqrt(rows.shape[1]))).reshape(-1, ROWS, FEATURES)


def split_kernel(core_ref, x_hbm, y_hbm, grad_ref, own_ref, other_ref, x_ref, y_ref, x_sems, y_sem):
    steps, depth, width = x_ref.shape
    x_copies = [
        pltpu.make_async_copy(x_hbm.at[:, pl.ds(i * width, width)], x_ref.at[i], x_sems.at[i])
        for i in range(steps)
    ]
    y_copy = pltpu.make_async_copy(y_hbm, y_ref, y_sem)
    x_copies[0].start()
    y_copy.start()
    for copy in x_copies[1:]:
        copy.start()
    is_first = core_ref[0] == 0
    half = width // 2
    per = half // ROWS
    for i in range(steps):
        x_copies[i].wait()
        blocks = x_ref[i].T.reshape(-1, 2, ROWS, depth)
        first = blocks[:, 0].reshape(-1, depth)
        second = blocks[:, 1].reshape(-1, depth)
        own_ref[pl.ds(i * half, half), :] = jnp.where(is_first, first, second)
        other = jnp.where(is_first, second, first)
        other_ref[pl.ds(i * half, half), :] = other
        if i == 0:
            y_copy.wait()
        grad_ref[pl.ds(i * per, per)] = scaled_dot(other, y_ref[...])


def split_and_grad(core, tokens, cotangent):
    depth, width = tokens.shape
    step = 512
    half = jax.ShapeDtypeStruct((width // 2, depth), jnp.bfloat16)
    hbm = pl.BlockSpec(memory_space=pltpu.HBM)
    return pl.pallas_call(
        split_kernel,
        out_shape=(jax.ShapeDtypeStruct((CHIPS, ROWS, FEATURES), jnp.float32), half, half),
        in_specs=[SMEM, hbm, hbm],
        out_specs=(VMEM, VMEM, VMEM),
        scratch_shapes=[
            pltpu.VMEM((width // step, depth, step), jnp.bfloat16),
            pltpu.VMEM(cotangent.shape, jnp.bfloat16),
            pltpu.SemaphoreType.DMA((width // step,)),
            pltpu.SemaphoreType.DMA,
        ],
        compiler_params=params(32),
        cost_estimate=cost(depth * width * FEATURES, 24 * MIB),
    )(core, tokens, cotangent)


def grad_kernel(x_ref, y_ref, o_ref):
    step = 256

    @pl.loop(0, x_ref.shape[0] // step)
    def _(i):
        rows = x_ref[pl.ds(pl.multiple_of(i * step, step), step), :]
        o_ref[pl.ds(i * (step // ROWS), step // ROWS)] = scaled_dot(rows, y_ref[...])


def grad(rows, cotangent):
    count, depth = rows.shape
    return pl.pallas_call(
        grad_kernel,
        out_shape=jax.ShapeDtypeStruct((CHIPS, ROWS, FEATURES), jnp.float32),
        in_specs=[VMEM, VMEM],
        out_specs=VMEM,
        compiler_params=params(20),
        cost_estimate=cost(2 * depth * count * FEATURES, 12 * MIB),
    )(rows, cotangent)


def pair_kernel(core_ref, a_ref, b_ref, o_ref, acc_ref):
    step = pl.program_id(0)

    @pl.when(step == 0)
    def _():
        acc_ref[...] = jnp.zeros_like(acc_ref)

    a = a_ref[...].reshape(-1, 8, FEATURES)
    b = b_ref[...].reshape(-1, 8, FEATURES)
    is_first = core_ref[0] == 0
    own, other = jnp.sum(a * a, axis=0), jnp.sum(b * b, axis=0)
    acc_ref[0] += jnp.sum(a * b, axis=0)
    acc_ref[1] += jnp.where(is_first, own, other)
    acc_ref[2] += jnp.where(is_first, other, own)

    @pl.when(step == pl.num_programs(0) - 1)
    def _():
        rows = [jnp.sum(acc_ref[k], axis=0, keepdims=True) for k in range(3)]
        rows = [jnp.sum(row, axis=1, keepdims=True) for row in rows]
        rows = [jnp.broadcast_to(row, (1, 128)) for row in rows]
        tile = jnp.concatenate(rows + [jnp.zeros((5, 128), jnp.float32)], axis=0)
        o_ref[...] = jnp.broadcast_to(tile[None], o_ref.shape)


def pair_sums(core, a, b, copies):
    spec = pl.BlockSpec((4, ROWS, FEATURES), lambda i: (i, 0, 0))
    return pl.pallas_call(
        pair_kernel,
        out_shape=jax.ShapeDtypeStruct((copies, 8, 128), jnp.float32),
        grid=(CHIPS // 4,),
        in_specs=[SMEM, spec, spec],
        out_specs=pl.BlockSpec((copies, 8, 128), lambda i: (0, 0, 0)),
        scratch_shapes=[pltpu.VMEM((3, 8, FEATURES), jnp.float32)],
        compiler_params=params(12),
        cost_estimate=cost(6 * a.size, 8 * a.size),
    )(core, a, b)


def merge_kernel(core_ref, a_ref, b_ref, *refs):
    sums_refs, (o_ref, norm_ref) = refs[:-2], refs[-2:]
    sums = sum(jnp.sum(ref[...], axis=0) for ref in sums_refs)
    cross, p, q = sums[0:1], sums[1:2], sums[2:3]
    is_first = core_ref[0] == 0
    first = 1.0 - cross / (2.0 * (p + EPSILON))
    second = 1.0 - cross / (2.0 * (q + EPSILON))
    squares = first * first * p + second * second * q
    square = jnp.maximum(squares + 2.0 * first * second * cross, 1e-6 * squares)
    norm = jnp.sqrt(jnp.maximum(square, 1e-30))
    scale = SENT_NORM / norm
    norm_ref[...] = jnp.broadcast_to(norm * (1.0 / SENT_NORM), norm_ref.shape)
    own = jnp.where(is_first, first, second) * scale
    other = jnp.where(is_first, second, first) * scale
    own = jnp.concatenate([own] * (FEATURES // 128), axis=1)[None]
    other = jnp.concatenate([other] * (FEATURES // 128), axis=1)[None]
    o_ref[...] = own * a_ref[...] + other * b_ref[...]


def merge_pair(core, a, b, sums):
    spec = pl.BlockSpec((4, ROWS, FEATURES), lambda i: (i, 0, 0))
    return pl.pallas_call(
        merge_kernel,
        out_shape=(
            jax.ShapeDtypeStruct(a.shape, jnp.float32),
            jax.ShapeDtypeStruct((8, 128), jnp.float32),
        ),
        grid=(CHIPS // 4,),
        in_specs=[SMEM, spec, spec] + [VMEM] * len(sums),
        out_specs=(spec, pl.BlockSpec((8, 128), lambda i: (0, 0))),
        compiler_params=params(12),
        cost_estimate=cost(3 * a.size, 12 * a.size),
    )(core, a, b, *sums)


def gram_kernel(place_ref, v_ref, norm_ref, *refs):
    earlier_refs, (o_ref, t_ref) = refs[:-2], refs[-2:]
    t_ref[...] = jnp.zeros_like(t_ref)
    for gi in range(4):
        for gj in range(gi, 4):
            pairs = [
                (i, j)
                for i in range(4 * gi, 4 * gi + 4)
                for j in range(4 * gj, 4 * gj + 4)
                if i <= j
            ]

            def body(r, sums, pairs=pairs):
                sums = list(sums)
                rows = pl.ds(pl.multiple_of(r * 8, 8), 8)
                for lane in range(FEATURES // 128):
                    held = {}
                    for i, j in pairs:
                        for k in (i, j):
                            if k not in held:
                                held[k] = v_ref[k, rows, pl.ds(lane * 128, 128)]
                    for n, (i, j) in enumerate(pairs):
                        sums[n] = sums[n] + held[i] * held[j]
                return tuple(sums)

            zero = jnp.zeros((8, 128), jnp.float32)
            sums = lax.fori_loop(0, ROWS // 8, body, (zero,) * len(pairs))
            for pair, total in zip(pairs, sums):
                t_ref[pl.ds(PAIRS[pair], 1), :] = jnp.sum(total, axis=0, keepdims=True)
    lane = lax.broadcasted_iota(jnp.int32, (1, 128), 1)
    shown = (lane == 0) & (place_ref[1] == 1)
    t_ref[pl.ds(len(PAIRS) + place_ref[0], 1), :] = jnp.where(shown, norm_ref[0:1, :], 0.0)
    rows = [ref[...] for ref in earlier_refs]
    for part in range(2):
        rows.append(jnp.sum(t_ref[pl.ds(part * 128, 128), :].T, axis=0, keepdims=True))
    tile = jnp.concatenate(rows, axis=0)
    o_ref[...] = tile if o_ref.ndim == 2 else jnp.broadcast_to(tile[None], o_ref.shape)


def gram(place, v, norm, earlier, out_dims):
    return pl.pallas_call(
        gram_kernel,
        out_shape=jax.ShapeDtypeStruct(out_dims, jnp.float32),
        in_specs=[SMEM] + [VMEM] * (2 + len(earlier)),
        out_specs=VMEM,
        scratch_shapes=[pltpu.VMEM((256, 128), jnp.float32)],
        compiler_params=params(16),
        cost_estimate=cost(20 << 20, 4 * v.size),
    )(place, v, norm, *earlier)


def tree_coefs(read):
    count = CHIPS
    scales = [read(len(PAIRS) + i) for i in range(count)]
    table = {
        (i, j): read(PAIRS[i, j]) * (scales[i] * scales[j])
        for i in range(count)
        for j in range(i, count)
    }
    weights = list(scales)
    span = 1
    while count > 1:
        own = []
        for k in range(count // 2):
            cross = table[2 * k, 2 * k + 1]
            own.append(1.0 - cross / (2.0 * (table[2 * k, 2 * k] + EPSILON)))
            own.append(1.0 - cross / (2.0 * (table[2 * k + 1, 2 * k + 1] + EPSILON)))
        weights = [w * own[i // span] for i, w in enumerate(weights)]
        table = {key: value * (own[key[0]] * own[key[1]]) for key, value in table.items()}
        count //= 2
        merged = {}
        for k in range(count):
            merged[k, k] = (
                table[2 * k, 2 * k]
                + 2.0 * table[2 * k, 2 * k + 1]
                + table[2 * k + 1, 2 * k + 1]
            )
            for m in range(k + 1, count):
                merged[k, m] = (
                    table[2 * k, 2 * m]
                    + table[2 * k, 2 * m + 1]
                    + table[2 * k + 1, 2 * m]
                    + table[2 * k + 1, 2 * m + 1]
                )
        table = merged
        span *= 2
    return weights


def update_kernel(totals_ref, *refs):
    ins, outs, coef_ref = refs[:6], refs[6:10], refs[10]

    @pl.when(pl.program_id(0) == 0)
    def _():
        for t in range(2):
            weights = tree_coefs(lambda n, t=t: totals_ref[2 * t + n // 128, n % 128])
            for i, w in enumerate(weights):
                coef_ref[t * CHIPS + i] = w

    for t in range(2):
        v_ref, weight_ref, moment_ref = ins[3 * t : 3 * t + 3]
        new_weight_ref, new_moment_ref = outs[2 * t : 2 * t + 2]
        merged = coef_ref[t * CHIPS] * v_ref[0]
        for i in range(1, CHIPS):
            merged = merged + coef_ref[t * CHIPS + i] * v_ref[i]
        moment = MOMENTUM_DECAY * moment_ref[...] + merged
        new_moment_ref[...] = moment
        new_weight_ref[...] = weight_ref[...] - STEP_SIZE * moment


def update(totals, *arrays):
    step = 16
    rows = pl.BlockSpec((step, FEATURES), lambda i: (i, 0))
    whole = pl.BlockSpec((CHIPS, step, FEATURES), lambda i: (0, i, 0))
    out = jax.ShapeDtypeStruct((ROWS, FEATURES), jnp.float32)
    return pl.pallas_call(
        update_kernel,
        out_shape=(out,) * 4,
        grid=(ROWS // step,),
        in_specs=[SMEM] + [whole, rows, rows] * 2,
        out_specs=(rows,) * 4,
        scratch_shapes=[pltpu.SMEM((2 * CHIPS,), jnp.float32)],
        compiler_params=params(60),
        cost_estimate=cost(8 << 20, 10 * MIB),
    )(totals, *arrays)


def after(value, *others):
    return lax.optimization_barrier((value,) + others)[0]


def shards(
    tokens, key_cotangent, value_cotangent, key_weight, value_weight, key_moment, value_moment
):
    shard_count, replicas = lax.axis_size("shard"), lax.axis_size("rep")
    index = lax.axis_index("rep").astype(jnp.int32)
    core = (index & 1)[None]
    leader = ((lax.axis_index("shard") == 0) & (index & 1 == 0)).astype(jnp.int32)
    place = jnp.stack([index >> 1, leader])
    swap = [(i, i ^ 1) for i in range(replicas)]
    core_groups = [list(range(c, replicas, 2)) for c in range(2)]

    def summed(sums):
        sums = sums + lax.ppermute(sums, "rep", swap)
        shifts = [
            [(s, (s + d) % shard_count) for s in range(shard_count)] for d in range(1, shard_count)
        ]
        return [sums] + [lax.ppermute(sums, "shard", shift) for shift in shifts]

    def gathered(merged):
        sent = merged.astype(jnp.float16)
        return lax.all_to_all(sent, "rep", 0, 0, axis_index_groups=core_groups)

    key_other, own_rows, other_rows = split_and_grad(core, tokens, key_cotangent)
    key_arrived = lax.ppermute(key_other, "rep", swap)
    key_own = grad(own_rows, key_cotangent)
    key_sums = summed(pair_sums(core, key_own, key_arrived, 1))
    value_other = grad(other_rows, value_cotangent)
    value_arrived = lax.ppermute(value_other, "rep", swap)
    key_merged, key_norm = merge_pair(core, key_own, key_arrived, key_sums)
    key_all = gathered(key_merged)

    value_own = grad(after(own_rows, key_merged), value_cotangent)
    value_sums = summed(pair_sums(core, value_own, value_arrived, 1))
    value_merged, value_norm = merge_pair(core, value_own, value_arrived, value_sums)
    value_all = gathered(value_merged)

    key_v = key_all.astype(jnp.float32)
    key_vector = gram(place, key_v, key_norm, [], (2, 128))
    value_v = value_all.astype(jnp.float32)
    vectors = gram(place, value_v, value_norm, [key_vector], (shard_count * replicas, 4, 128))
    totals = jnp.sum(lax.all_to_all(vectors, ("shard", "rep"), 0, 0), axis=0)
    new_key_weight, new_key_moment, new_value_weight, new_value_moment = update(
        totals, key_v, key_weight, key_moment, value_v, value_weight, value_moment
    )
    return (new_key_weight, new_value_weight, new_key_moment, new_value_moment)


def solution(mesh):
    in_specs = (
        P("rep", "shard"),
        P("rep", None),
        P("rep", None),
        P(("shard", "rep"), None),
        P(("shard", "rep"), None),
        P(("shard", "rep"), None),
        P(("shard", "rep"), None),
    )
    out_specs = (
        P(("shard", "rep"), None),
        P(("shard", "rep"), None),
        P(("shard", "rep"), None),
        P(("shard", "rep"), None),
    )
    return jax.shard_map(shards, mesh=mesh, in_specs=in_specs, out_specs=out_specs, check_vma=False)
```

time: 180 us -> 139 us (0.77)
  blocking collectives: 0 us -> 20.2 us
  starting transfers between devices: 44.2 us -> 25 us
  other arithmetic: 23 us -> 6.88 us
  waiting for transfers between devices: 39.6 us -> 27.3 us
  Pallas kernels: 58.3 us -> 47.7 us
  between operations: 10 us -> 0.97 us
  local copies, waits for them, and re-layouts: 3.82 us -> 10.5 us
    all_to_all x6 -> x2, starting transfers between devices: 42.7 us -> 14.8 us  [gathered(): return lax.all_to_all(sent, 'rep', 0, 0, axis_index_groups=core_groups)]
    all_to_all x0 -> x1, blocking collectives: none -> 20.2 us  [shards(): totals = jnp.sum(lax.all_to_all(vectors, ('shard', 'rep'), 0, 0), axis=0)]
    all_to_all x6 -> x2, waiting for transfers between devices: 39.6 us -> 19.5 us  [gathered(): return lax.all_to_all(sent, 'rep', 0, 0, axis_index_groups=core_groups)]
    convert_element_type x4, other arithmetic: 18.4 us -> 6.07 us  [the longest x2 3.5 us: gathered(): sent = merged.astype(jnp.float16)]
    pallas_call x8 -> x11, Pallas kernels: 58.3 us -> 47.7 us  [the longest x3 17 us: grad(): pl.pallas_call(grad_kernel, out_shape=jax.ShapeDtypeStruct((CHIPS, ROWS,...]
    unnamed x0 -> x16, local copies, waits for them, and re-layouts: none -> 10.5 us
    ppermute x0 -> x8, starting transfers between devices: none -> 8.68 us  [the longest x6 5.8 us: summed(): return [sums] + [lax.ppermute(sums, 'shard', shift) for shift in shifts]]
    ppermute x0 -> x8, waiting for transfers between devices: none -> 7.81 us  [the longest x6 6.17 us: summed(): return [sums] + [lax.ppermute(sums, 'shard', shift) for shift in shifts]]
  transfers between devices with their start and end apart: 8 -> 12, of which waited for: 3 -> 8; matrix products, arithmetic and copies ran while one was open for 13% -> 3% of each run, Pallas kernels for 22% -> 22%
where the time goes in v2:
time: 139 us
  Pallas kernels  47.7 us (34%)
  waiting for transfers between devices  27.3 us (20%)
  starting transfers between devices  25 us (18%)
  blocking collectives  20.2 us (15%)
  local copies, waits for them, and re-layouts  10.5 us (8%)
  other arithmetic  6.88 us (5%)
    all_to_all x1, blocking collectives, shards(): totals = jnp.sum(lax.all_to_all(vectors, ('shard', 'rep'), 0, 0), axis=0)  20.2 us
    all_to_all x2, waiting for transfers between devices, gathered(): return lax.all_to_all(sent, 'rep', 0, 0, axis_index_groups=core_groups)  19.5 us
    pallas_call x3, Pallas kernels, grad(): pl.pallas_call(grad_kernel, out_shape=jax.ShapeDtypeStruct((CHIPS, ROWS,...  17 us
    all_to_all x2, starting transfers between devices, gathered(): return lax.all_to_all(sent, 'rep', 0, 0, axis_index_groups=core_groups)  14.8 us
    unnamed x16, local copies, waits for them, and re-layouts  10.5 us
    pallas_call x1, Pallas kernels, split_and_grad(): pl.pallas_call(split_kernel, out_shape=(jax.ShapeDtypeStruct((CHIPS, ROWS...  7.8 us
    pallas_call x2, Pallas kernels, gram(): pl.pallas_call(gram_kernel, out_shape=jax.ShapeDtypeStruct(out_dims, jnp....  7.31 us
    pallas_call x1, Pallas kernels, update(): pl.pallas_call(update_kernel, out_shape=(out,) * 4, grid=(ROWS // step,),...  6.18 us
  transfers between devices with their start and end apart: 12, of which 8 were waited for; matrix products, arithmetic and copies ran while one was open for 3% of the time, Pallas kernels for 22%

profile of v2, /device:TPU:1, one launch (start us, length us, event | category | flops | bytes accessed | tf_op | source)
XLA Modules:
  0.0 138.5 jit_solution(12194715144168194733)
XLA Ops:
  0.6 2.2 %copy-done.2 = bf16[2048,1024]{1,0:T(8,128)(2,1)S(1)} copy-done((bf16[2048,1024]{1,0:T(8,128)(2,1)S(1)}, bf16[2048,1024]{1,0:T(8,128)(2,1)}, u32[]{:S(2)}) %copy-start.2) | copy-done | bytes 4194328
  2.8 7.8 %shard_map.102 = (f32[16,64,1024]{2,1,0:T(8,128)S(1)}, bf16[1024,2048]{1,0:T(8,128)(2,1)S(1)}, bf16[1024,2048]{1,0:T(8,128)(2,1)S(1)}) custom-call(s32[1]{0:T(128)} %bitcast.2.core_ref, bf16[2048,2048]{1,0:T(8,128)(2,1)} %x_hbm.1, bf16[2048,1024]{1,0:T(8,128)(2,1)S(1)} %copy-done.2), custom_call_target="tpu_custom_call" | custom-call | flops 4294967296 | bytes 25165824 | tf_op jit(solution)/shard_map/pallas_call | solution.py:71
  10.6 1.5 %collective-permute-start = (f32[16,64,1024]{2,1,0:T(8,128)S(1)}, f32[16,64,1024]{2,1,0:T(8,128)S(1)}, u32[]{:S(2)}, u32[]{:S(2)}) collective-permute-start(f32[16,64,1024]{2,1,0:T(8,128)S(1)} %get-tuple-element.17), channel_id=1, source_target_pairs={{0,1},{1,0},{2,3},{3,2},{4,5},{5,4},{6,7},{7,6},{8,9},{9,8},{10,11... | collective-permute-start | bytes 12582920 | tf_op jit(solution)/shard_map/ppermute | solution.py:335
  12.2 7.0 %shard_map.107 = f32[16,64,1024]{2,1,0:T(8,128)} custom-call(bf16[1024,2048]{1,0:T(8,128)(2,1)S(1)} %get-tuple-element.20.x_ref, bf16[2048,1024]{1,0:T(8,128)(2,1)S(1)} %copy-done.4), custom_call_target="tpu_custom_call" | custom-call | flops 4294967296 | bytes 12582912 | tf_op jit(solution)/shard_map/pallas_call | solution.py:98
  19.2 5.0 %shard_map.103.a_ref = f32[16,64,1024]{2,1,0:T(8,128)S(1)} custom-call(bf16[1024,2048]{1,0:T(8,128)(2,1)S(1)} %get-tuple-element.19.x_ref, bf16[2048,1024]{1,0:T(8,128)(2,1)S(1)} %copy-done.3), custom_call_target="tpu_custom_call" | custom-call | flops 4294967296 | bytes 12582912 | tf_op jit(solution)/shard_map/pallas_call | solution.py:98
  24.2 1.8 %shard_map.104 = f32[1,8,128]{2,1,0:T(8,128)S(1)} custom-call(s32[1]{0:T(128)} %bitcast.2.core_ref, f32[16,64,1024]{2,1,0:T(8,128)S(1)} %shard_map.103.a_ref, f32[16,64,1024]{2,1,0:T(8,128)S(1)} %collective-permute-done.b_ref), custom_call_target="tpu_custom_call" | custom-call | flops 6291456 | bytes 8388608 | tf_op jit(solution)/shard_map/pallas_call | solution.py:134
  26.5 0.8 collective-permute-done.1
  27.3 2.6 %collective-permute-start.4 = (f32[1,8,128]{2,1,0:T(8,128)S(1)}, f32[1,8,128]{2,1,0:T(8,128)S(1)}, u32[]{:S(2)}, u32[]{:S(2)}) collective-permute-start(f32[1,8,128]{2,1,0:T(8,128)S(1)} %add.6.refs_0_), channel_id=1, source_target_pairs={{0,96},{32,0},{64,32},{96,64},{1,97},{33,1},{65,33},{97,65},{2,98}... | collective-permute-start | bytes 12296 | tf_op jit(solution)/shard_map/ppermute | solution.py:328
  31.0 2.8 %collective-permute-done.3.refs_2_ = f32[1,8,128]{2,1,0:T(8,128)S(1)} collective-permute-done((f32[1,8,128]{2,1,0:T(8,128)S(1)}, f32[1,8,128]{2,1,0:T(8,128)S(1)}, u32[]{:S(2)}, u32[]{:S(2)}) %collective-permute-start.3) | collective-permute-done | bytes 4128 | tf_op jit(solution)/shard_map/ppermute | solution.py:328
  34.7 1.7 %convert_element_type.15 = f16[16,64,1024]{2,1,0:T(8,128)(2,1)} convert(f32[16,64,1024]{2,1,0:T(8,128)S(1)} %get-tuple-element.18) | non-fusion elementwise | flops 1048576 | bytes 6291456 | tf_op jit(solution)/shard_map/convert_element_type | solution.py:331
  36.4 7.8 %all-to-all-start.1 = ((f16[16,64,1024]{2,1,0:T(8,128)(2,1)}), f16[16,64,1024]{2,1,0:T(8,128)(2,1)S(1)}, u32[]{:S(2)}, u32[]{:S(2)}) async-start(f16[16,64,1024]{2,1,0:T(8,128)(2,1)} %convert_element_type.15), calls=%async_computation.1 | async-start | bytes 4194304 | tf_op jit(solution)/shard_map/all_to_all | solution.py:332
  44.2 2.2 %copy-done.5 = bf16[2048,1024]{1,0:T(8,128)(2,1)S(1)} copy-done((bf16[2048,1024]{1,0:T(8,128)(2,1)S(1)}, bf16[2048,1024]{1,0:T(8,128)(2,1)}, u32[]{:S(2)}) %copy-start.5) | copy-done | bytes 4194328
  46.4 2.2 %copy-done.7 = bf16[1024,2048]{1,0:T(8,128)(2,1)S(1)} copy-done((bf16[1024,2048]{1,0:T(8,128)(2,1)S(1)}, bf16[1024,2048]{1,0:T(8,128)(2,1)}, u32[]{:S(2)}) %copy-start.7) | copy-done | bytes 4194328
  48.6 5.0 %shard_map.106.a_ref = f32[16,64,1024]{2,1,0:T(8,128)S(1)} custom-call(bf16[1024,2048]{1,0:T(8,128)(2,1)S(1)} %copy-done.7, bf16[2048,1024]{1,0:T(8,128)(2,1)S(1)} %copy-done.5), custom_call_target="tpu_custom_call" | custom-call | flops 4294967296 | bytes 12582912 | tf_op jit(solution)/shard_map/pallas_call | solution.py:98
  53.6 3.9 %shard_map.108 = f32[1,8,128]{2,1,0:T(8,128)S(1)} custom-call(s32[1]{0:T(128)} %bitcast.2.core_ref, f32[16,64,1024]{2,1,0:T(8,128)S(1)} %shard_map.106.a_ref, f32[16,64,1024]{2,1,0:T(8,128)} %collective-permute-done.5.b_ref), custom_call_target="tpu_custom_call" | custom-call | flops 6291456 | bytes 8388608 | tf_op jit(solution)/shard_map/pallas_call | solution.py:134
  57.5 2.4 %collective-permute-start.6 = (f32[1,8,128]{2,1,0:T(8,128)S(1)}, f32[1,8,128]{2,1,0:T(8,128)S(1)}, u32[]{:S(2)}, u32[]{:S(2)}) collective-permute-start(f32[1,8,128]{2,1,0:T(8,128)S(1)} %shard_map.108), channel_id=1, source_target_pairs={{0,1},{1,0},{2,3},{3,2},{4,5},{5,4},{6,7},{7,6},{8,9},{9,8},{10,11... | collective-permute-start | bytes 12296 | tf_op jit(solution)/shard_map/ppermute | solution.py:324
  59.9 0.8 collective-permute-done.6
  60.7 1.2 collective-permute-start.8
  61.9 0.9 collective-permute-start.7
  63.4 1.5 %collective-permute-done.8.refs_2_ = f32[1,8,128]{2,1,0:T(8,128)S(1)} collective-permute-done((f32[1,8,128]{2,1,0:T(8,128)S(1)}, f32[1,8,128]{2,1,0:T(8,128)S(1)}, u32[]{:S(2)}, u32[]{:S(2)}) %collective-permute-start.8) | collective-permute-done | bytes 4128 | tf_op jit(solution)/shard_map/ppermute | solution.py:328
  65.0 0.9 collective-permute-done.7.refs_1_
  65.9 3.2 %shard_map.109 = (f32[16,64,1024]{2,1,0:T(8,128)S(1)}, f32[8,128]{1,0:T(8,128)S(1)}) custom-call(s32[1]{0:T(128)} %bitcast.2.core_ref, f32[16,64,1024]{2,1,0:T(8,128)S(1)} %shard_map.106.a_ref, f32[16,64,1024]{2,1,0:T(8,128)} %collective-permute-done.5.b_ref, f32[1,8,128]{2,1,0:T(8,128)S(1)} %add.7.refs_0_, f32[1,8,128]{2,1,0:T(8,128)S(1)} %collective-permute-done.7.refs_1_, ...), custom_call_target="tpu_custom_call" | custom-call | flops 3145728 | bytes 12582912 | tf_op jit(solution)/shard_map/pallas_call | solution.py:167
  69.1 1.8 %convert_element_type.13 = f16[16,64,1024]{2,1,0:T(8,128)(2,1)} convert(f32[16,64,1024]{2,1,0:T(8,128)S(1)} %get-tuple-element.21) | non-fusion elementwise | flops 1048576 | bytes 6291456 | tf_op jit(solution)/shard_map/convert_element_type | solution.py:331
  70.8 7.0 %all-to-all-start = ((f16[16,64,1024]{2,1,0:T(8,128)(2,1)}), f16[16,64,1024]{2,1,0:T(8,128)(2,1)}, u32[]{:S(2)}, u32[]{:S(2)}) async-start(f16[16,64,1024]{2,1,0:T(8,128)(2,1)} %convert_element_type.13), calls=%async_computation | async-start | bytes 4194304 | tf_op jit(solution)/shard_map/all_to_all | solution.py:332
  78.4 3.6 %shard_map.110.refs_0_ = f32[2,128]{1,0:T(2,128)S(1)} custom-call(s32[2]{0:T(128)S(1)} %pad_add_fusion.place_ref, f32[16,64,1024]{2,1,0:T(8,128)S(1)} %convert_element_type.16.v_ref.refs_0_, f32[8,128]{1,0:T(8,128)S(1)} %get-tuple-element.23.norm_ref), custom_call_target="tpu_custom_call" | custom-call | flops 20971520 | bytes 4194304 | tf_op jit(solution)/shard_map/pallas_call | solution.py:221
  82.1 1.9 %copy-done = f32[16,64,1024]{2,1,0:T(8,128)} copy-done((f32[16,64,1024]{2,1,0:T(8,128)}, f32[16,64,1024]{2,1,0:T(8,128)S(1)}, u32[]{:S(2)}) %copy-start) | copy-done | bytes 4194328
  84.0 19.5 %all-to-all-done = f16[16,64,1024]{2,1,0:T(8,128)(2,1)} async-done(((f16[16,64,1024]{2,1,0:T(8,128)(2,1)}), f16[16,64,1024]{2,1,0:T(8,128)(2,1)}, u32[]{:S(2)}, u32[]{:S(2)}) %all-to-all-start) | async-done | bytes 2097184 | tf_op jit(solution)/shard_map/all_to_all | solution.py:332
  103.5 2.1 %convert_element_type.14.v_ref.refs_3_ = f32[16,64,1024]{2,1,0:T(8,128)S(1)} convert(f16[16,64,1024]{2,1,0:T(8,128)(2,1)} %all-to-all-done) | non-fusion elementwise | flops 1048576 | bytes 6291456 | tf_op jit(solution)/shard_map/convert_element_type | solution.py:350
  105.6 3.7 %shard_map.111 = f32[128,4,128]{2,1,0:T(4,128)S(1)} custom-call(s32[2]{0:T(128)S(1)} %pad_add_fusion.place_ref, f32[16,64,1024]{2,1,0:T(8,128)S(1)} %convert_element_type.14.v_ref.refs_3_, f32[8,128]{1,0:T(8,128)S(1)} %get-tuple-element.22.norm_ref, f32[2,128]{1,0:T(2,128)S(1)} %shard_map.110.refs_0_), custom_call_target="tpu_custom_call" | custom-call | flops 20971520 | bytes 4194304 | tf_op jit(solution)/shard_map/pallas_call | solution.py:221
  109.3 2.0 %copy-done.1 = f32[16,64,1024]{2,1,0:T(8,128)} copy-done((f32[16,64,1024]{2,1,0:T(8,128)}, f32[16,64,1024]{2,1,0:T(8,128)S(1)}, u32[]{:S(2)}) %copy-start.1) | copy-done | bytes 4194328
  111.2 20.2 %all_to_all.15 = f32[128,4,128]{2,1,0:T(4,128)S(1)} all-to-all(f32[128,4,128]{2,1,0:T(4,128)S(1)} %shard_map.111), channel_id=1, replica_groups=mesh['shard'=4,'rep'=32] {'shard','rep'}, dimensions={0} | all-to-all | bytes 524288 | tf_op jit(solution)/shard_map/all_to_all | solution.py:352
  132.2 6.2 %shard_map.112 = (f32[64,1024]{1,0:T(8,128)}, f32[64,1024]{1,0:T(8,128)}, f32[64,1024]{1,0:T(8,128)}, f32[64,1024]{1,0:T(8,128)}) custom-call(f32[4,128]{1,0:T(4,128)} %reduce_sum.9.totals_ref, f32[16,64,1024]{2,1,0:T(8,128)} %copy-done, f32[64,1024]{1,0:T(8,128)} %refs_1_.1, f32[64,1024]{1,0:T(8,128)} %refs_2_.1, f32[16,64,1024]{2,1,0:T(8,128)} %copy-done.1, ...), custom_call_target="tpu_custom_call" | custom-call | flops 8388608 | bytes 10485760 | tf_op jit(solution)/shard_map/pallas_call | solution.py:296
  (28 shorter events, 4.5 us)
Async XLA Ops:
  0.6 2.2 %copy-start.2 = (bf16[2048,1024]{1,0:T(8,128)(2,1)S(1)}, bf16[2048,1024]{1,0:T(8,128)(2,1)}, u32[]{:S(2)}) copy-start(bf16[2048,1024]{1,0:T(8,128)(2,1)} %y_ref.3) | copy-start | bytes 12582916
  2.8 9.3 %copy-start.4 = (bf16[2048,1024]{1,0:T(8,128)(2,1)S(1)}, bf16[2048,1024]{1,0:T(8,128)(2,1)}, u32[]{:S(2)}) copy-start(bf16[2048,1024]{1,0:T(8,128)(2,1)} %y_ref.5) | copy-start | bytes 12582916
  10.6 8.6 %copy-start.6 = (bf16[1024,2048]{1,0:T(8,128)(2,1)}, bf16[1024,2048]{1,0:T(8,128)(2,1)S(1)}, u32[]{:S(2)}) copy-start(bf16[1024,2048]{1,0:T(8,128)(2,1)S(1)} %get-tuple-element.19.x_ref) | copy-start | bytes 12582916
  10.6 13.6 %collective-permute-start = (f32[16,64,1024]{2,1,0:T(8,128)S(1)}, f32[16,64,1024]{2,1,0:T(8,128)S(1)}, u32[]{:S(2)}, u32[]{:S(2)}) collective-permute-start(f32[16,64,1024]{2,1,0:T(8,128)S(1)} %get-tuple-element.17), channel_id=1, source_target_pairs={{0,1},{1,0},{2,3},{3,2},{4,5},{5,4},{6,7},{7,6},{8,9},{9,8},{10,11... | collective-permute-start | bytes 12582920 | tf_op jit(solution)/shard_map/ppermute | solution.py:335
  12.2 7.0 %copy-start.3 = (bf16[2048,1024]{1,0:T(8,128)(2,1)S(1)}, bf16[2048,1024]{1,0:T(8,128)(2,1)}, u32[]{:S(2)}) copy-start(bf16[2048,1024]{1,0:T(8,128)(2,1)} %y_ref.3) | copy-start | bytes 12582916
  19.2 34.4 %collective-permute-start.5 = (f32[16,64,1024]{2,1,0:T(8,128)}, f32[16,64,1024]{2,1,0:T(8,128)}, u32[]{:S(2)}, u32[]{:S(2)}) collective-permute-start(f32[16,64,1024]{2,1,0:T(8,128)} %shard_map.107), channel_id=1, source_target_pairs={{0,1},{1,0},{2,3},{3,2},{4,5},{5,4},{6,7},{7,6},{8,9},{9,8},{10,11... | collective-permute-start | bytes 12582920 | tf_op jit(solution)/shard_map/ppermute | solution.py:339
  26.0 1.3 collective-permute-start.1
  27.3 3.7 %collective-permute-start.4 = (f32[1,8,128]{2,1,0:T(8,128)S(1)}, f32[1,8,128]{2,1,0:T(8,128)S(1)}, u32[]{:S(2)}, u32[]{:S(2)}) collective-permute-start(f32[1,8,128]{2,1,0:T(8,128)S(1)} %add.6.refs_0_), channel_id=1, source_target_pairs={{0,96},{32,0},{64,32},{96,64},{1,97},{33,1},{65,33},{97,65},{2,98}... | collective-permute-start | bytes 12296 | tf_op jit(solution)/shard_map/ppermute | solution.py:328
  29.9 4.0 %collective-permute-start.3 = (f32[1,8,128]{2,1,0:T(8,128)S(1)}, f32[1,8,128]{2,1,0:T(8,128)S(1)}, u32[]{:S(2)}, u32[]{:S(2)}) collective-permute-start(f32[1,8,128]{2,1,0:T(8,128)S(1)} %add.6.refs_0_), channel_id=1, source_target_pairs={{0,64},{32,96},{64,0},{96,32},{1,65},{33,97},{65,1},{97,33},{2,66}... | collective-permute-start | bytes 12296 | tf_op jit(solution)/shard_map/ppermute | solution.py:328
  30.4 3.7 %collective-permute-start.2 = (f32[1,8,128]{2,1,0:T(8,128)S(1)}, f32[1,8,128]{2,1,0:T(8,128)S(1)}, u32[]{:S(2)}, u32[]{:S(2)}) collective-permute-start(f32[1,8,128]{2,1,0:T(8,128)S(1)} %add.6.refs_0_), channel_id=1, source_target_pairs={{0,32},{32,64},{64,96},{96,0},{1,33},{33,65},{65,97},{97,1},{2,34}... | collective-permute-start | bytes 12296 | tf_op jit(solution)/shard_map/ppermute | solution.py:328
  36.4 34.4 %all-to-all-start.1 = ((f16[16,64,1024]{2,1,0:T(8,128)(2,1)}), f16[16,64,1024]{2,1,0:T(8,128)(2,1)S(1)}, u32[]{:S(2)}, u32[]{:S(2)}) async-start(f16[16,64,1024]{2,1,0:T(8,128)(2,1)} %convert_element_type.15), calls=%async_computation.1 | async-start | bytes 4194304 | tf_op jit(solution)/shard_map/all_to_all | solution.py:332
  44.2 2.2 %copy-start.5 = (bf16[2048,1024]{1,0:T(8,128)(2,1)S(1)}, bf16[2048,1024]{1,0:T(8,128)(2,1)}, u32[]{:S(2)}) copy-start(bf16[2048,1024]{1,0:T(8,128)(2,1)} %y_ref.5) | copy-start | bytes 12582916
  46.4 2.2 %copy-start.7 = (bf16[1024,2048]{1,0:T(8,128)(2,1)S(1)}, bf16[1024,2048]{1,0:T(8,128)(2,1)}, u32[]{:S(2)}) copy-start(bf16[1024,2048]{1,0:T(8,128)(2,1)} %copy-done.6) | copy-start | bytes 12582916
  57.5 3.2 %collective-permute-start.6 = (f32[1,8,128]{2,1,0:T(8,128)S(1)}, f32[1,8,128]{2,1,0:T(8,128)S(1)}, u32[]{:S(2)}, u32[]{:S(2)}) collective-permute-start(f32[1,8,128]{2,1,0:T(8,128)S(1)} %shard_map.108), channel_id=1, source_target_pairs={{0,1},{1,0},{2,3},{3,2},{4,5},{5,4},{6,7},{7,6},{8,9},{9,8},{10,11... | collective-permute-start | bytes 12296 | tf_op jit(solution)/shard_map/ppermute | solution.py:324
  60.7 2.8 %collective-permute-start.9 = (f32[1,8,128]{2,1,0:T(8,128)S(1)}, f32[1,8,128]{2,1,0:T(8,128)S(1)}, u32[]{:S(2)}, u32[]{:S(2)}) collective-permute-start(f32[1,8,128]{2,1,0:T(8,128)S(1)} %add.7.refs_0_), channel_id=1, source_target_pairs={{0,96},{32,0},{64,32},{96,64},{1,97},{33,1},{65,33},{97,65},{2,98}... | collective-permute-start | bytes 12296 | tf_op jit(solution)/shard_map/ppermute | solution.py:328
  60.7 4.3 %collective-permute-start.8 = (f32[1,8,128]{2,1,0:T(8,128)S(1)}, f32[1,8,128]{2,1,0:T(8,128)S(1)}, u32[]{:S(2)}, u32[]{:S(2)}) collective-permute-start(f32[1,8,128]{2,1,0:T(8,128)S(1)} %add.7.refs_0_), channel_id=1, source_target_pairs={{0,64},{32,96},{64,0},{96,32},{1,65},{33,97},{65,1},{97,33},{2,66}... | collective-permute-start | bytes 12296 | tf_op jit(solution)/shard_map/ppermute | solution.py:328
  61.9 4.0 %collective-permute-start.7 = (f32[1,8,128]{2,1,0:T(8,128)S(1)}, f32[1,8,128]{2,1,0:T(8,128)S(1)}, u32[]{:S(2)}, u32[]{:S(2)}) collective-permute-start(f32[1,8,128]{2,1,0:T(8,128)S(1)} %add.7.refs_0_), channel_id=1, source_target_pairs={{0,32},{32,64},{64,96},{96,0},{1,33},{33,65},{65,97},{97,1},{2,34}... | collective-permute-start | bytes 12296 | tf_op jit(solution)/shard_map/ppermute | solution.py:328
  70.8 32.6 %all-to-all-start = ((f16[16,64,1024]{2,1,0:T(8,128)(2,1)}), f16[16,64,1024]{2,1,0:T(8,128)(2,1)}, u32[]{:S(2)}, u32[]{:S(2)}) async-start(f16[16,64,1024]{2,1,0:T(8,128)(2,1)} %convert_element_type.13), calls=%async_computation | async-start | bytes 4194304 | tf_op jit(solution)/shard_map/all_to_all | solution.py:332
  82.0 1.9 %copy-start = (f32[16,64,1024]{2,1,0:T(8,128)}, f32[16,64,1024]{2,1,0:T(8,128)S(1)}, u32[]{:S(2)}) copy-start(f32[16,64,1024]{2,1,0:T(8,128)S(1)} %convert_element_type.16.v_ref.refs_0_) | copy-start | bytes 12582916
  109.2 2.0 %copy-start.1 = (f32[16,64,1024]{2,1,0:T(8,128)}, f32[16,64,1024]{2,1,0:T(8,128)S(1)}, u32[]{:S(2)}) copy-start(f32[16,64,1024]{2,1,0:T(8,128)S(1)} %convert_element_type.14.v_ref.refs_3_) | copy-start | bytes 12582916

commit v3 on v2

--- a/solution.py
+++ b/solution.py
@@ -36,10 +36,27 @@
     return (product * (1.0 / math.sqrt(rows.shape[1]))).reshape(-1, ROWS, FEATURES)
 
 
-def split_kernel(core_ref, x_hbm, y_hbm, grad_ref, own_ref, other_ref, x_ref, y_ref, x_sems, y_sem):
-    steps, depth, width = x_ref.shape
+def split_part(is_first, x_ref, y_ref, grad_ref, own_ref, other_ref, i):
+    depth, width = x_ref.shape
+    half = width // 2
+    per = half // ROWS
+    blocks = x_ref[...].T.reshape(-1, 2, ROWS, depth)
+    first = blocks[:, 0].reshape(-1, depth)
+    second = blocks[:, 1].reshape(-1, depth)
+    own_ref[pl.ds(i * half, half), :] = jnp.where(is_first, first, second)
+    other = jnp.where(is_first, second, first)
+    other_ref[pl.ds(i * half, half), :] = other
+    if callable(y_ref):
+        y_ref = y_ref()
+    grad_ref[pl.ds(i * per, per)] = scaled_dot(other, y_ref[...])
+
+
+def split_kernel(core_ref, x_hbm, y_hbm, grad_ref, own_ref, other_ref, y_ref, x_ref, x_sems, y_sem, *, start):
+    steps, _, width = x_ref.shape
     x_copies = [
-        pltpu.make_async_copy(x_hbm.at[:, pl.ds(i * width, width)], x_ref.at[i], x_sems.at[i])
+        pltpu.make_async_copy(
+            x_hbm.at[:, pl.ds(start + i * width, width)], x_ref.at[i], x_sems.at[i]
+        )
         for i in range(steps)
     ]
     y_copy = pltpu.make_async_copy(y_hbm, y_ref, y_sem)
@@ -48,64 +65,95 @@
     for copy in x_copies[1:]:
         copy.start()
     is_first = core_ref[0] == 0
-    half = width // 2
-    per = half // ROWS
+
+    def waited():
+        y_copy.wait()
+        return y_ref
+
     for i in range(steps):
         x_copies[i].wait()
-        blocks = x_ref[i].T.reshape(-1, 2, ROWS, depth)
-        first = blocks[:, 0].reshape(-1, depth)
-        second = blocks[:, 1].reshape(-1, depth)
-        own_ref[pl.ds(i * half, half), :] = jnp.where(is_first, first, second)
-        other = jnp.where(is_first, second, first)
-        other_ref[pl.ds(i * half, half), :] = other
-        if i == 0:
-            y_copy.wait()
-        grad_ref[pl.ds(i * per, per)] = scaled_dot(other, y_ref[...])
+        y = waited if i == 0 else y_ref
+        split_part(is_first, x_ref.at[i], y, grad_ref, own_ref, other_ref, i)
 
 
 def split_and_grad(core, tokens, cotangent):
     depth, width = tokens.shape
     step = 512
-    half = jax.ShapeDtypeStruct((width // 2, depth), jnp.bfloat16)
+    steps = width // (2 * step)
+    half = jax.ShapeDtypeStruct((width // 4, depth), jnp.bfloat16)
+    part = jax.ShapeDtypeStruct((CHIPS // 2, ROWS, FEATURES), jnp.float32)
+    held = jax.ShapeDtypeStruct(cotangent.shape, jnp.bfloat16)
     hbm = pl.BlockSpec(memory_space=pltpu.HBM)
+    halves = []
+    for n in range(2):
+        scratch = [
+            pltpu.VMEM((steps, depth, step), jnp.bfloat16),
+            pltpu.SemaphoreType.DMA((steps,)),
+            pltpu.SemaphoreType.DMA,
+        ]
+        halves.append(
+            pl.pallas_call(
+                functools.partial(split_kernel, start=n * (width // 2)),
+                out_shape=(part, half, half) + (held,) * n,
+                in_specs=[SMEM, hbm, hbm],
+                out_specs=(VMEM,) * (3 + n),
+                scratch_shapes=([] if n else [pltpu.VMEM(held.shape, held.dtype)]) + scratch,
+                compiler_params=params(42 if n else 52),
+                cost_estimate=cost(depth * width * FEATURES // 2, 12 * MIB),
+            )(core, tokens, cotangent)
+        )
+    return [half[:3] for half in halves], halves[1][3]
+
+
+def grad_kernel(*refs, parts):
+    x_refs, y_ref, o_ref = refs[:parts], refs[parts], refs[-1]
+    step = 256
+    at = 0
+    for x_ref in x_refs:
+        count = x_ref.shape[0] // step
+
+        @pl.loop(0, count)
+        def _(i, x_ref=x_ref, at=at):
+            rows = x_ref[pl.ds(pl.multiple_of(i * step, step), step), :]
+            per = step // ROWS
+            o_ref[pl.ds(at + i * per, per)] = scaled_dot(rows, y_ref[...])
+
+        at += x_ref.shape[0] // ROWS
+
+
+def grad(rows, cotangent, kept=()):
+    depth = cotangent.shape[0]
+    count = sum(part.shape[0] for part in rows)
     return pl.pallas_call(
-        split_kernel,
-        out_shape=(jax.ShapeDtypeStruct((CHIPS, ROWS, FEATURES), jnp.float32), half, half),
-        in_specs=[SMEM, hbm, hbm],
-        out_specs=(VMEM, VMEM, VMEM),
-        scratch_shapes=[
-            pltpu.VMEM((width // step, depth, step), jnp.bfloat16),
-            pltpu.VMEM(cotangent.shape, jnp.bfloat16),
-            pltpu.SemaphoreType.DMA((width // step,)),
-            pltpu.SemaphoreType.DMA,
-        ],
-        compiler_params=params(32),
-        cost_estimate=cost(depth * width * FEATURES, 24 * MIB),
-    )(core, tokens, cotangent)
-
-
-def grad_kernel(x_ref, y_ref, o_ref):
-    step = 256
-
-    @pl.loop(0, x_ref.shape[0] // step)
-    def _(i):
-        rows = x_ref[pl.ds(pl.multiple_of(i * step, step), step), :]
-        o_ref[pl.ds(i * (step // ROWS), step // ROWS)] = scaled_dot(rows, y_ref[...])
-
-
-def grad(rows, cotangent):
-    count, depth = rows.shape
-    return pl.pallas_call(
-        grad_kernel,
-        out_shape=jax.ShapeDtypeStruct((CHIPS, ROWS, FEATURES), jnp.float32),
-        in_specs=[VMEM, VMEM],
+        functools.partial(grad_kernel, parts=len(rows)),
+        out_shape=jax.ShapeDtypeStruct((count // ROWS, ROWS, FEATURES), jnp.float32),
+        in_specs=[VMEM] * (len(rows) + 1 + len(kept)),
         out_specs=VMEM,
-        compiler_params=params(20),
-        cost_estimate=cost(2 * depth * count * FEATURES, 12 * MIB),
-    )(rows, cotangent)
-
-
-def pair_kernel(core_ref, a_ref, b_ref, o_ref, acc_ref):
+        compiler_params=params(8),
+        cost_estimate=cost(count, MIB),
+    )(*rows, cotangent, *kept)
+
+
+def parts_specs(parts):
+    steps = parts[0].shape[0] // 4
+    return [
+        pl.BlockSpec(
+            (4, ROWS, FEATURES),
+            lambda i, n=n: (jnp.clip(i - n * steps, 0, steps - 1), 0, 0),
+        )
+        for n in range(len(parts))
+    ]
+
+
+def block_of(refs, steps):
+    block = refs[0][...]
+    for n in range(1, len(refs)):
+        block = jnp.where(pl.program_id(0) >= n * steps, refs[n][...], block)
+    return block
+
+
+def pair_kernel(core_ref, a_ref, *refs, steps):
+    b_refs, (o_ref, acc_ref) = refs[:-2], refs[-2:]
     step = pl.program_id(0)
 
     @pl.when(step == 0)
@@ -113,7 +161,7 @@
         acc_ref[...] = jnp.zeros_like(acc_ref)
 
     a = a_ref[...].reshape(-1, 8, FEATURES)
-    b = b_ref[...].reshape(-1, 8, FEATURES)
+    b = block_of(b_refs, steps).reshape(-1, 8, FEATURES)
     is_first = core_ref[0] == 0
     own, other = jnp.sum(a * a, axis=0), jnp.sum(b * b, axis=0)
     acc_ref[0] += jnp.sum(a * b, axis=0)
@@ -132,19 +180,19 @@
 def pair_sums(core, a, b, copies):
     spec = pl.BlockSpec((4, ROWS, FEATURES), lambda i: (i, 0, 0))
     return pl.pallas_call(
-        pair_kernel,
+        functools.partial(pair_kernel, steps=b[0].shape[0] // 4),
         out_shape=jax.ShapeDtypeStruct((copies, 8, 128), jnp.float32),
         grid=(CHIPS // 4,),
-        in_specs=[SMEM, spec, spec],
+        in_specs=[SMEM, spec] + parts_specs(b),
         out_specs=pl.BlockSpec((copies, 8, 128), lambda i: (0, 0, 0)),
         scratch_shapes=[pltpu.VMEM((3, 8, FEATURES), jnp.float32)],
-        compiler_params=params(12),
-        cost_estimate=cost(6 * a.size, 8 * a.size),
-    )(core, a, b)
-
-
-def merge_kernel(core_ref, a_ref, b_ref, *refs):
-    sums_refs, (o_ref, norm_ref) = refs[:-2], refs[-2:]
+        compiler_params=params(10),
+        cost_estimate=cost(a.size, a.size),
+    )(core, a, *b)
+
+
+def merge_kernel(core_ref, a_ref, *refs, parts, steps):
+    b_refs, sums_refs, (o_ref, norm_ref) = refs[:parts], refs[parts:-2], refs[-2:]
     sums = sum(jnp.sum(ref[...], axis=0) for ref in sums_refs)
     cross, p, q = sums[0:1], sums[1:2], sums[2:3]
     is_first = core_ref[0] == 0
@@ -159,28 +207,32 @@
     other = jnp.where(is_first, second, first) * scale
     own = jnp.concatenate([own] * (FEATURES // 128), axis=1)[None]
     other = jnp.concatenate([other] * (FEATURES // 128), axis=1)[None]
-    o_ref[...] = own * a_ref[...] + other * b_ref[...]
+    o_ref[...] = own * a_ref[...] + other * block_of(b_refs, steps)
 
 
 def merge_pair(core, a, b, sums):
     spec = pl.BlockSpec((4, ROWS, FEATURES), lambda i: (i, 0, 0))
     return pl.pallas_call(
-        merge_kernel,
+        functools.partial(merge_kernel, parts=len(b), steps=b[0].shape[0] // 4),
         out_shape=(
             jax.ShapeDtypeStruct(a.shape, jnp.float32),
             jax.ShapeDtypeStruct((8, 128), jnp.float32),
         ),
         grid=(CHIPS // 4,),
-        in_specs=[SMEM, spec, spec] + [VMEM] * len(sums),
+        in_specs=[SMEM, spec] + parts_specs(b) + [VMEM] * len(sums),
         out_specs=(spec, pl.BlockSpec((8, 128), lambda i: (0, 0))),
         compiler_params=params(12),
-        cost_estimate=cost(3 * a.size, 12 * a.size),
-    )(core, a, b, *sums)
+        cost_estimate=cost(a.size, a.size),
+    )(core, a, *b, *sums)
 
 
 def gram_kernel(place_ref, v_ref, norm_ref, *refs):
     earlier_refs, (o_ref, t_ref) = refs[:-2], refs[-2:]
-    t_ref[...] = jnp.zeros_like(t_ref)
+
+    @pl.when(pl.program_id(0) == 0)
+    def _():
+        t_ref[...] = jnp.zeros_like(t_ref)
+
     for gi in range(4):
         for gj in range(gi, 4):
             pairs = [
@@ -204,27 +256,33 @@
                 return tuple(sums)
 
             zero = jnp.zeros((8, 128), jnp.float32)
-            sums = lax.fori_loop(0, ROWS // 8, body, (zero,) * len(pairs))
+            sums = lax.fori_loop(0, v_ref.shape[1] // 8, body, (zero,) * len(pairs))
             for pair, total in zip(pairs, sums):
-                t_ref[pl.ds(PAIRS[pair], 1), :] = jnp.sum(total, axis=0, keepdims=True)
-    lane = lax.broadcasted_iota(jnp.int32, (1, 128), 1)
-    shown = (lane == 0) & (place_ref[1] == 1)
-    t_ref[pl.ds(len(PAIRS) + place_ref[0], 1), :] = jnp.where(shown, norm_ref[0:1, :], 0.0)
-    rows = [ref[...] for ref in earlier_refs]
-    for part in range(2):
-        rows.append(jnp.sum(t_ref[pl.ds(part * 128, 128), :].T, axis=0, keepdims=True))
-    tile = jnp.concatenate(rows, axis=0)
-    o_ref[...] = tile if o_ref.ndim == 2 else jnp.broadcast_to(tile[None], o_ref.shape)
+                t_ref[pl.ds(PAIRS[pair], 1), :] += jnp.sum(total, axis=0, keepdims=True)
+
+    @pl.when(pl.program_id(0) == pl.num_programs(0) - 1)
+    def _():
+        lane = lax.broadcasted_iota(jnp.int32, (1, 128), 1)
+        shown = (lane == 0) & (place_ref[1] == 1)
+        t_ref[pl.ds(len(PAIRS) + place_ref[0], 1), :] = jnp.where(shown, norm_ref[0:1, :], 0.0)
+        rows = [ref[...] for ref in earlier_refs]
+        for part in range(2):
+            rows.append(jnp.sum(t_ref[pl.ds(part * 128, 128), :].T, axis=0, keepdims=True))
+        tile = jnp.concatenate(rows, axis=0)
+        o_ref[...] = tile if o_ref.ndim == 2 else jnp.broadcast_to(tile[None], o_ref.shape)
 
 
 def gram(place, v, norm, earlier, out_dims):
+    step = 16
     return pl.pallas_call(
         gram_kernel,
         out_shape=jax.ShapeDtypeStruct(out_dims, jnp.float32),
-        in_specs=[SMEM] + [VMEM] * (2 + len(earlier)),
+        grid=(ROWS // step,),
+        in_specs=[SMEM, pl.BlockSpec((CHIPS, step, FEATURES), lambda i: (0, i, 0))]
+        + [VMEM] * (1 + len(earlier)),
         out_specs=VMEM,
         scratch_shapes=[pltpu.VMEM((256, 128), jnp.float32)],
-        compiler_params=params(16),
+        compiler_params=params(56),
         cost_estimate=cost(20 << 20, 4 * v.size),
     )(place, v, norm, *earlier)
 
@@ -327,23 +385,25 @@
         ]
         return [sums] + [lax.ppermute(sums, "shard", shift) for shift in shifts]
 
-    def gathered(merged):
-        sent = merged.astype(jnp.float16)
+    def gathered(sent):
         return lax.all_to_all(sent, "rep", 0, 0, axis_index_groups=core_groups)
 
-    key_other, own_rows, other_rows = split_and_grad(core, tokens, key_cotangent)
-    key_arrived = lax.ppermute(key_other, "rep", swap)
+    halves, key_cotangent = split_and_grad(core, tokens, key_cotangent)
+    own_rows = [half[1] for half in halves]
+    other_rows = [half[2] for half in halves]
+    key_arrived = [lax.ppermute(half[0], "rep", swap) for half in halves]
     key_own = grad(own_rows, key_cotangent)
     key_sums = summed(pair_sums(core, key_own, key_arrived, 1))
-    value_other = grad(other_rows, value_cotangent)
-    value_arrived = lax.ppermute(value_other, "rep", swap)
+    value_other = grad(after(other_rows, key_sums[0]), value_cotangent, [key_own] + key_arrived)
     key_merged, key_norm = merge_pair(core, key_own, key_arrived, key_sums)
-    key_all = gathered(key_merged)
-
-    value_own = grad(after(own_rows, key_merged), value_cotangent)
+    key_sent = key_merged.astype(jnp.float16)
+    key_all = gathered(key_sent)
+
+    value_arrived = [lax.ppermute(after(value_other, key_sent), "rep", swap)]
+    value_own = grad(after(own_rows, key_sent), value_cotangent)
     value_sums = summed(pair_sums(core, value_own, value_arrived, 1))
     value_merged, value_norm = merge_pair(core, value_own, value_arrived, value_sums)
-    value_all = gathered(value_merged)
+    value_all = gathered(value_merged.astype(jnp.float16))
 
     key_v = key_all.astype(jnp.float32)
     key_vector = gram(place, key_v, key_norm, [], (2, 128))

time: 139 us -> 145 us (1.043)
  Pallas kernels: 47.7 us -> 58.9 us
  local copies, waits for them, and re-layouts: 10.5 us -> 4.39 us
  other arithmetic: 6.88 us -> 11.4 us
  waiting for transfers between devices: 27.3 us -> 23.1 us
    pallas_call x8 -> x9, Pallas kernels: 34.2 us -> 40.7 us  [the longest x3 17.2 us: grad(): pl.pallas_call(functools.partial(grad_kernel, parts=len(rows)), out_shape...]
    unnamed x16, local copies, waits for them, and re-layouts: 10.5 us -> 4.39 us
    pallas_call x2, Pallas kernels: 7.31 us -> 12 us  [gram(): pl.pallas_call(gram_kernel, out_shape=jax.ShapeDtypeStruct(out_dims, jnp....]
    convert_element_type x1, other arithmetic: 0.48 us -> 4.04 us  [shards(): key_v = key_all.astype(jnp.float32)]
    ppermute x6, waiting for transfers between devices: 6.17 us -> 3.97 us  [summed(): return [sums] + [lax.ppermute(sums, 'shard', shift) for shift in shifts]]
    ppermute x2, starting transfers between devices: 2.88 us -> 0.72 us  [summed(): sums = sums + lax.ppermute(sums, 'rep', swap)]
    all_to_all x2, waiting for transfers between devices: 19.5 us -> 17.4 us  [gathered(): return lax.all_to_all(sent, 'rep', 0, 0, axis_index_groups=core_groups)]
    ppermute x2 -> x3, starting transfers between devices: 1.53 us -> 2.92 us  [the longest x2 1.73 us: shards(): key_arrived = [lax.ppermute(half[0], 'rep', swap) for half in halves]]
  transfers between devices with their start and end apart: 12 -> 13, of which waited for: 8 -> 6; matrix products, arithmetic and copies ran while one was open for 3% -> 4% of each run, Pallas kernels for 22% -> 25%
where the time goes in v3:
time: 145 us; the launch traced here: 144 us
  Pallas kernels  58.9 us (41%)
  starting transfers between devices  24.2 us (17%)
  waiting for transfers between devices  23.1 us (16%)
  blocking collectives  21.4 us (15%)
  other arithmetic  11.4 us (8%)
  local copies, waits for them, and re-layouts  4.39 us (3%)
    all_to_all x1, blocking collectives, shards(): totals = jnp.sum(lax.all_to_all(vectors, ('shard', 'rep'), 0, 0), axis=0)  21.4 us
    all_to_all x2, waiting for transfers between devices, gathered(): return lax.all_to_all(sent, 'rep', 0, 0, axis_index_groups=core_groups)  17.4 us
    pallas_call x3, Pallas kernels, grad(): pl.pallas_call(functools.partial(grad_kernel, parts=len(rows)), out_shape...  17.2 us
    all_to_all x2, starting transfers between devices, gathered(): return lax.all_to_all(sent, 'rep', 0, 0, axis_index_groups=core_groups)  13.5 us
    pallas_call x2, Pallas kernels, split_and_grad(): pl.pallas_call(functools.partial(split_kernel, start=n * (width // 2)), o...  12.9 us
    pallas_call x2, Pallas kernels, gram(): pl.pallas_call(gram_kernel, out_shape=jax.ShapeDtypeStruct(out_dims, jnp....  12 us
    ppermute x6, starting transfers between devices, summed(): return [sums] + [lax.ppermute(sums, 'shard', shift) for shift in shifts]  6.97 us
    pallas_call x2, Pallas kernels, pair_sums(): pl.pallas_call(functools.partial(pair_kernel, steps=b[0].shape[0] // 4),...  6.36 us
  transfers between devices with their start and end apart: 13, of which 6 were waited for; matrix products, arithmetic and copies ran while one was open for 4% of the time, Pallas kernels for 25%

profile of v3, /device:TPU:1, one launch (start us, length us, event | category | flops | bytes accessed | tf_op | source)
XLA Modules:
  0.0 144.3 jit_solution(10567139478431344575)
XLA Ops:
  0.6 7.4 %shard_map.102 = (f32[8,64,1024]{2,1,0:T(8,128)}, bf16[512,2048]{1,0:T(8,128)(2,1)}, bf16[512,2048]{1,0:T(8,128)(2,1)}) custom-call(s32[1]{0:T(128)} %bitcast.2.core_ref, bf16[2048,2048]{1,0:T(8,128)(2,1)} %x_hbm.3, bf16[2048,1024]{1,0:T(8,128)(2,1)} %y_hbm.3), custom_call_target="tpu_custom_call" | custom-call | flops 2147483648 | bytes 12582912 | tf_op jit(solution)/shard_map/pallas_call | solution.py:95
  8.0 1.5 %collective-permute-start = (f32[8,64,1024]{2,1,0:T(8,128)}, f32[8,64,1024]{2,1,0:T(8,128)S(1)}, u32[]{:S(2)}, u32[]{:S(2)}) collective-permute-start(f32[8,64,1024]{2,1,0:T(8,128)} %get-tuple-element.27), channel_id=1, source_target_pairs={{0,1},{1,0},{2,3},{3,2},{4,5},{5,4},{6,7},{7,6},{8,9},{9,8},{10,11... | collective-permute-start | bytes 6291464 | tf_op jit(solution)/shard_map/ppermute | solution.py:394
  9.5 5.5 %shard_map.103 = (f32[8,64,1024]{2,1,0:T(8,128)S(1)}, bf16[512,2048]{1,0:T(8,128)(2,1)S(1)}, bf16[512,2048]{1,0:T(8,128)(2,1)S(1)}, bf16[2048,1024]{1,0:T(8,128)(2,1)S(1)}) custom-call(s32[1]{0:T(128)} %bitcast.2.core_ref, bf16[2048,2048]{1,0:T(8,128)(2,1)} %x_hbm.3, bf16[2048,1024]{1,0:T(8,128)(2,1)} %y_hbm.3), custom_call_target="tpu_custom_call" | custom-call | flops 2147483648 | bytes 12582912 | tf_op jit(solution)/shard_map/pallas_call | solution.py:95
  15.3 5.1 %shard_map.104.a_ref.refs_3_ = f32[16,64,1024]{2,1,0:T(8,128)S(1)} custom-call(bf16[512,2048]{1,0:T(8,128)(2,1)S(1)} %copy-done.2, bf16[512,2048]{1,0:T(8,128)(2,1)S(1)} %get-tuple-element.31.refs_1_, bf16[2048,1024]{1,0:T(8,128)(2,1)S(1)} %get-tuple-element.26.refs_2_), custom_call_target="tpu_custom_call" | custom-call | flops 1024 | bytes 1048576 | tf_op jit(solution)/shard_map/pallas_call | solution.py:127
  20.5 2.5 %shard_map.105 = f32[1,8,128]{2,1,0:T(8,128)S(1)} custom-call(s32[1]{0:T(128)} %bitcast.2.core_ref, f32[16,64,1024]{2,1,0:T(8,128)S(1)} %shard_map.104.a_ref.refs_3_, f32[8,64,1024]{2,1,0:T(8,128)S(1)} %collective-permute-done.refs_0_.refs_4_, f32[8,64,1024]{2,1,0:T(8,128)S(1)} %collective-permute-done.1.refs_1_.refs_5_), custom_call_target="tpu_custom_call" | custom-call | flops 1048576 | bytes 1048576 | tf_op jit(solution)/shard_map/pallas_call | solution.py:182
  23.4 0.8 collective-permute-done.2
  24.2 2.5 %collective-permute-start.5 = (f32[1,8,128]{2,1,0:T(8,128)S(1)}, f32[1,8,128]{2,1,0:T(8,128)S(1)}, u32[]{:S(2)}, u32[]{:S(2)}) collective-permute-start(f32[1,8,128]{2,1,0:T(8,128)S(1)} %add.6.refs_2_), channel_id=1, source_target_pairs={{0,96},{32,0},{64,32},{96,64},{1,97},{33,1},{65,33},{97,65},{2,98}... | collective-permute-start | bytes 12296 | tf_op jit(solution)/shard_map/ppermute | solution.py:386
  27.9 7.1 %shard_map.108 = f32[16,64,1024]{2,1,0:T(8,128)} custom-call(bf16[512,2048]{1,0:T(8,128)(2,1)S(1)} %copy-done.5, bf16[512,2048]{1,0:T(8,128)(2,1)S(1)} %get-tuple-element.35.refs_1_, bf16[2048,1024]{1,0:T(8,128)(2,1)S(1)} %copy-done, f32[16,64,1024]{2,1,0:T(8,128)S(1)} %shard_map.104.a_ref.refs_3_, f32[8,64,1024]{2,1,0:T(8,128)S(1)} %collective-permute-done.refs_0_.refs_4_, ...), custom_call_target="tpu_custom_call" | custom-call | flops 1024 | bytes 1048576 | tf_op jit(solution)/shard_map/pallas_call | solution.py:127
  35.0 1.0 shard_map.106
  36.0 1.8 %convert_element_type.13 = f16[16,64,1024]{2,1,0:T(8,128)(2,1)} convert(f32[16,64,1024]{2,1,0:T(8,128)S(1)} %get-tuple-element.29) | non-fusion elementwise | flops 1048576 | bytes 6291456 | tf_op jit(solution)/shard_map/convert_element_type | solution.py:399
  37.8 1.2 collective-permute-start.6
  39.0 7.8 %all-to-all-start.1 = ((f16[16,64,1024]{2,1,0:T(8,128)(2,1)}), f16[16,64,1024]{2,1,0:T(8,128)(2,1)}, u32[]{:S(2)}, u32[]{:S(2)}) async-start(f16[16,64,1024]{2,1,0:T(8,128)(2,1)} %convert_element_type.13), calls=%async_computation.1 | async-start | bytes 4194304 | tf_op jit(solution)/shard_map/all_to_all | solution.py:389
  46.8 2.2 %copy-done.1 = bf16[2048,1024]{1,0:T(8,128)(2,1)S(1)} copy-done((bf16[2048,1024]{1,0:T(8,128)(2,1)S(1)}, bf16[2048,1024]{1,0:T(8,128)(2,1)}, u32[]{:S(2)}) %copy-start.1) | copy-done | bytes 4194328
  49.0 1.6 %copy-done.4 = bf16[512,2048]{1,0:T(8,128)(2,1)S(1)} copy-done((bf16[512,2048]{1,0:T(8,128)(2,1)S(1)}, bf16[512,2048]{1,0:T(8,128)(2,1)}, u32[]{:S(2)}) %copy-start.4) | copy-done | bytes 2097176
  50.6 5.0 %shard_map.107.a_ref = f32[16,64,1024]{2,1,0:T(8,128)S(1)} custom-call(bf16[512,2048]{1,0:T(8,128)(2,1)S(1)} %copy-done.2, bf16[512,2048]{1,0:T(8,128)(2,1)S(1)} %copy-done.4, bf16[2048,1024]{1,0:T(8,128)(2,1)S(1)} %copy-done.1), custom_call_target="tpu_custom_call" | custom-call | flops 1024 | bytes 1048576 | tf_op jit(solution)/shard_map/pallas_call | solution.py:127
  55.6 3.9 %shard_map.109 = f32[1,8,128]{2,1,0:T(8,128)S(1)} custom-call(s32[1]{0:T(128)} %bitcast.2.core_ref, f32[16,64,1024]{2,1,0:T(8,128)S(1)} %shard_map.107.a_ref, f32[16,64,1024]{2,1,0:T(8,128)} %collective-permute-done.6.refs_0_), custom_call_target="tpu_custom_call" | custom-call | flops 1048576 | bytes 1048576 | tf_op jit(solution)/shard_map/pallas_call | solution.py:182
  59.8 0.9 collective-permute-done.7
  60.7 2.0 %collective-permute-start.10 = (f32[1,8,128]{2,1,0:T(8,128)S(1)}, f32[1,8,128]{2,1,0:T(8,128)S(1)}, u32[]{:S(2)}, u32[]{:S(2)}) collective-permute-start(f32[1,8,128]{2,1,0:T(8,128)S(1)} %add.7.refs_1_), channel_id=1, source_target_pairs={{0,96},{32,0},{64,32},{96,64},{1,97},{33,1},{65,33},{97,65},{2,98}... | collective-permute-start | bytes 12296 | tf_op jit(solution)/shard_map/ppermute | solution.py:386
  62.7 1.2 collective-permute-start.9
  64.0 3.1 %collective-permute-done.9.refs_3_ = f32[1,8,128]{2,1,0:T(8,128)S(1)} collective-permute-done((f32[1,8,128]{2,1,0:T(8,128)S(1)}, f32[1,8,128]{2,1,0:T(8,128)S(1)}, u32[]{:S(2)}, u32[]{:S(2)}) %collective-permute-start.9) | collective-permute-done | bytes 4128 | tf_op jit(solution)/shard_map/ppermute | solution.py:386
  67.1 0.8 collective-permute-done.8.refs_2_
  67.9 3.2 %shard_map.110 = (f32[16,64,1024]{2,1,0:T(8,128)S(1)}, f32[8,128]{1,0:T(8,128)S(1)}) custom-call(s32[1]{0:T(128)} %bitcast.2.core_ref, f32[16,64,1024]{2,1,0:T(8,128)S(1)} %shard_map.107.a_ref, f32[16,64,1024]{2,1,0:T(8,128)} %collective-permute-done.6.refs_0_, f32[1,8,128]{2,1,0:T(8,128)S(1)} %add.7.refs_1_, ...), custom_call_target="tpu_custom_call" | custom-call | flops 1048576 | bytes 1048576 | tf_op jit(solution)/shard_map/pallas_call | solution.py:215
  71.8 1.8 %convert_element_type.14 = f16[16,64,1024]{2,1,0:T(8,128)(2,1)} convert(f32[16,64,1024]{2,1,0:T(8,128)S(1)} %get-tuple-element.37) | non-fusion elementwise | flops 1048576 | bytes 6291456 | tf_op jit(solution)/shard_map/convert_element_type | solution.py:406
  73.6 2.4 %all-to-all-done.1 = f16[16,64,1024]{2,1,0:T(8,128)(2,1)} async-done(((f16[16,64,1024]{2,1,0:T(8,128)(2,1)}), f16[16,64,1024]{2,1,0:T(8,128)(2,1)}, u32[]{:S(2)}, u32[]{:S(2)}) %all-to-all-start.1) | async-done | bytes 2097184 | tf_op jit(solution)/shard_map/all_to_all | solution.py:389
  76.0 5.7 %all-to-all-start = ((f16[16,64,1024]{2,1,0:T(8,128)(2,1)}), f16[16,64,1024]{2,1,0:T(8,128)(2,1)S(1)}, u32[]{:S(2)}, u32[]{:S(2)}) async-start(f16[16,64,1024]{2,1,0:T(8,128)(2,1)} %convert_element_type.14), calls=%async_computation | async-start | bytes 4194304 | tf_op jit(solution)/shard_map/all_to_all | solution.py:389
  82.3 4.0 %convert_element_type.16.v_ref.refs_0_ = f32[16,64,1024]{2,1,0:T(8,128)} convert(f16[16,64,1024]{2,1,0:T(8,128)(2,1)} %all-to-all-done.1) | non-fusion elementwise | flops 1048576 | bytes 6291456 | tf_op jit(solution)/shard_map/convert_element_type | solution.py:408
  86.3 5.9 %shard_map.111.refs_0_ = f32[2,128]{1,0:T(2,128)} custom-call(s32[2]{0:T(128)} %pad_add_fusion.place_ref, f32[16,64,1024]{2,1,0:T(8,128)} %convert_element_type.16.v_ref.refs_0_, f32[8,128]{1,0:T(8,128)} %copy-done.7), custom_call_target="tpu_custom_call" | custom-call | flops 20971520 | bytes 4194304 | tf_op jit(solution)/shard_map/pallas_call | solution.py:277
  92.2 15.0 %all-to-all-done = f16[16,64,1024]{2,1,0:T(8,128)(2,1)S(1)} async-done(((f16[16,64,1024]{2,1,0:T(8,128)(2,1)}), f16[16,64,1024]{2,1,0:T(8,128)(2,1)S(1)}, u32[]{:S(2)}, u32[]{:S(2)}) %all-to-all-start) | async-done | bytes 2097184 | tf_op jit(solution)/shard_map/all_to_all | solution.py:389
  107.2 2.5 %convert_element_type.15.v_ref.refs_3_ = f32[16,64,1024]{2,1,0:T(8,128)} convert(f16[16,64,1024]{2,1,0:T(8,128)(2,1)S(1)} %all-to-all-done) | non-fusion elementwise | flops 1048576 | bytes 6291456 | tf_op jit(solution)/shard_map/convert_element_type | solution.py:410
  109.8 6.1 %shard_map.112 = f32[128,4,128]{2,1,0:T(4,128)} custom-call(s32[2]{0:T(128)} %pad_add_fusion.place_ref, f32[16,64,1024]{2,1,0:T(8,128)} %convert_element_type.15.v_ref.refs_3_, f32[8,128]{1,0:T(8,128)} %copy-done.6, f32[2,128]{1,0:T(2,128)} %shard_map.111.refs_0_), custom_call_target="tpu_custom_call" | custom-call | flops 20971520 | bytes 4194304 | tf_op jit(solution)/shard_map/pallas_call | solution.py:277
  115.9 21.4 %all_to_all.15 = f32[128,4,128]{2,1,0:T(4,128)S(1)} all-to-all(f32[128,4,128]{2,1,0:T(4,128)} %shard_map.112), channel_id=1, replica_groups=mesh['shard'=4,'rep'=32] {'shard','rep'}, dimensions={0} | all-to-all | bytes 524288 | tf_op jit(solution)/shard_map/all_to_all | solution.py:412
  138.0 6.2 %shard_map.113 = (f32[64,1024]{1,0:T(8,128)}, f32[64,1024]{1,0:T(8,128)}, f32[64,1024]{1,0:T(8,128)}, f32[64,1024]{1,0:T(8,128)}) custom-call(f32[4,128]{1,0:T(4,128)} %reduce_sum.9.totals_ref, f32[16,64,1024]{2,1,0:T(8,128)} %convert_element_type.16.v_ref.refs_0_, f32[64,1024]{1,0:T(8,128)} %refs_1_.1, f32[64,1024]{1,0:T(8,128)} %refs_2_.5, ...), custom_call_target="tpu_custom_call" | custom-call | flops 8388608 | bytes 10485760 | tf_op jit(solution)/shard_map/pallas_call | solution.py:354
  (31 shorter events, 4.0 us)
Async XLA Ops:
  8.0 7.3 %copy-start.2 = (bf16[512,2048]{1,0:T(8,128)(2,1)S(1)}, bf16[512,2048]{1,0:T(8,128)(2,1)}, u32[]{:S(2)}) copy-start(bf16[512,2048]{1,0:T(8,128)(2,1)} %get-tuple-element.30.refs_0_) | copy-start | bytes 6291460
  8.0 12.4 %collective-permute-start = (f32[8,64,1024]{2,1,0:T(8,128)}, f32[8,64,1024]{2,1,0:T(8,128)S(1)}, u32[]{:S(2)}, u32[]{:S(2)}) collective-permute-start(f32[8,64,1024]{2,1,0:T(8,128)} %get-tuple-element.27), channel_id=1, source_target_pairs={{0,1},{1,0},{2,3},{3,2},{4,5},{5,4},{6,7},{7,6},{8,9},{9,8},{10,11... | collective-permute-start | bytes 6291464 | tf_op jit(solution)/shard_map/ppermute | solution.py:394
  15.1 5.4 %copy-start.3 = (bf16[512,2048]{1,0:T(8,128)(2,1)}, bf16[512,2048]{1,0:T(8,128)(2,1)S(1)}, u32[]{:S(2)}) copy-start(bf16[512,2048]{1,0:T(8,128)(2,1)S(1)} %get-tuple-element.31.refs_1_) | copy-start | bytes 6291460
  15.1 5.4 %collective-permute-start.1 = (f32[8,64,1024]{2,1,0:T(8,128)S(1)}, f32[8,64,1024]{2,1,0:T(8,128)S(1)}, u32[]{:S(2)}, u32[]{:S(2)}) collective-permute-start(f32[8,64,1024]{2,1,0:T(8,128)S(1)} %get-tuple-element.28), channel_id=1, source_target_pairs={{0,1},{1,0},{2,3},{3,2},{4,5},{5,4},{6,7},{7,6},{8,9},{9,8},{10,11... | collective-permute-start | bytes 6291464 | tf_op jit(solution)/shard_map/ppermute | solution.py:394
  20.4 7.4 %copy-start = (bf16[2048,1024]{1,0:T(8,128)(2,1)S(1)}, bf16[2048,1024]{1,0:T(8,128)(2,1)}, u32[]{:S(2)}) copy-start(bf16[2048,1024]{1,0:T(8,128)(2,1)} %refs_2_.4) | copy-start | bytes 12582916
  20.5 7.4 %copy-start.5 = (bf16[512,2048]{1,0:T(8,128)(2,1)S(1)}, bf16[512,2048]{1,0:T(8,128)(2,1)}, u32[]{:S(2)}) copy-start(bf16[512,2048]{1,0:T(8,128)(2,1)} %get-tuple-element.34.refs_0_) | copy-start | bytes 6291460
  23.0 1.2 collective-permute-start.2
  24.2 10.8 %collective-permute-start.5 = (f32[1,8,128]{2,1,0:T(8,128)S(1)}, f32[1,8,128]{2,1,0:T(8,128)S(1)}, u32[]{:S(2)}, u32[]{:S(2)}) collective-permute-start(f32[1,8,128]{2,1,0:T(8,128)S(1)} %add.6.refs_2_), channel_id=1, source_target_pairs={{0,96},{32,0},{64,32},{96,64},{1,97},{33,1},{65,33},{97,65},{2,98}... | collective-permute-start | bytes 12296 | tf_op jit(solution)/shard_map/ppermute | solution.py:386
  26.7 8.3 %collective-permute-start.4 = (f32[1,8,128]{2,1,0:T(8,128)S(1)}, f32[1,8,128]{2,1,0:T(8,128)S(1)}, u32[]{:S(2)}, u32[]{:S(2)}) collective-permute-start(f32[1,8,128]{2,1,0:T(8,128)S(1)} %add.6.refs_2_), channel_id=1, source_target_pairs={{0,64},{32,96},{64,0},{96,32},{1,65},{33,97},{65,1},{97,33},{2,66}... | collective-permute-start | bytes 12296 | tf_op jit(solution)/shard_map/ppermute | solution.py:386
  27.3 7.7 %collective-permute-start.3 = (f32[1,8,128]{2,1,0:T(8,128)S(1)}, f32[1,8,128]{2,1,0:T(8,128)S(1)}, u32[]{:S(2)}, u32[]{:S(2)}) collective-permute-start(f32[1,8,128]{2,1,0:T(8,128)S(1)} %add.6.refs_2_), channel_id=1, source_target_pairs={{0,32},{32,64},{64,96},{96,0},{1,33},{33,65},{65,97},{97,1},{2,34}... | collective-permute-start | bytes 12296 | tf_op jit(solution)/shard_map/ppermute | solution.py:386
  36.0 1.8 %copy-start.7 = (f32[8,128]{1,0:T(8,128)}, f32[8,128]{1,0:T(8,128)S(1)}, u32[]{:S(2)}) copy-start(f32[8,128]{1,0:T(8,128)S(1)} %get-tuple-element.39.norm_ref) | copy-start | bytes 12292
  37.8 17.8 %collective-permute-start.6 = (f32[16,64,1024]{2,1,0:T(8,128)}, f32[16,64,1024]{2,1,0:T(8,128)}, u32[]{:S(2)}, u32[]{:S(2)}) collective-permute-start(f32[16,64,1024]{2,1,0:T(8,128)} %shard_map.108), channel_id=1, source_target_pairs={{0,1},{1,0},{2,3},{3,2},{4,5},{5,4},{6,7},{7,6},{8,9},{9,8},{10,11... | collective-permute-start | bytes 12582920 | tf_op jit(solution)/shard_map/ppermute | solution.py:402
  39.0 37.0 %all-to-all-start.1 = ((f16[16,64,1024]{2,1,0:T(8,128)(2,1)}), f16[16,64,1024]{2,1,0:T(8,128)(2,1)}, u32[]{:S(2)}, u32[]{:S(2)}) async-start(f16[16,64,1024]{2,1,0:T(8,128)(2,1)} %convert_element_type.13), calls=%async_computation.1 | async-start | bytes 4194304 | tf_op jit(solution)/shard_map/all_to_all | solution.py:389
  46.8 2.2 %copy-start.1 = (bf16[2048,1024]{1,0:T(8,128)(2,1)S(1)}, bf16[2048,1024]{1,0:T(8,128)(2,1)}, u32[]{:S(2)}) copy-start(bf16[2048,1024]{1,0:T(8,128)(2,1)} %refs_2_.4) | copy-start | bytes 12582916
  49.0 1.6 %copy-start.4 = (bf16[512,2048]{1,0:T(8,128)(2,1)S(1)}, bf16[512,2048]{1,0:T(8,128)(2,1)}, u32[]{:S(2)}) copy-start(bf16[512,2048]{1,0:T(8,128)(2,1)} %copy-done.3) | copy-start | bytes 6291460
  59.5 1.2 collective-permute-start.7
  60.7 3.3 %collective-permute-start.10 = (f32[1,8,128]{2,1,0:T(8,128)S(1)}, f32[1,8,128]{2,1,0:T(8,128)S(1)}, u32[]{:S(2)}, u32[]{:S(2)}) collective-permute-start(f32[1,8,128]{2,1,0:T(8,128)S(1)} %add.7.refs_1_), channel_id=1, source_target_pairs={{0,96},{32,0},{64,32},{96,64},{1,97},{33,1},{65,33},{97,65},{2,98}... | collective-permute-start | bytes 12296 | tf_op jit(solution)/shard_map/ppermute | solution.py:386
  62.7 4.4 %collective-permute-start.9 = (f32[1,8,128]{2,1,0:T(8,128)S(1)}, f32[1,8,128]{2,1,0:T(8,128)S(1)}, u32[]{:S(2)}, u32[]{:S(2)}) collective-permute-start(f32[1,8,128]{2,1,0:T(8,128)S(1)} %add.7.refs_1_), channel_id=1, source_target_pairs={{0,64},{32,96},{64,0},{96,32},{1,65},{33,97},{65,1},{97,33},{2,66}... | collective-permute-start | bytes 12296 | tf_op jit(solution)/shard_map/ppermute | solution.py:386
  64.0 4.0 %collective-permute-start.8 = (f32[1,8,128]{2,1,0:T(8,128)S(1)}, f32[1,8,128]{2,1,0:T(8,128)S(1)}, u32[]{:S(2)}, u32[]{:S(2)}) collective-permute-start(f32[1,8,128]{2,1,0:T(8,128)S(1)} %add.7.refs_1_), channel_id=1, source_target_pairs={{0,32},{32,64},{64,96},{96,0},{1,33},{33,65},{65,97},{97,1},{2,34}... | collective-permute-start | bytes 12296 | tf_op jit(solution)/shard_map/ppermute | solution.py:386
  71.2 0.6 copy-start.6
  76.0 31.3 %all-to-all-start = ((f16[16,64,1024]{2,1,0:T(8,128)(2,1)}), f16[16,64,1024]{2,1,0:T(8,128)(2,1)S(1)}, u32[]{:S(2)}, u32[]{:S(2)}) async-start(f16[16,64,1024]{2,1,0:T(8,128)(2,1)} %convert_element_type.14), calls=%async_computation | async-start | bytes 4194304 | tf_op jit(solution)/shard_map/all_to_all | solution.py:389

commit v4 on v3

--- a/solution.py
+++ b/solution.py
@@ -36,27 +36,10 @@
     return (product * (1.0 / math.sqrt(rows.shape[1]))).reshape(-1, ROWS, FEATURES)
 
 
-def split_part(is_first, x_ref, y_ref, grad_ref, own_ref, other_ref, i):
-    depth, width = x_ref.shape
-    half = width // 2
-    per = half // ROWS
-    blocks = x_ref[...].T.reshape(-1, 2, ROWS, depth)
-    first = blocks[:, 0].reshape(-1, depth)
-    second = blocks[:, 1].reshape(-1, depth)
-    own_ref[pl.ds(i * half, half), :] = jnp.where(is_first, first, second)
-    other = jnp.where(is_first, second, first)
-    other_ref[pl.ds(i * half, half), :] = other
-    if callable(y_ref):
-        y_ref = y_ref()
-    grad_ref[pl.ds(i * per, per)] = scaled_dot(other, y_ref[...])
-
-
-def split_kernel(core_ref, x_hbm, y_hbm, grad_ref, own_ref, other_ref, y_ref, x_ref, x_sems, y_sem, *, start):
-    steps, _, width = x_ref.shape
+def split_kernel(core_ref, x_hbm, y_hbm, grad_ref, own_ref, other_ref, y_ref, x_ref, x_sems, y_sem):
+    steps, depth, width = x_ref.shape
     x_copies = [
-        pltpu.make_async_copy(
-            x_hbm.at[:, pl.ds(start + i * width, width)], x_ref.at[i], x_sems.at[i]
-        )
+        pltpu.make_async_copy(x_hbm.at[:, pl.ds(i * width, width)], x_ref.at[i], x_sems.at[i])
         for i in range(steps)
     ]
     y_copy = pltpu.make_async_copy(y_hbm, y_ref, y_sem)
@@ -65,73 +48,67 @@
     for copy in x_copies[1:]:
         copy.start()
     is_first = core_ref[0] == 0
-
-    def waited():
-        y_copy.wait()
-        return y_ref
-
+    half = width // 2
+    per = half // ROWS
     for i in range(steps):
         x_copies[i].wait()
-        y = waited if i == 0 else y_ref
-        split_part(is_first, x_ref.at[i], y, grad_ref, own_ref, other_ref, i)
+        blocks = x_ref[i].T.reshape(-1, 2, ROWS, depth)
+        first = blocks[:, 0].reshape(-1, depth)
+        second = blocks[:, 1].reshape(-1, depth)
+        own_ref[pl.ds(i * half, half), :] = jnp.where(is_first, first, second)
+        other = jnp.where(is_first, second, first)
+        other_ref[pl.ds(i * half, half), :] = other
+        if i == 0:
+            y_copy.wait()
+        grad_ref[pl.ds(i * per, per)] = scaled_dot(other, y_ref[...])
 
 
 def split_and_grad(core, tokens, cotangent):
     depth, width = tokens.shape
     step = 512
-    steps = width // (2 * step)
-    half = jax.ShapeDtypeStruct((width // 4, depth), jnp.bfloat16)
-    part = jax.ShapeDtypeStruct((CHIPS // 2, ROWS, FEATURES), jnp.float32)
-    held = jax.ShapeDtypeStruct(cotangent.shape, jnp.bfloat16)
+    half = jax.ShapeDtypeStruct((width // 2, depth), jnp.bfloat16)
     hbm = pl.BlockSpec(memory_space=pltpu.HBM)
-    halves = []
-    for n in range(2):
-        scratch = [
-            pltpu.VMEM((steps, depth, step), jnp.bfloat16),
-            pltpu.SemaphoreType.DMA((steps,)),
+    return pl.pallas_call(
+        split_kernel,
+        out_shape=(
+            jax.ShapeDtypeStruct((CHIPS, ROWS, FEATURES), jnp.float32),
+            half,
+            half,
+            jax.ShapeDtypeStruct(cotangent.shape, jnp.bfloat16),
+        ),
+        in_specs=[SMEM, hbm, hbm],
+        out_specs=(VMEM,) * 4,
+        scratch_shapes=[
+            pltpu.VMEM((width // step, depth, step), jnp.bfloat16),
+            pltpu.SemaphoreType.DMA((width // step,)),
             pltpu.SemaphoreType.DMA,
-        ]
-        halves.append(
-            pl.pallas_call(
-                functools.partial(split_kernel, start=n * (width // 2)),
-                out_shape=(part, half, half) + (held,) * n,
-                in_specs=[SMEM, hbm, hbm],
-                out_specs=(VMEM,) * (3 + n),
-                scratch_shapes=([] if n else [pltpu.VMEM(held.shape, held.dtype)]) + scratch,
-                compiler_params=params(42 if n else 52),
-                cost_estimate=cost(depth * width * FEATURES // 2, 12 * MIB),
-            )(core, tokens, cotangent)
-        )
-    return [half[:3] for half in halves], halves[1][3]
-
-
-def grad_kernel(*refs, parts):
-    x_refs, y_ref, o_ref = refs[:parts], refs[parts], refs[-1]
+        ],
+        compiler_params=params(41),
+        cost_estimate=cost(depth * width * FEATURES, 24 * MIB),
+    )(core, tokens, cotangent)
+
+
+def grad_kernel(x_ref, y_ref, *refs, start):
+    o_ref = refs[-1]
     step = 256
-    at = 0
-    for x_ref in x_refs:
-        count = x_ref.shape[0] // step
-
-        @pl.loop(0, count)
-        def _(i, x_ref=x_ref, at=at):
-            rows = x_ref[pl.ds(pl.multiple_of(i * step, step), step), :]
-            per = step // ROWS
-            o_ref[pl.ds(at + i * per, per)] = scaled_dot(rows, y_ref[...])
-
-        at += x_ref.shape[0] // ROWS
-
-
-def grad(rows, cotangent, kept=()):
-    depth = cotangent.shape[0]
-    count = sum(part.shape[0] for part in rows)
-    return pl.pallas_call(
-        functools.partial(grad_kernel, parts=len(rows)),
+    per = step // ROWS
+
+    @pl.loop(0, o_ref.shape[0] // per)
+    def _(i):
+        rows = x_ref[pl.ds(pl.multiple_of(start + i * step, step), step), :]
+        o_ref[pl.ds(i * per, per)] = scaled_dot(rows, y_ref[...])
+
+
+def grad(rows, cotangent, start=0, count=None, kept=()):
+    count = count or rows.shape[0]
+    return pl.pallas_call(
+        functools.partial(grad_kernel, start=start),
         out_shape=jax.ShapeDtypeStruct((count // ROWS, ROWS, FEATURES), jnp.float32),
-        in_specs=[VMEM] * (len(rows) + 1 + len(kept)),
+        in_specs=[VMEM] * (2 + len(kept)),
         out_specs=VMEM,
         compiler_params=params(8),
-        cost_estimate=cost(count, MIB),
-    )(*rows, cotangent, *kept)
+        cost_estimate=cost(2 * cotangent.shape[0] * count * FEATURES, 12 * MIB),
+    )(rows, cotangent, *kept)
 
 
 def parts_specs(parts):
@@ -227,11 +204,11 @@
 
 
 def gram_kernel(place_ref, v_ref, norm_ref, *refs):
-    earlier_refs, (o_ref, t_ref) = refs[:-2], refs[-2:]
+    earlier_refs, (o_ref, sums_ref, t_ref) = refs[:-3], refs[-3:]
 
     @pl.when(pl.program_id(0) == 0)
     def _():
-        t_ref[...] = jnp.zeros_like(t_ref)
+        sums_ref[...] = jnp.zeros_like(sums_ref)
 
     for gi in range(4):
         for gj in range(gi, 4):
@@ -258,10 +235,12 @@
             zero = jnp.zeros((8, 128), jnp.float32)
             sums = lax.fori_loop(0, v_ref.shape[1] // 8, body, (zero,) * len(pairs))
             for pair, total in zip(pairs, sums):
-                t_ref[pl.ds(PAIRS[pair], 1), :] += jnp.sum(total, axis=0, keepdims=True)
+                sums_ref[PAIRS[pair]] += total
 
     @pl.when(pl.program_id(0) == pl.num_programs(0) - 1)
     def _():
+        t_ref[pl.ds(0, len(PAIRS)), :] = jnp.sum(sums_ref[...], axis=1)
+        t_ref[pl.ds(len(PAIRS), 256 - len(PAIRS)), :] = jnp.zeros((256 - len(PAIRS), 128), jnp.float32)
         lane = lax.broadcasted_iota(jnp.int32, (1, 128), 1)
         shown = (lane == 0) & (place_ref[1] == 1)
         t_ref[pl.ds(len(PAIRS) + place_ref[0], 1), :] = jnp.where(shown, norm_ref[0:1, :], 0.0)
@@ -281,7 +260,10 @@
         in_specs=[SMEM, pl.BlockSpec((CHIPS, step, FEATURES), lambda i: (0, i, 0))]
         + [VMEM] * (1 + len(earlier)),
         out_specs=VMEM,
-        scratch_shapes=[pltpu.VMEM((256, 128), jnp.float32)],
+        scratch_shapes=[
+            pltpu.VMEM((len(PAIRS), 8, 128), jnp.float32),
+            pltpu.VMEM((256, 128), jnp.float32),
+        ],
         compiler_params=params(56),
         cost_estimate=cost(20 << 20, 4 * v.size),
     )(place, v, norm, *earlier)
@@ -289,22 +271,20 @@
 
 def tree_coefs(read):
     count = CHIPS
-    scales = [read(len(PAIRS) + i) for i in range(count)]
-    table = {
-        (i, j): read(PAIRS[i, j]) * (scales[i] * scales[j])
-        for i in range(count)
-        for j in range(i, count)
-    }
-    weights = list(scales)
+    norms = [read(len(PAIRS) + i) for i in range(count)]
+    table = {pair: read(n) for pair, n in PAIRS.items()}
+    weights = list(norms)
     span = 1
     while count > 1:
         own = []
-        for k in range(count // 2):
-            cross = table[2 * k, 2 * k + 1]
-            own.append(1.0 - cross / (2.0 * (table[2 * k, 2 * k] + EPSILON)))
-            own.append(1.0 - cross / (2.0 * (table[2 * k + 1, 2 * k + 1] + EPSILON)))
+        for k in range(0, count, 2):
+            cross = table[k, k + 1] * (norms[k] * norms[k + 1])
+            for m in (k, k + 1):
+                square = table[m, m] * (norms[m] * norms[m])
+                own.append(1.0 - cross / (2.0 * (square + EPSILON)))
         weights = [w * own[i // span] for i, w in enumerate(weights)]
-        table = {key: value * (own[key[0]] * own[key[1]]) for key, value in table.items()}
+        factors = [c * n for c, n in zip(own, norms)]
+        table = {key: value * (factors[key[0]] * factors[key[1]]) for key, value in table.items()}
         count //= 2
         merged = {}
         for k in range(count):
@@ -321,43 +301,48 @@
                     + table[2 * k + 1, 2 * m + 1]
                 )
         table = merged
+        norms = [1.0] * count
         span *= 2
     return weights
 
 
 def update_kernel(totals_ref, *refs):
-    ins, outs, coef_ref = refs[:6], refs[6:10], refs[10]
-
-    @pl.when(pl.program_id(0) == 0)
-    def _():
-        for t in range(2):
-            weights = tree_coefs(lambda n, t=t: totals_ref[2 * t + n // 128, n % 128])
-            for i, w in enumerate(weights):
-                coef_ref[t * CHIPS + i] = w
-
+    hbms, outs, held_refs, sems = refs[:6], refs[6:10], refs[10:16], refs[16]
+    copies = [
+        pltpu.make_async_copy(hbm, held, sems.at[n]) for n, (hbm, held) in enumerate(zip(hbms, held_refs))
+    ]
+    for copy in copies:
+        copy.start()
+    weights = [
+        tree_coefs(lambda n, t=t: totals_ref[2 * t + n // 128, n % 128]) for t in range(2)
+    ]
     for t in range(2):
-        v_ref, weight_ref, moment_ref = ins[3 * t : 3 * t + 3]
+        for copy in copies[3 * t : 3 * t + 3]:
+            copy.wait()
+        v_ref, weight_ref, moment_ref = held_refs[3 * t : 3 * t + 3]
         new_weight_ref, new_moment_ref = outs[2 * t : 2 * t + 2]
-        merged = coef_ref[t * CHIPS] * v_ref[0]
-        for i in range(1, CHIPS):
-            merged = merged + coef_ref[t * CHIPS + i] * v_ref[i]
-        moment = MOMENTUM_DECAY * moment_ref[...] + merged
-        new_moment_ref[...] = moment
-        new_weight_ref[...] = weight_ref[...] - STEP_SIZE * moment
+
+        @pl.loop(0, ROWS // 8)
+        def _(r, t=t, v_ref=v_ref, weight_ref=weight_ref, moment_ref=moment_ref, new_weight_ref=new_weight_ref, new_moment_ref=new_moment_ref):
+            rows = pl.ds(pl.multiple_of(r * 8, 8), 8)
+            merged = weights[t][0] * v_ref[0, rows, :]
+            for i in range(1, CHIPS):
+                merged = merged + weights[t][i] * v_ref[i, rows, :]
+            moment = MOMENTUM_DECAY * moment_ref[rows, :] + merged
+            new_moment_ref[rows, :] = moment
+            new_weight_ref[rows, :] = weight_ref[rows, :] - STEP_SIZE * moment
 
 
 def update(totals, *arrays):
-    step = 16
-    rows = pl.BlockSpec((step, FEATURES), lambda i: (i, 0))
-    whole = pl.BlockSpec((CHIPS, step, FEATURES), lambda i: (0, i, 0))
     out = jax.ShapeDtypeStruct((ROWS, FEATURES), jnp.float32)
+    hbm = pl.BlockSpec(memory_space=pltpu.HBM)
     return pl.pallas_call(
         update_kernel,
         out_shape=(out,) * 4,
-        grid=(ROWS // step,),
-        in_specs=[SMEM] + [whole, rows, rows] * 2,
-        out_specs=(rows,) * 4,
-        scratch_shapes=[pltpu.SMEM((2 * CHIPS,), jnp.float32)],
+        in_specs=[SMEM] + [hbm] * 6,
+        out_specs=(VMEM,) * 4,
+        scratch_shapes=[pltpu.VMEM(a.shape, a.dtype) for a in arrays]
+        + [pltpu.SemaphoreType.DMA((6,))],
         compiler_params=params(60),
         cost_estimate=cost(8 << 20, 10 * MIB),
     )(totals, *arrays)
@@ -388,18 +373,23 @@
     def gathered(sent):
         return lax.all_to_all(sent, "rep", 0, 0, axis_index_groups=core_groups)
 
-    halves, key_cotangent = split_and_grad(core, tokens, key_cotangent)
-    own_rows = [half[1] for half in halves]
-    other_rows = [half[2] for half in halves]
-    key_arrived = [lax.ppermute(half[0], "rep", swap) for half in halves]
+    key_other, own_rows, other_rows, key_cotangent = split_and_grad(core, tokens, key_cotangent)
+    key_arrived = [lax.ppermute(key_other, "rep", swap)]
     key_own = grad(own_rows, key_cotangent)
-    key_sums = summed(pair_sums(core, key_own, key_arrived, 1))
-    value_other = grad(after(other_rows, key_sums[0]), value_cotangent, [key_own] + key_arrived)
+    half = other_rows.shape[0] // 2
+    value_first = grad(after(other_rows, key_own), value_cotangent, 0, half, [key_own])
+    key_sums = summed(pair_sums(after(core, value_first), key_own, key_arrived, 1))
+    value_second = grad(
+        after(other_rows, key_sums[0]), value_cotangent, half, half, [key_own] + key_arrived
+    )
     key_merged, key_norm = merge_pair(core, key_own, key_arrived, key_sums)
     key_sent = key_merged.astype(jnp.float16)
     key_all = gathered(key_sent)
 
-    value_arrived = [lax.ppermute(after(value_other, key_sent), "rep", swap)]
+    value_arrived = [
+        lax.ppermute(value_first, "rep", swap),
+        lax.ppermute(after(value_second, key_sent), "rep", swap),
+    ]
     value_own = grad(after(own_rows, key_sent), value_cotangent)
     value_sums = summed(pair_sums(core, value_own, value_arrived, 1))
     value_merged, value_norm = merge_pair(core, value_own, value_arrived, value_sums)

time: 145 us -> 145 us (level)
  Pallas kernels: 58.9 us -> 55.5 us
  local copies, waits for them, and re-layouts: 4.39 us -> 7.74 us
    unnamed x16 -> x14, local copies, waits for them, and re-layouts: 4.39 us -> 7.74 us
    pallas_call x6, Pallas kernels: 36.3 us -> 34.2 us  [the longest x4 17.7 us: grad(): pl.pallas_call(functools.partial(grad_kernel, start=start), out_shape=jax...]
  transfers between devices with their start and end apart: 13 -> 13, of which waited for: 6 -> 6; matrix products, arithmetic and copies ran while one was open for 4% -> 6% of each run, Pallas kernels for 25% -> 22%
where the time goes in v4:
time: 145 us
  Pallas kernels  55.5 us (38%)
  starting transfers between devices  25.1 us (17%)
  waiting for transfers between devices  22.4 us (15%)
  blocking collectives  21.4 us (15%)
  other arithmetic  11.5 us (8%)
  local copies, waits for them, and re-layouts  7.74 us (5%)
    all_to_all x1, blocking collectives, shards(): totals = jnp.sum(lax.all_to_all(vectors, ('shard', 'rep'), 0, 0), axis=0)  21.4 us
    pallas_call x4, Pallas kernels, grad(): pl.pallas_call(functools.partial(grad_kernel, start=start), out_shape=jax...  17.7 us
    all_to_all x2, waiting for transfers between devices, gathered(): return lax.all_to_all(sent, 'rep', 0, 0, axis_index_groups=core_groups)  16.7 us
    all_to_all x2, starting transfers between devices, gathered(): return lax.all_to_all(sent, 'rep', 0, 0, axis_index_groups=core_groups)  13.5 us
    pallas_call x2, Pallas kernels, gram(): pl.pallas_call(gram_kernel, out_shape=jax.ShapeDtypeStruct(out_dims, jnp....  11.5 us
    pallas_call x1, Pallas kernels, split_and_grad(): pl.pallas_call(split_kernel, out_shape=(jax.ShapeDtypeStruct((CHIPS, ROWS...  10.1 us
    unnamed x14, local copies, waits for them, and re-layouts  7.74 us
    ppermute x6, starting transfers between devices, summed(): return [sums] + [lax.ppermute(sums, 'shard', shift) for shift in shifts]  6.94 us
  transfers between devices with their start and end apart: 13, of which 6 were waited for; matrix products, arithmetic and copies ran while one was open for 6% of the time, Pallas kernels for 22%

profile of v4, /device:TPU:1, one launch (start us, length us, event | category | flops | bytes accessed | tf_op | source)
XLA Modules:
  0.0 144.5 jit_solution(11920633688111540992)
XLA Ops:
  0.6 10.1 %shard_map.102 = (f32[16,64,1024]{2,1,0:T(8,128)S(1)}, bf16[1024,2048]{1,0:T(8,128)(2,1)S(1)}, bf16[1024,2048]{1,0:T(8,128)(2,1)S(1)}, bf16[2048,1024]{1,0:T(8,128)(2,1)}) custom-call(s32[1]{0:T(128)} %bitcast.2.core_ref, bf16[2048,2048]{1,0:T(8,128)(2,1)} %x_hbm.1, bf16[2048,1024]{1,0:T(8,128)(2,1)} %y_hbm.1), custom_call_target="tpu_custom_call" | custom-call | flops 4294967296 | bytes 25165824 | tf_op jit(solution)/shard_map/pallas_call | solution.py:71
  10.8 1.5 %collective-permute-start = (f32[16,64,1024]{2,1,0:T(8,128)S(1)}, f32[16,64,1024]{2,1,0:T(8,128)S(1)}, u32[]{:S(2)}, u32[]{:S(2)}) collective-permute-start(f32[16,64,1024]{2,1,0:T(8,128)S(1)} %get-tuple-element.23), channel_id=1, source_target_pairs={{0,1},{1,0},{2,3},{3,2},{4,5},{5,4},{6,7},{7,6},{8,9},{9,8},{10,11... | collective-permute-start | bytes 12582920 | tf_op jit(solution)/shard_map/ppermute | solution.py:377
  12.3 2.2 %copy-done.6 = bf16[2048,1024]{1,0:T(8,128)(2,1)S(1)} copy-done((bf16[2048,1024]{1,0:T(8,128)(2,1)S(1)}, bf16[2048,1024]{1,0:T(8,128)(2,1)}, u32[]{:S(2)}) %copy-start.6) | copy-done | bytes 4194328
  14.5 5.0 %shard_map.103.refs_0_.a_ref = f32[16,64,1024]{2,1,0:T(8,128)S(1)} custom-call(bf16[1024,2048]{1,0:T(8,128)(2,1)S(1)} %get-tuple-element.28.x_ref, bf16[2048,1024]{1,0:T(8,128)(2,1)S(1)} %copy-done.6), custom_call_target="tpu_custom_call" | custom-call | flops 4294967296 | bytes 12582912 | tf_op jit(solution)/shard_map/pallas_call | solution.py:104
  19.5 3.9 %shard_map.104 = f32[8,64,1024]{2,1,0:T(8,128)} custom-call(bf16[1024,2048]{1,0:T(8,128)(2,1)S(1)} %get-tuple-element.29.x_ref, bf16[2048,1024]{1,0:T(8,128)(2,1)S(1)} %copy-done, f32[16,64,1024]{2,1,0:T(8,128)S(1)} %shard_map.103.refs_0_.a_ref), custom_call_target="tpu_custom_call" | custom-call | flops 2147483648 | bytes 12582912 | tf_op jit(solution)/shard_map/pallas_call | solution.py:104
  23.4 1.8 %shard_map.105 = f32[1,8,128]{2,1,0:T(8,128)S(1)} custom-call(s32[1]{0:T(128)} %bitcast.2.core_ref, f32[16,64,1024]{2,1,0:T(8,128)S(1)} %shard_map.103.refs_0_.a_ref, f32[16,64,1024]{2,1,0:T(8,128)S(1)} %collective-permute-done.refs_0_.refs_1_), custom_call_target="tpu_custom_call" | custom-call | flops 1048576 | bytes 1048576 | tf_op jit(solution)/shard_map/pallas_call | solution.py:159
  25.1 1.5 %collective-permute-start.1 = (f32[1,8,128]{2,1,0:T(8,128)S(1)}, f32[1,8,128]{2,1,0:T(8,128)S(1)}, u32[]{:S(2)}, u32[]{:S(2)}) collective-permute-start(f32[1,8,128]{2,1,0:T(8,128)S(1)} %shard_map.105), channel_id=1, source_target_pairs={{0,1},{1,0},{2,3},{3,2},{4,5},{5,4},{6,7},{7,6},{8,9},{9,8},{10,11... | collective-permute-start | bytes 12296 | tf_op jit(solution)/shard_map/ppermute | solution.py:367
  27.4 2.6 %collective-permute-start.4 = (f32[1,8,128]{2,1,0:T(8,128)S(1)}, f32[1,8,128]{2,1,0:T(8,128)S(1)}, u32[]{:S(2)}, u32[]{:S(2)}) collective-permute-start(f32[1,8,128]{2,1,0:T(8,128)S(1)} %add.6.refs_1_), channel_id=1, source_target_pairs={{0,96},{32,0},{64,32},{96,64},{1,97},{33,1},{65,33},{97,65},{2,98}... | collective-permute-start | bytes 12296 | tf_op jit(solution)/shard_map/ppermute | solution.py:371
  31.1 3.8 %shard_map.108 = f32[8,64,1024]{2,1,0:T(8,128)} custom-call(bf16[1024,2048]{1,0:T(8,128)(2,1)S(1)} %get-tuple-element.29.x_ref, bf16[2048,1024]{1,0:T(8,128)(2,1)S(1)} %copy-done, f32[16,64,1024]{2,1,0:T(8,128)S(1)} %shard_map.103.refs_0_.a_ref, f32[16,64,1024]{2,1,0:T(8,128)S(1)} %collective-permute-done.refs_0_.refs_1_), custom_call_target="tpu_custom_call" | custom-call | flops 2147483648 | bytes 12582912 | tf_op jit(solution)/shard_map/pallas_call | solution.py:104
  36.2 1.8 %convert_element_type.13 = f16[16,64,1024]{2,1,0:T(8,128)(2,1)} convert(f32[16,64,1024]{2,1,0:T(8,128)S(1)} %get-tuple-element.27) | non-fusion elementwise | flops 1048576 | bytes 6291456 | tf_op jit(solution)/shard_map/convert_element_type | solution.py:386
  38.0 1.2 collective-permute-start.6
  39.3 7.8 %all-to-all-start.1 = ((f16[16,64,1024]{2,1,0:T(8,128)(2,1)}), f16[16,64,1024]{2,1,0:T(8,128)(2,1)}, u32[]{:S(2)}, u32[]{:S(2)}) async-start(f16[16,64,1024]{2,1,0:T(8,128)(2,1)} %convert_element_type.13), calls=%async_computation.1 | async-start | bytes 4194304 | tf_op jit(solution)/shard_map/all_to_all | solution.py:374
  47.1 2.2 %copy-done.1 = bf16[2048,1024]{1,0:T(8,128)(2,1)S(1)} copy-done((bf16[2048,1024]{1,0:T(8,128)(2,1)S(1)}, bf16[2048,1024]{1,0:T(8,128)(2,1)}, u32[]{:S(2)}) %copy-start.1) | copy-done | bytes 4194328
  49.3 2.2 %copy-done.5 = bf16[1024,2048]{1,0:T(8,128)(2,1)S(1)} copy-done((bf16[1024,2048]{1,0:T(8,128)(2,1)S(1)}, bf16[1024,2048]{1,0:T(8,128)(2,1)}, u32[]{:S(2)}) %copy-start.5) | copy-done | bytes 4194328
  51.5 5.0 %shard_map.107.a_ref = f32[16,64,1024]{2,1,0:T(8,128)S(1)} custom-call(bf16[1024,2048]{1,0:T(8,128)(2,1)S(1)} %copy-done.5, bf16[2048,1024]{1,0:T(8,128)(2,1)S(1)} %copy-done.1), custom_call_target="tpu_custom_call" | custom-call | flops 4294967296 | bytes 12582912 | tf_op jit(solution)/shard_map/pallas_call | solution.py:104
  56.5 4.3 %shard_map.109 = f32[1,8,128]{2,1,0:T(8,128)S(1)} custom-call(s32[1]{0:T(128)} %bitcast.2.core_ref, f32[16,64,1024]{2,1,0:T(8,128)S(1)} %shard_map.107.a_ref, f32[8,64,1024]{2,1,0:T(8,128)S(1)} %collective-permute-done.5.refs_0_, f32[8,64,1024]{2,1,0:T(8,128)} %collective-permute-done.6.refs_1_), custom_call_target="tpu_custom_call" | custom-call | flops 1048576 | bytes 1048576 | tf_op jit(solution)/shard_map/pallas_call | solution.py:159
  61.1 0.9 collective-permute-done.7
  62.0 2.0 %collective-permute-start.10 = (f32[1,8,128]{2,1,0:T(8,128)S(1)}, f32[1,8,128]{2,1,0:T(8,128)S(1)}, u32[]{:S(2)}, u32[]{:S(2)}) collective-permute-start(f32[1,8,128]{2,1,0:T(8,128)S(1)} %add.7.refs_2_), channel_id=1, source_target_pairs={{0,96},{32,0},{64,32},{96,64},{1,97},{33,1},{65,33},{97,65},{2,98}... | collective-permute-start | bytes 12296 | tf_op jit(solution)/shard_map/ppermute | solution.py:371
  64.0 1.2 collective-permute-start.9
  65.3 2.7 %collective-permute-done.9.refs_4_ = f32[1,8,128]{2,1,0:T(8,128)S(1)} collective-permute-done((f32[1,8,128]{2,1,0:T(8,128)S(1)}, f32[1,8,128]{2,1,0:T(8,128)S(1)}, u32[]{:S(2)}, u32[]{:S(2)}) %collective-permute-start.9) | collective-permute-done | bytes 4128 | tf_op jit(solution)/shard_map/ppermute | solution.py:371
  68.0 1.4 collective-permute-done.8.refs_3_
  69.4 3.0 %shard_map.110 = (f32[16,64,1024]{2,1,0:T(8,128)S(1)}, f32[8,128]{1,0:T(8,128)S(1)}) custom-call(s32[1]{0:T(128)} %bitcast.2.core_ref, f32[16,64,1024]{2,1,0:T(8,128)S(1)} %shard_map.107.a_ref, f32[8,64,1024]{2,1,0:T(8,128)S(1)} %collective-permute-done.5.refs_0_, f32[8,64,1024]{2,1,0:T(8,128)} %collective-permute-done.6.refs_1_, ...), custom_call_target="tpu_custom_call" | custom-call | flops 1048576 | bytes 1048576 | tf_op jit(solution)/shard_map/pallas_call | solution.py:192
  73.0 1.8 %convert_element_type.14 = f16[16,64,1024]{2,1,0:T(8,128)(2,1)} convert(f32[16,64,1024]{2,1,0:T(8,128)S(1)} %get-tuple-element.31) | non-fusion elementwise | flops 1048576 | bytes 6291456 | tf_op jit(solution)/shard_map/convert_element_type | solution.py:396
  74.8 1.4 %all-to-all-done.1 = f16[16,64,1024]{2,1,0:T(8,128)(2,1)} async-done(((f16[16,64,1024]{2,1,0:T(8,128)(2,1)}), f16[16,64,1024]{2,1,0:T(8,128)(2,1)}, u32[]{:S(2)}, u32[]{:S(2)}) %all-to-all-start.1) | async-done | bytes 2097184 | tf_op jit(solution)/shard_map/all_to_all | solution.py:374
  76.2 5.7 %all-to-all-start = ((f16[16,64,1024]{2,1,0:T(8,128)(2,1)}), f16[16,64,1024]{2,1,0:T(8,128)(2,1)S(1)}, u32[]{:S(2)}, u32[]{:S(2)}) async-start(f16[16,64,1024]{2,1,0:T(8,128)(2,1)} %convert_element_type.14), calls=%async_computation | async-start | bytes 4194304 | tf_op jit(solution)/shard_map/all_to_all | solution.py:374
  82.6 4.0 %convert_element_type.16.v_ref.refs_0_ = f32[16,64,1024]{2,1,0:T(8,128)} convert(f16[16,64,1024]{2,1,0:T(8,128)(2,1)} %all-to-all-done.1) | non-fusion elementwise | flops 1048576 | bytes 6291456 | tf_op jit(solution)/shard_map/convert_element_type | solution.py:398
  86.6 5.7 %shard_map.111.refs_0_ = f32[2,128]{1,0:T(2,128)} custom-call(s32[2]{0:T(128)} %pad_add_fusion.place_ref, f32[16,64,1024]{2,1,0:T(8,128)} %convert_element_type.16.v_ref.refs_0_, f32[8,128]{1,0:T(8,128)} %copy-done.3), custom_call_target="tpu_custom_call" | custom-call | flops 20971520 | bytes 4194304 | tf_op jit(solution)/shard_map/pallas_call | solution.py:256
  92.3 15.2 %all-to-all-done = f16[16,64,1024]{2,1,0:T(8,128)(2,1)S(1)} async-done(((f16[16,64,1024]{2,1,0:T(8,128)(2,1)}), f16[16,64,1024]{2,1,0:T(8,128)(2,1)S(1)}, u32[]{:S(2)}, u32[]{:S(2)}) %all-to-all-start) | async-done | bytes 2097184 | tf_op jit(solution)/shard_map/all_to_all | solution.py:374
  107.5 2.5 %convert_element_type.15.v_ref.refs_3_ = f32[16,64,1024]{2,1,0:T(8,128)} convert(f16[16,64,1024]{2,1,0:T(8,128)(2,1)S(1)} %all-to-all-done) | non-fusion elementwise | flops 1048576 | bytes 6291456 | tf_op jit(solution)/shard_map/convert_element_type | solution.py:400
  110.0 5.9 %shard_map.112 = f32[128,4,128]{2,1,0:T(4,128)} custom-call(s32[2]{0:T(128)} %pad_add_fusion.place_ref, f32[16,64,1024]{2,1,0:T(8,128)} %convert_element_type.15.v_ref.refs_3_, f32[8,128]{1,0:T(8,128)} %copy-done.2, f32[2,128]{1,0:T(2,128)} %shard_map.111.refs_0_), custom_call_target="tpu_custom_call" | custom-call | flops 20971520 | bytes 4194304 | tf_op jit(solution)/shard_map/pallas_call | solution.py:256
  115.9 21.4 %all_to_all.15 = f32[128,4,128]{2,1,0:T(4,128)S(1)} all-to-all(f32[128,4,128]{2,1,0:T(4,128)} %shard_map.112), channel_id=1, replica_groups=mesh['shard'=4,'rep'=32] {'shard','rep'}, dimensions={0} | all-to-all | bytes 524288 | tf_op jit(solution)/shard_map/all_to_all | solution.py:402
  138.0 6.4 %shard_map.113 = (f32[64,1024]{1,0:T(8,128)}, f32[64,1024]{1,0:T(8,128)}, f32[64,1024]{1,0:T(8,128)}, f32[64,1024]{1,0:T(8,128)}) custom-call(f32[4,128]{1,0:T(4,128)} %reduce_sum.9.totals_ref, f32[16,64,1024]{2,1,0:T(8,128)} %convert_element_type.16.v_ref.refs_0_, f32[64,1024]{1,0:T(8,128)} %refs_1_.1, f32[64,1024]{1,0:T(8,128)} %refs_2_.1, ...), custom_call_target="tpu_custom_call" | custom-call | flops 8388608 | bytes 10485760 | tf_op jit(solution)/shard_map/pallas_call | solution.py:339
  (29 shorter events, 5.4 us)
Async XLA Ops:
  10.8 8.7 %copy-start.4 = (bf16[1024,2048]{1,0:T(8,128)(2,1)}, bf16[1024,2048]{1,0:T(8,128)(2,1)S(1)}, u32[]{:S(2)}) copy-start(bf16[1024,2048]{1,0:T(8,128)(2,1)S(1)} %get-tuple-element.28.x_ref) | copy-start | bytes 12582916
  10.8 12.6 %collective-permute-start = (f32[16,64,1024]{2,1,0:T(8,128)S(1)}, f32[16,64,1024]{2,1,0:T(8,128)S(1)}, u32[]{:S(2)}, u32[]{:S(2)}) collective-permute-start(f32[16,64,1024]{2,1,0:T(8,128)S(1)} %get-tuple-element.23), channel_id=1, source_target_pairs={{0,1},{1,0},{2,3},{3,2},{4,5},{5,4},{6,7},{7,6},{8,9},{9,8},{10,11... | collective-permute-start | bytes 12582920 | tf_op jit(solution)/shard_map/ppermute | solution.py:377
  12.3 2.2 %copy-start.6 = (bf16[2048,1024]{1,0:T(8,128)(2,1)S(1)}, bf16[2048,1024]{1,0:T(8,128)(2,1)}, u32[]{:S(2)}) copy-start(bf16[2048,1024]{1,0:T(8,128)(2,1)} %get-tuple-element.22.y_ref) | copy-start | bytes 12582916
  14.5 5.0 %copy-start = (bf16[2048,1024]{1,0:T(8,128)(2,1)S(1)}, bf16[2048,1024]{1,0:T(8,128)(2,1)}, u32[]{:S(2)}) copy-start(bf16[2048,1024]{1,0:T(8,128)(2,1)} %y_ref.5) | copy-start | bytes 12582916
  25.1 2.3 %collective-permute-start.1 = (f32[1,8,128]{2,1,0:T(8,128)S(1)}, f32[1,8,128]{2,1,0:T(8,128)S(1)}, u32[]{:S(2)}, u32[]{:S(2)}) collective-permute-start(f32[1,8,128]{2,1,0:T(8,128)S(1)} %shard_map.105), channel_id=1, source_target_pairs={{0,1},{1,0},{2,3},{3,2},{4,5},{5,4},{6,7},{7,6},{8,9},{9,8},{10,11... | collective-permute-start | bytes 12296 | tf_op jit(solution)/shard_map/ppermute | solution.py:367
  26.6 29.9 %collective-permute-start.5 = (f32[8,64,1024]{2,1,0:T(8,128)}, f32[8,64,1024]{2,1,0:T(8,128)S(1)}, u32[]{:S(2)}, u32[]{:S(2)}) collective-permute-start(f32[8,64,1024]{2,1,0:T(8,128)} %shard_map.104), channel_id=1, source_target_pairs={{0,1},{1,0},{2,3},{3,2},{4,5},{5,4},{6,7},{7,6},{8,9},{9,8},{10,11... | collective-permute-start | bytes 6291464 | tf_op jit(solution)/shard_map/ppermute | solution.py:390
  27.4 7.5 %collective-permute-start.4 = (f32[1,8,128]{2,1,0:T(8,128)S(1)}, f32[1,8,128]{2,1,0:T(8,128)S(1)}, u32[]{:S(2)}, u32[]{:S(2)}) collective-permute-start(f32[1,8,128]{2,1,0:T(8,128)S(1)} %add.6.refs_1_), channel_id=1, source_target_pairs={{0,96},{32,0},{64,32},{96,64},{1,97},{33,1},{65,33},{97,65},{2,98}... | collective-permute-start | bytes 12296 | tf_op jit(solution)/shard_map/ppermute | solution.py:371
  30.0 5.0 %collective-permute-start.3 = (f32[1,8,128]{2,1,0:T(8,128)S(1)}, f32[1,8,128]{2,1,0:T(8,128)S(1)}, u32[]{:S(2)}, u32[]{:S(2)}) collective-permute-start(f32[1,8,128]{2,1,0:T(8,128)S(1)} %add.6.refs_1_), channel_id=1, source_target_pairs={{0,64},{32,96},{64,0},{96,32},{1,65},{33,97},{65,1},{97,33},{2,66}... | collective-permute-start | bytes 12296 | tf_op jit(solution)/shard_map/ppermute | solution.py:371
  30.5 4.5 %collective-permute-start.2 = (f32[1,8,128]{2,1,0:T(8,128)S(1)}, f32[1,8,128]{2,1,0:T(8,128)S(1)}, u32[]{:S(2)}, u32[]{:S(2)}) collective-permute-start(f32[1,8,128]{2,1,0:T(8,128)S(1)} %add.6.refs_1_), channel_id=1, source_target_pairs={{0,32},{32,64},{64,96},{96,0},{1,33},{33,65},{65,97},{97,1},{2,34}... | collective-permute-start | bytes 12296 | tf_op jit(solution)/shard_map/ppermute | solution.py:371
  35.6 0.6 copy-start.3
  38.0 18.5 %collective-permute-start.6 = (f32[8,64,1024]{2,1,0:T(8,128)}, f32[8,64,1024]{2,1,0:T(8,128)}, u32[]{:S(2)}, u32[]{:S(2)}) collective-permute-start(f32[8,64,1024]{2,1,0:T(8,128)} %shard_map.108), channel_id=1, source_target_pairs={{0,1},{1,0},{2,3},{3,2},{4,5},{5,4},{6,7},{7,6},{8,9},{9,8},{10,11... | collective-permute-start | bytes 6291464 | tf_op jit(solution)/shard_map/ppermute | solution.py:391
  39.3 37.0 %all-to-all-start.1 = ((f16[16,64,1024]{2,1,0:T(8,128)(2,1)}), f16[16,64,1024]{2,1,0:T(8,128)(2,1)}, u32[]{:S(2)}, u32[]{:S(2)}) async-start(f16[16,64,1024]{2,1,0:T(8,128)(2,1)} %convert_element_type.13), calls=%async_computation.1 | async-start | bytes 4194304 | tf_op jit(solution)/shard_map/all_to_all | solution.py:374
  47.1 2.2 %copy-start.1 = (bf16[2048,1024]{1,0:T(8,128)(2,1)S(1)}, bf16[2048,1024]{1,0:T(8,128)(2,1)}, u32[]{:S(2)}) copy-start(bf16[2048,1024]{1,0:T(8,128)(2,1)} %y_ref.5) | copy-start | bytes 12582916
  49.3 2.2 %copy-start.5 = (bf16[1024,2048]{1,0:T(8,128)(2,1)S(1)}, bf16[1024,2048]{1,0:T(8,128)(2,1)}, u32[]{:S(2)}) copy-start(bf16[1024,2048]{1,0:T(8,128)(2,1)} %copy-done.4) | copy-start | bytes 12582916
  60.8 1.2 collective-permute-start.7
  62.0 3.3 %collective-permute-start.10 = (f32[1,8,128]{2,1,0:T(8,128)S(1)}, f32[1,8,128]{2,1,0:T(8,128)S(1)}, u32[]{:S(2)}, u32[]{:S(2)}) collective-permute-start(f32[1,8,128]{2,1,0:T(8,128)S(1)} %add.7.refs_2_), channel_id=1, source_target_pairs={{0,96},{32,0},{64,32},{96,64},{1,97},{33,1},{65,33},{97,65},{2,98}... | collective-permute-start | bytes 12296 | tf_op jit(solution)/shard_map/ppermute | solution.py:371
  64.0 4.0 %collective-permute-start.9 = (f32[1,8,128]{2,1,0:T(8,128)S(1)}, f32[1,8,128]{2,1,0:T(8,128)S(1)}, u32[]{:S(2)}, u32[]{:S(2)}) collective-permute-start(f32[1,8,128]{2,1,0:T(8,128)S(1)} %add.7.refs_2_), channel_id=1, source_target_pairs={{0,64},{32,96},{64,0},{96,32},{1,65},{33,97},{65,1},{97,33},{2,66}... | collective-permute-start | bytes 12296 | tf_op jit(solution)/shard_map/ppermute | solution.py:371
  65.3 4.1 %collective-permute-start.8 = (f32[1,8,128]{2,1,0:T(8,128)S(1)}, f32[1,8,128]{2,1,0:T(8,128)S(1)}, u32[]{:S(2)}, u32[]{:S(2)}) collective-permute-start(f32[1,8,128]{2,1,0:T(8,128)S(1)} %add.7.refs_2_), channel_id=1, source_target_pairs={{0,32},{32,64},{64,96},{96,0},{1,33},{33,65},{65,97},{97,1},{2,34}... | collective-permute-start | bytes 12296 | tf_op jit(solution)/shard_map/ppermute | solution.py:371
  72.4 0.6 copy-start.2
  76.2 31.3 %all-to-all-start = ((f16[16,64,1024]{2,1,0:T(8,128)(2,1)}), f16[16,64,1024]{2,1,0:T(8,128)(2,1)S(1)}, u32[]{:S(2)}, u32[]{:S(2)}) async-start(f16[16,64,1024]{2,1,0:T(8,128)(2,1)} %convert_element_type.14), calls=%async_computation | async-start | bytes 4194304 | tf_op jit(solution)/shard_map/all_to_all | solution.py:374

commit v5 on v4

--- a/solution.py
+++ b/solution.py
@@ -36,7 +36,7 @@
     return (product * (1.0 / math.sqrt(rows.shape[1]))).reshape(-1, ROWS, FEATURES)
 
 
-def split_kernel(core_ref, x_hbm, y_hbm, grad_ref, own_ref, other_ref, y_ref, x_ref, x_sems, y_sem):
+def split_kernel(core_ref, x_hbm, y_hbm, grad_ref, own_ref, other_ref, x_ref, y_ref, x_sems, y_sem):
     steps, depth, width = x_ref.shape
     x_copies = [
         pltpu.make_async_copy(x_hbm.at[:, pl.ds(i * width, width)], x_ref.at[i], x_sems.at[i])
@@ -74,16 +74,16 @@
             jax.ShapeDtypeStruct((CHIPS, ROWS, FEATURES), jnp.float32),
             half,
             half,
-            jax.ShapeDtypeStruct(cotangent.shape, jnp.bfloat16),
         ),
         in_specs=[SMEM, hbm, hbm],
-        out_specs=(VMEM,) * 4,
+        out_specs=(VMEM,) * 3,
         scratch_shapes=[
             pltpu.VMEM((width // step, depth, step), jnp.bfloat16),
+            pltpu.VMEM(cotangent.shape, jnp.bfloat16),
             pltpu.SemaphoreType.DMA((width // step,)),
             pltpu.SemaphoreType.DMA,
         ],
-        compiler_params=params(41),
+        compiler_params=params(32),
         cost_estimate=cost(depth * width * FEATURES, 24 * MIB),
     )(core, tokens, cotangent)
 
@@ -204,12 +204,8 @@
 
 
 def gram_kernel(place_ref, v_ref, norm_ref, *refs):
-    earlier_refs, (o_ref, sums_ref, t_ref) = refs[:-3], refs[-3:]
-
-    @pl.when(pl.program_id(0) == 0)
-    def _():
-        sums_ref[...] = jnp.zeros_like(sums_ref)
-
+    earlier_refs, (o_ref, t_ref) = refs[:-2], refs[-2:]
+    t_ref[...] = jnp.zeros_like(t_ref)
     for gi in range(4):
         for gj in range(gi, 4):
             pairs = [
@@ -233,38 +229,27 @@
                 return tuple(sums)
 
             zero = jnp.zeros((8, 128), jnp.float32)
-            sums = lax.fori_loop(0, v_ref.shape[1] // 8, body, (zero,) * len(pairs))
+            sums = lax.fori_loop(0, ROWS // 8, body, (zero,) * len(pairs))
             for pair, total in zip(pairs, sums):
-                sums_ref[PAIRS[pair]] += total
-
-    @pl.when(pl.program_id(0) == pl.num_programs(0) - 1)
-    def _():
-        t_ref[pl.ds(0, len(PAIRS)), :] = jnp.sum(sums_ref[...], axis=1)
-        t_ref[pl.ds(len(PAIRS), 256 - len(PAIRS)), :] = jnp.zeros((256 - len(PAIRS), 128), jnp.float32)
-        lane = lax.broadcasted_iota(jnp.int32, (1, 128), 1)
-        shown = (lane == 0) & (place_ref[1] == 1)
-        t_ref[pl.ds(len(PAIRS) + place_ref[0], 1), :] = jnp.where(shown, norm_ref[0:1, :], 0.0)
-        rows = [ref[...] for ref in earlier_refs]
-        for part in range(2):
-            rows.append(jnp.sum(t_ref[pl.ds(part * 128, 128), :].T, axis=0, keepdims=True))
-        tile = jnp.concatenate(rows, axis=0)
-        o_ref[...] = tile if o_ref.ndim == 2 else jnp.broadcast_to(tile[None], o_ref.shape)
+                t_ref[pl.ds(PAIRS[pair], 1), :] = jnp.sum(total, axis=0, keepdims=True)
+    lane = lax.broadcasted_iota(jnp.int32, (1, 128), 1)
+    shown = (lane == 0) & (place_ref[1] == 1)
+    t_ref[pl.ds(len(PAIRS) + place_ref[0], 1), :] = jnp.where(shown, norm_ref[0:1, :], 0.0)
+    rows = [ref[...] for ref in earlier_refs]
+    for part in range(2):
+        rows.append(jnp.sum(t_ref[pl.ds(part * 128, 128), :].T, axis=0, keepdims=True))
+    tile = jnp.concatenate(rows, axis=0)
+    o_ref[...] = tile if o_ref.ndim == 2 else jnp.broadcast_to(tile[None], o_ref.shape)
 
 
 def gram(place, v, norm, earlier, out_dims):
-    step = 16
     return pl.pallas_call(
         gram_kernel,
         out_shape=jax.ShapeDtypeStruct(out_dims, jnp.float32),
-        grid=(ROWS // step,),
-        in_specs=[SMEM, pl.BlockSpec((CHIPS, step, FEATURES), lambda i: (0, i, 0))]
-        + [VMEM] * (1 + len(earlier)),
+        in_specs=[SMEM] + [VMEM] * (2 + len(earlier)),
         out_specs=VMEM,
-        scratch_shapes=[
-            pltpu.VMEM((len(PAIRS), 8, 128), jnp.float32),
-            pltpu.VMEM((256, 128), jnp.float32),
-        ],
-        compiler_params=params(56),
+        scratch_shapes=[pltpu.VMEM((256, 128), jnp.float32)],
+        compiler_params=params(16),
         cost_estimate=cost(20 << 20, 4 * v.size),
     )(place, v, norm, *earlier)
 
@@ -373,7 +358,7 @@
     def gathered(sent):
         return lax.all_to_all(sent, "rep", 0, 0, axis_index_groups=core_groups)
 
-    key_other, own_rows, other_rows, key_cotangent = split_and_grad(core, tokens, key_cotangent)
+    key_other, own_rows, other_rows = split_and_grad(core, tokens, key_cotangent)
     key_arrived = [lax.ppermute(key_other, "rep", swap)]
     key_own = grad(own_rows, key_cotangent)
     half = other_rows.shape[0] // 2

time: 145 us -> 140 us (0.966)
  Pallas kernels: 55.5 us -> 49.1 us
  waiting for transfers between devices: 22.4 us -> 25.3 us
  other arithmetic: 11.5 us -> 8.6 us
  local copies, waits for them, and re-layouts: 7.74 us -> 10.5 us
    pallas_call x2, Pallas kernels: 11.5 us -> 7.31 us  [gram(): pl.pallas_call(gram_kernel, out_shape=jax.ShapeDtypeStruct(out_dims, jnp....]
    all_to_all x2, waiting for transfers between devices: 16.7 us -> 19.7 us  [gathered(): return lax.all_to_all(sent, 'rep', 0, 0, axis_index_groups=core_groups)]
    unnamed x14 -> x16, local copies, waits for them, and re-layouts: 7.74 us -> 10.5 us
    pallas_call x1, Pallas kernels: 10.1 us -> 7.8 us  [split_and_grad(): pl.pallas_call(split_kernel, out_shape=(jax.ShapeDtypeStruct((CHIPS, ROWS...]
    convert_element_type x1, other arithmetic: 4.03 us -> 2.09 us  [shards(): key_v = key_all.astype(jnp.float32)]
  transfers between devices with their start and end apart: 13 -> 13, of which waited for: 6 -> 6; matrix products, arithmetic and copies ran while one was open for 6% -> 4% of each run, Pallas kernels for 22% -> 21%
where the time goes in v5:
time: 140 us
  Pallas kernels  49.1 us (35%)
  waiting for transfers between devices  25.3 us (18%)
  starting transfers between devices  24 us (17%)
  blocking collectives  21.2 us (15%)
  local copies, waits for them, and re-layouts  10.5 us (8%)
  other arithmetic  8.6 us (6%)
    all_to_all x1, blocking collectives, shards(): totals = jnp.sum(lax.all_to_all(vectors, ('shard', 'rep'), 0, 0), axis=0)  21.2 us
    all_to_all x2, waiting for transfers between devices, gathered(): return lax.all_to_all(sent, 'rep', 0, 0, axis_index_groups=core_groups)  19.7 us
    pallas_call x4, Pallas kernels, grad(): pl.pallas_call(functools.partial(grad_kernel, start=start), out_shape=jax...  17.7 us
    all_to_all x2, starting transfers between devices, gathered(): return lax.all_to_all(sent, 'rep', 0, 0, axis_index_groups=core_groups)  13.6 us
    unnamed x16, local copies, waits for them, and re-layouts  10.5 us
    pallas_call x1, Pallas kernels, split_and_grad(): pl.pallas_call(split_kernel, out_shape=(jax.ShapeDtypeStruct((CHIPS, ROWS...  7.8 us
    pallas_call x2, Pallas kernels, gram(): pl.pallas_call(gram_kernel, out_shape=jax.ShapeDtypeStruct(out_dims, jnp....  7.31 us
    ppermute x6, starting transfers between devices, summed(): return [sums] + [lax.ppermute(sums, 'shard', shift) for shift in shifts]  6.96 us
  transfers between devices with their start and end apart: 13, of which 6 were waited for; matrix products, arithmetic and copies ran while one was open for 4% of the time, Pallas kernels for 21%

profile of v5, /device:TPU:1, one launch (start us, length us, event | category | flops | bytes accessed | tf_op | source)
XLA Modules:
  0.0 139.7 jit_solution(16681895181808092543)
XLA Ops:
  0.6 2.2 %copy-done.4 = bf16[2048,1024]{1,0:T(8,128)(2,1)S(1)} copy-done((bf16[2048,1024]{1,0:T(8,128)(2,1)S(1)}, bf16[2048,1024]{1,0:T(8,128)(2,1)}, u32[]{:S(2)}) %copy-start.4) | copy-done | bytes 4194328
  2.8 7.8 %shard_map.102 = (f32[16,64,1024]{2,1,0:T(8,128)S(1)}, bf16[1024,2048]{1,0:T(8,128)(2,1)S(1)}, bf16[1024,2048]{1,0:T(8,128)(2,1)S(1)}) custom-call(s32[1]{0:T(128)} %bitcast.2.core_ref, bf16[2048,2048]{1,0:T(8,128)(2,1)} %x_hbm.1, bf16[2048,1024]{1,0:T(8,128)(2,1)S(1)} %copy-done.4), custom_call_target="tpu_custom_call" | custom-call | flops 4294967296 | bytes 25165824 | tf_op jit(solution)/shard_map/pallas_call | solution.py:71
  10.6 1.5 %collective-permute-start = (f32[16,64,1024]{2,1,0:T(8,128)S(1)}, f32[16,64,1024]{2,1,0:T(8,128)S(1)}, u32[]{:S(2)}, u32[]{:S(2)}) collective-permute-start(f32[16,64,1024]{2,1,0:T(8,128)S(1)} %get-tuple-element.21), channel_id=1, source_target_pairs={{0,1},{1,0},{2,3},{3,2},{4,5},{5,4},{6,7},{7,6},{8,9},{9,8},{10,11... | collective-permute-start | bytes 12582920 | tf_op jit(solution)/shard_map/ppermute | solution.py:362
  12.2 5.0 %shard_map.103.refs_0_.a_ref = f32[16,64,1024]{2,1,0:T(8,128)S(1)} custom-call(bf16[1024,2048]{1,0:T(8,128)(2,1)S(1)} %get-tuple-element.26.x_ref, bf16[2048,1024]{1,0:T(8,128)(2,1)S(1)} %copy-done.5), custom_call_target="tpu_custom_call" | custom-call | flops 4294967296 | bytes 12582912 | tf_op jit(solution)/shard_map/pallas_call | solution.py:104
  17.2 3.9 %shard_map.104 = f32[8,64,1024]{2,1,0:T(8,128)} custom-call(bf16[1024,2048]{1,0:T(8,128)(2,1)S(1)} %get-tuple-element.27.x_ref, bf16[2048,1024]{1,0:T(8,128)(2,1)S(1)} %copy-done.2, f32[16,64,1024]{2,1,0:T(8,128)S(1)} %shard_map.103.refs_0_.a_ref), custom_call_target="tpu_custom_call" | custom-call | flops 2147483648 | bytes 12582912 | tf_op jit(solution)/shard_map/pallas_call | solution.py:104
  21.1 1.8 %shard_map.105 = f32[1,8,128]{2,1,0:T(8,128)S(1)} custom-call(s32[1]{0:T(128)} %bitcast.2.core_ref, f32[16,64,1024]{2,1,0:T(8,128)S(1)} %shard_map.103.refs_0_.a_ref, f32[16,64,1024]{2,1,0:T(8,128)S(1)} %collective-permute-done.refs_0_.refs_1_), custom_call_target="tpu_custom_call" | custom-call | flops 1048576 | bytes 1048576 | tf_op jit(solution)/shard_map/pallas_call | solution.py:159
  24.0 2.6 %collective-permute-start.4 = (f32[1,8,128]{2,1,0:T(8,128)S(1)}, f32[1,8,128]{2,1,0:T(8,128)S(1)}, u32[]{:S(2)}, u32[]{:S(2)}) collective-permute-start(f32[1,8,128]{2,1,0:T(8,128)S(1)} %add.6.refs_1_), channel_id=1, source_target_pairs={{0,96},{32,0},{64,32},{96,64},{1,97},{33,1},{65,33},{97,65},{2,98}... | collective-permute-start | bytes 12296 | tf_op jit(solution)/shard_map/ppermute | solution.py:356
  27.7 3.9 %shard_map.108 = f32[8,64,1024]{2,1,0:T(8,128)} custom-call(bf16[1024,2048]{1,0:T(8,128)(2,1)S(1)} %get-tuple-element.27.x_ref, bf16[2048,1024]{1,0:T(8,128)(2,1)S(1)} %copy-done.2, f32[16,64,1024]{2,1,0:T(8,128)S(1)} %shard_map.103.refs_0_.a_ref, f32[16,64,1024]{2,1,0:T(8,128)S(1)} %collective-permute-done.refs_0_.refs_1_), custom_call_target="tpu_custom_call" | custom-call | flops 2147483648 | bytes 12582912 | tf_op jit(solution)/shard_map/pallas_call | solution.py:104
  32.2 1.8 %convert_element_type.13 = f16[16,64,1024]{2,1,0:T(8,128)(2,1)} convert(f32[16,64,1024]{2,1,0:T(8,128)S(1)} %get-tuple-element.25) | non-fusion elementwise | flops 1048576 | bytes 6291456 | tf_op jit(solution)/shard_map/convert_element_type | solution.py:371
  34.0 1.1 collective-permute-start.6
  35.1 7.8 %all-to-all-start.1 = ((f16[16,64,1024]{2,1,0:T(8,128)(2,1)}), f16[16,64,1024]{2,1,0:T(8,128)(2,1)}, u32[]{:S(2)}, u32[]{:S(2)}) async-start(f16[16,64,1024]{2,1,0:T(8,128)(2,1)} %convert_element_type.13), calls=%async_computation.1 | async-start | bytes 4194304 | tf_op jit(solution)/shard_map/all_to_all | solution.py:359
  42.9 2.2 %copy-done.3 = bf16[2048,1024]{1,0:T(8,128)(2,1)S(1)} copy-done((bf16[2048,1024]{1,0:T(8,128)(2,1)S(1)}, bf16[2048,1024]{1,0:T(8,128)(2,1)}, u32[]{:S(2)}) %copy-start.3) | copy-done | bytes 4194328
  45.1 2.2 %copy-done.7 = bf16[1024,2048]{1,0:T(8,128)(2,1)S(1)} copy-done((bf16[1024,2048]{1,0:T(8,128)(2,1)S(1)}, bf16[1024,2048]{1,0:T(8,128)(2,1)}, u32[]{:S(2)}) %copy-start.7) | copy-done | bytes 4194328
  47.3 5.0 %shard_map.107.a_ref = f32[16,64,1024]{2,1,0:T(8,128)S(1)} custom-call(bf16[1024,2048]{1,0:T(8,128)(2,1)S(1)} %copy-done.7, bf16[2048,1024]{1,0:T(8,128)(2,1)S(1)} %copy-done.3), custom_call_target="tpu_custom_call" | custom-call | flops 4294967296 | bytes 12582912 | tf_op jit(solution)/shard_map/pallas_call | solution.py:104
  52.3 4.3 %shard_map.109 = f32[1,8,128]{2,1,0:T(8,128)S(1)} custom-call(s32[1]{0:T(128)} %bitcast.2.core_ref, f32[16,64,1024]{2,1,0:T(8,128)S(1)} %shard_map.107.a_ref, f32[8,64,1024]{2,1,0:T(8,128)S(1)} %collective-permute-done.5.refs_0_, f32[8,64,1024]{2,1,0:T(8,128)} %collective-permute-done.6.refs_1_), custom_call_target="tpu_custom_call" | custom-call | flops 1048576 | bytes 1048576 | tf_op jit(solution)/shard_map/pallas_call | solution.py:159
  57.9 2.0 %collective-permute-start.10 = (f32[1,8,128]{2,1,0:T(8,128)S(1)}, f32[1,8,128]{2,1,0:T(8,128)S(1)}, u32[]{:S(2)}, u32[]{:S(2)}) collective-permute-start(f32[1,8,128]{2,1,0:T(8,128)S(1)} %add.7.refs_2_), channel_id=1, source_target_pairs={{0,96},{32,0},{64,32},{96,64},{1,97},{33,1},{65,33},{97,65},{2,98}... | collective-permute-start | bytes 12296 | tf_op jit(solution)/shard_map/ppermute | solution.py:356
  59.9 1.2 collective-permute-start.9
  61.2 2.7 %collective-permute-done.9.refs_4_ = f32[1,8,128]{2,1,0:T(8,128)S(1)} collective-permute-done((f32[1,8,128]{2,1,0:T(8,128)S(1)}, f32[1,8,128]{2,1,0:T(8,128)S(1)}, u32[]{:S(2)}, u32[]{:S(2)}) %collective-permute-start.9) | collective-permute-done | bytes 4128 | tf_op jit(solution)/shard_map/ppermute | solution.py:356
  63.9 1.4 collective-permute-done.8.refs_3_
  65.2 3.2 %shard_map.110 = (f32[16,64,1024]{2,1,0:T(8,128)S(1)}, f32[8,128]{1,0:T(8,128)S(1)}) custom-call(s32[1]{0:T(128)} %bitcast.2.core_ref, f32[16,64,1024]{2,1,0:T(8,128)S(1)} %shard_map.107.a_ref, f32[8,64,1024]{2,1,0:T(8,128)S(1)} %collective-permute-done.5.refs_0_, f32[8,64,1024]{2,1,0:T(8,128)} %collective-permute-done.6.refs_1_, ...), custom_call_target="tpu_custom_call" | custom-call | flops 1048576 | bytes 1048576 | tf_op jit(solution)/shard_map/pallas_call | solution.py:192
  68.4 1.8 %convert_element_type.14 = f16[16,64,1024]{2,1,0:T(8,128)(2,1)} convert(f32[16,64,1024]{2,1,0:T(8,128)S(1)} %get-tuple-element.29) | non-fusion elementwise | flops 1048576 | bytes 6291456 | tf_op jit(solution)/shard_map/convert_element_type | solution.py:381
  70.2 1.9 %all-to-all-done.1 = f16[16,64,1024]{2,1,0:T(8,128)(2,1)} async-done(((f16[16,64,1024]{2,1,0:T(8,128)(2,1)}), f16[16,64,1024]{2,1,0:T(8,128)(2,1)}, u32[]{:S(2)}, u32[]{:S(2)}) %all-to-all-start.1) | async-done | bytes 2097184 | tf_op jit(solution)/shard_map/all_to_all | solution.py:359
  72.1 5.8 %all-to-all-start = ((f16[16,64,1024]{2,1,0:T(8,128)(2,1)}), f16[16,64,1024]{2,1,0:T(8,128)(2,1)}, u32[]{:S(2)}, u32[]{:S(2)}) async-start(f16[16,64,1024]{2,1,0:T(8,128)(2,1)} %convert_element_type.14), calls=%async_computation | async-start | bytes 4194304 | tf_op jit(solution)/shard_map/all_to_all | solution.py:359
  77.9 2.1 %convert_element_type.16.v_ref.refs_0_ = f32[16,64,1024]{2,1,0:T(8,128)S(1)} convert(f16[16,64,1024]{2,1,0:T(8,128)(2,1)} %all-to-all-done.1) | non-fusion elementwise | flops 1048576 | bytes 6291456 | tf_op jit(solution)/shard_map/convert_element_type | solution.py:383
  80.0 3.6 %shard_map.111.refs_0_ = f32[2,128]{1,0:T(2,128)S(1)} custom-call(s32[2]{0:T(128)S(1)} %pad_add_fusion.place_ref, f32[16,64,1024]{2,1,0:T(8,128)S(1)} %convert_element_type.16.v_ref.refs_0_, f32[8,128]{1,0:T(8,128)S(1)} %get-tuple-element.31.norm_ref), custom_call_target="tpu_custom_call" | custom-call | flops 20971520 | bytes 4194304 | tf_op jit(solution)/shard_map/pallas_call | solution.py:246
  83.7 1.9 %copy-done = f32[16,64,1024]{2,1,0:T(8,128)} copy-done((f32[16,64,1024]{2,1,0:T(8,128)}, f32[16,64,1024]{2,1,0:T(8,128)S(1)}, u32[]{:S(2)}) %copy-start) | copy-done | bytes 4194328
  85.6 17.8 %all-to-all-done = f16[16,64,1024]{2,1,0:T(8,128)(2,1)} async-done(((f16[16,64,1024]{2,1,0:T(8,128)(2,1)}), f16[16,64,1024]{2,1,0:T(8,128)(2,1)}, u32[]{:S(2)}, u32[]{:S(2)}) %all-to-all-start) | async-done | bytes 2097184 | tf_op jit(solution)/shard_map/all_to_all | solution.py:359
  103.5 2.1 %convert_element_type.15.v_ref.refs_3_ = f32[16,64,1024]{2,1,0:T(8,128)S(1)} convert(f16[16,64,1024]{2,1,0:T(8,128)(2,1)} %all-to-all-done) | non-fusion elementwise | flops 1048576 | bytes 6291456 | tf_op jit(solution)/shard_map/convert_element_type | solution.py:385
  105.6 3.7 %shard_map.112 = f32[128,4,128]{2,1,0:T(4,128)S(1)} custom-call(s32[2]{0:T(128)S(1)} %pad_add_fusion.place_ref, f32[16,64,1024]{2,1,0:T(8,128)S(1)} %convert_element_type.15.v_ref.refs_3_, f32[8,128]{1,0:T(8,128)S(1)} %get-tuple-element.30.norm_ref, f32[2,128]{1,0:T(2,128)S(1)} %shard_map.111.refs_0_), custom_call_target="tpu_custom_call" | custom-call | flops 20971520 | bytes 4194304 | tf_op jit(solution)/shard_map/pallas_call | solution.py:246
  109.3 2.0 %copy-done.1 = f32[16,64,1024]{2,1,0:T(8,128)} copy-done((f32[16,64,1024]{2,1,0:T(8,128)}, f32[16,64,1024]{2,1,0:T(8,128)S(1)}, u32[]{:S(2)}) %copy-start.1) | copy-done | bytes 4194328
  111.2 21.2 %all_to_all.15 = f32[128,4,128]{2,1,0:T(4,128)S(1)} all-to-all(f32[128,4,128]{2,1,0:T(4,128)S(1)} %shard_map.112), channel_id=1, replica_groups=mesh['shard'=4,'rep'=32] {'shard','rep'}, dimensions={0} | all-to-all | bytes 524288 | tf_op jit(solution)/shard_map/all_to_all | solution.py:387
  133.1 6.4 %shard_map.113 = (f32[64,1024]{1,0:T(8,128)}, f32[64,1024]{1,0:T(8,128)}, f32[64,1024]{1,0:T(8,128)}, f32[64,1024]{1,0:T(8,128)}) custom-call(f32[4,128]{1,0:T(4,128)} %reduce_sum.9.totals_ref, f32[16,64,1024]{2,1,0:T(8,128)} %copy-done, f32[64,1024]{1,0:T(8,128)} %refs_1_.1, f32[64,1024]{1,0:T(8,128)} %refs_2_.1, f32[16,64,1024]{2,1,0:T(8,128)} %copy-done.1, ...), custom_call_target="tpu_custom_call" | custom-call | flops 8388608 | bytes 10485760 | tf_op jit(solution)/shard_map/pallas_call | solution.py:324
  (31 shorter events, 5.0 us)
Async XLA Ops:
  0.6 2.2 %copy-start.4 = (bf16[2048,1024]{1,0:T(8,128)(2,1)S(1)}, bf16[2048,1024]{1,0:T(8,128)(2,1)}, u32[]{:S(2)}) copy-start(bf16[2048,1024]{1,0:T(8,128)(2,1)} %y_ref.4) | copy-start | bytes 12582916
  2.8 9.3 %copy-start.5 = (bf16[2048,1024]{1,0:T(8,128)(2,1)S(1)}, bf16[2048,1024]{1,0:T(8,128)(2,1)}, u32[]{:S(2)}) copy-start(bf16[2048,1024]{1,0:T(8,128)(2,1)} %y_ref.4) | copy-start | bytes 12582916
  10.6 6.5 %copy-start.6 = (bf16[1024,2048]{1,0:T(8,128)(2,1)}, bf16[1024,2048]{1,0:T(8,128)(2,1)S(1)}, u32[]{:S(2)}) copy-start(bf16[1024,2048]{1,0:T(8,128)(2,1)S(1)} %get-tuple-element.26.x_ref) | copy-start | bytes 12582916
  10.6 10.4 %collective-permute-start = (f32[16,64,1024]{2,1,0:T(8,128)S(1)}, f32[16,64,1024]{2,1,0:T(8,128)S(1)}, u32[]{:S(2)}, u32[]{:S(2)}) collective-permute-start(f32[16,64,1024]{2,1,0:T(8,128)S(1)} %get-tuple-element.21), channel_id=1, source_target_pairs={{0,1},{1,0},{2,3},{3,2},{4,5},{5,4},{6,7},{7,6},{8,9},{9,8},{10,11... | collective-permute-start | bytes 12582920 | tf_op jit(solution)/shard_map/ppermute | solution.py:362
  12.2 5.0 %copy-start.2 = (bf16[2048,1024]{1,0:T(8,128)(2,1)S(1)}, bf16[2048,1024]{1,0:T(8,128)(2,1)}, u32[]{:S(2)}) copy-start(bf16[2048,1024]{1,0:T(8,128)(2,1)} %y_ref.7) | copy-start | bytes 12582916
  22.8 1.2 collective-permute-start.1
  22.9 29.4 %collective-permute-start.5 = (f32[8,64,1024]{2,1,0:T(8,128)}, f32[8,64,1024]{2,1,0:T(8,128)S(1)}, u32[]{:S(2)}, u32[]{:S(2)}) collective-permute-start(f32[8,64,1024]{2,1,0:T(8,128)} %shard_map.104), channel_id=1, source_target_pairs={{0,1},{1,0},{2,3},{3,2},{4,5},{5,4},{6,7},{7,6},{8,9},{9,8},{10,11... | collective-permute-start | bytes 6291464 | tf_op jit(solution)/shard_map/ppermute | solution.py:375
  24.0 7.5 %collective-permute-start.4 = (f32[1,8,128]{2,1,0:T(8,128)S(1)}, f32[1,8,128]{2,1,0:T(8,128)S(1)}, u32[]{:S(2)}, u32[]{:S(2)}) collective-permute-start(f32[1,8,128]{2,1,0:T(8,128)S(1)} %add.6.refs_1_), channel_id=1, source_target_pairs={{0,96},{32,0},{64,32},{96,64},{1,97},{33,1},{65,33},{97,65},{2,98}... | collective-permute-start | bytes 12296 | tf_op jit(solution)/shard_map/ppermute | solution.py:356
  26.6 5.0 %collective-permute-start.3 = (f32[1,8,128]{2,1,0:T(8,128)S(1)}, f32[1,8,128]{2,1,0:T(8,128)S(1)}, u32[]{:S(2)}, u32[]{:S(2)}) collective-permute-start(f32[1,8,128]{2,1,0:T(8,128)S(1)} %add.6.refs_1_), channel_id=1, source_target_pairs={{0,64},{32,96},{64,0},{96,32},{1,65},{33,97},{65,1},{97,33},{2,66}... | collective-permute-start | bytes 12296 | tf_op jit(solution)/shard_map/ppermute | solution.py:356
  27.1 4.5 %collective-permute-start.2 = (f32[1,8,128]{2,1,0:T(8,128)S(1)}, f32[1,8,128]{2,1,0:T(8,128)S(1)}, u32[]{:S(2)}, u32[]{:S(2)}) collective-permute-start(f32[1,8,128]{2,1,0:T(8,128)S(1)} %add.6.refs_1_), channel_id=1, source_target_pairs={{0,32},{32,64},{64,96},{96,0},{1,33},{33,65},{65,97},{97,1},{2,34}... | collective-permute-start | bytes 12296 | tf_op jit(solution)/shard_map/ppermute | solution.py:356
  34.0 18.3 %collective-permute-start.6 = (f32[8,64,1024]{2,1,0:T(8,128)}, f32[8,64,1024]{2,1,0:T(8,128)}, u32[]{:S(2)}, u32[]{:S(2)}) collective-permute-start(f32[8,64,1024]{2,1,0:T(8,128)} %shard_map.108), channel_id=1, source_target_pairs={{0,1},{1,0},{2,3},{3,2},{4,5},{5,4},{6,7},{7,6},{8,9},{9,8},{10,11... | collective-permute-start | bytes 6291464 | tf_op jit(solution)/shard_map/ppermute | solution.py:376
  35.1 37.0 %all-to-all-start.1 = ((f16[16,64,1024]{2,1,0:T(8,128)(2,1)}), f16[16,64,1024]{2,1,0:T(8,128)(2,1)}, u32[]{:S(2)}, u32[]{:S(2)}) async-start(f16[16,64,1024]{2,1,0:T(8,128)(2,1)} %convert_element_type.13), calls=%async_computation.1 | async-start | bytes 4194304 | tf_op jit(solution)/shard_map/all_to_all | solution.py:359
  42.9 2.2 %copy-start.3 = (bf16[2048,1024]{1,0:T(8,128)(2,1)S(1)}, bf16[2048,1024]{1,0:T(8,128)(2,1)}, u32[]{:S(2)}) copy-start(bf16[2048,1024]{1,0:T(8,128)(2,1)} %y_ref.7) | copy-start | bytes 12582916
  45.1 2.2 %copy-start.7 = (bf16[1024,2048]{1,0:T(8,128)(2,1)S(1)}, bf16[1024,2048]{1,0:T(8,128)(2,1)}, u32[]{:S(2)}) copy-start(bf16[1024,2048]{1,0:T(8,128)(2,1)} %copy-done.6) | copy-start | bytes 12582916
  56.7 1.2 collective-permute-start.7
  57.9 3.3 %collective-permute-start.10 = (f32[1,8,128]{2,1,0:T(8,128)S(1)}, f32[1,8,128]{2,1,0:T(8,128)S(1)}, u32[]{:S(2)}, u32[]{:S(2)}) collective-permute-start(f32[1,8,128]{2,1,0:T(8,128)S(1)} %add.7.refs_2_), channel_id=1, source_target_pairs={{0,96},{32,0},{64,32},{96,64},{1,97},{33,1},{65,33},{97,65},{2,98}... | collective-permute-start | bytes 12296 | tf_op jit(solution)/shard_map/ppermute | solution.py:356
  59.9 4.0 %collective-permute-start.9 = (f32[1,8,128]{2,1,0:T(8,128)S(1)}, f32[1,8,128]{2,1,0:T(8,128)S(1)}, u32[]{:S(2)}, u32[]{:S(2)}) collective-permute-start(f32[1,8,128]{2,1,0:T(8,128)S(1)} %add.7.refs_2_), channel_id=1, source_target_pairs={{0,64},{32,96},{64,0},{96,32},{1,65},{33,97},{65,1},{97,33},{2,66}... | collective-permute-start | bytes 12296 | tf_op jit(solution)/shard_map/ppermute | solution.py:356
  61.1 4.1 %collective-permute-start.8 = (f32[1,8,128]{2,1,0:T(8,128)S(1)}, f32[1,8,128]{2,1,0:T(8,128)S(1)}, u32[]{:S(2)}, u32[]{:S(2)}) collective-permute-start(f32[1,8,128]{2,1,0:T(8,128)S(1)} %add.7.refs_2_), channel_id=1, source_target_pairs={{0,32},{32,64},{64,96},{96,0},{1,33},{33,65},{65,97},{97,1},{2,34}... | collective-permute-start | bytes 12296 | tf_op jit(solution)/shard_map/ppermute | solution.py:356
  72.1 31.4 %all-to-all-start = ((f16[16,64,1024]{2,1,0:T(8,128)(2,1)}), f16[16,64,1024]{2,1,0:T(8,128)(2,1)}, u32[]{:S(2)}, u32[]{:S(2)}) async-start(f16[16,64,1024]{2,1,0:T(8,128)(2,1)} %convert_element_type.14), calls=%async_computation | async-start | bytes 4194304 | tf_op jit(solution)/shard_map/all_to_all | solution.py:359
  83.7 1.9 %copy-start = (f32[16,64,1024]{2,1,0:T(8,128)}, f32[16,64,1024]{2,1,0:T(8,128)S(1)}, u32[]{:S(2)}) copy-start(f32[16,64,1024]{2,1,0:T(8,128)S(1)} %convert_element_type.16.v_ref.refs_0_) | copy-start | bytes 12582916
  109.2 2.0 %copy-start.1 = (f32[16,64,1024]{2,1,0:T(8,128)}, f32[16,64,1024]{2,1,0:T(8,128)S(1)}, u32[]{:S(2)}) copy-start(f32[16,64,1024]{2,1,0:T(8,128)S(1)} %convert_element_type.15.v_ref.refs_3_) | copy-start | bytes 12582916

commit v6 on v5

--- a/solution.py
+++ b/solution.py
@@ -39,7 +39,9 @@
 def split_kernel(core_ref, x_hbm, y_hbm, grad_ref, own_ref, other_ref, x_ref, y_ref, x_sems, y_sem):
     steps, depth, width = x_ref.shape
     x_copies = [
-        pltpu.make_async_copy(x_hbm.at[:, pl.ds(i * width, width)], x_ref.at[i], x_sems.at[i])
+        pltpu.make_async_copy(
+            x_hbm.at[:, pl.ds((steps - 1 - i) * width, width)], x_ref.at[i], x_sems.at[i]
+        )
         for i in range(steps)
     ]
     y_copy = pltpu.make_async_copy(y_hbm, y_ref, y_sem)
@@ -53,8 +55,9 @@
     for i in range(steps):
         x_copies[i].wait()
         blocks = x_ref[i].T.reshape(-1, 2, ROWS, depth)
-        first = blocks[:, 0].reshape(-1, depth)
-        second = blocks[:, 1].reshape(-1, depth)
+        order = range(blocks.shape[0] - 1, -1, -1)
+        first = jnp.concatenate([blocks[n, 0] for n in order], axis=0)
+        second = jnp.concatenate([blocks[n, 1] for n in order], axis=0)
         own_ref[pl.ds(i * half, half), :] = jnp.where(is_first, first, second)
         other = jnp.where(is_first, second, first)
         other_ref[pl.ds(i * half, half), :] = other
@@ -292,19 +295,16 @@
 
 
 def update_kernel(totals_ref, *refs):
-    hbms, outs, held_refs, sems = refs[:6], refs[6:10], refs[10:16], refs[16]
-    copies = [
-        pltpu.make_async_copy(hbm, held, sems.at[n]) for n, (hbm, held) in enumerate(zip(hbms, held_refs))
-    ]
-    for copy in copies:
-        copy.start()
+    ins, outs, (sum_ref, scalar_ref, sem) = refs[:6], refs[6:10], refs[10:]
+    sum_ref[...] = jnp.sum(totals_ref[...], axis=0)
+    copy = pltpu.make_async_copy(sum_ref, scalar_ref, sem)
+    copy.start()
+    copy.wait()
     weights = [
-        tree_coefs(lambda n, t=t: totals_ref[2 * t + n // 128, n % 128]) for t in range(2)
+        tree_coefs(lambda n, t=t: scalar_ref[2 * t + n // 128, n % 128]) for t in range(2)
     ]
     for t in range(2):
-        for copy in copies[3 * t : 3 * t + 3]:
-            copy.wait()
-        v_ref, weight_ref, moment_ref = held_refs[3 * t : 3 * t + 3]
+        v_ref, weight_ref, moment_ref = ins[3 * t : 3 * t + 3]
         new_weight_ref, new_moment_ref = outs[2 * t : 2 * t + 2]
 
         @pl.loop(0, ROWS // 8)
@@ -320,15 +320,17 @@
 
 def update(totals, *arrays):
     out = jax.ShapeDtypeStruct((ROWS, FEATURES), jnp.float32)
-    hbm = pl.BlockSpec(memory_space=pltpu.HBM)
     return pl.pallas_call(
         update_kernel,
         out_shape=(out,) * 4,
-        in_specs=[SMEM] + [hbm] * 6,
+        in_specs=[VMEM] * 7,
         out_specs=(VMEM,) * 4,
-        scratch_shapes=[pltpu.VMEM(a.shape, a.dtype) for a in arrays]
-        + [pltpu.SemaphoreType.DMA((6,))],
-        compiler_params=params(60),
+        scratch_shapes=[
+            pltpu.VMEM((4, 128), jnp.float32),
+            pltpu.SMEM((4, 128), jnp.float32),
+            pltpu.SemaphoreType.DMA,
+        ],
+        compiler_params=params(8),
         cost_estimate=cost(8 << 20, 10 * MIB),
     )(totals, *arrays)
 
@@ -344,9 +346,9 @@
     index = lax.axis_index("rep").astype(jnp.int32)
     core = (index & 1)[None]
     leader = ((lax.axis_index("shard") == 0) & (index & 1 == 0)).astype(jnp.int32)
-    place = jnp.stack([index >> 1, leader])
+    place = jnp.stack([CHIPS - 1 - (index >> 1), leader])
     swap = [(i, i ^ 1) for i in range(replicas)]
-    core_groups = [list(range(c, replicas, 2)) for c in range(2)]
+    core_groups = [list(range(c, replicas, 2))[::-1] for c in range(2)]
 
     def summed(sums):
         sums = sums + lax.ppermute(sums, "rep", swap)
@@ -384,7 +386,7 @@
     key_vector = gram(place, key_v, key_norm, [], (2, 128))
     value_v = value_all.astype(jnp.float32)
     vectors = gram(place, value_v, value_norm, [key_vector], (shard_count * replicas, 4, 128))
-    totals = jnp.sum(lax.all_to_all(vectors, ("shard", "rep"), 0, 0), axis=0)
+    totals = lax.all_to_all(vectors, ("shard", "rep"), 0, 0)
     new_key_weight, new_key_moment, new_value_weight, new_value_moment = update(
         totals, key_v, key_weight, key_moment, value_v, value_weight, value_moment
     )

time: 140 us -> 137 us (0.979)
  starting transfers between devices: 24 us -> 29.5 us
  waiting for transfers between devices: 25.3 us -> 21.6 us
  Pallas kernels: 49.1 us -> 46.2 us
  local copies, waits for them, and re-layouts: 10.5 us -> 8.53 us
    all_to_all x2, starting transfers between devices: 13.6 us -> 19.1 us  [gathered(): return lax.all_to_all(sent, 'rep', 0, 0, axis_index_groups=core_groups)]
    all_to_all x2, waiting for transfers between devices: 19.7 us -> 15.9 us  [gathered(): return lax.all_to_all(sent, 'rep', 0, 0, axis_index_groups=core_groups)]
    pallas_call x1, Pallas kernels: 6.37 us -> 3.25 us  [update(): pl.pallas_call(update_kernel, out_shape=(out,) * 4, in_specs=[VMEM] * 7,...]
    unnamed x16 -> x24, local copies, waits for them, and re-layouts: 10.5 us -> 8.53 us
  transfers between devices with their start and end apart: 13 -> 13, of which waited for: 6 -> 5; matrix products, arithmetic and copies ran while one was open for 4% -> 4% of each run, Pallas kernels for 21% -> 22%
where the time goes in v6:
time: 137 us; the launch traced here: 136 us
  Pallas kernels  46.2 us (34%)
  starting transfers between devices  29.5 us (22%)
  waiting for transfers between devices  21.6 us (16%)
  blocking collectives  21.3 us (16%)
  local copies, waits for them, and re-layouts  8.53 us (6%)
  other arithmetic  8.05 us (6%)
    all_to_all x1, blocking collectives, shards(): totals = lax.all_to_all(vectors, ('shard', 'rep'), 0, 0)  21.3 us
    all_to_all x2, starting transfers between devices, gathered(): return lax.all_to_all(sent, 'rep', 0, 0, axis_index_groups=core_groups)  19.1 us
    pallas_call x4, Pallas kernels, grad(): pl.pallas_call(functools.partial(grad_kernel, start=start), out_shape=jax...  17.8 us
    all_to_all x2, waiting for transfers between devices, gathered(): return lax.all_to_all(sent, 'rep', 0, 0, axis_index_groups=core_groups)  15.9 us
    unnamed x24, local copies, waits for them, and re-layouts  8.53 us
    pallas_call x1, Pallas kernels, split_and_grad(): pl.pallas_call(split_kernel, out_shape=(jax.ShapeDtypeStruct((CHIPS, ROWS...  7.79 us
    pallas_call x2, Pallas kernels, gram(): pl.pallas_call(gram_kernel, out_shape=jax.ShapeDtypeStruct(out_dims, jnp....  7.31 us
    ppermute x6, starting transfers between devices, summed(): return [sums] + [lax.ppermute(sums, 'shard', shift) for shift in shifts]  6.98 us
  transfers between devices with their start and end apart: 13, of which 5 were waited for; matrix products, arithmetic and copies ran while one was open for 4% of the time, Pallas kernels for 22%

profile of v6, /device:TPU:1, one launch (start us, length us, event | category | flops | bytes accessed | tf_op | source)
XLA Modules:
  0.0 136.1 jit_solution(10789503591302377234)
XLA Ops:
  0.6 2.2 %copy-done.8 = bf16[2048,1024]{1,0:T(8,128)(2,1)S(1)} copy-done((bf16[2048,1024]{1,0:T(8,128)(2,1)S(1)}, bf16[2048,1024]{1,0:T(8,128)(2,1)}, u32[]{:S(2)}) %copy-start.8) | copy-done | bytes 4194328
  2.8 7.8 %shard_map.102 = (f32[16,64,1024]{2,1,0:T(8,128)S(1)}, bf16[1024,2048]{1,0:T(8,128)(2,1)S(1)}, bf16[1024,2048]{1,0:T(8,128)(2,1)S(1)}) custom-call(s32[1]{0:T(128)} %bitcast.2.core_ref, bf16[2048,2048]{1,0:T(8,128)(2,1)} %x_hbm.1, bf16[2048,1024]{1,0:T(8,128)(2,1)S(1)} %copy-done.8), custom_call_target="tpu_custom_call" | custom-call | flops 4294967296 | bytes 25165824 | tf_op jit(solution)/shard_map/pallas_call | solution.py:74
  10.6 1.5 %collective-permute-start = (f32[16,64,1024]{2,1,0:T(8,128)S(1)}, f32[16,64,1024]{2,1,0:T(8,128)S(1)}, u32[]{:S(2)}, u32[]{:S(2)}) collective-permute-start(f32[16,64,1024]{2,1,0:T(8,128)S(1)} %get-tuple-element.21), channel_id=1, source_target_pairs={{0,1},{1,0},{2,3},{3,2},{4,5},{5,4},{6,7},{7,6},{8,9},{9,8},{10,11... | collective-permute-start | bytes 12582920 | tf_op jit(solution)/shard_map/ppermute | solution.py:364
  12.1 5.0 %shard_map.103.refs_0_.a_ref = f32[16,64,1024]{2,1,0:T(8,128)S(1)} custom-call(bf16[1024,2048]{1,0:T(8,128)(2,1)S(1)} %get-tuple-element.26.x_ref, bf16[2048,1024]{1,0:T(8,128)(2,1)S(1)} %copy-done.9), custom_call_target="tpu_custom_call" | custom-call | flops 4294967296 | bytes 12582912 | tf_op jit(solution)/shard_map/pallas_call | solution.py:107
  17.2 3.9 %shard_map.104 = f32[8,64,1024]{2,1,0:T(8,128)} custom-call(bf16[1024,2048]{1,0:T(8,128)(2,1)S(1)} %get-tuple-element.27.x_ref, bf16[2048,1024]{1,0:T(8,128)(2,1)S(1)} %copy-done.2, f32[16,64,1024]{2,1,0:T(8,128)S(1)} %shard_map.103.refs_0_.a_ref), custom_call_target="tpu_custom_call" | custom-call | flops 2147483648 | bytes 12582912 | tf_op jit(solution)/shard_map/pallas_call | solution.py:107
  21.1 1.8 %shard_map.105 = f32[1,8,128]{2,1,0:T(8,128)S(1)} custom-call(s32[1]{0:T(128)} %bitcast.2.core_ref, f32[16,64,1024]{2,1,0:T(8,128)S(1)} %shard_map.103.refs_0_.a_ref, f32[16,64,1024]{2,1,0:T(8,128)S(1)} %collective-permute-done.refs_0_.refs_1_), custom_call_target="tpu_custom_call" | custom-call | flops 1048576 | bytes 1048576 | tf_op jit(solution)/shard_map/pallas_call | solution.py:162
  23.5 0.7 collective-permute-done.1
  24.1 2.6 %collective-permute-start.4 = (f32[1,8,128]{2,1,0:T(8,128)S(1)}, f32[1,8,128]{2,1,0:T(8,128)S(1)}, u32[]{:S(2)}, u32[]{:S(2)}) collective-permute-start(f32[1,8,128]{2,1,0:T(8,128)S(1)} %add.6.refs_1_), channel_id=1, source_target_pairs={{0,96},{32,0},{64,32},{96,64},{1,97},{33,1},{65,33},{97,65},{2,98}... | collective-permute-start | bytes 12296 | tf_op jit(solution)/shard_map/ppermute | solution.py:358
  27.8 3.9 %shard_map.108 = f32[8,64,1024]{2,1,0:T(8,128)} custom-call(bf16[1024,2048]{1,0:T(8,128)(2,1)S(1)} %get-tuple-element.27.x_ref, bf16[2048,1024]{1,0:T(8,128)(2,1)S(1)} %copy-done.2, f32[16,64,1024]{2,1,0:T(8,128)S(1)} %shard_map.103.refs_0_.a_ref, f32[16,64,1024]{2,1,0:T(8,128)S(1)} %collective-permute-done.refs_0_.refs_1_), custom_call_target="tpu_custom_call" | custom-call | flops 2147483648 | bytes 12582912 | tf_op jit(solution)/shard_map/pallas_call | solution.py:107
  32.3 1.8 %convert_element_type.13 = f16[16,64,1024]{2,1,0:T(8,128)(2,1)} convert(f32[16,64,1024]{2,1,0:T(8,128)S(1)} %get-tuple-element.25) | non-fusion elementwise | flops 1048576 | bytes 6291456 | tf_op jit(solution)/shard_map/convert_element_type | solution.py:373
  34.2 1.0 collective-permute-start.6
  35.2 10.5 %all-to-all-start.1 = ((f16[16,64,1024]{2,1,0:T(8,128)(2,1)}), f16[16,64,1024]{2,1,0:T(8,128)(2,1)}, u32[]{:S(2)}, u32[]{:S(2)}) async-start(f16[16,64,1024]{2,1,0:T(8,128)(2,1)} %convert_element_type.13), calls=%async_computation.1 | async-start | bytes 4194304 | tf_op jit(solution)/shard_map/all_to_all | solution.py:361
  45.7 2.2 %copy-done.3 = bf16[2048,1024]{1,0:T(8,128)(2,1)S(1)} copy-done((bf16[2048,1024]{1,0:T(8,128)(2,1)S(1)}, bf16[2048,1024]{1,0:T(8,128)(2,1)}, u32[]{:S(2)}) %copy-start.3) | copy-done | bytes 4194328
  47.9 2.2 %copy-done.11 = bf16[1024,2048]{1,0:T(8,128)(2,1)S(1)} copy-done((bf16[1024,2048]{1,0:T(8,128)(2,1)S(1)}, bf16[1024,2048]{1,0:T(8,128)(2,1)}, u32[]{:S(2)}) %copy-start.11) | copy-done | bytes 4194328
  50.1 5.0 %shard_map.107.a_ref = f32[16,64,1024]{2,1,0:T(8,128)S(1)} custom-call(bf16[1024,2048]{1,0:T(8,128)(2,1)S(1)} %copy-done.11, bf16[2048,1024]{1,0:T(8,128)(2,1)S(1)} %copy-done.3), custom_call_target="tpu_custom_call" | custom-call | flops 4294967296 | bytes 12582912 | tf_op jit(solution)/shard_map/pallas_call | solution.py:107
  55.1 4.3 %shard_map.109 = f32[1,8,128]{2,1,0:T(8,128)S(1)} custom-call(s32[1]{0:T(128)} %bitcast.2.core_ref, f32[16,64,1024]{2,1,0:T(8,128)S(1)} %shard_map.107.a_ref, f32[8,64,1024]{2,1,0:T(8,128)S(1)} %collective-permute-done.5.refs_0_, f32[8,64,1024]{2,1,0:T(8,128)} %collective-permute-done.6.refs_1_), custom_call_target="tpu_custom_call" | custom-call | flops 1048576 | bytes 1048576 | tf_op jit(solution)/shard_map/pallas_call | solution.py:162
  59.8 0.9 collective-permute-done.7
  60.7 2.0 %collective-permute-start.10 = (f32[1,8,128]{2,1,0:T(8,128)S(1)}, f32[1,8,128]{2,1,0:T(8,128)S(1)}, u32[]{:S(2)}, u32[]{:S(2)}) collective-permute-start(f32[1,8,128]{2,1,0:T(8,128)S(1)} %add.7.refs_2_), channel_id=1, source_target_pairs={{0,96},{32,0},{64,32},{96,64},{1,97},{33,1},{65,33},{97,65},{2,98}... | collective-permute-start | bytes 12296 | tf_op jit(solution)/shard_map/ppermute | solution.py:358
  62.7 1.2 collective-permute-start.9
  64.0 3.1 %collective-permute-done.9.refs_4_ = f32[1,8,128]{2,1,0:T(8,128)S(1)} collective-permute-done((f32[1,8,128]{2,1,0:T(8,128)S(1)}, f32[1,8,128]{2,1,0:T(8,128)S(1)}, u32[]{:S(2)}, u32[]{:S(2)}) %collective-permute-start.9) | collective-permute-done | bytes 4128 | tf_op jit(solution)/shard_map/ppermute | solution.py:358
  67.1 0.9 collective-permute-done.8.refs_3_
  68.0 3.2 %shard_map.110 = (f32[16,64,1024]{2,1,0:T(8,128)S(1)}, f32[8,128]{1,0:T(8,128)S(1)}) custom-call(s32[1]{0:T(128)} %bitcast.2.core_ref, f32[16,64,1024]{2,1,0:T(8,128)S(1)} %shard_map.107.a_ref, f32[8,64,1024]{2,1,0:T(8,128)S(1)} %collective-permute-done.5.refs_0_, f32[8,64,1024]{2,1,0:T(8,128)} %collective-permute-done.6.refs_1_, ...), custom_call_target="tpu_custom_call" | custom-call | flops 1048576 | bytes 1048576 | tf_op jit(solution)/shard_map/pallas_call | solution.py:195
  71.2 1.8 %convert_element_type.14 = f16[16,64,1024]{2,1,0:T(8,128)(2,1)} convert(f32[16,64,1024]{2,1,0:T(8,128)S(1)} %get-tuple-element.29) | non-fusion elementwise | flops 1048576 | bytes 6291456 | tf_op jit(solution)/shard_map/convert_element_type | solution.py:383
  73.1 8.6 %all-to-all-start = ((f16[16,64,1024]{2,1,0:T(8,128)(2,1)}), f16[16,64,1024]{2,1,0:T(8,128)(2,1)}, u32[]{:S(2)}, u32[]{:S(2)}) async-start(f16[16,64,1024]{2,1,0:T(8,128)(2,1)} %convert_element_type.14), calls=%async_computation | async-start | bytes 4194304 | tf_op jit(solution)/shard_map/all_to_all | solution.py:361
  81.8 2.1 %convert_element_type.16.v_ref.refs_0_ = f32[16,64,1024]{2,1,0:T(8,128)S(1)} convert(f16[16,64,1024]{2,1,0:T(8,128)(2,1)} %all-to-all-done.1) | non-fusion elementwise | flops 1048576 | bytes 6291456 | tf_op jit(solution)/shard_map/convert_element_type | solution.py:385
  83.9 3.6 %shard_map.111.refs_0_ = f32[2,128]{1,0:T(2,128)S(1)} custom-call(s32[2]{0:T(128)S(1)} %pad_add_fusion.place_ref, f32[16,64,1024]{2,1,0:T(8,128)S(1)} %convert_element_type.16.v_ref.refs_0_, f32[8,128]{1,0:T(8,128)S(1)} %get-tuple-element.31.norm_ref), custom_call_target="tpu_custom_call" | custom-call | flops 20971520 | bytes 4194304 | tf_op jit(solution)/shard_map/pallas_call | solution.py:249
  87.5 1.9 %copy-done = f32[16,64,1024]{2,1,0:T(8,128)} copy-done((f32[16,64,1024]{2,1,0:T(8,128)}, f32[16,64,1024]{2,1,0:T(8,128)S(1)}, u32[]{:S(2)}) %copy-start) | copy-done | bytes 4194328
  89.5 15.9 %all-to-all-done = f16[16,64,1024]{2,1,0:T(8,128)(2,1)} async-done(((f16[16,64,1024]{2,1,0:T(8,128)(2,1)}), f16[16,64,1024]{2,1,0:T(8,128)(2,1)}, u32[]{:S(2)}, u32[]{:S(2)}) %all-to-all-start) | async-done | bytes 2097184 | tf_op jit(solution)/shard_map/all_to_all | solution.py:361
  105.4 2.2 %convert_element_type.15.v_ref.refs_3_ = f32[16,64,1024]{2,1,0:T(8,128)S(1)} convert(f16[16,64,1024]{2,1,0:T(8,128)(2,1)} %all-to-all-done) | non-fusion elementwise | flops 1048576 | bytes 6291456 | tf_op jit(solution)/shard_map/convert_element_type | solution.py:387
  107.7 3.7 %shard_map.112 = f32[128,4,128]{2,1,0:T(4,128)S(1)} custom-call(s32[2]{0:T(128)S(1)} %pad_add_fusion.place_ref, f32[16,64,1024]{2,1,0:T(8,128)S(1)} %convert_element_type.15.v_ref.refs_3_, f32[8,128]{1,0:T(8,128)S(1)} %get-tuple-element.30.norm_ref, f32[2,128]{1,0:T(2,128)S(1)} %shard_map.111.refs_0_), custom_call_target="tpu_custom_call" | custom-call | flops 20971520 | bytes 4194304 | tf_op jit(solution)/shard_map/pallas_call | solution.py:249
  111.3 21.3 %all_to_all.15.totals_ref = f32[128,4,128]{2,1,0:T(4,128)S(1)} all-to-all(f32[128,4,128]{2,1,0:T(4,128)S(1)} %shard_map.112), channel_id=1, replica_groups=mesh['shard'=4,'rep'=32] {'shard','rep'}, dimensions={0} | all-to-all | bytes 524288 | tf_op jit(solution)/shard_map/all_to_all | solution.py:389
  132.7 3.3 %shard_map.113 = (f32[64,1024]{1,0:T(8,128)}, f32[64,1024]{1,0:T(8,128)}, f32[64,1024]{1,0:T(8,128)}, f32[64,1024]{1,0:T(8,128)}) custom-call(f32[128,4,128]{2,1,0:T(4,128)S(1)} %all_to_all.15.totals_ref, f32[16,64,1024]{2,1,0:T(8,128)S(1)} %copy-done.1, f32[64,1024]{1,0:T(8,128)S(1)} %copy-done.4, f32[64,1024]{1,0:T(8,128)S(1)} %copy-done.5, ...), custom_call_target="tpu_custom_call" | custom-call | flops 8388608 | bytes 10485760 | tf_op jit(solution)/shard_map/pallas_call | solution.py:323
  (38 shorter events, 2.8 us)
Async XLA Ops:
  0.6 2.2 %copy-start.8 = (bf16[2048,1024]{1,0:T(8,128)(2,1)S(1)}, bf16[2048,1024]{1,0:T(8,128)(2,1)}, u32[]{:S(2)}) copy-start(bf16[2048,1024]{1,0:T(8,128)(2,1)} %y_ref.4) | copy-start | bytes 12582916
  2.8 9.3 %copy-start.9 = (bf16[2048,1024]{1,0:T(8,128)(2,1)S(1)}, bf16[2048,1024]{1,0:T(8,128)(2,1)}, u32[]{:S(2)}) copy-start(bf16[2048,1024]{1,0:T(8,128)(2,1)} %y_ref.4) | copy-start | bytes 12582916
  10.6 6.6 %copy-start.10 = (bf16[1024,2048]{1,0:T(8,128)(2,1)}, bf16[1024,2048]{1,0:T(8,128)(2,1)S(1)}, u32[]{:S(2)}) copy-start(bf16[1024,2048]{1,0:T(8,128)(2,1)S(1)} %get-tuple-element.26.x_ref) | copy-start | bytes 12582916
  10.6 10.5 %collective-permute-start = (f32[16,64,1024]{2,1,0:T(8,128)S(1)}, f32[16,64,1024]{2,1,0:T(8,128)S(1)}, u32[]{:S(2)}, u32[]{:S(2)}) collective-permute-start(f32[16,64,1024]{2,1,0:T(8,128)S(1)} %get-tuple-element.21), channel_id=1, source_target_pairs={{0,1},{1,0},{2,3},{3,2},{4,5},{5,4},{6,7},{7,6},{8,9},{9,8},{10,11... | collective-permute-start | bytes 12582920 | tf_op jit(solution)/shard_map/ppermute | solution.py:364
  12.1 5.1 %copy-start.2 = (bf16[2048,1024]{1,0:T(8,128)(2,1)S(1)}, bf16[2048,1024]{1,0:T(8,128)(2,1)}, u32[]{:S(2)}) copy-start(bf16[2048,1024]{1,0:T(8,128)(2,1)} %y_ref.7) | copy-start | bytes 12582916
  22.9 1.2 collective-permute-start.1
  23.0 32.1 %collective-permute-start.5 = (f32[8,64,1024]{2,1,0:T(8,128)}, f32[8,64,1024]{2,1,0:T(8,128)S(1)}, u32[]{:S(2)}, u32[]{:S(2)}) collective-permute-start(f32[8,64,1024]{2,1,0:T(8,128)} %shard_map.104), channel_id=1, source_target_pairs={{0,1},{1,0},{2,3},{3,2},{4,5},{5,4},{6,7},{7,6},{8,9},{9,8},{10,11... | collective-permute-start | bytes 6291464 | tf_op jit(solution)/shard_map/ppermute | solution.py:377
  24.1 7.6 %collective-permute-start.4 = (f32[1,8,128]{2,1,0:T(8,128)S(1)}, f32[1,8,128]{2,1,0:T(8,128)S(1)}, u32[]{:S(2)}, u32[]{:S(2)}) collective-permute-start(f32[1,8,128]{2,1,0:T(8,128)S(1)} %add.6.refs_1_), channel_id=1, source_target_pairs={{0,96},{32,0},{64,32},{96,64},{1,97},{33,1},{65,33},{97,65},{2,98}... | collective-permute-start | bytes 12296 | tf_op jit(solution)/shard_map/ppermute | solution.py:358
  26.7 5.0 %collective-permute-start.3 = (f32[1,8,128]{2,1,0:T(8,128)S(1)}, f32[1,8,128]{2,1,0:T(8,128)S(1)}, u32[]{:S(2)}, u32[]{:S(2)}) collective-permute-start(f32[1,8,128]{2,1,0:T(8,128)S(1)} %add.6.refs_1_), channel_id=1, source_target_pairs={{0,64},{32,96},{64,0},{96,32},{1,65},{33,97},{65,1},{97,33},{2,66}... | collective-permute-start | bytes 12296 | tf_op jit(solution)/shard_map/ppermute | solution.py:358
  27.2 4.5 %collective-permute-start.2 = (f32[1,8,128]{2,1,0:T(8,128)S(1)}, f32[1,8,128]{2,1,0:T(8,128)S(1)}, u32[]{:S(2)}, u32[]{:S(2)}) collective-permute-start(f32[1,8,128]{2,1,0:T(8,128)S(1)} %add.6.refs_1_), channel_id=1, source_target_pairs={{0,32},{32,64},{64,96},{96,0},{1,33},{33,65},{65,97},{97,1},{2,34}... | collective-permute-start | bytes 12296 | tf_op jit(solution)/shard_map/ppermute | solution.py:358
  34.2 20.9 %collective-permute-start.6 = (f32[8,64,1024]{2,1,0:T(8,128)}, f32[8,64,1024]{2,1,0:T(8,128)}, u32[]{:S(2)}, u32[]{:S(2)}) collective-permute-start(f32[8,64,1024]{2,1,0:T(8,128)} %shard_map.108), channel_id=1, source_target_pairs={{0,1},{1,0},{2,3},{3,2},{4,5},{5,4},{6,7},{7,6},{8,9},{9,8},{10,11... | collective-permute-start | bytes 6291464 | tf_op jit(solution)/shard_map/ppermute | solution.py:378
  35.2 37.8 %all-to-all-start.1 = ((f16[16,64,1024]{2,1,0:T(8,128)(2,1)}), f16[16,64,1024]{2,1,0:T(8,128)(2,1)}, u32[]{:S(2)}, u32[]{:S(2)}) async-start(f16[16,64,1024]{2,1,0:T(8,128)(2,1)} %convert_element_type.13), calls=%async_computation.1 | async-start | bytes 4194304 | tf_op jit(solution)/shard_map/all_to_all | solution.py:361
  45.7 2.2 %copy-start.3 = (bf16[2048,1024]{1,0:T(8,128)(2,1)S(1)}, bf16[2048,1024]{1,0:T(8,128)(2,1)}, u32[]{:S(2)}) copy-start(bf16[2048,1024]{1,0:T(8,128)(2,1)} %y_ref.7) | copy-start | bytes 12582916
  47.9 2.2 %copy-start.11 = (bf16[1024,2048]{1,0:T(8,128)(2,1)S(1)}, bf16[1024,2048]{1,0:T(8,128)(2,1)}, u32[]{:S(2)}) copy-start(bf16[1024,2048]{1,0:T(8,128)(2,1)} %copy-done.10) | copy-start | bytes 12582916
  59.5 1.2 collective-permute-start.7
  60.7 3.3 %collective-permute-start.10 = (f32[1,8,128]{2,1,0:T(8,128)S(1)}, f32[1,8,128]{2,1,0:T(8,128)S(1)}, u32[]{:S(2)}, u32[]{:S(2)}) collective-permute-start(f32[1,8,128]{2,1,0:T(8,128)S(1)} %add.7.refs_2_), channel_id=1, source_target_pairs={{0,96},{32,0},{64,32},{96,64},{1,97},{33,1},{65,33},{97,65},{2,98}... | collective-permute-start | bytes 12296 | tf_op jit(solution)/shard_map/ppermute | solution.py:358
  62.7 4.4 %collective-permute-start.9 = (f32[1,8,128]{2,1,0:T(8,128)S(1)}, f32[1,8,128]{2,1,0:T(8,128)S(1)}, u32[]{:S(2)}, u32[]{:S(2)}) collective-permute-start(f32[1,8,128]{2,1,0:T(8,128)S(1)} %add.7.refs_2_), channel_id=1, source_target_pairs={{0,64},{32,96},{64,0},{96,32},{1,65},{33,97},{65,1},{97,33},{2,66}... | collective-permute-start | bytes 12296 | tf_op jit(solution)/shard_map/ppermute | solution.py:358
  64.0 4.1 %collective-permute-start.8 = (f32[1,8,128]{2,1,0:T(8,128)S(1)}, f32[1,8,128]{2,1,0:T(8,128)S(1)}, u32[]{:S(2)}, u32[]{:S(2)}) collective-permute-start(f32[1,8,128]{2,1,0:T(8,128)S(1)} %add.7.refs_2_), channel_id=1, source_target_pairs={{0,32},{32,64},{64,96},{96,0},{1,33},{33,65},{65,97},{97,1},{2,34}... | collective-permute-start | bytes 12296 | tf_op jit(solution)/shard_map/ppermute | solution.py:358
  73.1 32.3 %all-to-all-start = ((f16[16,64,1024]{2,1,0:T(8,128)(2,1)}), f16[16,64,1024]{2,1,0:T(8,128)(2,1)}, u32[]{:S(2)}, u32[]{:S(2)}) async-start(f16[16,64,1024]{2,1,0:T(8,128)(2,1)} %convert_element_type.14), calls=%async_computation | async-start | bytes 4194304 | tf_op jit(solution)/shard_map/all_to_all | solution.py:361
  87.5 2.0 %copy-start = (f32[16,64,1024]{2,1,0:T(8,128)}, f32[16,64,1024]{2,1,0:T(8,128)S(1)}, u32[]{:S(2)}) copy-start(f32[16,64,1024]{2,1,0:T(8,128)S(1)} %convert_element_type.16.v_ref.refs_0_) | copy-start | bytes 12582916
  89.5 43.2 %copy-start.4 = (f32[64,1024]{1,0:T(8,128)S(1)}, f32[64,1024]{1,0:T(8,128)}, u32[]{:S(2)}) copy-start(f32[64,1024]{1,0:T(8,128)} %refs_1_.1) | copy-start | bytes 786436
  89.5 43.2 %copy-start.5 = (f32[64,1024]{1,0:T(8,128)S(1)}, f32[64,1024]{1,0:T(8,128)}, u32[]{:S(2)}) copy-start(f32[64,1024]{1,0:T(8,128)} %refs_2_.1) | copy-start | bytes 786436
  89.5 43.2 %copy-start.6 = (f32[64,1024]{1,0:T(8,128)S(1)}, f32[64,1024]{1,0:T(8,128)}, u32[]{:S(2)}) copy-start(f32[64,1024]{1,0:T(8,128)} %refs_4_.1) | copy-start | bytes 786436
  89.5 43.2 %copy-start.7 = (f32[64,1024]{1,0:T(8,128)S(1)}, f32[64,1024]{1,0:T(8,128)}, u32[]{:S(2)}) copy-start(f32[64,1024]{1,0:T(8,128)} %refs_5_.1) | copy-start | bytes 786436
  105.4 27.3 %copy-start.1 = (f32[16,64,1024]{2,1,0:T(8,128)S(1)}, f32[16,64,1024]{2,1,0:T(8,128)}, u32[]{:S(2)}) copy-start(f32[16,64,1024]{2,1,0:T(8,128)} %copy-done) | copy-start | bytes 12582916

commit v7 on v6

--- a/solution.py
+++ b/solution.py
@@ -132,17 +132,15 @@
     return block
 
 
-def pair_kernel(core_ref, a_ref, *refs, steps):
-    b_refs, (o_ref, acc_ref) = refs[:-2], refs[-2:]
+def add_sums(is_first, a, b, acc_ref, o_ref):
     step = pl.program_id(0)
 
     @pl.when(step == 0)
     def _():
         acc_ref[...] = jnp.zeros_like(acc_ref)
 
-    a = a_ref[...].reshape(-1, 8, FEATURES)
-    b = block_of(b_refs, steps).reshape(-1, 8, FEATURES)
-    is_first = core_ref[0] == 0
+    a = a.reshape(-1, 8, FEATURES)
+    b = b.reshape(-1, 8, FEATURES)
     own, other = jnp.sum(a * a, axis=0), jnp.sum(b * b, axis=0)
     acc_ref[0] += jnp.sum(a * b, axis=0)
     acc_ref[1] += jnp.where(is_first, own, other)
@@ -153,22 +151,56 @@
         rows = [jnp.sum(acc_ref[k], axis=0, keepdims=True) for k in range(3)]
         rows = [jnp.sum(row, axis=1, keepdims=True) for row in rows]
         rows = [jnp.broadcast_to(row, (1, 128)) for row in rows]
-        tile = jnp.concatenate(rows + [jnp.zeros((5, 128), jnp.float32)], axis=0)
-        o_ref[...] = jnp.broadcast_to(tile[None], o_ref.shape)
-
-
-def pair_sums(core, a, b, copies):
+        o_ref[0] = jnp.concatenate(rows + [jnp.zeros((5, 128), jnp.float32)], axis=0)
+
+
+def pair_kernel(core_ref, a_ref, *refs, steps):
+    b_refs, (o_ref, acc_ref) = refs[:-2], refs[-2:]
+    add_sums(core_ref[0] == 0, a_ref[...], block_of(b_refs, steps), acc_ref, o_ref)
+
+
+SUMS = jax.ShapeDtypeStruct((1, 8, 128), jnp.float32)
+SUMS_SPEC = pl.BlockSpec((1, 8, 128), lambda i: (0, 0, 0))
+
+
+def pair_sums(core, a, b):
     spec = pl.BlockSpec((4, ROWS, FEATURES), lambda i: (i, 0, 0))
     return pl.pallas_call(
         functools.partial(pair_kernel, steps=b[0].shape[0] // 4),
-        out_shape=jax.ShapeDtypeStruct((copies, 8, 128), jnp.float32),
+        out_shape=SUMS,
         grid=(CHIPS // 4,),
         in_specs=[SMEM, spec] + parts_specs(b),
-        out_specs=pl.BlockSpec((copies, 8, 128), lambda i: (0, 0, 0)),
+        out_specs=SUMS_SPEC,
         scratch_shapes=[pltpu.VMEM((3, 8, FEATURES), jnp.float32)],
         compiler_params=params(10),
         cost_estimate=cost(a.size, a.size),
     )(core, a, *b)
+
+
+def grad_pair_kernel(core_ref, x_ref, y_ref, *refs, steps):
+    b_refs, (grad_ref, o_ref, acc_ref) = refs[:-3], refs[-3:]
+    grad_ref[...] = scaled_dot(x_ref[...], y_ref[...])
+    add_sums(core_ref[0] == 0, grad_ref[...], block_of(b_refs, steps), acc_ref, o_ref)
+
+
+def grad_and_pair_sums(core, rows, cotangent, b):
+    count, depth = rows.shape
+    step = 4 * ROWS
+    return pl.pallas_call(
+        functools.partial(grad_pair_kernel, steps=b[0].shape[0] // 4),
+        out_shape=(jax.ShapeDtypeStruct((CHIPS, ROWS, FEATURES), jnp.float32), SUMS),
+        grid=(count // step,),
+        in_specs=[
+            SMEM,
+            pl.BlockSpec((step, depth), lambda i: (i, 0)),
+            pl.BlockSpec((depth, FEATURES), lambda i: (0, 0)),
+        ]
+        + parts_specs(b),
+        out_specs=(pl.BlockSpec((4, ROWS, FEATURES), lambda i: (i, 0, 0)), SUMS_SPEC),
+        scratch_shapes=[pltpu.VMEM((3, 8, FEATURES), jnp.float32)],
+        compiler_params=params(56),
+        cost_estimate=cost(2 * depth * count * FEATURES, 16 * MIB),
+    )(core, rows, cotangent, *b)
 
 
 def merge_kernel(core_ref, a_ref, *refs, parts, steps):
@@ -190,7 +222,7 @@
     o_ref[...] = own * a_ref[...] + other * block_of(b_refs, steps)
 
 
-def merge_pair(core, a, b, sums):
+def merge_pair(core, a, b, sums, mib):
     spec = pl.BlockSpec((4, ROWS, FEATURES), lambda i: (i, 0, 0))
     return pl.pallas_call(
         functools.partial(merge_kernel, parts=len(b), steps=b[0].shape[0] // 4),
@@ -201,7 +233,7 @@
         grid=(CHIPS // 4,),
         in_specs=[SMEM, spec] + parts_specs(b) + [VMEM] * len(sums),
         out_specs=(spec, pl.BlockSpec((8, 128), lambda i: (0, 0))),
-        compiler_params=params(12),
+        compiler_params=params(mib),
         cost_estimate=cost(a.size, a.size),
     )(core, a, *b, *sums)
 
@@ -365,11 +397,11 @@
     key_own = grad(own_rows, key_cotangent)
     half = other_rows.shape[0] // 2
     value_first = grad(after(other_rows, key_own), value_cotangent, 0, half, [key_own])
-    key_sums = summed(pair_sums(after(core, value_first), key_own, key_arrived, 1))
+    key_sums = summed(pair_sums(after(core, value_first), key_own, key_arrived))
     value_second = grad(
         after(other_rows, key_sums[0]), value_cotangent, half, half, [key_own] + key_arrived
     )
-    key_merged, key_norm = merge_pair(core, key_own, key_arrived, key_sums)
+    key_merged, key_norm = merge_pair(core, key_own, key_arrived, key_sums, 12)
     key_sent = key_merged.astype(jnp.float16)
     key_all = gathered(key_sent)
 
@@ -377,9 +409,11 @@
         lax.ppermute(value_first, "rep", swap),
         lax.ppermute(after(value_second, key_sent), "rep", swap),
     ]
-    value_own = grad(after(own_rows, key_sent), value_cotangent)
-    value_sums = summed(pair_sums(core, value_own, value_arrived, 1))
-    value_merged, value_norm = merge_pair(core, value_own, value_arrived, value_sums)
+    value_own, value_sums = grad_and_pair_sums(
+        core, after(own_rows, key_sent), value_cotangent, value_arrived
+    )
+    value_sums = summed(value_sums)
+    value_merged, value_norm = merge_pair(core, value_own, value_arrived, value_sums, 50)
     value_all = gathered(value_merged.astype(jnp.float16))
 
     key_v = key_all.astype(jnp.float32)

time: 137 us -> 133 us (0.971)
  local copies, waits for them, and re-layouts: 8.53 us -> 4.16 us
  Pallas kernels: 46.2 us -> 49.7 us
  starting transfers between devices: 29.5 us -> 27.4 us
  blocking collectives: 21.3 us -> 19.8 us
    pallas_call x0 -> x1, Pallas kernels: none -> 11.6 us  [grad_and_pair_sums(): pl.pallas_call(functools.partial(grad_pair_kernel, steps=b[0].shape[0] //...]
    pallas_call x4 -> x3, Pallas kernels: 17.8 us -> 11.4 us  [grad(): pl.pallas_call(functools.partial(grad_kernel, start=start), out_shape=jax...]
    pallas_call x2 -> x1, Pallas kernels: 6.14 us -> 1.74 us  [pair_sums(): pl.pallas_call(functools.partial(pair_kernel, steps=b[0].shape[0] // 4),...]
    unnamed x24 -> x20, local copies, waits for them, and re-layouts: 8.53 us -> 4.16 us
    pallas_call x2, Pallas kernels: 3.85 us -> 6.51 us  [merge_pair(): pl.pallas_call(functools.partial(merge_kernel, parts=len(b), steps=b[0].s...]
    convert_element_type x1, other arithmetic: 1.81 us -> 3.97 us  [shards(): value_all = gathered(value_merged.astype(jnp.float16))]
    all_to_all x2, starting transfers between devices: 19.1 us -> 17.1 us  [gathered(): return lax.all_to_all(sent, 'rep', 0, 0, axis_index_groups=core_groups)]
    convert_element_type x1, other arithmetic: 2.25 us -> 0.49 us  [shards(): value_v = value_all.astype(jnp.float32)]
  transfers between devices with their start and end apart: 13 -> 13, of which waited for: 5 -> 5; matrix products, arithmetic and copies ran while one was open for 4% -> 6% of each run, Pallas kernels for 22% -> 25%
where the time goes in v7:
time: 133 us
  Pallas kernels  49.7 us (37%)
  starting transfers between devices  27.4 us (21%)
  waiting for transfers between devices  21.7 us (16%)
  blocking collectives  19.8 us (15%)
  other arithmetic  9.12 us (7%)
  local copies, waits for them, and re-layouts  4.16 us (3%)
    all_to_all x1, blocking collectives, shards(): totals = lax.all_to_all(vectors, ('shard', 'rep'), 0, 0)  19.8 us
    all_to_all x2, starting transfers between devices, gathered(): return lax.all_to_all(sent, 'rep', 0, 0, axis_index_groups=core_groups)  17.1 us
    all_to_all x2, waiting for transfers between devices, gathered(): return lax.all_to_all(sent, 'rep', 0, 0, axis_index_groups=core_groups)  15.8 us
    pallas_call x1, Pallas kernels, grad_and_pair_sums(): pl.pallas_call(functools.partial(grad_pair_kernel, steps=b[0].shape[0] //...  11.6 us
    pallas_call x3, Pallas kernels, grad(): pl.pallas_call(functools.partial(grad_kernel, start=start), out_shape=jax...  11.4 us
    pallas_call x1, Pallas kernels, split_and_grad(): pl.pallas_call(split_kernel, out_shape=(jax.ShapeDtypeStruct((CHIPS, ROWS...  7.79 us
    pallas_call x2, Pallas kernels, gram(): pl.pallas_call(gram_kernel, out_shape=jax.ShapeDtypeStruct(out_dims, jnp....  7.31 us
    ppermute x6, starting transfers between devices, summed(): return [sums] + [lax.ppermute(sums, 'shard', shift) for shift in shifts]  6.99 us
  transfers between devices with their start and end apart: 13, of which 5 were waited for; matrix products, arithmetic and copies ran while one was open for 6% of the time, Pallas kernels for 25%

profile of v7, /device:TPU:1, one launch (start us, length us, event | category | flops | bytes accessed | tf_op | source)
XLA Modules:
  0.0 132.8 jit_solution(8682963068291868896)
XLA Ops:
  0.6 2.2 %copy-done.7 = bf16[2048,1024]{1,0:T(8,128)(2,1)S(1)} copy-done((bf16[2048,1024]{1,0:T(8,128)(2,1)S(1)}, bf16[2048,1024]{1,0:T(8,128)(2,1)}, u32[]{:S(2)}) %copy-start.7) | copy-done | bytes 4194328
  2.8 7.8 %shard_map.102 = (f32[16,64,1024]{2,1,0:T(8,128)S(1)}, bf16[1024,2048]{1,0:T(8,128)(2,1)S(1)}, bf16[1024,2048]{1,0:T(8,128)(2,1)S(1)}) custom-call(s32[1]{0:T(128)} %bitcast.2.core_ref, bf16[2048,2048]{1,0:T(8,128)(2,1)} %x_hbm.1, bf16[2048,1024]{1,0:T(8,128)(2,1)S(1)} %copy-done.7), custom_call_target="tpu_custom_call" | custom-call | flops 4294967296 | bytes 25165824 | tf_op jit(solution)/shard_map/pallas_call | solution.py:74
  10.6 1.5 %collective-permute-start = (f32[16,64,1024]{2,1,0:T(8,128)S(1)}, f32[16,64,1024]{2,1,0:T(8,128)S(1)}, u32[]{:S(2)}, u32[]{:S(2)}) collective-permute-start(f32[16,64,1024]{2,1,0:T(8,128)S(1)} %get-tuple-element.23), channel_id=1, source_target_pairs={{0,1},{1,0},{2,3},{3,2},{4,5},{5,4},{6,7},{7,6},{8,9},{9,8},{10,11... | collective-permute-start | bytes 12582920 | tf_op jit(solution)/shard_map/ppermute | solution.py:396
  12.1 5.0 %shard_map.103.refs_0_.a_ref = f32[16,64,1024]{2,1,0:T(8,128)S(1)} custom-call(bf16[1024,2048]{1,0:T(8,128)(2,1)S(1)} %get-tuple-element.28.x_ref, bf16[2048,1024]{1,0:T(8,128)(2,1)S(1)} %copy-done.8), custom_call_target="tpu_custom_call" | custom-call | flops 4294967296 | bytes 12582912 | tf_op jit(solution)/shard_map/pallas_call | solution.py:107
  17.2 2.5 %shard_map.104 = f32[8,64,1024]{2,1,0:T(8,128)S(1)} custom-call(bf16[1024,2048]{1,0:T(8,128)(2,1)S(1)} %get-tuple-element.29.x_ref, bf16[2048,1024]{1,0:T(8,128)(2,1)S(1)} %copy-done.2, f32[16,64,1024]{2,1,0:T(8,128)S(1)} %shard_map.103.refs_0_.a_ref), custom_call_target="tpu_custom_call" | custom-call | flops 2147483648 | bytes 12582912 | tf_op jit(solution)/shard_map/pallas_call | solution.py:107
  19.7 1.7 %shard_map.105 = f32[1,8,128]{2,1,0:T(8,128)S(1)} custom-call(s32[1]{0:T(128)} %bitcast.2.core_ref, f32[16,64,1024]{2,1,0:T(8,128)S(1)} %shard_map.103.refs_0_.a_ref, f32[16,64,1024]{2,1,0:T(8,128)S(1)} %collective-permute-done.refs_0_.refs_1_), custom_call_target="tpu_custom_call" | custom-call | flops 1048576 | bytes 1048576 | tf_op jit(solution)/shard_map/pallas_call | solution.py:168
  22.0 0.7 collective-permute-done.1
  22.7 2.6 %collective-permute-start.4 = (f32[1,8,128]{2,1,0:T(8,128)S(1)}, f32[1,8,128]{2,1,0:T(8,128)S(1)}, u32[]{:S(2)}, u32[]{:S(2)}) collective-permute-start(f32[1,8,128]{2,1,0:T(8,128)S(1)} %add.6.refs_1_), channel_id=1, source_target_pairs={{0,96},{32,0},{64,32},{96,64},{1,97},{33,1},{65,33},{97,65},{2,98}... | collective-permute-start | bytes 12296 | tf_op jit(solution)/shard_map/ppermute | solution.py:390
  25.2 0.5 collective-permute-start.3
  25.8 0.6 collective-permute-start.2
  26.4 3.9 %shard_map.107 = f32[8,64,1024]{2,1,0:T(8,128)} custom-call(bf16[1024,2048]{1,0:T(8,128)(2,1)S(1)} %get-tuple-element.29.x_ref, bf16[2048,1024]{1,0:T(8,128)(2,1)S(1)} %copy-done.2, f32[16,64,1024]{2,1,0:T(8,128)S(1)} %shard_map.103.refs_0_.a_ref, f32[16,64,1024]{2,1,0:T(8,128)S(1)} %collective-permute-done.refs_0_.refs_1_), custom_call_target="tpu_custom_call" | custom-call | flops 2147483648 | bytes 12582912 | tf_op jit(solution)/shard_map/pallas_call | solution.py:107
  30.3 0.6 shard_map.106
  30.9 1.8 %convert_element_type.13 = f16[16,64,1024]{2,1,0:T(8,128)(2,1)} convert(f32[16,64,1024]{2,1,0:T(8,128)S(1)} %get-tuple-element.27) | non-fusion elementwise | flops 1048576 | bytes 6291456 | tf_op jit(solution)/shard_map/convert_element_type | solution.py:405
  32.7 1.0 collective-permute-start.6
  33.8 10.5 %all-to-all-start.1 = ((f16[16,64,1024]{2,1,0:T(8,128)(2,1)}), f16[16,64,1024]{2,1,0:T(8,128)(2,1)}, u32[]{:S(2)}, u32[]{:S(2)}) async-start(f16[16,64,1024]{2,1,0:T(8,128)(2,1)} %convert_element_type.13), calls=%async_computation.1 | async-start | bytes 4194304 | tf_op jit(solution)/shard_map/all_to_all | solution.py:393
  44.2 11.6 %shard_map.108 = (f32[16,64,1024]{2,1,0:T(8,128)}, f32[1,8,128]{2,1,0:T(8,128)}) custom-call(s32[1]{0:T(128)} %bitcast.2.core_ref, bf16[1024,2048]{1,0:T(8,128)(2,1)} %copy-done.9, bf16[2048,1024]{1,0:T(8,128)(2,1)} %y_ref.7, f32[8,64,1024]{2,1,0:T(8,128)} %collective-permute-done.5.refs_0_, f32[8,64,1024]{2,1,0:T(8,128)} %collective-permute-done.6.refs_1_), custom_call_target="tpu_custom_call" | custom-call | flops 4294967296 | bytes 16777216 | tf_op jit(solution)/shard_map/pallas_call | solution.py:189
  56.1 1.1 collective-permute-done.7
  57.2 0.7 add.7.refs_2_
  57.9 2.1 %collective-permute-start.10 = (f32[1,8,128]{2,1,0:T(8,128)S(1)}, f32[1,8,128]{2,1,0:T(8,128)S(1)}, u32[]{:S(2)}, u32[]{:S(2)}) collective-permute-start(f32[1,8,128]{2,1,0:T(8,128)S(1)} %add.7.refs_2_), channel_id=1, source_target_pairs={{0,96},{32,0},{64,32},{96,64},{1,97},{33,1},{65,33},{97,65},{2,98}... | collective-permute-start | bytes 12296 | tf_op jit(solution)/shard_map/ppermute | solution.py:390
  60.0 1.2 collective-permute-start.9
  61.2 3.1 %collective-permute-done.9.refs_4_ = f32[1,8,128]{2,1,0:T(8,128)S(1)} collective-permute-done((f32[1,8,128]{2,1,0:T(8,128)S(1)}, f32[1,8,128]{2,1,0:T(8,128)S(1)}, u32[]{:S(2)}, u32[]{:S(2)}) %collective-permute-start.9) | collective-permute-done | bytes 4128 | tf_op jit(solution)/shard_map/ppermute | solution.py:390
  64.3 0.9 collective-permute-done.8.refs_3_
  65.3 5.9 %shard_map.109 = (f32[16,64,1024]{2,1,0:T(8,128)}, f32[8,128]{1,0:T(8,128)S(1)}) custom-call(s32[1]{0:T(128)} %bitcast.2.core_ref, f32[16,64,1024]{2,1,0:T(8,128)} %get-tuple-element.31.a_ref, f32[8,64,1024]{2,1,0:T(8,128)} %collective-permute-done.5.refs_0_, f32[8,64,1024]{2,1,0:T(8,128)} %collective-permute-done.6.refs_1_, f32[1,8,128]{2,1,0:T(8,128)S(1)} %add.7.refs_2_, ...), custom_call_target="tpu_custom_call" | custom-call | flops 1048576 | bytes 1048576 | tf_op jit(solution)/shard_map/pallas_call | solution.py:227
  71.2 4.0 %convert_element_type.14 = f16[16,64,1024]{2,1,0:T(8,128)(2,1)} convert(f32[16,64,1024]{2,1,0:T(8,128)} %get-tuple-element.33) | non-fusion elementwise | flops 1048576 | bytes 6291456 | tf_op jit(solution)/shard_map/convert_element_type | solution.py:417
  75.1 6.6 %all-to-all-start = ((f16[16,64,1024]{2,1,0:T(8,128)(2,1)}), f16[16,64,1024]{2,1,0:T(8,128)(2,1)S(1)}, u32[]{:S(2)}, u32[]{:S(2)}) async-start(f16[16,64,1024]{2,1,0:T(8,128)(2,1)} %convert_element_type.14), calls=%async_computation | async-start | bytes 4194304 | tf_op jit(solution)/shard_map/all_to_all | solution.py:393
  81.8 2.1 %convert_element_type.16.v_ref.refs_0_ = f32[16,64,1024]{2,1,0:T(8,128)S(1)} convert(f16[16,64,1024]{2,1,0:T(8,128)(2,1)} %all-to-all-done.1) | non-fusion elementwise | flops 1048576 | bytes 6291456 | tf_op jit(solution)/shard_map/convert_element_type | solution.py:419
  83.9 3.6 %shard_map.110.refs_0_ = f32[2,128]{1,0:T(2,128)S(1)} custom-call(s32[2]{0:T(128)S(1)} %pad_add_fusion.place_ref, f32[16,64,1024]{2,1,0:T(8,128)S(1)} %convert_element_type.16.v_ref.refs_0_, f32[8,128]{1,0:T(8,128)S(1)} %get-tuple-element.35.norm_ref), custom_call_target="tpu_custom_call" | custom-call | flops 20971520 | bytes 4194304 | tf_op jit(solution)/shard_map/pallas_call | solution.py:281
  87.6 1.9 %copy-done = f32[16,64,1024]{2,1,0:T(8,128)} copy-done((f32[16,64,1024]{2,1,0:T(8,128)}, f32[16,64,1024]{2,1,0:T(8,128)S(1)}, u32[]{:S(2)}) %copy-start) | copy-done | bytes 4194328
  89.6 15.8 %all-to-all-done = f16[16,64,1024]{2,1,0:T(8,128)(2,1)S(1)} async-done(((f16[16,64,1024]{2,1,0:T(8,128)(2,1)}), f16[16,64,1024]{2,1,0:T(8,128)(2,1)S(1)}, u32[]{:S(2)}, u32[]{:S(2)}) %all-to-all-start) | async-done | bytes 2097184 | tf_op jit(solution)/shard_map/all_to_all | solution.py:393
  105.9 3.7 %shard_map.111 = f32[128,4,128]{2,1,0:T(4,128)S(1)} custom-call(s32[2]{0:T(128)S(1)} %pad_add_fusion.place_ref, f32[16,64,1024]{2,1,0:T(8,128)S(1)} %convert_element_type.15.v_ref.refs_3_, f32[8,128]{1,0:T(8,128)S(1)} %get-tuple-element.34.norm_ref, f32[2,128]{1,0:T(2,128)S(1)} %shard_map.110.refs_0_), custom_call_target="tpu_custom_call" | custom-call | flops 20971520 | bytes 4194304 | tf_op jit(solution)/shard_map/pallas_call | solution.py:281
  109.6 19.8 %all_to_all.15.totals_ref = f32[128,4,128]{2,1,0:T(4,128)S(1)} all-to-all(f32[128,4,128]{2,1,0:T(4,128)S(1)} %shard_map.111), channel_id=1, replica_groups=mesh['shard'=4,'rep'=32] {'shard','rep'}, dimensions={0} | all-to-all | bytes 524288 | tf_op jit(solution)/shard_map/all_to_all | solution.py:423
  129.4 3.2 %shard_map.112 = (f32[64,1024]{1,0:T(8,128)}, f32[64,1024]{1,0:T(8,128)}, f32[64,1024]{1,0:T(8,128)}, f32[64,1024]{1,0:T(8,128)}) custom-call(f32[128,4,128]{2,1,0:T(4,128)S(1)} %all_to_all.15.totals_ref, f32[16,64,1024]{2,1,0:T(8,128)S(1)} %copy-done.1, f32[64,1024]{1,0:T(8,128)S(1)} %copy-done.3, f32[64,1024]{1,0:T(8,128)S(1)} %copy-done.4, ...), custom_call_target="tpu_custom_call" | custom-call | flops 8388608 | bytes 10485760 | tf_op jit(solution)/shard_map/pallas_call | solution.py:355
  (33 shorter events, 1.5 us)
Async XLA Ops:
  0.6 2.2 %copy-start.7 = (bf16[2048,1024]{1,0:T(8,128)(2,1)S(1)}, bf16[2048,1024]{1,0:T(8,128)(2,1)}, u32[]{:S(2)}) copy-start(bf16[2048,1024]{1,0:T(8,128)(2,1)} %y_ref.4) | copy-start | bytes 12582916
  2.8 9.3 %copy-start.8 = (bf16[2048,1024]{1,0:T(8,128)(2,1)S(1)}, bf16[2048,1024]{1,0:T(8,128)(2,1)}, u32[]{:S(2)}) copy-start(bf16[2048,1024]{1,0:T(8,128)(2,1)} %y_ref.4) | copy-start | bytes 12582916
  10.6 6.6 %copy-start.9 = (bf16[1024,2048]{1,0:T(8,128)(2,1)}, bf16[1024,2048]{1,0:T(8,128)(2,1)S(1)}, u32[]{:S(2)}) copy-start(bf16[1024,2048]{1,0:T(8,128)(2,1)S(1)} %get-tuple-element.28.x_ref) | copy-start | bytes 12582916
  10.6 9.1 %collective-permute-start = (f32[16,64,1024]{2,1,0:T(8,128)S(1)}, f32[16,64,1024]{2,1,0:T(8,128)S(1)}, u32[]{:S(2)}, u32[]{:S(2)}) collective-permute-start(f32[16,64,1024]{2,1,0:T(8,128)S(1)} %get-tuple-element.23), channel_id=1, source_target_pairs={{0,1},{1,0},{2,3},{3,2},{4,5},{5,4},{6,7},{7,6},{8,9},{9,8},{10,11... | collective-permute-start | bytes 12582920 | tf_op jit(solution)/shard_map/ppermute | solution.py:396
  12.1 5.1 %copy-start.2 = (bf16[2048,1024]{1,0:T(8,128)(2,1)S(1)}, bf16[2048,1024]{1,0:T(8,128)(2,1)}, u32[]{:S(2)}) copy-start(bf16[2048,1024]{1,0:T(8,128)(2,1)} %y_ref.7) | copy-start | bytes 12582916
  21.5 1.2 collective-permute-start.1
  21.5 22.7 %collective-permute-start.5 = (f32[8,64,1024]{2,1,0:T(8,128)S(1)}, f32[8,64,1024]{2,1,0:T(8,128)}, u32[]{:S(2)}, u32[]{:S(2)}) collective-permute-start(f32[8,64,1024]{2,1,0:T(8,128)S(1)} %shard_map.104), channel_id=1, source_target_pairs={{0,1},{1,0},{2,3},{3,2},{4,5},{5,4},{6,7},{7,6},{8,9},{9,8},{10,11... | collective-permute-start | bytes 6291464 | tf_op jit(solution)/shard_map/ppermute | solution.py:409
  22.7 7.6 %collective-permute-start.4 = (f32[1,8,128]{2,1,0:T(8,128)S(1)}, f32[1,8,128]{2,1,0:T(8,128)S(1)}, u32[]{:S(2)}, u32[]{:S(2)}) collective-permute-start(f32[1,8,128]{2,1,0:T(8,128)S(1)} %add.6.refs_1_), channel_id=1, source_target_pairs={{0,96},{32,0},{64,32},{96,64},{1,97},{33,1},{65,33},{97,65},{2,98}... | collective-permute-start | bytes 12296 | tf_op jit(solution)/shard_map/ppermute | solution.py:390
  25.2 5.0 %collective-permute-start.3 = (f32[1,8,128]{2,1,0:T(8,128)S(1)}, f32[1,8,128]{2,1,0:T(8,128)S(1)}, u32[]{:S(2)}, u32[]{:S(2)}) collective-permute-start(f32[1,8,128]{2,1,0:T(8,128)S(1)} %add.6.refs_1_), channel_id=1, source_target_pairs={{0,64},{32,96},{64,0},{96,32},{1,65},{33,97},{65,1},{97,33},{2,66}... | collective-permute-start | bytes 12296 | tf_op jit(solution)/shard_map/ppermute | solution.py:390
  25.8 4.5 %collective-permute-start.2 = (f32[1,8,128]{2,1,0:T(8,128)S(1)}, f32[1,8,128]{2,1,0:T(8,128)S(1)}, u32[]{:S(2)}, u32[]{:S(2)}) collective-permute-start(f32[1,8,128]{2,1,0:T(8,128)S(1)} %add.6.refs_1_), channel_id=1, source_target_pairs={{0,32},{32,64},{64,96},{96,0},{1,33},{33,65},{65,97},{97,1},{2,34}... | collective-permute-start | bytes 12296 | tf_op jit(solution)/shard_map/ppermute | solution.py:390
  32.7 11.5 %collective-permute-start.6 = (f32[8,64,1024]{2,1,0:T(8,128)}, f32[8,64,1024]{2,1,0:T(8,128)}, u32[]{:S(2)}, u32[]{:S(2)}) collective-permute-start(f32[8,64,1024]{2,1,0:T(8,128)} %shard_map.107), channel_id=1, source_target_pairs={{0,1},{1,0},{2,3},{3,2},{4,5},{5,4},{6,7},{7,6},{8,9},{9,8},{10,11... | collective-permute-start | bytes 6291464 | tf_op jit(solution)/shard_map/ppermute | solution.py:410
  33.8 41.4 %all-to-all-start.1 = ((f16[16,64,1024]{2,1,0:T(8,128)(2,1)}), f16[16,64,1024]{2,1,0:T(8,128)(2,1)}, u32[]{:S(2)}, u32[]{:S(2)}) async-start(f16[16,64,1024]{2,1,0:T(8,128)(2,1)} %convert_element_type.13), calls=%async_computation.1 | async-start | bytes 4194304 | tf_op jit(solution)/shard_map/all_to_all | solution.py:393
  55.9 1.4 %collective-permute-start.7 = (f32[1,8,128]{2,1,0:T(8,128)}, f32[1,8,128]{2,1,0:T(8,128)S(1)}, u32[]{:S(2)}, u32[]{:S(2)}) collective-permute-start(f32[1,8,128]{2,1,0:T(8,128)} %get-tuple-element.32), channel_id=1, source_target_pairs={{0,1},{1,0},{2,3},{3,2},{4,5},{5,4},{6,7},{7,6},{8,9},{9,8},{10,11... | collective-permute-start | bytes 12296 | tf_op jit(solution)/shard_map/ppermute | solution.py:386
  57.9 3.3 %collective-permute-start.10 = (f32[1,8,128]{2,1,0:T(8,128)S(1)}, f32[1,8,128]{2,1,0:T(8,128)S(1)}, u32[]{:S(2)}, u32[]{:S(2)}) collective-permute-start(f32[1,8,128]{2,1,0:T(8,128)S(1)} %add.7.refs_2_), channel_id=1, source_target_pairs={{0,96},{32,0},{64,32},{96,64},{1,97},{33,1},{65,33},{97,65},{2,98}... | collective-permute-start | bytes 12296 | tf_op jit(solution)/shard_map/ppermute | solution.py:390
  60.0 4.4 %collective-permute-start.9 = (f32[1,8,128]{2,1,0:T(8,128)S(1)}, f32[1,8,128]{2,1,0:T(8,128)S(1)}, u32[]{:S(2)}, u32[]{:S(2)}) collective-permute-start(f32[1,8,128]{2,1,0:T(8,128)S(1)} %add.7.refs_2_), channel_id=1, source_target_pairs={{0,64},{32,96},{64,0},{96,32},{1,65},{33,97},{65,1},{97,33},{2,66}... | collective-permute-start | bytes 12296 | tf_op jit(solution)/shard_map/ppermute | solution.py:390
  61.2 4.1 %collective-permute-start.8 = (f32[1,8,128]{2,1,0:T(8,128)S(1)}, f32[1,8,128]{2,1,0:T(8,128)S(1)}, u32[]{:S(2)}, u32[]{:S(2)}) collective-permute-start(f32[1,8,128]{2,1,0:T(8,128)S(1)} %add.7.refs_2_), channel_id=1, source_target_pairs={{0,32},{32,64},{64,96},{96,0},{1,33},{33,65},{65,97},{97,1},{2,34}... | collective-permute-start | bytes 12296 | tf_op jit(solution)/shard_map/ppermute | solution.py:390
  75.1 30.2 %all-to-all-start = ((f16[16,64,1024]{2,1,0:T(8,128)(2,1)}), f16[16,64,1024]{2,1,0:T(8,128)(2,1)S(1)}, u32[]{:S(2)}, u32[]{:S(2)}) async-start(f16[16,64,1024]{2,1,0:T(8,128)(2,1)} %convert_element_type.14), calls=%async_computation | async-start | bytes 4194304 | tf_op jit(solution)/shard_map/all_to_all | solution.py:393
  87.6 2.0 %copy-start = (f32[16,64,1024]{2,1,0:T(8,128)}, f32[16,64,1024]{2,1,0:T(8,128)S(1)}, u32[]{:S(2)}) copy-start(f32[16,64,1024]{2,1,0:T(8,128)S(1)} %convert_element_type.16.v_ref.refs_0_) | copy-start | bytes 12582916
  89.5 39.8 %copy-start.3 = (f32[64,1024]{1,0:T(8,128)S(1)}, f32[64,1024]{1,0:T(8,128)}, u32[]{:S(2)}) copy-start(f32[64,1024]{1,0:T(8,128)} %refs_1_.1) | copy-start | bytes 786436
  89.5 39.8 %copy-start.4 = (f32[64,1024]{1,0:T(8,128)S(1)}, f32[64,1024]{1,0:T(8,128)}, u32[]{:S(2)}) copy-start(f32[64,1024]{1,0:T(8,128)} %refs_2_.1) | copy-start | bytes 786436
  89.5 39.8 %copy-start.5 = (f32[64,1024]{1,0:T(8,128)S(1)}, f32[64,1024]{1,0:T(8,128)}, u32[]{:S(2)}) copy-start(f32[64,1024]{1,0:T(8,128)} %refs_4_.1) | copy-start | bytes 786436
  89.5 39.8 %copy-start.6 = (f32[64,1024]{1,0:T(8,128)S(1)}, f32[64,1024]{1,0:T(8,128)}, u32[]{:S(2)}) copy-start(f32[64,1024]{1,0:T(8,128)} %refs_5_.1) | copy-start | bytes 786436
  105.4 24.0 %copy-start.1 = (f32[16,64,1024]{2,1,0:T(8,128)S(1)}, f32[16,64,1024]{2,1,0:T(8,128)}, u32[]{:S(2)}) copy-start(f32[16,64,1024]{2,1,0:T(8,128)} %copy-done) | copy-start | bytes 12582916

commit v8 on v7

--- a/solution.py
+++ b/solution.py
@@ -198,7 +198,7 @@
         + parts_specs(b),
         out_specs=(pl.BlockSpec((4, ROWS, FEATURES), lambda i: (i, 0, 0)), SUMS_SPEC),
         scratch_shapes=[pltpu.VMEM((3, 8, FEATURES), jnp.float32)],
-        compiler_params=params(56),
+        compiler_params=params(24),
         cost_estimate=cost(2 * depth * count * FEATURES, 16 * MIB),
     )(core, rows, cotangent, *b)
 
@@ -413,7 +413,7 @@
         core, after(own_rows, key_sent), value_cotangent, value_arrived
     )
     value_sums = summed(value_sums)
-    value_merged, value_norm = merge_pair(core, value_own, value_arrived, value_sums, 50)
+    value_merged, value_norm = merge_pair(core, value_own, value_arrived, value_sums, 12)
     value_all = gathered(value_merged.astype(jnp.float16))
 
     key_v = key_all.astype(jnp.float32)

time: 133 us -> 133 us (level)
  Pallas kernels: 49.7 us -> 44.1 us
  local copies, waits for them, and re-layouts: 4.16 us -> 8.54 us
  other arithmetic: 9.12 us -> 6.27 us
  starting transfers between devices: 27.4 us -> 29.7 us
  blocking collectives: 19.8 us -> 21.3 us
    unnamed x20 -> x24, local copies, waits for them, and re-layouts: 4.16 us -> 8.54 us
    pallas_call x1, Pallas kernels: 11.6 us -> 8.33 us  [grad_and_pair_sums(): pl.pallas_call(functools.partial(grad_pair_kernel, steps=b[0].shape[0] //...]
    pallas_call x2, Pallas kernels: 6.51 us -> 4.27 us  [merge_pair(): pl.pallas_call(functools.partial(merge_kernel, parts=len(b), steps=b[0].s...]
    all_to_all x2, starting transfers between devices: 17.1 us -> 19.3 us  [gathered(): return lax.all_to_all(sent, 'rep', 0, 0, axis_index_groups=core_groups)]
    convert_element_type x1, other arithmetic: 3.97 us -> 1.8 us  [shards(): value_all = gathered(value_merged.astype(jnp.float16))]
    all_to_all x1, blocking collectives: 19.8 us -> 21.3 us  [shards(): totals = lax.all_to_all(vectors, ('shard', 'rep'), 0, 0)]
  transfers between devices with their start and end apart: 13 -> 13, of which waited for: 5 -> 6; matrix products, arithmetic and copies ran while one was open for 6% -> 4% of each run, Pallas kernels for 25% -> 21%
where the time goes in v8:
time: 133 us
  Pallas kernels  44.1 us (33%)
  starting transfers between devices  29.7 us (22%)
  waiting for transfers between devices  21.9 us (16%)
  blocking collectives  21.3 us (16%)
  local copies, waits for them, and re-layouts  8.54 us (6%)
  other arithmetic  6.27 us (5%)
    all_to_all x1, blocking collectives, shards(): totals = lax.all_to_all(vectors, ('shard', 'rep'), 0, 0)  21.3 us
    all_to_all x2, starting transfers between devices, gathered(): return lax.all_to_all(sent, 'rep', 0, 0, axis_index_groups=core_groups)  19.3 us
    all_to_all x2, waiting for transfers between devices, gathered(): return lax.all_to_all(sent, 'rep', 0, 0, axis_index_groups=core_groups)  16.3 us
    pallas_call x3, Pallas kernels, grad(): pl.pallas_call(functools.partial(grad_kernel, start=start), out_shape=jax...  11.4 us
    unnamed x24, local copies, waits for them, and re-layouts  8.54 us
    pallas_call x1, Pallas kernels, grad_and_pair_sums(): pl.pallas_call(functools.partial(grad_pair_kernel, steps=b[0].shape[0] //...  8.33 us
    pallas_call x1, Pallas kernels, split_and_grad(): pl.pallas_call(split_kernel, out_shape=(jax.ShapeDtypeStruct((CHIPS, ROWS...  7.79 us
    pallas_call x2, Pallas kernels, gram(): pl.pallas_call(gram_kernel, out_shape=jax.ShapeDtypeStruct(out_dims, jnp....  7.31 us
  transfers between devices with their start and end apart: 13, of which 6 were waited for; matrix products, arithmetic and copies ran while one was open for 4% of the time, Pallas kernels for 21%

profile of v8, /device:TPU:1, one launch (start us, length us, event | category | flops | bytes accessed | tf_op | source)
XLA Modules:
  0.0 132.7 jit_solution(13999225384878821358)
XLA Ops:
  0.6 2.2 %copy-done.8 = bf16[2048,1024]{1,0:T(8,128)(2,1)S(1)} copy-done((bf16[2048,1024]{1,0:T(8,128)(2,1)S(1)}, bf16[2048,1024]{1,0:T(8,128)(2,1)}, u32[]{:S(2)}) %copy-start.8) | copy-done | bytes 4194328
  2.8 7.8 %shard_map.102 = (f32[16,64,1024]{2,1,0:T(8,128)S(1)}, bf16[1024,2048]{1,0:T(8,128)(2,1)S(1)}, bf16[1024,2048]{1,0:T(8,128)(2,1)S(1)}) custom-call(s32[1]{0:T(128)} %bitcast.2.core_ref, bf16[2048,2048]{1,0:T(8,128)(2,1)} %x_hbm.1, bf16[2048,1024]{1,0:T(8,128)(2,1)S(1)} %copy-done.8), custom_call_target="tpu_custom_call" | custom-call | flops 4294967296 | bytes 25165824 | tf_op jit(solution)/shard_map/pallas_call | solution.py:74
  10.6 1.5 %collective-permute-start = (f32[16,64,1024]{2,1,0:T(8,128)S(1)}, f32[16,64,1024]{2,1,0:T(8,128)S(1)}, u32[]{:S(2)}, u32[]{:S(2)}) collective-permute-start(f32[16,64,1024]{2,1,0:T(8,128)S(1)} %get-tuple-element.23), channel_id=1, source_target_pairs={{0,1},{1,0},{2,3},{3,2},{4,5},{5,4},{6,7},{7,6},{8,9},{9,8},{10,11... | collective-permute-start | bytes 12582920 | tf_op jit(solution)/shard_map/ppermute | solution.py:396
  12.1 5.0 %shard_map.103.refs_0_.a_ref = f32[16,64,1024]{2,1,0:T(8,128)S(1)} custom-call(bf16[1024,2048]{1,0:T(8,128)(2,1)S(1)} %get-tuple-element.28.x_ref, bf16[2048,1024]{1,0:T(8,128)(2,1)S(1)} %copy-done.9), custom_call_target="tpu_custom_call" | custom-call | flops 4294967296 | bytes 12582912 | tf_op jit(solution)/shard_map/pallas_call | solution.py:107
  17.2 2.5 %shard_map.104 = f32[8,64,1024]{2,1,0:T(8,128)S(1)} custom-call(bf16[1024,2048]{1,0:T(8,128)(2,1)S(1)} %get-tuple-element.29.x_ref, bf16[2048,1024]{1,0:T(8,128)(2,1)S(1)} %copy-done.2, f32[16,64,1024]{2,1,0:T(8,128)S(1)} %shard_map.103.refs_0_.a_ref), custom_call_target="tpu_custom_call" | custom-call | flops 2147483648 | bytes 12582912 | tf_op jit(solution)/shard_map/pallas_call | solution.py:107
  19.7 1.7 %shard_map.105 = f32[1,8,128]{2,1,0:T(8,128)S(1)} custom-call(s32[1]{0:T(128)} %bitcast.2.core_ref, f32[16,64,1024]{2,1,0:T(8,128)S(1)} %shard_map.103.refs_0_.a_ref, f32[16,64,1024]{2,1,0:T(8,128)S(1)} %collective-permute-done.refs_0_.refs_1_), custom_call_target="tpu_custom_call" | custom-call | flops 1048576 | bytes 1048576 | tf_op jit(solution)/shard_map/pallas_call | solution.py:168
  22.0 0.7 collective-permute-done.1
  22.7 2.6 %collective-permute-start.4 = (f32[1,8,128]{2,1,0:T(8,128)S(1)}, f32[1,8,128]{2,1,0:T(8,128)S(1)}, u32[]{:S(2)}, u32[]{:S(2)}) collective-permute-start(f32[1,8,128]{2,1,0:T(8,128)S(1)} %add.6.refs_1_), channel_id=1, source_target_pairs={{0,96},{32,0},{64,32},{96,64},{1,97},{33,1},{65,33},{97,65},{2,98}... | collective-permute-start | bytes 12296 | tf_op jit(solution)/shard_map/ppermute | solution.py:390
  25.8 0.6 collective-permute-start.2
  26.4 3.8 %shard_map.107 = f32[8,64,1024]{2,1,0:T(8,128)} custom-call(bf16[1024,2048]{1,0:T(8,128)(2,1)S(1)} %get-tuple-element.29.x_ref, bf16[2048,1024]{1,0:T(8,128)(2,1)S(1)} %copy-done.2, f32[16,64,1024]{2,1,0:T(8,128)S(1)} %shard_map.103.refs_0_.a_ref, f32[16,64,1024]{2,1,0:T(8,128)S(1)} %collective-permute-done.refs_0_.refs_1_), custom_call_target="tpu_custom_call" | custom-call | flops 2147483648 | bytes 12582912 | tf_op jit(solution)/shard_map/pallas_call | solution.py:107
  30.2 0.6 shard_map.106
  30.9 1.8 %convert_element_type.13 = f16[16,64,1024]{2,1,0:T(8,128)(2,1)} convert(f32[16,64,1024]{2,1,0:T(8,128)S(1)} %get-tuple-element.27) | non-fusion elementwise | flops 1048576 | bytes 6291456 | tf_op jit(solution)/shard_map/convert_element_type | solution.py:405
  32.7 1.1 collective-permute-start.6
  33.8 10.5 %all-to-all-start.1 = ((f16[16,64,1024]{2,1,0:T(8,128)(2,1)}), f16[16,64,1024]{2,1,0:T(8,128)(2,1)}, u32[]{:S(2)}, u32[]{:S(2)}) async-start(f16[16,64,1024]{2,1,0:T(8,128)(2,1)} %convert_element_type.13), calls=%async_computation.1 | async-start | bytes 4194304 | tf_op jit(solution)/shard_map/all_to_all | solution.py:393
  44.2 2.2 %copy-done.3 = bf16[2048,1024]{1,0:T(8,128)(2,1)S(1)} copy-done((bf16[2048,1024]{1,0:T(8,128)(2,1)S(1)}, bf16[2048,1024]{1,0:T(8,128)(2,1)}, u32[]{:S(2)}) %copy-start.3) | copy-done | bytes 4194328
  46.4 2.2 %copy-done.11 = bf16[1024,2048]{1,0:T(8,128)(2,1)S(1)} copy-done((bf16[1024,2048]{1,0:T(8,128)(2,1)S(1)}, bf16[1024,2048]{1,0:T(8,128)(2,1)}, u32[]{:S(2)}) %copy-start.11) | copy-done | bytes 4194328
  48.6 8.3 %shard_map.108 = (f32[16,64,1024]{2,1,0:T(8,128)S(1)}, f32[1,8,128]{2,1,0:T(8,128)S(1)}) custom-call(s32[1]{0:T(128)} %bitcast.2.core_ref, bf16[1024,2048]{1,0:T(8,128)(2,1)S(1)} %copy-done.11, bf16[2048,1024]{1,0:T(8,128)(2,1)S(1)} %copy-done.3, f32[8,64,1024]{2,1,0:T(8,128)} %collective-permute-done.5.refs_0_, f32[8,64,1024]{2,1,0:T(8,128)} %collective-permute-done.6.refs_1_), custom_call_target="tpu_custom_call" | custom-call | flops 4294967296 | bytes 16777216 | tf_op jit(solution)/shard_map/pallas_call | solution.py:189
  57.3 0.9 collective-permute-done.7
  58.2 2.0 %collective-permute-start.10 = (f32[1,8,128]{2,1,0:T(8,128)S(1)}, f32[1,8,128]{2,1,0:T(8,128)S(1)}, u32[]{:S(2)}, u32[]{:S(2)}) collective-permute-start(f32[1,8,128]{2,1,0:T(8,128)S(1)} %add.7.refs_2_), channel_id=1, source_target_pairs={{0,96},{32,0},{64,32},{96,64},{1,97},{33,1},{65,33},{97,65},{2,98}... | collective-permute-start | bytes 12296 | tf_op jit(solution)/shard_map/ppermute | solution.py:390
  60.2 1.2 collective-permute-start.9
  61.4 3.1 %collective-permute-done.9.refs_4_ = f32[1,8,128]{2,1,0:T(8,128)S(1)} collective-permute-done((f32[1,8,128]{2,1,0:T(8,128)S(1)}, f32[1,8,128]{2,1,0:T(8,128)S(1)}, u32[]{:S(2)}, u32[]{:S(2)}) %collective-permute-start.9) | collective-permute-done | bytes 4128 | tf_op jit(solution)/shard_map/ppermute | solution.py:390
  64.5 0.9 collective-permute-done.8.refs_3_
  65.5 3.6 %shard_map.109 = (f32[16,64,1024]{2,1,0:T(8,128)S(1)}, f32[8,128]{1,0:T(8,128)S(1)}) custom-call(s32[1]{0:T(128)} %bitcast.2.core_ref, f32[16,64,1024]{2,1,0:T(8,128)S(1)} %get-tuple-element.31.a_ref, f32[8,64,1024]{2,1,0:T(8,128)} %collective-permute-done.5.refs_0_, f32[8,64,1024]{2,1,0:T(8,128)} %collective-permute-done.6.refs_1_, ...), custom_call_target="tpu_custom_call" | custom-call | flops 1048576 | bytes 1048576 | tf_op jit(solution)/shard_map/pallas_call | solution.py:227
  69.1 1.8 %convert_element_type.14 = f16[16,64,1024]{2,1,0:T(8,128)(2,1)} convert(f32[16,64,1024]{2,1,0:T(8,128)S(1)} %get-tuple-element.33) | non-fusion elementwise | flops 1048576 | bytes 6291456 | tf_op jit(solution)/shard_map/convert_element_type | solution.py:417
  71.4 8.8 %all-to-all-start = ((f16[16,64,1024]{2,1,0:T(8,128)(2,1)}), f16[16,64,1024]{2,1,0:T(8,128)(2,1)S(1)}, u32[]{:S(2)}, u32[]{:S(2)}) async-start(f16[16,64,1024]{2,1,0:T(8,128)(2,1)} %convert_element_type.14), calls=%async_computation | async-start | bytes 4194304 | tf_op jit(solution)/shard_map/all_to_all | solution.py:393
  80.3 2.1 %convert_element_type.16.v_ref.refs_0_ = f32[16,64,1024]{2,1,0:T(8,128)S(1)} convert(f16[16,64,1024]{2,1,0:T(8,128)(2,1)} %all-to-all-done.1) | non-fusion elementwise | flops 1048576 | bytes 6291456 | tf_op jit(solution)/shard_map/convert_element_type | solution.py:419
  82.4 3.6 %shard_map.110.refs_0_ = f32[2,128]{1,0:T(2,128)S(1)} custom-call(s32[2]{0:T(128)S(1)} %pad_add_fusion.place_ref, f32[16,64,1024]{2,1,0:T(8,128)S(1)} %convert_element_type.16.v_ref.refs_0_, f32[8,128]{1,0:T(8,128)S(1)} %get-tuple-element.35.norm_ref), custom_call_target="tpu_custom_call" | custom-call | flops 20971520 | bytes 4194304 | tf_op jit(solution)/shard_map/pallas_call | solution.py:281
  86.0 2.0 %copy-done = f32[16,64,1024]{2,1,0:T(8,128)} copy-done((f32[16,64,1024]{2,1,0:T(8,128)}, f32[16,64,1024]{2,1,0:T(8,128)S(1)}, u32[]{:S(2)}) %copy-start) | copy-done | bytes 4194328
  88.0 15.8 %all-to-all-done = f16[16,64,1024]{2,1,0:T(8,128)(2,1)S(1)} async-done(((f16[16,64,1024]{2,1,0:T(8,128)(2,1)}), f16[16,64,1024]{2,1,0:T(8,128)(2,1)S(1)}, u32[]{:S(2)}, u32[]{:S(2)}) %all-to-all-start) | async-done | bytes 2097184 | tf_op jit(solution)/shard_map/all_to_all | solution.py:393
  104.3 3.7 %shard_map.111 = f32[128,4,128]{2,1,0:T(4,128)S(1)} custom-call(s32[2]{0:T(128)S(1)} %pad_add_fusion.place_ref, f32[16,64,1024]{2,1,0:T(8,128)S(1)} %convert_element_type.15.v_ref.refs_3_, f32[8,128]{1,0:T(8,128)S(1)} %get-tuple-element.34.norm_ref, f32[2,128]{1,0:T(2,128)S(1)} %shard_map.110.refs_0_), custom_call_target="tpu_custom_call" | custom-call | flops 20971520 | bytes 4194304 | tf_op jit(solution)/shard_map/pallas_call | solution.py:281
  108.0 21.3 %all_to_all.15.totals_ref = f32[128,4,128]{2,1,0:T(4,128)S(1)} all-to-all(f32[128,4,128]{2,1,0:T(4,128)S(1)} %shard_map.111), channel_id=1, replica_groups=mesh['shard'=4,'rep'=32] {'shard','rep'}, dimensions={0} | all-to-all | bytes 524288 | tf_op jit(solution)/shard_map/all_to_all | solution.py:423
  129.3 3.2 %shard_map.112 = (f32[64,1024]{1,0:T(8,128)}, f32[64,1024]{1,0:T(8,128)}, f32[64,1024]{1,0:T(8,128)}, f32[64,1024]{1,0:T(8,128)}) custom-call(f32[128,4,128]{2,1,0:T(4,128)S(1)} %all_to_all.15.totals_ref, f32[16,64,1024]{2,1,0:T(8,128)S(1)} %copy-done.1, f32[64,1024]{1,0:T(8,128)S(1)} %copy-done.4, f32[64,1024]{1,0:T(8,128)S(1)} %copy-done.5, ...), custom_call_target="tpu_custom_call" | custom-call | flops 8388608 | bytes 10485760 | tf_op jit(solution)/shard_map/pallas_call | solution.py:355
  (37 shorter events, 2.5 us)
Async XLA Ops:
  0.6 2.2 %copy-start.8 = (bf16[2048,1024]{1,0:T(8,128)(2,1)S(1)}, bf16[2048,1024]{1,0:T(8,128)(2,1)}, u32[]{:S(2)}) copy-start(bf16[2048,1024]{1,0:T(8,128)(2,1)} %y_ref.4) | copy-start | bytes 12582916
  2.8 9.3 %copy-start.9 = (bf16[2048,1024]{1,0:T(8,128)(2,1)S(1)}, bf16[2048,1024]{1,0:T(8,128)(2,1)}, u32[]{:S(2)}) copy-start(bf16[2048,1024]{1,0:T(8,128)(2,1)} %y_ref.4) | copy-start | bytes 12582916
  10.6 6.6 %copy-start.10 = (bf16[1024,2048]{1,0:T(8,128)(2,1)}, bf16[1024,2048]{1,0:T(8,128)(2,1)S(1)}, u32[]{:S(2)}) copy-start(bf16[1024,2048]{1,0:T(8,128)(2,1)S(1)} %get-tuple-element.28.x_ref) | copy-start | bytes 12582916
  10.6 9.1 %collective-permute-start = (f32[16,64,1024]{2,1,0:T(8,128)S(1)}, f32[16,64,1024]{2,1,0:T(8,128)S(1)}, u32[]{:S(2)}, u32[]{:S(2)}) collective-permute-start(f32[16,64,1024]{2,1,0:T(8,128)S(1)} %get-tuple-element.23), channel_id=1, source_target_pairs={{0,1},{1,0},{2,3},{3,2},{4,5},{5,4},{6,7},{7,6},{8,9},{9,8},{10,11... | collective-permute-start | bytes 12582920 | tf_op jit(solution)/shard_map/ppermute | solution.py:396
  12.1 5.1 %copy-start.2 = (bf16[2048,1024]{1,0:T(8,128)(2,1)S(1)}, bf16[2048,1024]{1,0:T(8,128)(2,1)}, u32[]{:S(2)}) copy-start(bf16[2048,1024]{1,0:T(8,128)(2,1)} %y_ref.7) | copy-start | bytes 12582916
  21.5 1.2 collective-permute-start.1
  21.5 22.7 %collective-permute-start.5 = (f32[8,64,1024]{2,1,0:T(8,128)S(1)}, f32[8,64,1024]{2,1,0:T(8,128)}, u32[]{:S(2)}, u32[]{:S(2)}) collective-permute-start(f32[8,64,1024]{2,1,0:T(8,128)S(1)} %shard_map.104), channel_id=1, source_target_pairs={{0,1},{1,0},{2,3},{3,2},{4,5},{5,4},{6,7},{7,6},{8,9},{9,8},{10,11... | collective-permute-start | bytes 6291464 | tf_op jit(solution)/shard_map/ppermute | solution.py:409
  22.7 7.5 %collective-permute-start.4 = (f32[1,8,128]{2,1,0:T(8,128)S(1)}, f32[1,8,128]{2,1,0:T(8,128)S(1)}, u32[]{:S(2)}, u32[]{:S(2)}) collective-permute-start(f32[1,8,128]{2,1,0:T(8,128)S(1)} %add.6.refs_1_), channel_id=1, source_target_pairs={{0,96},{32,0},{64,32},{96,64},{1,97},{33,1},{65,33},{97,65},{2,98}... | collective-permute-start | bytes 12296 | tf_op jit(solution)/shard_map/ppermute | solution.py:390
  25.2 5.0 %collective-permute-start.3 = (f32[1,8,128]{2,1,0:T(8,128)S(1)}, f32[1,8,128]{2,1,0:T(8,128)S(1)}, u32[]{:S(2)}, u32[]{:S(2)}) collective-permute-start(f32[1,8,128]{2,1,0:T(8,128)S(1)} %add.6.refs_1_), channel_id=1, source_target_pairs={{0,64},{32,96},{64,0},{96,32},{1,65},{33,97},{65,1},{97,33},{2,66}... | collective-permute-start | bytes 12296 | tf_op jit(solution)/shard_map/ppermute | solution.py:390
  25.8 4.4 %collective-permute-start.2 = (f32[1,8,128]{2,1,0:T(8,128)S(1)}, f32[1,8,128]{2,1,0:T(8,128)S(1)}, u32[]{:S(2)}, u32[]{:S(2)}) collective-permute-start(f32[1,8,128]{2,1,0:T(8,128)S(1)} %add.6.refs_1_), channel_id=1, source_target_pairs={{0,32},{32,64},{64,96},{96,0},{1,33},{33,65},{65,97},{97,1},{2,34}... | collective-permute-start | bytes 12296 | tf_op jit(solution)/shard_map/ppermute | solution.py:390
  32.7 11.6 %collective-permute-start.6 = (f32[8,64,1024]{2,1,0:T(8,128)}, f32[8,64,1024]{2,1,0:T(8,128)}, u32[]{:S(2)}, u32[]{:S(2)}) collective-permute-start(f32[8,64,1024]{2,1,0:T(8,128)} %shard_map.107), channel_id=1, source_target_pairs={{0,1},{1,0},{2,3},{3,2},{4,5},{5,4},{6,7},{7,6},{8,9},{9,8},{10,11... | collective-permute-start | bytes 6291464 | tf_op jit(solution)/shard_map/ppermute | solution.py:410
  33.8 37.6 %all-to-all-start.1 = ((f16[16,64,1024]{2,1,0:T(8,128)(2,1)}), f16[16,64,1024]{2,1,0:T(8,128)(2,1)}, u32[]{:S(2)}, u32[]{:S(2)}) async-start(f16[16,64,1024]{2,1,0:T(8,128)(2,1)} %convert_element_type.13), calls=%async_computation.1 | async-start | bytes 4194304 | tf_op jit(solution)/shard_map/all_to_all | solution.py:393
  44.2 2.2 %copy-start.3 = (bf16[2048,1024]{1,0:T(8,128)(2,1)S(1)}, bf16[2048,1024]{1,0:T(8,128)(2,1)}, u32[]{:S(2)}) copy-start(bf16[2048,1024]{1,0:T(8,128)(2,1)} %y_ref.7) | copy-start | bytes 12582916
  46.4 2.2 %copy-start.11 = (bf16[1024,2048]{1,0:T(8,128)(2,1)S(1)}, bf16[1024,2048]{1,0:T(8,128)(2,1)}, u32[]{:S(2)}) copy-start(bf16[1024,2048]{1,0:T(8,128)(2,1)} %copy-done.10) | copy-start | bytes 12582916
  56.9 1.2 collective-permute-start.7
  58.2 3.2 %collective-permute-start.10 = (f32[1,8,128]{2,1,0:T(8,128)S(1)}, f32[1,8,128]{2,1,0:T(8,128)S(1)}, u32[]{:S(2)}, u32[]{:S(2)}) collective-permute-start(f32[1,8,128]{2,1,0:T(8,128)S(1)} %add.7.refs_2_), channel_id=1, source_target_pairs={{0,96},{32,0},{64,32},{96,64},{1,97},{33,1},{65,33},{97,65},{2,98}... | collective-permute-start | bytes 12296 | tf_op jit(solution)/shard_map/ppermute | solution.py:390
  60.2 4.4 %collective-permute-start.9 = (f32[1,8,128]{2,1,0:T(8,128)S(1)}, f32[1,8,128]{2,1,0:T(8,128)S(1)}, u32[]{:S(2)}, u32[]{:S(2)}) collective-permute-start(f32[1,8,128]{2,1,0:T(8,128)S(1)} %add.7.refs_2_), channel_id=1, source_target_pairs={{0,64},{32,96},{64,0},{96,32},{1,65},{33,97},{65,1},{97,33},{2,66}... | collective-permute-start | bytes 12296 | tf_op jit(solution)/shard_map/ppermute | solution.py:390
  61.4 4.1 %collective-permute-start.8 = (f32[1,8,128]{2,1,0:T(8,128)S(1)}, f32[1,8,128]{2,1,0:T(8,128)S(1)}, u32[]{:S(2)}, u32[]{:S(2)}) collective-permute-start(f32[1,8,128]{2,1,0:T(8,128)S(1)} %add.7.refs_2_), channel_id=1, source_target_pairs={{0,32},{32,64},{64,96},{96,0},{1,33},{33,65},{65,97},{97,1},{2,34}... | collective-permute-start | bytes 12296 | tf_op jit(solution)/shard_map/ppermute | solution.py:390
  71.4 32.4 %all-to-all-start = ((f16[16,64,1024]{2,1,0:T(8,128)(2,1)}), f16[16,64,1024]{2,1,0:T(8,128)(2,1)S(1)}, u32[]{:S(2)}, u32[]{:S(2)}) async-start(f16[16,64,1024]{2,1,0:T(8,128)(2,1)} %convert_element_type.14), calls=%async_computation | async-start | bytes 4194304 | tf_op jit(solution)/shard_map/all_to_all | solution.py:393
  86.0 2.0 %copy-start = (f32[16,64,1024]{2,1,0:T(8,128)}, f32[16,64,1024]{2,1,0:T(8,128)S(1)}, u32[]{:S(2)}) copy-start(f32[16,64,1024]{2,1,0:T(8,128)S(1)} %convert_element_type.16.v_ref.refs_0_) | copy-start | bytes 12582916
  88.0 41.3 %copy-start.4 = (f32[64,1024]{1,0:T(8,128)S(1)}, f32[64,1024]{1,0:T(8,128)}, u32[]{:S(2)}) copy-start(f32[64,1024]{1,0:T(8,128)} %refs_1_.1) | copy-start | bytes 786436
  88.0 41.3 %copy-start.5 = (f32[64,1024]{1,0:T(8,128)S(1)}, f32[64,1024]{1,0:T(8,128)}, u32[]{:S(2)}) copy-start(f32[64,1024]{1,0:T(8,128)} %refs_2_.1) | copy-start | bytes 786436
  88.0 41.3 %copy-start.6 = (f32[64,1024]{1,0:T(8,128)S(1)}, f32[64,1024]{1,0:T(8,128)}, u32[]{:S(2)}) copy-start(f32[64,1024]{1,0:T(8,128)} %refs_4_.1) | copy-start | bytes 786436
  88.0 41.3 %copy-start.7 = (f32[64,1024]{1,0:T(8,128)S(1)}, f32[64,1024]{1,0:T(8,128)}, u32[]{:S(2)}) copy-start(f32[64,1024]{1,0:T(8,128)} %refs_5_.1) | copy-start | bytes 786436
  103.8 25.5 %copy-start.1 = (f32[16,64,1024]{2,1,0:T(8,128)S(1)}, f32[16,64,1024]{2,1,0:T(8,128)}, u32[]{:S(2)}) copy-start(f32[16,64,1024]{2,1,0:T(8,128)} %copy-done) | copy-start | bytes 12582916

commit v9 on v8

--- a/solution.py
+++ b/solution.py
@@ -40,7 +40,7 @@
     steps, depth, width = x_ref.shape
     x_copies = [
         pltpu.make_async_copy(
-            x_hbm.at[:, pl.ds((steps - 1 - i) * width, width)], x_ref.at[i], x_sems.at[i]
+            x_hbm.at[:, pl.ds(i * width, width)], x_ref.at[i], x_sems.at[i]
         )
         for i in range(steps)
     ]
@@ -55,9 +55,8 @@
     for i in range(steps):
         x_copies[i].wait()
         blocks = x_ref[i].T.reshape(-1, 2, ROWS, depth)
-        order = range(blocks.shape[0] - 1, -1, -1)
-        first = jnp.concatenate([blocks[n, 0] for n in order], axis=0)
-        second = jnp.concatenate([blocks[n, 1] for n in order], axis=0)
+        first = blocks[:, 0].reshape(-1, depth)
+        second = blocks[:, 1].reshape(-1, depth)
         own_ref[pl.ds(i * half, half), :] = jnp.where(is_first, first, second)
         other = jnp.where(is_first, second, first)
         other_ref[pl.ds(i * half, half), :] = other
@@ -203,7 +202,7 @@
     )(core, rows, cotangent, *b)
 
 
-def merge_kernel(core_ref, a_ref, *refs, parts, steps):
+def merge_kernel(core_ref, a_ref, *refs, parts, steps, backwards):
     b_refs, sums_refs, (o_ref, norm_ref) = refs[:parts], refs[parts:-2], refs[-2:]
     sums = sum(jnp.sum(ref[...], axis=0) for ref in sums_refs)
     cross, p, q = sums[0:1], sums[1:2], sums[2:3]
@@ -219,21 +218,30 @@
     other = jnp.where(is_first, second, first) * scale
     own = jnp.concatenate([own] * (FEATURES // 128), axis=1)[None]
     other = jnp.concatenate([other] * (FEATURES // 128), axis=1)[None]
-    o_ref[...] = own * a_ref[...] + other * block_of(b_refs, steps)
-
-
-def merge_pair(core, a, b, sums, mib):
+    merged = own * a_ref[...] + other * block_of(b_refs, steps)
+    count = merged.shape[0]
+    for n in range(count):
+        o_ref[n] = merged[count - 1 - n if backwards else n]
+
+
+def merge_pair(core, a, b, sums, backwards):
+    steps = CHIPS // 4
+    out_spec = pl.BlockSpec(
+        (4, ROWS, FEATURES), lambda i: (steps - 1 - i if backwards else i, 0, 0)
+    )
     spec = pl.BlockSpec((4, ROWS, FEATURES), lambda i: (i, 0, 0))
     return pl.pallas_call(
-        functools.partial(merge_kernel, parts=len(b), steps=b[0].shape[0] // 4),
+        functools.partial(
+            merge_kernel, parts=len(b), steps=b[0].shape[0] // 4, backwards=backwards
+        ),
         out_shape=(
             jax.ShapeDtypeStruct(a.shape, jnp.float32),
             jax.ShapeDtypeStruct((8, 128), jnp.float32),
         ),
         grid=(CHIPS // 4,),
         in_specs=[SMEM, spec] + parts_specs(b) + [VMEM] * len(sums),
-        out_specs=(spec, pl.BlockSpec((8, 128), lambda i: (0, 0))),
-        compiler_params=params(mib),
+        out_specs=(out_spec, pl.BlockSpec((8, 128), lambda i: (0, 0))),
+        compiler_params=params(12),
         cost_estimate=cost(a.size, a.size),
     )(core, a, *b, *sums)
 
@@ -378,9 +386,11 @@
     index = lax.axis_index("rep").astype(jnp.int32)
     core = (index & 1)[None]
     leader = ((lax.axis_index("shard") == 0) & (index & 1 == 0)).astype(jnp.int32)
-    place = jnp.stack([CHIPS - 1 - (index >> 1), leader])
+    place = jnp.stack([index >> 1, leader])
+    backwards_place = jnp.stack([CHIPS - 1 - (index >> 1), leader])
     swap = [(i, i ^ 1) for i in range(replicas)]
-    core_groups = [list(range(c, replicas, 2))[::-1] for c in range(2)]
+    core_groups = [list(range(c, replicas, 2)) for c in range(2)]
+    backwards_groups = [group[::-1] for group in core_groups]
 
     def summed(sums):
         sums = sums + lax.ppermute(sums, "rep", swap)
@@ -389,8 +399,8 @@
         ]
         return [sums] + [lax.ppermute(sums, "shard", shift) for shift in shifts]
 
-    def gathered(sent):
-        return lax.all_to_all(sent, "rep", 0, 0, axis_index_groups=core_groups)
+    def gathered(sent, groups):
+        return lax.all_to_all(sent, "rep", 0, 0, axis_index_groups=groups)
 
     key_other, own_rows, other_rows = split_and_grad(core, tokens, key_cotangent)
     key_arrived = [lax.ppermute(key_other, "rep", swap)]
@@ -401,9 +411,9 @@
     value_second = grad(
         after(other_rows, key_sums[0]), value_cotangent, half, half, [key_own] + key_arrived
     )
-    key_merged, key_norm = merge_pair(core, key_own, key_arrived, key_sums, 12)
+    key_merged, key_norm = merge_pair(core, key_own, key_arrived, key_sums, False)
     key_sent = key_merged.astype(jnp.float16)
-    key_all = gathered(key_sent)
+    key_all = gathered(key_sent, core_groups)
 
     value_arrived = [
         lax.ppermute(value_first, "rep", swap),
@@ -413,13 +423,13 @@
         core, after(own_rows, key_sent), value_cotangent, value_arrived
     )
     value_sums = summed(value_sums)
-    value_merged, value_norm = merge_pair(core, value_own, value_arrived, value_sums, 12)
-    value_all = gathered(value_merged.astype(jnp.float16))
+    value_merged, value_norm = merge_pair(core, value_own, value_arrived, value_sums, True)
+    value_all = gathered(value_merged.astype(jnp.float16), backwards_groups)
 
     key_v = key_all.astype(jnp.float32)
     key_vector = gram(place, key_v, key_norm, [], (2, 128))
     value_v = value_all.astype(jnp.float32)
-    vectors = gram(place, value_v, value_norm, [key_vector], (shard_count * replicas, 4, 128))
+    vectors = gram(backwards_place, value_v, value_norm, [key_vector], (shard_count * replicas, 4, 128))
     totals = lax.all_to_all(vectors, ("shard", "rep"), 0, 0)
     new_key_weight, new_key_moment, new_value_weight, new_value_moment = update(
         totals, key_v, key_weight, key_moment, value_v, value_weight, value_moment

time: 133 us -> 129 us (0.970)
  starting transfers between devices: 29.7 us -> 24.5 us
  waiting for transfers between devices: 21.9 us -> 23.8 us
    all_to_all x2, starting transfers between devices: 19.3 us -> 14.1 us  [gathered(): return lax.all_to_all(sent, 'rep', 0, 0, axis_index_groups=groups)]
    all_to_all x2, waiting for transfers between devices: 16.3 us -> 18.3 us  [gathered(): return lax.all_to_all(sent, 'rep', 0, 0, axis_index_groups=groups)]
  transfers between devices with their start and end apart: 13 -> 13, of which waited for: 6 -> 6; matrix products, arithmetic and copies ran while one was open for 4% -> 5% of each run, Pallas kernels for 21% -> 21%
where the time goes in v9:
time: 129 us
  Pallas kernels  44.1 us (34%)
  starting transfers between devices  24.5 us (19%)
  waiting for transfers between devices  23.8 us (18%)
  blocking collectives  20.8 us (16%)
  local copies, waits for them, and re-layouts  8.54 us (7%)
  other arithmetic  6.35 us (5%)
    all_to_all x1, blocking collectives, shards(): totals = lax.all_to_all(vectors, ('shard', 'rep'), 0, 0)  20.8 us
    all_to_all x2, waiting for transfers between devices, gathered(): return lax.all_to_all(sent, 'rep', 0, 0, axis_index_groups=groups)  18.3 us
    all_to_all x2, starting transfers between devices, gathered(): return lax.all_to_all(sent, 'rep', 0, 0, axis_index_groups=groups)  14.1 us
    pallas_call x3, Pallas kernels, grad(): pl.pallas_call(functools.partial(grad_kernel, start=start), out_shape=jax...  11.4 us
    unnamed x24, local copies, waits for them, and re-layouts  8.54 us
    pallas_call x1, Pallas kernels, grad_and_pair_sums(): pl.pallas_call(functools.partial(grad_pair_kernel, steps=b[0].shape[0] //...  8.33 us
    pallas_call x1, Pallas kernels, split_and_grad(): pl.pallas_call(split_kernel, out_shape=(jax.ShapeDtypeStruct((CHIPS, ROWS...  7.8 us
    pallas_call x2, Pallas kernels, gram(): pl.pallas_call(gram_kernel, out_shape=jax.ShapeDtypeStruct(out_dims, jnp....  7.31 us
  transfers between devices with their start and end apart: 13, of which 6 were waited for; matrix products, arithmetic and copies ran while one was open for 5% of the time, Pallas kernels for 21%

profile of v9, /device:TPU:1, one launch (start us, length us, event | category | flops | bytes accessed | tf_op | source)
XLA Modules:
  0.0 129.1 jit_solution(13232124184144040188)
XLA Ops:
  0.6 2.2 %copy-done.8 = bf16[2048,1024]{1,0:T(8,128)(2,1)S(1)} copy-done((bf16[2048,1024]{1,0:T(8,128)(2,1)S(1)}, bf16[2048,1024]{1,0:T(8,128)(2,1)}, u32[]{:S(2)}) %copy-start.8) | copy-done | bytes 4194328
  2.8 7.8 %shard_map.102 = (f32[16,64,1024]{2,1,0:T(8,128)S(1)}, bf16[1024,2048]{1,0:T(8,128)(2,1)S(1)}, bf16[1024,2048]{1,0:T(8,128)(2,1)S(1)}) custom-call(s32[1]{0:T(128)} %bitcast.2.core_ref, bf16[2048,2048]{1,0:T(8,128)(2,1)} %x_hbm.1, bf16[2048,1024]{1,0:T(8,128)(2,1)S(1)} %copy-done.8), custom_call_target="tpu_custom_call" | custom-call | flops 4294967296 | bytes 25165824 | tf_op jit(solution)/shard_map/pallas_call | solution.py:73
  10.6 1.5 %collective-permute-start = (f32[16,64,1024]{2,1,0:T(8,128)S(1)}, f32[16,64,1024]{2,1,0:T(8,128)S(1)}, u32[]{:S(2)}, u32[]{:S(2)}) collective-permute-start(f32[16,64,1024]{2,1,0:T(8,128)S(1)} %get-tuple-element.23), channel_id=1, source_target_pairs={{0,1},{1,0},{2,3},{3,2},{4,5},{5,4},{6,7},{7,6},{8,9},{9,8},{10,11... | collective-permute-start | bytes 12582920 | tf_op jit(solution)/shard_map/ppermute | solution.py:406
  12.2 5.0 %shard_map.103.refs_0_.a_ref = f32[16,64,1024]{2,1,0:T(8,128)S(1)} custom-call(bf16[1024,2048]{1,0:T(8,128)(2,1)S(1)} %get-tuple-element.28.x_ref, bf16[2048,1024]{1,0:T(8,128)(2,1)S(1)} %copy-done.9), custom_call_target="tpu_custom_call" | custom-call | flops 4294967296 | bytes 12582912 | tf_op jit(solution)/shard_map/pallas_call | solution.py:106
  17.2 2.5 %shard_map.104 = f32[8,64,1024]{2,1,0:T(8,128)S(1)} custom-call(bf16[1024,2048]{1,0:T(8,128)(2,1)S(1)} %get-tuple-element.29.x_ref, bf16[2048,1024]{1,0:T(8,128)(2,1)S(1)} %copy-done.2, f32[16,64,1024]{2,1,0:T(8,128)S(1)} %shard_map.103.refs_0_.a_ref), custom_call_target="tpu_custom_call" | custom-call | flops 2147483648 | bytes 12582912 | tf_op jit(solution)/shard_map/pallas_call | solution.py:106
  19.8 1.7 %shard_map.105 = f32[1,8,128]{2,1,0:T(8,128)S(1)} custom-call(s32[1]{0:T(128)} %bitcast.2.core_ref, f32[16,64,1024]{2,1,0:T(8,128)S(1)} %shard_map.103.refs_0_.a_ref, f32[16,64,1024]{2,1,0:T(8,128)S(1)} %collective-permute-done.refs_0_.refs_1_), custom_call_target="tpu_custom_call" | custom-call | flops 1048576 | bytes 1048576 | tf_op jit(solution)/shard_map/pallas_call | solution.py:167
  22.0 0.7 collective-permute-done.1
  22.7 2.6 %collective-permute-start.4 = (f32[1,8,128]{2,1,0:T(8,128)S(1)}, f32[1,8,128]{2,1,0:T(8,128)S(1)}, u32[]{:S(2)}, u32[]{:S(2)}) collective-permute-start(f32[1,8,128]{2,1,0:T(8,128)S(1)} %add.6.refs_1_), channel_id=1, source_target_pairs={{0,96},{32,0},{64,32},{96,64},{1,97},{33,1},{65,33},{97,65},{2,98}... | collective-permute-start | bytes 12296 | tf_op jit(solution)/shard_map/ppermute | solution.py:400
  26.4 3.8 %shard_map.107 = f32[8,64,1024]{2,1,0:T(8,128)} custom-call(bf16[1024,2048]{1,0:T(8,128)(2,1)S(1)} %get-tuple-element.29.x_ref, bf16[2048,1024]{1,0:T(8,128)(2,1)S(1)} %copy-done.2, f32[16,64,1024]{2,1,0:T(8,128)S(1)} %shard_map.103.refs_0_.a_ref, f32[16,64,1024]{2,1,0:T(8,128)S(1)} %collective-permute-done.refs_0_.refs_1_), custom_call_target="tpu_custom_call" | custom-call | flops 2147483648 | bytes 12582912 | tf_op jit(solution)/shard_map/pallas_call | solution.py:106
  30.2 0.6 shard_map.106
  30.9 1.8 %convert_element_type.13 = f16[16,64,1024]{2,1,0:T(8,128)(2,1)} convert(f32[16,64,1024]{2,1,0:T(8,128)S(1)} %get-tuple-element.27) | non-fusion elementwise | flops 1048576 | bytes 6291456 | tf_op jit(solution)/shard_map/convert_element_type | solution.py:415
  32.7 1.1 collective-permute-start.6
  33.8 7.8 %all-to-all-start.1 = ((f16[16,64,1024]{2,1,0:T(8,128)(2,1)}), f16[16,64,1024]{2,1,0:T(8,128)(2,1)}, u32[]{:S(2)}, u32[]{:S(2)}) async-start(f16[16,64,1024]{2,1,0:T(8,128)(2,1)} %convert_element_type.13), calls=%async_computation.1 | async-start | bytes 4194304 | tf_op jit(solution)/shard_map/all_to_all | solution.py:403
  41.6 2.2 %copy-done.3 = bf16[2048,1024]{1,0:T(8,128)(2,1)S(1)} copy-done((bf16[2048,1024]{1,0:T(8,128)(2,1)S(1)}, bf16[2048,1024]{1,0:T(8,128)(2,1)}, u32[]{:S(2)}) %copy-start.3) | copy-done | bytes 4194328
  43.8 2.2 %copy-done.11 = bf16[1024,2048]{1,0:T(8,128)(2,1)S(1)} copy-done((bf16[1024,2048]{1,0:T(8,128)(2,1)S(1)}, bf16[1024,2048]{1,0:T(8,128)(2,1)}, u32[]{:S(2)}) %copy-start.11) | copy-done | bytes 4194328
  46.0 8.3 %shard_map.108 = (f32[16,64,1024]{2,1,0:T(8,128)S(1)}, f32[1,8,128]{2,1,0:T(8,128)S(1)}) custom-call(s32[1]{0:T(128)} %bitcast.2.core_ref, bf16[1024,2048]{1,0:T(8,128)(2,1)S(1)} %copy-done.11, bf16[2048,1024]{1,0:T(8,128)(2,1)S(1)} %copy-done.3, f32[8,64,1024]{2,1,0:T(8,128)} %collective-permute-done.5.refs_0_, f32[8,64,1024]{2,1,0:T(8,128)} %collective-permute-done.6.refs_1_), custom_call_target="tpu_custom_call" | custom-call | flops 4294967296 | bytes 16777216 | tf_op jit(solution)/shard_map/pallas_call | solution.py:188
  54.7 0.9 collective-permute-done.7
  55.6 2.0 %collective-permute-start.10 = (f32[1,8,128]{2,1,0:T(8,128)S(1)}, f32[1,8,128]{2,1,0:T(8,128)S(1)}, u32[]{:S(2)}, u32[]{:S(2)}) collective-permute-start(f32[1,8,128]{2,1,0:T(8,128)S(1)} %add.7.refs_2_), channel_id=1, source_target_pairs={{0,96},{32,0},{64,32},{96,64},{1,97},{33,1},{65,33},{97,65},{2,98}... | collective-permute-start | bytes 12296 | tf_op jit(solution)/shard_map/ppermute | solution.py:400
  57.6 1.3 collective-permute-start.9
  58.8 3.1 %collective-permute-done.9.refs_4_ = f32[1,8,128]{2,1,0:T(8,128)S(1)} collective-permute-done((f32[1,8,128]{2,1,0:T(8,128)S(1)}, f32[1,8,128]{2,1,0:T(8,128)S(1)}, u32[]{:S(2)}, u32[]{:S(2)}) %collective-permute-start.9) | collective-permute-done | bytes 4128 | tf_op jit(solution)/shard_map/ppermute | solution.py:400
  61.9 0.9 collective-permute-done.8.refs_3_
  62.8 3.6 %shard_map.109 = (f32[16,64,1024]{2,1,0:T(8,128)S(1)}, f32[8,128]{1,0:T(8,128)S(1)}) custom-call(s32[1]{0:T(128)} %bitcast.2.core_ref, f32[16,64,1024]{2,1,0:T(8,128)S(1)} %get-tuple-element.31.a_ref, f32[8,64,1024]{2,1,0:T(8,128)} %collective-permute-done.5.refs_0_, f32[8,64,1024]{2,1,0:T(8,128)} %collective-permute-done.6.refs_1_, ...), custom_call_target="tpu_custom_call" | custom-call | flops 1048576 | bytes 1048576 | tf_op jit(solution)/shard_map/pallas_call | solution.py:233
  66.4 1.8 %convert_element_type.14 = f16[16,64,1024]{2,1,0:T(8,128)(2,1)} convert(f32[16,64,1024]{2,1,0:T(8,128)S(1)} %get-tuple-element.33) | non-fusion elementwise | flops 1048576 | bytes 6291456 | tf_op jit(solution)/shard_map/convert_element_type | solution.py:427
  68.2 2.5 %all-to-all-done.1 = f16[16,64,1024]{2,1,0:T(8,128)(2,1)} async-done(((f16[16,64,1024]{2,1,0:T(8,128)(2,1)}), f16[16,64,1024]{2,1,0:T(8,128)(2,1)}, u32[]{:S(2)}, u32[]{:S(2)}) %all-to-all-start.1) | async-done | bytes 2097184 | tf_op jit(solution)/shard_map/all_to_all | solution.py:403
  70.8 6.3 %all-to-all-start = ((f16[16,64,1024]{2,1,0:T(8,128)(2,1)}), f16[16,64,1024]{2,1,0:T(8,128)(2,1)S(1)}, u32[]{:S(2)}, u32[]{:S(2)}) async-start(f16[16,64,1024]{2,1,0:T(8,128)(2,1)} %convert_element_type.14), calls=%async_computation | async-start | bytes 4194304 | tf_op jit(solution)/shard_map/all_to_all | solution.py:403
  77.2 2.1 %convert_element_type.16.v_ref.refs_0_ = f32[16,64,1024]{2,1,0:T(8,128)S(1)} convert(f16[16,64,1024]{2,1,0:T(8,128)(2,1)} %all-to-all-done.1) | non-fusion elementwise | flops 1048576 | bytes 6291456 | tf_op jit(solution)/shard_map/convert_element_type | solution.py:429
  79.3 3.6 %shard_map.110.refs_0_ = f32[2,128]{1,0:T(2,128)S(1)} custom-call(s32[2]{0:T(128)S(1)} %pad_add_fusion.1.place_ref, f32[16,64,1024]{2,1,0:T(8,128)S(1)} %convert_element_type.16.v_ref.refs_0_, f32[8,128]{1,0:T(8,128)S(1)} %get-tuple-element.35.norm_ref), custom_call_target="tpu_custom_call" | custom-call | flops 20971520 | bytes 4194304 | tf_op jit(solution)/shard_map/pallas_call | solution.py:289
  83.0 2.0 %copy-done = f32[16,64,1024]{2,1,0:T(8,128)} copy-done((f32[16,64,1024]{2,1,0:T(8,128)}, f32[16,64,1024]{2,1,0:T(8,128)S(1)}, u32[]{:S(2)}) %copy-start) | copy-done | bytes 4194328
  84.9 15.7 %all-to-all-done = f16[16,64,1024]{2,1,0:T(8,128)(2,1)S(1)} async-done(((f16[16,64,1024]{2,1,0:T(8,128)(2,1)}), f16[16,64,1024]{2,1,0:T(8,128)(2,1)S(1)}, u32[]{:S(2)}, u32[]{:S(2)}) %all-to-all-start) | async-done | bytes 2097184 | tf_op jit(solution)/shard_map/all_to_all | solution.py:403
  101.2 3.7 %shard_map.111 = f32[128,4,128]{2,1,0:T(4,128)S(1)} custom-call(s32[2]{0:T(128)S(1)} %pad_add_fusion.place_ref, f32[16,64,1024]{2,1,0:T(8,128)S(1)} %convert_element_type.15.v_ref.refs_3_, f32[8,128]{1,0:T(8,128)S(1)} %get-tuple-element.34.norm_ref, f32[2,128]{1,0:T(2,128)S(1)} %shard_map.110.refs_0_), custom_call_target="tpu_custom_call" | custom-call | flops 20971520 | bytes 4194304 | tf_op jit(solution)/shard_map/pallas_call | solution.py:289
  104.9 20.8 %all_to_all.15.totals_ref = f32[128,4,128]{2,1,0:T(4,128)S(1)} all-to-all(f32[128,4,128]{2,1,0:T(4,128)S(1)} %shard_map.111), channel_id=1, replica_groups=mesh['shard'=4,'rep'=32] {'shard','rep'}, dimensions={0} | all-to-all | bytes 524288 | tf_op jit(solution)/shard_map/all_to_all | solution.py:433
  125.7 3.2 %shard_map.112 = (f32[64,1024]{1,0:T(8,128)}, f32[64,1024]{1,0:T(8,128)}, f32[64,1024]{1,0:T(8,128)}, f32[64,1024]{1,0:T(8,128)}) custom-call(f32[128,4,128]{2,1,0:T(4,128)S(1)} %all_to_all.15.totals_ref, f32[16,64,1024]{2,1,0:T(8,128)S(1)} %copy-done.1, f32[64,1024]{1,0:T(8,128)S(1)} %copy-done.4, f32[64,1024]{1,0:T(8,128)S(1)} %copy-done.5, ...), custom_call_target="tpu_custom_call" | custom-call | flops 8388608 | bytes 10485760 | tf_op jit(solution)/shard_map/pallas_call | solution.py:363
  (38 shorter events, 2.7 us)
Async XLA Ops:
  0.6 2.2 %copy-start.8 = (bf16[2048,1024]{1,0:T(8,128)(2,1)S(1)}, bf16[2048,1024]{1,0:T(8,128)(2,1)}, u32[]{:S(2)}) copy-start(bf16[2048,1024]{1,0:T(8,128)(2,1)} %y_ref.4) | copy-start | bytes 12582916
  2.8 9.3 %copy-start.9 = (bf16[2048,1024]{1,0:T(8,128)(2,1)S(1)}, bf16[2048,1024]{1,0:T(8,128)(2,1)}, u32[]{:S(2)}) copy-start(bf16[2048,1024]{1,0:T(8,128)(2,1)} %y_ref.4) | copy-start | bytes 12582916
  10.6 6.6 %copy-start.10 = (bf16[1024,2048]{1,0:T(8,128)(2,1)}, bf16[1024,2048]{1,0:T(8,128)(2,1)S(1)}, u32[]{:S(2)}) copy-start(bf16[1024,2048]{1,0:T(8,128)(2,1)S(1)} %get-tuple-element.28.x_ref) | copy-start | bytes 12582916
  10.6 9.1 %collective-permute-start = (f32[16,64,1024]{2,1,0:T(8,128)S(1)}, f32[16,64,1024]{2,1,0:T(8,128)S(1)}, u32[]{:S(2)}, u32[]{:S(2)}) collective-permute-start(f32[16,64,1024]{2,1,0:T(8,128)S(1)} %get-tuple-element.23), channel_id=1, source_target_pairs={{0,1},{1,0},{2,3},{3,2},{4,5},{5,4},{6,7},{7,6},{8,9},{9,8},{10,11... | collective-permute-start | bytes 12582920 | tf_op jit(solution)/shard_map/ppermute | solution.py:406
  12.2 5.1 %copy-start.2 = (bf16[2048,1024]{1,0:T(8,128)(2,1)S(1)}, bf16[2048,1024]{1,0:T(8,128)(2,1)}, u32[]{:S(2)}) copy-start(bf16[2048,1024]{1,0:T(8,128)(2,1)} %y_ref.7) | copy-start | bytes 12582916
  21.5 1.2 collective-permute-start.1
  21.6 20.0 %collective-permute-start.5 = (f32[8,64,1024]{2,1,0:T(8,128)S(1)}, f32[8,64,1024]{2,1,0:T(8,128)}, u32[]{:S(2)}, u32[]{:S(2)}) collective-permute-start(f32[8,64,1024]{2,1,0:T(8,128)S(1)} %shard_map.104), channel_id=1, source_target_pairs={{0,1},{1,0},{2,3},{3,2},{4,5},{5,4},{6,7},{7,6},{8,9},{9,8},{10,11... | collective-permute-start | bytes 6291464 | tf_op jit(solution)/shard_map/ppermute | solution.py:419
  22.7 7.5 %collective-permute-start.4 = (f32[1,8,128]{2,1,0:T(8,128)S(1)}, f32[1,8,128]{2,1,0:T(8,128)S(1)}, u32[]{:S(2)}, u32[]{:S(2)}) collective-permute-start(f32[1,8,128]{2,1,0:T(8,128)S(1)} %add.6.refs_1_), channel_id=1, source_target_pairs={{0,96},{32,0},{64,32},{96,64},{1,97},{33,1},{65,33},{97,65},{2,98}... | collective-permute-start | bytes 12296 | tf_op jit(solution)/shard_map/ppermute | solution.py:400
  25.3 4.9 %collective-permute-start.3 = (f32[1,8,128]{2,1,0:T(8,128)S(1)}, f32[1,8,128]{2,1,0:T(8,128)S(1)}, u32[]{:S(2)}, u32[]{:S(2)}) collective-permute-start(f32[1,8,128]{2,1,0:T(8,128)S(1)} %add.6.refs_1_), channel_id=1, source_target_pairs={{0,64},{32,96},{64,0},{96,32},{1,65},{33,97},{65,1},{97,33},{2,66}... | collective-permute-start | bytes 12296 | tf_op jit(solution)/shard_map/ppermute | solution.py:400
  25.8 4.4 %collective-permute-start.2 = (f32[1,8,128]{2,1,0:T(8,128)S(1)}, f32[1,8,128]{2,1,0:T(8,128)S(1)}, u32[]{:S(2)}, u32[]{:S(2)}) collective-permute-start(f32[1,8,128]{2,1,0:T(8,128)S(1)} %add.6.refs_1_), channel_id=1, source_target_pairs={{0,32},{32,64},{64,96},{96,0},{1,33},{33,65},{65,97},{97,1},{2,34}... | collective-permute-start | bytes 12296 | tf_op jit(solution)/shard_map/ppermute | solution.py:400
  32.7 8.9 %collective-permute-start.6 = (f32[8,64,1024]{2,1,0:T(8,128)}, f32[8,64,1024]{2,1,0:T(8,128)}, u32[]{:S(2)}, u32[]{:S(2)}) collective-permute-start(f32[8,64,1024]{2,1,0:T(8,128)} %shard_map.107), channel_id=1, source_target_pairs={{0,1},{1,0},{2,3},{3,2},{4,5},{5,4},{6,7},{7,6},{8,9},{9,8},{10,11... | collective-permute-start | bytes 6291464 | tf_op jit(solution)/shard_map/ppermute | solution.py:420
  33.8 37.0 %all-to-all-start.1 = ((f16[16,64,1024]{2,1,0:T(8,128)(2,1)}), f16[16,64,1024]{2,1,0:T(8,128)(2,1)}, u32[]{:S(2)}, u32[]{:S(2)}) async-start(f16[16,64,1024]{2,1,0:T(8,128)(2,1)} %convert_element_type.13), calls=%async_computation.1 | async-start | bytes 4194304 | tf_op jit(solution)/shard_map/all_to_all | solution.py:403
  41.6 2.2 %copy-start.3 = (bf16[2048,1024]{1,0:T(8,128)(2,1)S(1)}, bf16[2048,1024]{1,0:T(8,128)(2,1)}, u32[]{:S(2)}) copy-start(bf16[2048,1024]{1,0:T(8,128)(2,1)} %y_ref.7) | copy-start | bytes 12582916
  43.8 2.2 %copy-start.11 = (bf16[1024,2048]{1,0:T(8,128)(2,1)S(1)}, bf16[1024,2048]{1,0:T(8,128)(2,1)}, u32[]{:S(2)}) copy-start(bf16[1024,2048]{1,0:T(8,128)(2,1)} %copy-done.10) | copy-start | bytes 12582916
  54.3 1.2 collective-permute-start.7
  55.6 3.3 %collective-permute-start.10 = (f32[1,8,128]{2,1,0:T(8,128)S(1)}, f32[1,8,128]{2,1,0:T(8,128)S(1)}, u32[]{:S(2)}, u32[]{:S(2)}) collective-permute-start(f32[1,8,128]{2,1,0:T(8,128)S(1)} %add.7.refs_2_), channel_id=1, source_target_pairs={{0,96},{32,0},{64,32},{96,64},{1,97},{33,1},{65,33},{97,65},{2,98}... | collective-permute-start | bytes 12296 | tf_op jit(solution)/shard_map/ppermute | solution.py:400
  57.6 4.4 %collective-permute-start.9 = (f32[1,8,128]{2,1,0:T(8,128)S(1)}, f32[1,8,128]{2,1,0:T(8,128)S(1)}, u32[]{:S(2)}, u32[]{:S(2)}) collective-permute-start(f32[1,8,128]{2,1,0:T(8,128)S(1)} %add.7.refs_2_), channel_id=1, source_target_pairs={{0,64},{32,96},{64,0},{96,32},{1,65},{33,97},{65,1},{97,33},{2,66}... | collective-permute-start | bytes 12296 | tf_op jit(solution)/shard_map/ppermute | solution.py:400
  58.8 4.0 %collective-permute-start.8 = (f32[1,8,128]{2,1,0:T(8,128)S(1)}, f32[1,8,128]{2,1,0:T(8,128)S(1)}, u32[]{:S(2)}, u32[]{:S(2)}) collective-permute-start(f32[1,8,128]{2,1,0:T(8,128)S(1)} %add.7.refs_2_), channel_id=1, source_target_pairs={{0,32},{32,64},{64,96},{96,0},{1,33},{33,65},{65,97},{97,1},{2,34}... | collective-permute-start | bytes 12296 | tf_op jit(solution)/shard_map/ppermute | solution.py:400
  70.8 29.9 %all-to-all-start = ((f16[16,64,1024]{2,1,0:T(8,128)(2,1)}), f16[16,64,1024]{2,1,0:T(8,128)(2,1)S(1)}, u32[]{:S(2)}, u32[]{:S(2)}) async-start(f16[16,64,1024]{2,1,0:T(8,128)(2,1)} %convert_element_type.14), calls=%async_computation | async-start | bytes 4194304 | tf_op jit(solution)/shard_map/all_to_all | solution.py:403
  83.0 2.0 %copy-start = (f32[16,64,1024]{2,1,0:T(8,128)}, f32[16,64,1024]{2,1,0:T(8,128)S(1)}, u32[]{:S(2)}) copy-start(f32[16,64,1024]{2,1,0:T(8,128)S(1)} %convert_element_type.16.v_ref.refs_0_) | copy-start | bytes 12582916
  84.9 40.7 %copy-start.4 = (f32[64,1024]{1,0:T(8,128)S(1)}, f32[64,1024]{1,0:T(8,128)}, u32[]{:S(2)}) copy-start(f32[64,1024]{1,0:T(8,128)} %refs_1_.1) | copy-start | bytes 786436
  84.9 40.7 %copy-start.5 = (f32[64,1024]{1,0:T(8,128)S(1)}, f32[64,1024]{1,0:T(8,128)}, u32[]{:S(2)}) copy-start(f32[64,1024]{1,0:T(8,128)} %refs_2_.1) | copy-start | bytes 786436
  84.9 40.7 %copy-start.6 = (f32[64,1024]{1,0:T(8,128)S(1)}, f32[64,1024]{1,0:T(8,128)}, u32[]{:S(2)}) copy-start(f32[64,1024]{1,0:T(8,128)} %refs_4_.1) | copy-start | bytes 786436
  84.9 40.7 %copy-start.7 = (f32[64,1024]{1,0:T(8,128)S(1)}, f32[64,1024]{1,0:T(8,128)}, u32[]{:S(2)}) copy-start(f32[64,1024]{1,0:T(8,128)} %refs_5_.1) | copy-start | bytes 786436
  100.7 25.0 %copy-start.1 = (f32[16,64,1024]{2,1,0:T(8,128)S(1)}, f32[16,64,1024]{2,1,0:T(8,128)}, u32[]{:S(2)}) copy-start(f32[16,64,1024]{2,1,0:T(8,128)} %copy-done) | copy-start | bytes 12582916

commit v10 on v9

--- a/solution.py
+++ b/solution.py
@@ -430,7 +430,8 @@
     key_vector = gram(place, key_v, key_norm, [], (2, 128))
     value_v = value_all.astype(jnp.float32)
     vectors = gram(backwards_place, value_v, value_norm, [key_vector], (shard_count * replicas, 4, 128))
-    totals = lax.all_to_all(vectors, ("shard", "rep"), 0, 0)
+    everyone = list(range(shard_count * replicas))[::-1]
+    totals = lax.all_to_all(vectors, ("shard", "rep"), 0, 0, axis_index_groups=[everyone])
     new_key_weight, new_key_moment, new_value_weight, new_value_moment = update(
         totals, key_v, key_weight, key_moment, value_v, value_weight, value_moment
     )

time: 129 us -> 130 us (level)
  no operation moved by 1% of the time
where the time goes in v10:
time: 130 us; the launch traced here: 129 us
  Pallas kernels  44.1 us (34%)
  starting transfers between devices  24.5 us (19%)
  waiting for transfers between devices  23.8 us (18%)
  blocking collectives  21.1 us (16%)
  local copies, waits for them, and re-layouts  8.54 us (7%)
  other arithmetic  6.35 us (5%)
    all_to_all x1, blocking collectives, shards(): lax.all_to_all(vectors, ('shard', 'rep'), 0, 0, axis_index_groups=[everyo...  21.1 us
    all_to_all x2, waiting for transfers between devices, gathered(): return lax.all_to_all(sent, 'rep', 0, 0, axis_index_groups=groups)  18.3 us
    all_to_all x2, starting transfers between devices, gathered(): return lax.all_to_all(sent, 'rep', 0, 0, axis_index_groups=groups)  14.1 us
    pallas_call x3, Pallas kernels, grad(): pl.pallas_call(functools.partial(grad_kernel, start=start), out_shape=jax...  11.4 us
    unnamed x24, local copies, waits for them, and re-layouts  8.54 us
    pallas_call x1, Pallas kernels, grad_and_pair_sums(): pl.pallas_call(functools.partial(grad_pair_kernel, steps=b[0].shape[0] //...  8.33 us
    pallas_call x1, Pallas kernels, split_and_grad(): pl.pallas_call(split_kernel, out_shape=(jax.ShapeDtypeStruct((CHIPS, ROWS...  7.8 us
    pallas_call x2, Pallas kernels, gram(): pl.pallas_call(gram_kernel, out_shape=jax.ShapeDtypeStruct(out_dims, jnp....  7.31 us
  transfers between devices with their start and end apart: 13, of which 6 were waited for; matrix products, arithmetic and copies ran while one was open for 5% of the time, Pallas kernels for 21%

profile of v10, /device:TPU:1, one launch (start us, length us, event | category | flops | bytes accessed | tf_op | source)
XLA Modules:
  0.0 129.3 jit_solution(14225191972909675803)
XLA Ops:
  0.6 2.2 %copy-done.8 = bf16[2048,1024]{1,0:T(8,128)(2,1)S(1)} copy-done((bf16[2048,1024]{1,0:T(8,128)(2,1)S(1)}, bf16[2048,1024]{1,0:T(8,128)(2,1)}, u32[]{:S(2)}) %copy-start.8) | copy-done | bytes 4194328
  2.8 7.8 %shard_map.102 = (f32[16,64,1024]{2,1,0:T(8,128)S(1)}, bf16[1024,2048]{1,0:T(8,128)(2,1)S(1)}, bf16[1024,2048]{1,0:T(8,128)(2,1)S(1)}) custom-call(s32[1]{0:T(128)} %bitcast.2.core_ref, bf16[2048,2048]{1,0:T(8,128)(2,1)} %x_hbm.1, bf16[2048,1024]{1,0:T(8,128)(2,1)S(1)} %copy-done.8), custom_call_target="tpu_custom_call" | custom-call | flops 4294967296 | bytes 25165824 | tf_op jit(solution)/shard_map/pallas_call | solution.py:73
  10.6 1.5 %collective-permute-start = (f32[16,64,1024]{2,1,0:T(8,128)S(1)}, f32[16,64,1024]{2,1,0:T(8,128)S(1)}, u32[]{:S(2)}, u32[]{:S(2)}) collective-permute-start(f32[16,64,1024]{2,1,0:T(8,128)S(1)} %get-tuple-element.23), channel_id=1, source_target_pairs={{0,1},{1,0},{2,3},{3,2},{4,5},{5,4},{6,7},{7,6},{8,9},{9,8},{10,11... | collective-permute-start | bytes 12582920 | tf_op jit(solution)/shard_map/ppermute | solution.py:406
  12.2 5.0 %shard_map.103.refs_0_.a_ref = f32[16,64,1024]{2,1,0:T(8,128)S(1)} custom-call(bf16[1024,2048]{1,0:T(8,128)(2,1)S(1)} %get-tuple-element.28.x_ref, bf16[2048,1024]{1,0:T(8,128)(2,1)S(1)} %copy-done.9), custom_call_target="tpu_custom_call" | custom-call | flops 4294967296 | bytes 12582912 | tf_op jit(solution)/shard_map/pallas_call | solution.py:106
  17.2 2.5 %shard_map.104 = f32[8,64,1024]{2,1,0:T(8,128)S(1)} custom-call(bf16[1024,2048]{1,0:T(8,128)(2,1)S(1)} %get-tuple-element.29.x_ref, bf16[2048,1024]{1,0:T(8,128)(2,1)S(1)} %copy-done.2, f32[16,64,1024]{2,1,0:T(8,128)S(1)} %shard_map.103.refs_0_.a_ref), custom_call_target="tpu_custom_call" | custom-call | flops 2147483648 | bytes 12582912 | tf_op jit(solution)/shard_map/pallas_call | solution.py:106
  19.8 1.7 %shard_map.105 = f32[1,8,128]{2,1,0:T(8,128)S(1)} custom-call(s32[1]{0:T(128)} %bitcast.2.core_ref, f32[16,64,1024]{2,1,0:T(8,128)S(1)} %shard_map.103.refs_0_.a_ref, f32[16,64,1024]{2,1,0:T(8,128)S(1)} %collective-permute-done.refs_0_.refs_1_), custom_call_target="tpu_custom_call" | custom-call | flops 1048576 | bytes 1048576 | tf_op jit(solution)/shard_map/pallas_call | solution.py:167
  22.0 0.7 collective-permute-done.1
  22.7 2.6 %collective-permute-start.4 = (f32[1,8,128]{2,1,0:T(8,128)S(1)}, f32[1,8,128]{2,1,0:T(8,128)S(1)}, u32[]{:S(2)}, u32[]{:S(2)}) collective-permute-start(f32[1,8,128]{2,1,0:T(8,128)S(1)} %add.6.refs_1_), channel_id=1, source_target_pairs={{0,96},{32,0},{64,32},{96,64},{1,97},{33,1},{65,33},{97,65},{2,98}... | collective-permute-start | bytes 12296 | tf_op jit(solution)/shard_map/ppermute | solution.py:400
  26.4 3.8 %shard_map.107 = f32[8,64,1024]{2,1,0:T(8,128)} custom-call(bf16[1024,2048]{1,0:T(8,128)(2,1)S(1)} %get-tuple-element.29.x_ref, bf16[2048,1024]{1,0:T(8,128)(2,1)S(1)} %copy-done.2, f32[16,64,1024]{2,1,0:T(8,128)S(1)} %shard_map.103.refs_0_.a_ref, f32[16,64,1024]{2,1,0:T(8,128)S(1)} %collective-permute-done.refs_0_.refs_1_), custom_call_target="tpu_custom_call" | custom-call | flops 2147483648 | bytes 12582912 | tf_op jit(solution)/shard_map/pallas_call | solution.py:106
  30.2 0.6 shard_map.106
  30.9 1.8 %convert_element_type.13 = f16[16,64,1024]{2,1,0:T(8,128)(2,1)} convert(f32[16,64,1024]{2,1,0:T(8,128)S(1)} %get-tuple-element.27) | non-fusion elementwise | flops 1048576 | bytes 6291456 | tf_op jit(solution)/shard_map/convert_element_type | solution.py:415
  32.7 1.1 collective-permute-start.6
  33.8 7.8 %all-to-all-start.1 = ((f16[16,64,1024]{2,1,0:T(8,128)(2,1)}), f16[16,64,1024]{2,1,0:T(8,128)(2,1)}, u32[]{:S(2)}, u32[]{:S(2)}) async-start(f16[16,64,1024]{2,1,0:T(8,128)(2,1)} %convert_element_type.13), calls=%async_computation.1 | async-start | bytes 4194304 | tf_op jit(solution)/shard_map/all_to_all | solution.py:403
  41.6 2.2 %copy-done.3 = bf16[2048,1024]{1,0:T(8,128)(2,1)S(1)} copy-done((bf16[2048,1024]{1,0:T(8,128)(2,1)S(1)}, bf16[2048,1024]{1,0:T(8,128)(2,1)}, u32[]{:S(2)}) %copy-start.3) | copy-done | bytes 4194328
  43.8 2.2 %copy-done.11 = bf16[1024,2048]{1,0:T(8,128)(2,1)S(1)} copy-done((bf16[1024,2048]{1,0:T(8,128)(2,1)S(1)}, bf16[1024,2048]{1,0:T(8,128)(2,1)}, u32[]{:S(2)}) %copy-start.11) | copy-done | bytes 4194328
  46.0 8.3 %shard_map.108 = (f32[16,64,1024]{2,1,0:T(8,128)S(1)}, f32[1,8,128]{2,1,0:T(8,128)S(1)}) custom-call(s32[1]{0:T(128)} %bitcast.2.core_ref, bf16[1024,2048]{1,0:T(8,128)(2,1)S(1)} %copy-done.11, bf16[2048,1024]{1,0:T(8,128)(2,1)S(1)} %copy-done.3, f32[8,64,1024]{2,1,0:T(8,128)} %collective-permute-done.5.refs_0_, f32[8,64,1024]{2,1,0:T(8,128)} %collective-permute-done.6.refs_1_), custom_call_target="tpu_custom_call" | custom-call | flops 4294967296 | bytes 16777216 | tf_op jit(solution)/shard_map/pallas_call | solution.py:188
  54.7 0.9 collective-permute-done.7
  55.6 2.0 %collective-permute-start.10 = (f32[1,8,128]{2,1,0:T(8,128)S(1)}, f32[1,8,128]{2,1,0:T(8,128)S(1)}, u32[]{:S(2)}, u32[]{:S(2)}) collective-permute-start(f32[1,8,128]{2,1,0:T(8,128)S(1)} %add.7.refs_2_), channel_id=1, source_target_pairs={{0,96},{32,0},{64,32},{96,64},{1,97},{33,1},{65,33},{97,65},{2,98}... | collective-permute-start | bytes 12296 | tf_op jit(solution)/shard_map/ppermute | solution.py:400
  57.6 1.3 collective-permute-start.9
  58.8 3.1 %collective-permute-done.9.refs_4_ = f32[1,8,128]{2,1,0:T(8,128)S(1)} collective-permute-done((f32[1,8,128]{2,1,0:T(8,128)S(1)}, f32[1,8,128]{2,1,0:T(8,128)S(1)}, u32[]{:S(2)}, u32[]{:S(2)}) %collective-permute-start.9) | collective-permute-done | bytes 4128 | tf_op jit(solution)/shard_map/ppermute | solution.py:400
  61.9 0.9 collective-permute-done.8.refs_3_
  62.8 3.6 %shard_map.109 = (f32[16,64,1024]{2,1,0:T(8,128)S(1)}, f32[8,128]{1,0:T(8,128)S(1)}) custom-call(s32[1]{0:T(128)} %bitcast.2.core_ref, f32[16,64,1024]{2,1,0:T(8,128)S(1)} %get-tuple-element.31.a_ref, f32[8,64,1024]{2,1,0:T(8,128)} %collective-permute-done.5.refs_0_, f32[8,64,1024]{2,1,0:T(8,128)} %collective-permute-done.6.refs_1_, ...), custom_call_target="tpu_custom_call" | custom-call | flops 1048576 | bytes 1048576 | tf_op jit(solution)/shard_map/pallas_call | solution.py:233
  66.4 1.8 %convert_element_type.14 = f16[16,64,1024]{2,1,0:T(8,128)(2,1)} convert(f32[16,64,1024]{2,1,0:T(8,128)S(1)} %get-tuple-element.33) | non-fusion elementwise | flops 1048576 | bytes 6291456 | tf_op jit(solution)/shard_map/convert_element_type | solution.py:427
  68.2 2.5 %all-to-all-done.1 = f16[16,64,1024]{2,1,0:T(8,128)(2,1)} async-done(((f16[16,64,1024]{2,1,0:T(8,128)(2,1)}), f16[16,64,1024]{2,1,0:T(8,128)(2,1)}, u32[]{:S(2)}, u32[]{:S(2)}) %all-to-all-start.1) | async-done | bytes 2097184 | tf_op jit(solution)/shard_map/all_to_all | solution.py:403
  70.8 6.3 %all-to-all-start = ((f16[16,64,1024]{2,1,0:T(8,128)(2,1)}), f16[16,64,1024]{2,1,0:T(8,128)(2,1)S(1)}, u32[]{:S(2)}, u32[]{:S(2)}) async-start(f16[16,64,1024]{2,1,0:T(8,128)(2,1)} %convert_element_type.14), calls=%async_computation | async-start | bytes 4194304 | tf_op jit(solution)/shard_map/all_to_all | solution.py:403
  77.2 2.1 %convert_element_type.16.v_ref.refs_0_ = f32[16,64,1024]{2,1,0:T(8,128)S(1)} convert(f16[16,64,1024]{2,1,0:T(8,128)(2,1)} %all-to-all-done.1) | non-fusion elementwise | flops 1048576 | bytes 6291456 | tf_op jit(solution)/shard_map/convert_element_type | solution.py:429
  79.3 3.6 %shard_map.110.refs_0_ = f32[2,128]{1,0:T(2,128)S(1)} custom-call(s32[2]{0:T(128)S(1)} %pad_add_fusion.1.place_ref, f32[16,64,1024]{2,1,0:T(8,128)S(1)} %convert_element_type.16.v_ref.refs_0_, f32[8,128]{1,0:T(8,128)S(1)} %get-tuple-element.35.norm_ref), custom_call_target="tpu_custom_call" | custom-call | flops 20971520 | bytes 4194304 | tf_op jit(solution)/shard_map/pallas_call | solution.py:289
  83.0 2.0 %copy-done = f32[16,64,1024]{2,1,0:T(8,128)} copy-done((f32[16,64,1024]{2,1,0:T(8,128)}, f32[16,64,1024]{2,1,0:T(8,128)S(1)}, u32[]{:S(2)}) %copy-start) | copy-done | bytes 4194328
  84.9 15.7 %all-to-all-done = f16[16,64,1024]{2,1,0:T(8,128)(2,1)S(1)} async-done(((f16[16,64,1024]{2,1,0:T(8,128)(2,1)}), f16[16,64,1024]{2,1,0:T(8,128)(2,1)S(1)}, u32[]{:S(2)}, u32[]{:S(2)}) %all-to-all-start) | async-done | bytes 2097184 | tf_op jit(solution)/shard_map/all_to_all | solution.py:403
  101.2 3.7 %shard_map.111 = f32[128,4,128]{2,1,0:T(4,128)S(1)} custom-call(s32[2]{0:T(128)S(1)} %pad_add_fusion.place_ref, f32[16,64,1024]{2,1,0:T(8,128)S(1)} %convert_element_type.15.v_ref.refs_3_, f32[8,128]{1,0:T(8,128)S(1)} %get-tuple-element.34.norm_ref, f32[2,128]{1,0:T(2,128)S(1)} %shard_map.110.refs_0_), custom_call_target="tpu_custom_call" | custom-call | flops 20971520 | bytes 4194304 | tf_op jit(solution)/shard_map/pallas_call | solution.py:289
  104.9 21.1 %all_to_all.15.totals_ref = f32[128,4,128]{2,1,0:T(4,128)S(1)} all-to-all(f32[128,4,128]{2,1,0:T(4,128)S(1)} %shard_map.111), channel_id=1, replica_groups={{127,126,125,124,123,122,121,120,119,118,117,116,115,114,113,112,111,11..., dimensions={0} | all-to-all | bytes 524288 | tf_op jit(solution)/shard_map/all_to_all | solution.py:434
  125.9 3.2 %shard_map.112 = (f32[64,1024]{1,0:T(8,128)}, f32[64,1024]{1,0:T(8,128)}, f32[64,1024]{1,0:T(8,128)}, f32[64,1024]{1,0:T(8,128)}) custom-call(f32[128,4,128]{2,1,0:T(4,128)S(1)} %all_to_all.15.totals_ref, f32[16,64,1024]{2,1,0:T(8,128)S(1)} %copy-done.1, f32[64,1024]{1,0:T(8,128)S(1)} %copy-done.4, f32[64,1024]{1,0:T(8,128)S(1)} %copy-done.5, ...), custom_call_target="tpu_custom_call" | custom-call | flops 8388608 | bytes 10485760 | tf_op jit(solution)/shard_map/pallas_call | solution.py:363
  (38 shorter events, 2.7 us)
Async XLA Ops:
  0.6 2.2 %copy-start.8 = (bf16[2048,1024]{1,0:T(8,128)(2,1)S(1)}, bf16[2048,1024]{1,0:T(8,128)(2,1)}, u32[]{:S(2)}) copy-start(bf16[2048,1024]{1,0:T(8,128)(2,1)} %y_ref.4) | copy-start | bytes 12582916
  2.8 9.3 %copy-start.9 = (bf16[2048,1024]{1,0:T(8,128)(2,1)S(1)}, bf16[2048,1024]{1,0:T(8,128)(2,1)}, u32[]{:S(2)}) copy-start(bf16[2048,1024]{1,0:T(8,128)(2,1)} %y_ref.4) | copy-start | bytes 12582916
  10.6 6.6 %copy-start.10 = (bf16[1024,2048]{1,0:T(8,128)(2,1)}, bf16[1024,2048]{1,0:T(8,128)(2,1)S(1)}, u32[]{:S(2)}) copy-start(bf16[1024,2048]{1,0:T(8,128)(2,1)S(1)} %get-tuple-element.28.x_ref) | copy-start | bytes 12582916
  10.6 9.1 %collective-permute-start = (f32[16,64,1024]{2,1,0:T(8,128)S(1)}, f32[16,64,1024]{2,1,0:T(8,128)S(1)}, u32[]{:S(2)}, u32[]{:S(2)}) collective-permute-start(f32[16,64,1024]{2,1,0:T(8,128)S(1)} %get-tuple-element.23), channel_id=1, source_target_pairs={{0,1},{1,0},{2,3},{3,2},{4,5},{5,4},{6,7},{7,6},{8,9},{9,8},{10,11... | collective-permute-start | bytes 12582920 | tf_op jit(solution)/shard_map/ppermute | solution.py:406
  12.2 5.1 %copy-start.2 = (bf16[2048,1024]{1,0:T(8,128)(2,1)S(1)}, bf16[2048,1024]{1,0:T(8,128)(2,1)}, u32[]{:S(2)}) copy-start(bf16[2048,1024]{1,0:T(8,128)(2,1)} %y_ref.7) | copy-start | bytes 12582916
  21.5 1.2 collective-permute-start.1
  21.6 20.0 %collective-permute-start.5 = (f32[8,64,1024]{2,1,0:T(8,128)S(1)}, f32[8,64,1024]{2,1,0:T(8,128)}, u32[]{:S(2)}, u32[]{:S(2)}) collective-permute-start(f32[8,64,1024]{2,1,0:T(8,128)S(1)} %shard_map.104), channel_id=1, source_target_pairs={{0,1},{1,0},{2,3},{3,2},{4,5},{5,4},{6,7},{7,6},{8,9},{9,8},{10,11... | collective-permute-start | bytes 6291464 | tf_op jit(solution)/shard_map/ppermute | solution.py:419
  22.7 7.5 %collective-permute-start.4 = (f32[1,8,128]{2,1,0:T(8,128)S(1)}, f32[1,8,128]{2,1,0:T(8,128)S(1)}, u32[]{:S(2)}, u32[]{:S(2)}) collective-permute-start(f32[1,8,128]{2,1,0:T(8,128)S(1)} %add.6.refs_1_), channel_id=1, source_target_pairs={{0,96},{32,0},{64,32},{96,64},{1,97},{33,1},{65,33},{97,65},{2,98}... | collective-permute-start | bytes 12296 | tf_op jit(solution)/shard_map/ppermute | solution.py:400
  25.3 4.9 %collective-permute-start.3 = (f32[1,8,128]{2,1,0:T(8,128)S(1)}, f32[1,8,128]{2,1,0:T(8,128)S(1)}, u32[]{:S(2)}, u32[]{:S(2)}) collective-permute-start(f32[1,8,128]{2,1,0:T(8,128)S(1)} %add.6.refs_1_), channel_id=1, source_target_pairs={{0,64},{32,96},{64,0},{96,32},{1,65},{33,97},{65,1},{97,33},{2,66}... | collective-permute-start | bytes 12296 | tf_op jit(solution)/shard_map/ppermute | solution.py:400
  25.8 4.4 %collective-permute-start.2 = (f32[1,8,128]{2,1,0:T(8,128)S(1)}, f32[1,8,128]{2,1,0:T(8,128)S(1)}, u32[]{:S(2)}, u32[]{:S(2)}) collective-permute-start(f32[1,8,128]{2,1,0:T(8,128)S(1)} %add.6.refs_1_), channel_id=1, source_target_pairs={{0,32},{32,64},{64,96},{96,0},{1,33},{33,65},{65,97},{97,1},{2,34}... | collective-permute-start | bytes 12296 | tf_op jit(solution)/shard_map/ppermute | solution.py:400
  32.7 8.9 %collective-permute-start.6 = (f32[8,64,1024]{2,1,0:T(8,128)}, f32[8,64,1024]{2,1,0:T(8,128)}, u32[]{:S(2)}, u32[]{:S(2)}) collective-permute-start(f32[8,64,1024]{2,1,0:T(8,128)} %shard_map.107), channel_id=1, source_target_pairs={{0,1},{1,0},{2,3},{3,2},{4,5},{5,4},{6,7},{7,6},{8,9},{9,8},{10,11... | collective-permute-start | bytes 6291464 | tf_op jit(solution)/shard_map/ppermute | solution.py:420
  33.8 37.0 %all-to-all-start.1 = ((f16[16,64,1024]{2,1,0:T(8,128)(2,1)}), f16[16,64,1024]{2,1,0:T(8,128)(2,1)}, u32[]{:S(2)}, u32[]{:S(2)}) async-start(f16[16,64,1024]{2,1,0:T(8,128)(2,1)} %convert_element_type.13), calls=%async_computation.1 | async-start | bytes 4194304 | tf_op jit(solution)/shard_map/all_to_all | solution.py:403
  41.6 2.2 %copy-start.3 = (bf16[2048,1024]{1,0:T(8,128)(2,1)S(1)}, bf16[2048,1024]{1,0:T(8,128)(2,1)}, u32[]{:S(2)}) copy-start(bf16[2048,1024]{1,0:T(8,128)(2,1)} %y_ref.7) | copy-start | bytes 12582916
  43.8 2.2 %copy-start.11 = (bf16[1024,2048]{1,0:T(8,128)(2,1)S(1)}, bf16[1024,2048]{1,0:T(8,128)(2,1)}, u32[]{:S(2)}) copy-start(bf16[1024,2048]{1,0:T(8,128)(2,1)} %copy-done.10) | copy-start | bytes 12582916
  54.3 1.2 collective-permute-start.7
  55.6 3.3 %collective-permute-start.10 = (f32[1,8,128]{2,1,0:T(8,128)S(1)}, f32[1,8,128]{2,1,0:T(8,128)S(1)}, u32[]{:S(2)}, u32[]{:S(2)}) collective-permute-start(f32[1,8,128]{2,1,0:T(8,128)S(1)} %add.7.refs_2_), channel_id=1, source_target_pairs={{0,96},{32,0},{64,32},{96,64},{1,97},{33,1},{65,33},{97,65},{2,98}... | collective-permute-start | bytes 12296 | tf_op jit(solution)/shard_map/ppermute | solution.py:400
  57.6 4.4 %collective-permute-start.9 = (f32[1,8,128]{2,1,0:T(8,128)S(1)}, f32[1,8,128]{2,1,0:T(8,128)S(1)}, u32[]{:S(2)}, u32[]{:S(2)}) collective-permute-start(f32[1,8,128]{2,1,0:T(8,128)S(1)} %add.7.refs_2_), channel_id=1, source_target_pairs={{0,64},{32,96},{64,0},{96,32},{1,65},{33,97},{65,1},{97,33},{2,66}... | collective-permute-start | bytes 12296 | tf_op jit(solution)/shard_map/ppermute | solution.py:400
  58.8 4.0 %collective-permute-start.8 = (f32[1,8,128]{2,1,0:T(8,128)S(1)}, f32[1,8,128]{2,1,0:T(8,128)S(1)}, u32[]{:S(2)}, u32[]{:S(2)}) collective-permute-start(f32[1,8,128]{2,1,0:T(8,128)S(1)} %add.7.refs_2_), channel_id=1, source_target_pairs={{0,32},{32,64},{64,96},{96,0},{1,33},{33,65},{65,97},{97,1},{2,34}... | collective-permute-start | bytes 12296 | tf_op jit(solution)/shard_map/ppermute | solution.py:400
  70.8 29.9 %all-to-all-start = ((f16[16,64,1024]{2,1,0:T(8,128)(2,1)}), f16[16,64,1024]{2,1,0:T(8,128)(2,1)S(1)}, u32[]{:S(2)}, u32[]{:S(2)}) async-start(f16[16,64,1024]{2,1,0:T(8,128)(2,1)} %convert_element_type.14), calls=%async_computation | async-start | bytes 4194304 | tf_op jit(solution)/shard_map/all_to_all | solution.py:403
  83.0 2.0 %copy-start = (f32[16,64,1024]{2,1,0:T(8,128)}, f32[16,64,1024]{2,1,0:T(8,128)S(1)}, u32[]{:S(2)}) copy-start(f32[16,64,1024]{2,1,0:T(8,128)S(1)} %convert_element_type.16.v_ref.refs_0_) | copy-start | bytes 12582916
  84.9 41.0 %copy-start.4 = (f32[64,1024]{1,0:T(8,128)S(1)}, f32[64,1024]{1,0:T(8,128)}, u32[]{:S(2)}) copy-start(f32[64,1024]{1,0:T(8,128)} %refs_1_.1) | copy-start | bytes 786436
  84.9 41.0 %copy-start.5 = (f32[64,1024]{1,0:T(8,128)S(1)}, f32[64,1024]{1,0:T(8,128)}, u32[]{:S(2)}) copy-start(f32[64,1024]{1,0:T(8,128)} %refs_2_.1) | copy-start | bytes 786436
  84.9 41.0 %copy-start.6 = (f32[64,1024]{1,0:T(8,128)S(1)}, f32[64,1024]{1,0:T(8,128)}, u32[]{:S(2)}) copy-start(f32[64,1024]{1,0:T(8,128)} %refs_4_.1) | copy-start | bytes 786436
  84.9 41.0 %copy-start.7 = (f32[64,1024]{1,0:T(8,128)S(1)}, f32[64,1024]{1,0:T(8,128)}, u32[]{:S(2)}) copy-start(f32[64,1024]{1,0:T(8,128)} %refs_5_.1) | copy-start | bytes 786436
  100.7 25.3 %copy-start.1 = (f32[16,64,1024]{2,1,0:T(8,128)S(1)}, f32[16,64,1024]{2,1,0:T(8,128)}, u32[]{:S(2)}) copy-start(f32[16,64,1024]{2,1,0:T(8,128)} %copy-done) | copy-start | bytes 12582916

commit v11 on v10

--- a/solution.py
+++ b/solution.py
@@ -227,7 +227,7 @@
 def merge_pair(core, a, b, sums, backwards):
     steps = CHIPS // 4
     out_spec = pl.BlockSpec(
-        (4, ROWS, FEATURES), lambda i: (steps - 1 - i if backwards else i, 0, 0)
+        (4, ROWS, FEATURES), lambda i: (steps - 1 - i if backwards else (i + steps // 2) % steps, 0, 0)
     )
     spec = pl.BlockSpec((4, ROWS, FEATURES), lambda i: (i, 0, 0))
     return pl.pallas_call(
@@ -386,10 +386,11 @@
     index = lax.axis_index("rep").astype(jnp.int32)
     core = (index & 1)[None]
     leader = ((lax.axis_index("shard") == 0) & (index & 1 == 0)).astype(jnp.int32)
-    place = jnp.stack([index >> 1, leader])
+    place = jnp.stack([(index >> 1) ^ CHIPS // 2, leader])
     backwards_place = jnp.stack([CHIPS - 1 - (index >> 1), leader])
     swap = [(i, i ^ 1) for i in range(replicas)]
     core_groups = [list(range(c, replicas, 2)) for c in range(2)]
+    halves_groups = [group[CHIPS // 2 :] + group[: CHIPS // 2] for group in core_groups]
     backwards_groups = [group[::-1] for group in core_groups]
 
     def summed(sums):
@@ -413,7 +414,7 @@
     )
     key_merged, key_norm = merge_pair(core, key_own, key_arrived, key_sums, False)
     key_sent = key_merged.astype(jnp.float16)
-    key_all = gathered(key_sent, core_groups)
+    key_all = gathered(key_sent, halves_groups)
 
     value_arrived = [
         lax.ppermute(value_first, "rep", swap),

time: 130 us -> 130 us (level)
  waiting for transfers between devices: 23.8 us -> 21.3 us
  starting transfers between devices: 24.5 us -> 26.8 us
    all_to_all x2, waiting for transfers between devices: 18.3 us -> 15.8 us  [gathered(): return lax.all_to_all(sent, 'rep', 0, 0, axis_index_groups=groups)]
    all_to_all x2, starting transfers between devices: 14.1 us -> 16.1 us  [gathered(): return lax.all_to_all(sent, 'rep', 0, 0, axis_index_groups=groups)]
  transfers between devices with their start and end apart: 13 -> 13, of which waited for: 6 -> 5; matrix products, arithmetic and copies ran while one was open for 5% -> 5% of each run, Pallas kernels for 21% -> 21%
where the time goes in v11:
time: 130 us; the launch traced here: 129 us
  Pallas kernels  44.1 us (34%)
  starting transfers between devices  26.8 us (21%)
  waiting for transfers between devices  21.3 us (16%)
  blocking collectives  21.2 us (16%)
  local copies, waits for them, and re-layouts  8.54 us (7%)
  other arithmetic  6.35 us (5%)
    all_to_all x1, blocking collectives, shards(): lax.all_to_all(vectors, ('shard', 'rep'), 0, 0, axis_index_groups=[everyo...  21.2 us
    all_to_all x2, starting transfers between devices, gathered(): return lax.all_to_all(sent, 'rep', 0, 0, axis_index_groups=groups)  16.1 us
    all_to_all x2, waiting for transfers between devices, gathered(): return lax.all_to_all(sent, 'rep', 0, 0, axis_index_groups=groups)  15.8 us
    pallas_call x3, Pallas kernels, grad(): pl.pallas_call(functools.partial(grad_kernel, start=start), out_shape=jax...  11.4 us
    unnamed x24, local copies, waits for them, and re-layouts  8.54 us
    pallas_call x1, Pallas kernels, grad_and_pair_sums(): pl.pallas_call(functools.partial(grad_pair_kernel, steps=b[0].shape[0] //...  8.33 us
    pallas_call x1, Pallas kernels, split_and_grad(): pl.pallas_call(split_kernel, out_shape=(jax.ShapeDtypeStruct((CHIPS, ROWS...  7.8 us
    pallas_call x2, Pallas kernels, gram(): pl.pallas_call(gram_kernel, out_shape=jax.ShapeDtypeStruct(out_dims, jnp....  7.31 us
  transfers between devices with their start and end apart: 13, of which 5 were waited for; matrix products, arithmetic and copies ran while one was open for 5% of the time, Pallas kernels for 21%

profile of v11, /device:TPU:1, one launch (start us, length us, event | category | flops | bytes accessed | tf_op | source)
XLA Modules:
  0.0 129.2 jit_solution(14209384367078970323)
XLA Ops:
  0.6 2.2 %copy-done.8 = bf16[2048,1024]{1,0:T(8,128)(2,1)S(1)} copy-done((bf16[2048,1024]{1,0:T(8,128)(2,1)S(1)}, bf16[2048,1024]{1,0:T(8,128)(2,1)}, u32[]{:S(2)}) %copy-start.8) | copy-done | bytes 4194328
  2.8 7.8 %shard_map.102 = (f32[16,64,1024]{2,1,0:T(8,128)S(1)}, bf16[1024,2048]{1,0:T(8,128)(2,1)S(1)}, bf16[1024,2048]{1,0:T(8,128)(2,1)S(1)}) custom-call(s32[1]{0:T(128)} %bitcast.2.core_ref, bf16[2048,2048]{1,0:T(8,128)(2,1)} %x_hbm.1, bf16[2048,1024]{1,0:T(8,128)(2,1)S(1)} %copy-done.8), custom_call_target="tpu_custom_call" | custom-call | flops 4294967296 | bytes 25165824 | tf_op jit(solution)/shard_map/pallas_call | solution.py:73
  10.6 1.5 %collective-permute-start = (f32[16,64,1024]{2,1,0:T(8,128)S(1)}, f32[16,64,1024]{2,1,0:T(8,128)S(1)}, u32[]{:S(2)}, u32[]{:S(2)}) collective-permute-start(f32[16,64,1024]{2,1,0:T(8,128)S(1)} %get-tuple-element.23), channel_id=1, source_target_pairs={{0,1},{1,0},{2,3},{3,2},{4,5},{5,4},{6,7},{7,6},{8,9},{9,8},{10,11... | collective-permute-start | bytes 12582920 | tf_op jit(solution)/shard_map/ppermute | solution.py:407
  12.2 5.0 %shard_map.103.refs_0_.a_ref = f32[16,64,1024]{2,1,0:T(8,128)S(1)} custom-call(bf16[1024,2048]{1,0:T(8,128)(2,1)S(1)} %get-tuple-element.28.x_ref, bf16[2048,1024]{1,0:T(8,128)(2,1)S(1)} %copy-done.9), custom_call_target="tpu_custom_call" | custom-call | flops 4294967296 | bytes 12582912 | tf_op jit(solution)/shard_map/pallas_call | solution.py:106
  17.2 2.5 %shard_map.104 = f32[8,64,1024]{2,1,0:T(8,128)S(1)} custom-call(bf16[1024,2048]{1,0:T(8,128)(2,1)S(1)} %get-tuple-element.29.x_ref, bf16[2048,1024]{1,0:T(8,128)(2,1)S(1)} %copy-done.2, f32[16,64,1024]{2,1,0:T(8,128)S(1)} %shard_map.103.refs_0_.a_ref), custom_call_target="tpu_custom_call" | custom-call | flops 2147483648 | bytes 12582912 | tf_op jit(solution)/shard_map/pallas_call | solution.py:106
  19.8 1.7 %shard_map.105 = f32[1,8,128]{2,1,0:T(8,128)S(1)} custom-call(s32[1]{0:T(128)} %bitcast.2.core_ref, f32[16,64,1024]{2,1,0:T(8,128)S(1)} %shard_map.103.refs_0_.a_ref, f32[16,64,1024]{2,1,0:T(8,128)S(1)} %collective-permute-done.refs_0_.refs_1_), custom_call_target="tpu_custom_call" | custom-call | flops 1048576 | bytes 1048576 | tf_op jit(solution)/shard_map/pallas_call | solution.py:167
  22.0 0.7 collective-permute-done.1
  22.7 2.6 %collective-permute-start.4 = (f32[1,8,128]{2,1,0:T(8,128)S(1)}, f32[1,8,128]{2,1,0:T(8,128)S(1)}, u32[]{:S(2)}, u32[]{:S(2)}) collective-permute-start(f32[1,8,128]{2,1,0:T(8,128)S(1)} %add.6.refs_1_), channel_id=1, source_target_pairs={{0,96},{32,0},{64,32},{96,64},{1,97},{33,1},{65,33},{97,65},{2,98}... | collective-permute-start | bytes 12296 | tf_op jit(solution)/shard_map/ppermute | solution.py:401
  26.4 3.8 %shard_map.107 = f32[8,64,1024]{2,1,0:T(8,128)} custom-call(bf16[1024,2048]{1,0:T(8,128)(2,1)S(1)} %get-tuple-element.29.x_ref, bf16[2048,1024]{1,0:T(8,128)(2,1)S(1)} %copy-done.2, f32[16,64,1024]{2,1,0:T(8,128)S(1)} %shard_map.103.refs_0_.a_ref, f32[16,64,1024]{2,1,0:T(8,128)S(1)} %collective-permute-done.refs_0_.refs_1_), custom_call_target="tpu_custom_call" | custom-call | flops 2147483648 | bytes 12582912 | tf_op jit(solution)/shard_map/pallas_call | solution.py:106
  30.2 0.6 shard_map.106
  30.9 1.8 %convert_element_type.13 = f16[16,64,1024]{2,1,0:T(8,128)(2,1)} convert(f32[16,64,1024]{2,1,0:T(8,128)S(1)} %get-tuple-element.27) | non-fusion elementwise | flops 1048576 | bytes 6291456 | tf_op jit(solution)/shard_map/convert_element_type | solution.py:416
  32.7 1.1 collective-permute-start.6
  33.8 8.7 %all-to-all-start.1 = ((f16[16,64,1024]{2,1,0:T(8,128)(2,1)}), f16[16,64,1024]{2,1,0:T(8,128)(2,1)}, u32[]{:S(2)}, u32[]{:S(2)}) async-start(f16[16,64,1024]{2,1,0:T(8,128)(2,1)} %convert_element_type.13), calls=%async_computation.1 | async-start | bytes 4194304 | tf_op jit(solution)/shard_map/all_to_all | solution.py:404
  42.5 2.2 %copy-done.3 = bf16[2048,1024]{1,0:T(8,128)(2,1)S(1)} copy-done((bf16[2048,1024]{1,0:T(8,128)(2,1)S(1)}, bf16[2048,1024]{1,0:T(8,128)(2,1)}, u32[]{:S(2)}) %copy-start.3) | copy-done | bytes 4194328
  44.7 2.2 %copy-done.11 = bf16[1024,2048]{1,0:T(8,128)(2,1)S(1)} copy-done((bf16[1024,2048]{1,0:T(8,128)(2,1)S(1)}, bf16[1024,2048]{1,0:T(8,128)(2,1)}, u32[]{:S(2)}) %copy-start.11) | copy-done | bytes 4194328
  46.8 8.3 %shard_map.108 = (f32[16,64,1024]{2,1,0:T(8,128)S(1)}, f32[1,8,128]{2,1,0:T(8,128)S(1)}) custom-call(s32[1]{0:T(128)} %bitcast.2.core_ref, bf16[1024,2048]{1,0:T(8,128)(2,1)S(1)} %copy-done.11, bf16[2048,1024]{1,0:T(8,128)(2,1)S(1)} %copy-done.3, f32[8,64,1024]{2,1,0:T(8,128)} %collective-permute-done.5.refs_0_, f32[8,64,1024]{2,1,0:T(8,128)} %collective-permute-done.6.refs_1_), custom_call_target="tpu_custom_call" | custom-call | flops 4294967296 | bytes 16777216 | tf_op jit(solution)/shard_map/pallas_call | solution.py:188
  55.2 0.6 collective-permute-start.7
  55.8 0.8 collective-permute-done.7
  56.6 2.0 %collective-permute-start.10 = (f32[1,8,128]{2,1,0:T(8,128)S(1)}, f32[1,8,128]{2,1,0:T(8,128)S(1)}, u32[]{:S(2)}, u32[]{:S(2)}) collective-permute-start(f32[1,8,128]{2,1,0:T(8,128)S(1)} %add.7.refs_2_), channel_id=1, source_target_pairs={{0,96},{32,0},{64,32},{96,64},{1,97},{33,1},{65,33},{97,65},{2,98}... | collective-permute-start | bytes 12296 | tf_op jit(solution)/shard_map/ppermute | solution.py:401
  58.6 1.3 collective-permute-start.9
  59.9 3.1 %collective-permute-done.9.refs_4_ = f32[1,8,128]{2,1,0:T(8,128)S(1)} collective-permute-done((f32[1,8,128]{2,1,0:T(8,128)S(1)}, f32[1,8,128]{2,1,0:T(8,128)S(1)}, u32[]{:S(2)}, u32[]{:S(2)}) %collective-permute-start.9) | collective-permute-done | bytes 4128 | tf_op jit(solution)/shard_map/ppermute | solution.py:401
  63.0 1.0 collective-permute-done.8.refs_3_
  63.9 3.6 %shard_map.109 = (f32[16,64,1024]{2,1,0:T(8,128)S(1)}, f32[8,128]{1,0:T(8,128)S(1)}) custom-call(s32[1]{0:T(128)} %bitcast.2.core_ref, f32[16,64,1024]{2,1,0:T(8,128)S(1)} %get-tuple-element.31.a_ref, f32[8,64,1024]{2,1,0:T(8,128)} %collective-permute-done.5.refs_0_, f32[8,64,1024]{2,1,0:T(8,128)} %collective-permute-done.6.refs_1_, ...), custom_call_target="tpu_custom_call" | custom-call | flops 1048576 | bytes 1048576 | tf_op jit(solution)/shard_map/pallas_call | solution.py:233
  67.6 1.8 %convert_element_type.14 = f16[16,64,1024]{2,1,0:T(8,128)(2,1)} convert(f32[16,64,1024]{2,1,0:T(8,128)S(1)} %get-tuple-element.33) | non-fusion elementwise | flops 1048576 | bytes 6291456 | tf_op jit(solution)/shard_map/convert_element_type | solution.py:428
  69.4 7.4 %all-to-all-start = ((f16[16,64,1024]{2,1,0:T(8,128)(2,1)}), f16[16,64,1024]{2,1,0:T(8,128)(2,1)S(1)}, u32[]{:S(2)}, u32[]{:S(2)}) async-start(f16[16,64,1024]{2,1,0:T(8,128)(2,1)} %convert_element_type.14), calls=%async_computation | async-start | bytes 4194304 | tf_op jit(solution)/shard_map/all_to_all | solution.py:404
  77.0 2.1 %convert_element_type.16.v_ref.refs_0_ = f32[16,64,1024]{2,1,0:T(8,128)S(1)} convert(f16[16,64,1024]{2,1,0:T(8,128)(2,1)} %all-to-all-done.1) | non-fusion elementwise | flops 1048576 | bytes 6291456 | tf_op jit(solution)/shard_map/convert_element_type | solution.py:430
  79.1 3.6 %shard_map.110.refs_0_ = f32[2,128]{1,0:T(2,128)S(1)} custom-call(s32[2]{0:T(128)S(1)} %pad_add_fusion.1.place_ref, f32[16,64,1024]{2,1,0:T(8,128)S(1)} %convert_element_type.16.v_ref.refs_0_, f32[8,128]{1,0:T(8,128)S(1)} %get-tuple-element.35.norm_ref), custom_call_target="tpu_custom_call" | custom-call | flops 20971520 | bytes 4194304 | tf_op jit(solution)/shard_map/pallas_call | solution.py:289
  82.7 2.0 %copy-done = f32[16,64,1024]{2,1,0:T(8,128)} copy-done((f32[16,64,1024]{2,1,0:T(8,128)}, f32[16,64,1024]{2,1,0:T(8,128)S(1)}, u32[]{:S(2)}) %copy-start) | copy-done | bytes 4194328
  84.7 15.7 %all-to-all-done = f16[16,64,1024]{2,1,0:T(8,128)(2,1)S(1)} async-done(((f16[16,64,1024]{2,1,0:T(8,128)(2,1)}), f16[16,64,1024]{2,1,0:T(8,128)(2,1)S(1)}, u32[]{:S(2)}, u32[]{:S(2)}) %all-to-all-start) | async-done | bytes 2097184 | tf_op jit(solution)/shard_map/all_to_all | solution.py:404
  100.9 3.7 %shard_map.111 = f32[128,4,128]{2,1,0:T(4,128)S(1)} custom-call(s32[2]{0:T(128)S(1)} %pad_add_fusion.place_ref, f32[16,64,1024]{2,1,0:T(8,128)S(1)} %convert_element_type.15.v_ref.refs_3_, f32[8,128]{1,0:T(8,128)S(1)} %get-tuple-element.34.norm_ref, f32[2,128]{1,0:T(2,128)S(1)} %shard_map.110.refs_0_), custom_call_target="tpu_custom_call" | custom-call | flops 20971520 | bytes 4194304 | tf_op jit(solution)/shard_map/pallas_call | solution.py:289
  104.6 21.2 %all_to_all.15.totals_ref = f32[128,4,128]{2,1,0:T(4,128)S(1)} all-to-all(f32[128,4,128]{2,1,0:T(4,128)S(1)} %shard_map.111), channel_id=1, replica_groups={{127,126,125,124,123,122,121,120,119,118,117,116,115,114,113,112,111,11..., dimensions={0} | all-to-all | bytes 524288 | tf_op jit(solution)/shard_map/all_to_all | solution.py:435
  125.8 3.2 %shard_map.112 = (f32[64,1024]{1,0:T(8,128)}, f32[64,1024]{1,0:T(8,128)}, f32[64,1024]{1,0:T(8,128)}, f32[64,1024]{1,0:T(8,128)}) custom-call(f32[128,4,128]{2,1,0:T(4,128)S(1)} %all_to_all.15.totals_ref, f32[16,64,1024]{2,1,0:T(8,128)S(1)} %copy-done.1, f32[64,1024]{1,0:T(8,128)S(1)} %copy-done.4, f32[64,1024]{1,0:T(8,128)S(1)} %copy-done.5, ...), custom_call_target="tpu_custom_call" | custom-call | flops 8388608 | bytes 10485760 | tf_op jit(solution)/shard_map/pallas_call | solution.py:363
  (38 shorter events, 2.4 us)
Async XLA Ops:
  0.6 2.2 %copy-start.8 = (bf16[2048,1024]{1,0:T(8,128)(2,1)S(1)}, bf16[2048,1024]{1,0:T(8,128)(2,1)}, u32[]{:S(2)}) copy-start(bf16[2048,1024]{1,0:T(8,128)(2,1)} %y_ref.4) | copy-start | bytes 12582916
  2.8 9.3 %copy-start.9 = (bf16[2048,1024]{1,0:T(8,128)(2,1)S(1)}, bf16[2048,1024]{1,0:T(8,128)(2,1)}, u32[]{:S(2)}) copy-start(bf16[2048,1024]{1,0:T(8,128)(2,1)} %y_ref.4) | copy-start | bytes 12582916
  10.6 6.6 %copy-start.10 = (bf16[1024,2048]{1,0:T(8,128)(2,1)}, bf16[1024,2048]{1,0:T(8,128)(2,1)S(1)}, u32[]{:S(2)}) copy-start(bf16[1024,2048]{1,0:T(8,128)(2,1)S(1)} %get-tuple-element.28.x_ref) | copy-start | bytes 12582916
  10.6 9.1 %collective-permute-start = (f32[16,64,1024]{2,1,0:T(8,128)S(1)}, f32[16,64,1024]{2,1,0:T(8,128)S(1)}, u32[]{:S(2)}, u32[]{:S(2)}) collective-permute-start(f32[16,64,1024]{2,1,0:T(8,128)S(1)} %get-tuple-element.23), channel_id=1, source_target_pairs={{0,1},{1,0},{2,3},{3,2},{4,5},{5,4},{6,7},{7,6},{8,9},{9,8},{10,11... | collective-permute-start | bytes 12582920 | tf_op jit(solution)/shard_map/ppermute | solution.py:407
  12.2 5.1 %copy-start.2 = (bf16[2048,1024]{1,0:T(8,128)(2,1)S(1)}, bf16[2048,1024]{1,0:T(8,128)(2,1)}, u32[]{:S(2)}) copy-start(bf16[2048,1024]{1,0:T(8,128)(2,1)} %y_ref.7) | copy-start | bytes 12582916
  21.5 1.2 collective-permute-start.1
  21.6 20.9 %collective-permute-start.5 = (f32[8,64,1024]{2,1,0:T(8,128)S(1)}, f32[8,64,1024]{2,1,0:T(8,128)}, u32[]{:S(2)}, u32[]{:S(2)}) collective-permute-start(f32[8,64,1024]{2,1,0:T(8,128)S(1)} %shard_map.104), channel_id=1, source_target_pairs={{0,1},{1,0},{2,3},{3,2},{4,5},{5,4},{6,7},{7,6},{8,9},{9,8},{10,11... | collective-permute-start | bytes 6291464 | tf_op jit(solution)/shard_map/ppermute | solution.py:420
  22.7 7.5 %collective-permute-start.4 = (f32[1,8,128]{2,1,0:T(8,128)S(1)}, f32[1,8,128]{2,1,0:T(8,128)S(1)}, u32[]{:S(2)}, u32[]{:S(2)}) collective-permute-start(f32[1,8,128]{2,1,0:T(8,128)S(1)} %add.6.refs_1_), channel_id=1, source_target_pairs={{0,96},{32,0},{64,32},{96,64},{1,97},{33,1},{65,33},{97,65},{2,98}... | collective-permute-start | bytes 12296 | tf_op jit(solution)/shard_map/ppermute | solution.py:401
  25.3 4.9 %collective-permute-start.3 = (f32[1,8,128]{2,1,0:T(8,128)S(1)}, f32[1,8,128]{2,1,0:T(8,128)S(1)}, u32[]{:S(2)}, u32[]{:S(2)}) collective-permute-start(f32[1,8,128]{2,1,0:T(8,128)S(1)} %add.6.refs_1_), channel_id=1, source_target_pairs={{0,64},{32,96},{64,0},{96,32},{1,65},{33,97},{65,1},{97,33},{2,66}... | collective-permute-start | bytes 12296 | tf_op jit(solution)/shard_map/ppermute | solution.py:401
  25.8 4.4 %collective-permute-start.2 = (f32[1,8,128]{2,1,0:T(8,128)S(1)}, f32[1,8,128]{2,1,0:T(8,128)S(1)}, u32[]{:S(2)}, u32[]{:S(2)}) collective-permute-start(f32[1,8,128]{2,1,0:T(8,128)S(1)} %add.6.refs_1_), channel_id=1, source_target_pairs={{0,32},{32,64},{64,96},{96,0},{1,33},{33,65},{65,97},{97,1},{2,34}... | collective-permute-start | bytes 12296 | tf_op jit(solution)/shard_map/ppermute | solution.py:401
  32.7 9.8 %collective-permute-start.6 = (f32[8,64,1024]{2,1,0:T(8,128)}, f32[8,64,1024]{2,1,0:T(8,128)}, u32[]{:S(2)}, u32[]{:S(2)}) collective-permute-start(f32[8,64,1024]{2,1,0:T(8,128)} %shard_map.107), channel_id=1, source_target_pairs={{0,1},{1,0},{2,3},{3,2},{4,5},{5,4},{6,7},{7,6},{8,9},{9,8},{10,11... | collective-permute-start | bytes 6291464 | tf_op jit(solution)/shard_map/ppermute | solution.py:421
  33.8 35.6 %all-to-all-start.1 = ((f16[16,64,1024]{2,1,0:T(8,128)(2,1)}), f16[16,64,1024]{2,1,0:T(8,128)(2,1)}, u32[]{:S(2)}, u32[]{:S(2)}) async-start(f16[16,64,1024]{2,1,0:T(8,128)(2,1)} %convert_element_type.13), calls=%async_computation.1 | async-start | bytes 4194304 | tf_op jit(solution)/shard_map/all_to_all | solution.py:404
  42.5 2.2 %copy-start.3 = (bf16[2048,1024]{1,0:T(8,128)(2,1)S(1)}, bf16[2048,1024]{1,0:T(8,128)(2,1)}, u32[]{:S(2)}) copy-start(bf16[2048,1024]{1,0:T(8,128)(2,1)} %y_ref.7) | copy-start | bytes 12582916
  44.7 2.2 %copy-start.11 = (bf16[1024,2048]{1,0:T(8,128)(2,1)S(1)}, bf16[1024,2048]{1,0:T(8,128)(2,1)}, u32[]{:S(2)}) copy-start(bf16[1024,2048]{1,0:T(8,128)(2,1)} %copy-done.10) | copy-start | bytes 12582916
  55.2 1.4 %collective-permute-start.7 = (f32[1,8,128]{2,1,0:T(8,128)S(1)}, f32[1,8,128]{2,1,0:T(8,128)S(1)}, u32[]{:S(2)}, u32[]{:S(2)}) collective-permute-start(f32[1,8,128]{2,1,0:T(8,128)S(1)} %get-tuple-element.32), channel_id=1, source_target_pairs={{0,1},{1,0},{2,3},{3,2},{4,5},{5,4},{6,7},{7,6},{8,9},{9,8},{10,11... | collective-permute-start | bytes 12296 | tf_op jit(solution)/shard_map/ppermute | solution.py:397
  56.6 3.3 %collective-permute-start.10 = (f32[1,8,128]{2,1,0:T(8,128)S(1)}, f32[1,8,128]{2,1,0:T(8,128)S(1)}, u32[]{:S(2)}, u32[]{:S(2)}) collective-permute-start(f32[1,8,128]{2,1,0:T(8,128)S(1)} %add.7.refs_2_), channel_id=1, source_target_pairs={{0,96},{32,0},{64,32},{96,64},{1,97},{33,1},{65,33},{97,65},{2,98}... | collective-permute-start | bytes 12296 | tf_op jit(solution)/shard_map/ppermute | solution.py:401
  58.6 4.4 %collective-permute-start.9 = (f32[1,8,128]{2,1,0:T(8,128)S(1)}, f32[1,8,128]{2,1,0:T(8,128)S(1)}, u32[]{:S(2)}, u32[]{:S(2)}) collective-permute-start(f32[1,8,128]{2,1,0:T(8,128)S(1)} %add.7.refs_2_), channel_id=1, source_target_pairs={{0,64},{32,96},{64,0},{96,32},{1,65},{33,97},{65,1},{97,33},{2,66}... | collective-permute-start | bytes 12296 | tf_op jit(solution)/shard_map/ppermute | solution.py:401
  59.9 4.1 %collective-permute-start.8 = (f32[1,8,128]{2,1,0:T(8,128)S(1)}, f32[1,8,128]{2,1,0:T(8,128)S(1)}, u32[]{:S(2)}, u32[]{:S(2)}) collective-permute-start(f32[1,8,128]{2,1,0:T(8,128)S(1)} %add.7.refs_2_), channel_id=1, source_target_pairs={{0,32},{32,64},{64,96},{96,0},{1,33},{33,65},{65,97},{97,1},{2,34}... | collective-permute-start | bytes 12296 | tf_op jit(solution)/shard_map/ppermute | solution.py:401
  69.4 31.1 %all-to-all-start = ((f16[16,64,1024]{2,1,0:T(8,128)(2,1)}), f16[16,64,1024]{2,1,0:T(8,128)(2,1)S(1)}, u32[]{:S(2)}, u32[]{:S(2)}) async-start(f16[16,64,1024]{2,1,0:T(8,128)(2,1)} %convert_element_type.14), calls=%async_computation | async-start | bytes 4194304 | tf_op jit(solution)/shard_map/all_to_all | solution.py:404
  82.7 2.0 %copy-start = (f32[16,64,1024]{2,1,0:T(8,128)}, f32[16,64,1024]{2,1,0:T(8,128)S(1)}, u32[]{:S(2)}) copy-start(f32[16,64,1024]{2,1,0:T(8,128)S(1)} %convert_element_type.16.v_ref.refs_0_) | copy-start | bytes 12582916
  84.7 41.1 %copy-start.4 = (f32[64,1024]{1,0:T(8,128)S(1)}, f32[64,1024]{1,0:T(8,128)}, u32[]{:S(2)}) copy-start(f32[64,1024]{1,0:T(8,128)} %refs_1_.1) | copy-start | bytes 786436
  84.7 41.1 %copy-start.5 = (f32[64,1024]{1,0:T(8,128)S(1)}, f32[64,1024]{1,0:T(8,128)}, u32[]{:S(2)}) copy-start(f32[64,1024]{1,0:T(8,128)} %refs_2_.1) | copy-start | bytes 786436
  84.7 41.1 %copy-start.6 = (f32[64,1024]{1,0:T(8,128)S(1)}, f32[64,1024]{1,0:T(8,128)}, u32[]{:S(2)}) copy-start(f32[64,1024]{1,0:T(8,128)} %refs_4_.1) | copy-start | bytes 786436
  84.7 41.1 %copy-start.7 = (f32[64,1024]{1,0:T(8,128)S(1)}, f32[64,1024]{1,0:T(8,128)}, u32[]{:S(2)}) copy-start(f32[64,1024]{1,0:T(8,128)} %refs_5_.1) | copy-start | bytes 786436
  100.4 25.4 %copy-start.1 = (f32[16,64,1024]{2,1,0:T(8,128)S(1)}, f32[16,64,1024]{2,1,0:T(8,128)}, u32[]{:S(2)}) copy-start(f32[16,64,1024]{2,1,0:T(8,128)} %copy-done) | copy-start | bytes 12582916
